TPU v7x, 32 devices: a whole 2x2x4 slice. The times are simulated.
32 devices in a mesh: blk: 4 (over x, core), inner: 8 (over z, y).
Axes of the slice: x: 2, y: 2, z: 4, core: 2. Of those that a mesh axis runs over, the one named last changes fastest.
Arguments:
- queries: bfloat16 [8192, 4096], P(('blk', 'inner')), may hold values from -5 to 5
- keys: bfloat16 [8192, 512], P(('blk', 'inner')), may hold values from -5 to 5
- values: bfloat16 [8192, 512], P(('blk', 'inner')), may hold values from -6 to 6
- out_grad: bfloat16 [8192, 4096], P(('blk', 'inner')), may hold values from -6 to 6
- doc_lengths: int32 [16], replicated, may hold values from 1 to 768, 8192 in all
Outputs:
- attended: bfloat16 [8192, 4096], P(('blk', 'inner'))
- query_grad: bfloat16 [8192, 4096], P(('blk', 'inner'))
- key_grad: bfloat16 [8192, 512], P(('blk', 'inner'))
- value_grad: bfloat16 [8192, 512], P(('blk', 'inner'))
All inputs are finite; a program needn't handle non-finite values.
Results may differ from a plain program's by a relative error of at most 0.025.
Values may be sent and summed in bfloat16 or wider, within the bound.
No kernel may reach another device: no remote copies, remote signals or barrier semaphores. Data moves between devices by JAX's collectives and lax.ppermute only.
A program may use at most 128 MiB of HBM per device.

v0:
```python
import functools
import math

import jax
import jax.numpy as jnp
from jax import lax
from jax.experimental import pallas as pl
from jax.experimental.pallas import tpu as pltpu
from jax.sharding import PartitionSpec as P

HEAD_SIZE = 128
QUERY_HEADS = 32
KEY_VALUE_HEADS = 4
GROUP = QUERY_HEADS // KEY_VALUE_HEADS
SPAN = 4
AXES = ("blk", "inner")
CHUNK = 2
PAIR = 2
MASKED = -1e30
SCALE = 1.0 / math.sqrt(HEAD_SIZE)
EXP2_SCALE = SCALE * math.log2(math.e)

NN = (((1,), (0,)), ((), ()))
NT = (((1,), (1,)), ((), ()))
TN = (((0,), (0,)), ((), ()))


def dot(a, b, dims):
    return lax.dot_general(a, b, dims, preferred_element_type=jnp.float32)


def passed_along(value, steps):
    count = lax.axis_size("blk") * lax.axis_size("inner")
    first, last = (max(0, -steps), min(count, count - steps))
    return lax.ppermute(value, AXES, [(source, source + steps) for source in range(first, last)])


def write_bias(bias_ref, lengths_ref, first_ref, rows):
    docs = lengths_ref.shape[0]
    first = first_ref[0]
    query_pos = first + lax.broadcasted_iota(jnp.int32, (rows, 128), 0)

    def step(doc, carry):
        end, start = carry
        end = end + lengths_ref[doc]
        return end, jnp.where(query_pos >= end, end, start)

    _, start = lax.fori_loop(
        0, docs, step, (jnp.int32(0), jnp.zeros((rows, 128), jnp.int32))
    )
    lane = lax.broadcasted_iota(jnp.int32, (rows, 128), 1)
    for part in range(SPAN * rows // 128):
        key_pos = first - (SPAN - 1) * rows + part * 128 + lane
        allowed = (key_pos >= start) & (key_pos <= query_pos)
        bias_ref[:, part * 128 : (part + 1) * 128] = jnp.where(allowed, 0.0, MASKED)


def attention_kernel(
    first_ref,
    lengths_ref,
    q_ref,
    g_ref,
    far_ref,
    near_ref,
    own_ref,
    *refs,
):
    out_ref, dq_ref, dfar_ref, dnear_ref, down_ref, bias_ref, dk_ref, dv_ref = refs[-8:]
    rows = q_ref.shape[0]

    @pl.when(pl.program_id(0) == 0)
    def _():
        write_bias(bias_ref, lengths_ref, first_ref, rows)

    blocks = [far_ref.at[1], far_ref.at[0], near_ref, own_ref]

    def keys(j):
        return blocks[j][:, :HEAD_SIZE]

    def values(j):
        return blocks[j][:, HEAD_SIZE:]

    dk_ref[...] = jnp.zeros_like(dk_ref)
    dv_ref[...] = jnp.zeros_like(dv_ref)

    def pair_step(pair, carry):
        qs, gs, ps, ds, gls = [], [], [], [], []
        for sub in range(PAIR):
            cols = pl.ds(pl.multiple_of((pair * PAIR + sub) * HEAD_SIZE, HEAD_SIZE), HEAD_SIZE)
            q = q_ref[:, cols]
            g = g_ref[:, cols]
            s = [
                dot(q, keys(j), NT) * EXP2_SCALE + bias_ref[:, j * rows : (j + 1) * rows]
                for j in range(SPAN)
            ]
            m = jnp.max(functools.reduce(jnp.maximum, s), axis=1, keepdims=True)
            e = [jnp.exp2(x - m) for x in s]
            inv = 1.0 / jnp.sum(functools.reduce(jnp.add, e), axis=1, keepdims=True)
            p = [x.astype(jnp.bfloat16) for x in e]
            mixed = functools.reduce(jnp.add, [dot(p[j], values(j), NN) for j in range(SPAN)])
            out = (mixed * inv).astype(jnp.bfloat16)
            out_ref[:, cols] = out
            wide = g.astype(jnp.float32)
            delta = jnp.sum(wide * out.astype(jnp.float32), axis=1, keepdims=True) * inv
            gl = (wide * inv).astype(jnp.bfloat16)
            d = [
                (p[j].astype(jnp.float32) * (dot(gl, values(j), NT) - delta)).astype(jnp.bfloat16)
                for j in range(SPAN)
            ]
            dq = functools.reduce(jnp.add, [dot(d[j], keys(j), NN) for j in range(SPAN)])
            dq_ref[:, cols] = (dq * SCALE).astype(jnp.bfloat16)
            qs.append(q)
            gls.append(gl)
            ps.append(p)
            ds.append(d)
        for j in range(SPAN):
            span = slice(j * rows, (j + 1) * rows)
            dk_ref[:, span] += functools.reduce(
                jnp.add, [dot(qs[i], ds[i][j], TN) for i in range(PAIR)]
            )
            dv_ref[:, span] += functools.reduce(
                jnp.add, [dot(gls[i], ps[i][j], TN) for i in range(PAIR)]
            )
        return carry

    lax.fori_loop(0, GROUP // PAIR, pair_step, 0)
    targets = [dfar_ref.at[1], dfar_ref.at[0], dnear_ref, down_ref]
    for j in range(SPAN):
        span = slice(j * rows, (j + 1) * rows)
        target = targets[j]
        target[:, :HEAD_SIZE] = (dk_ref[:, span].T * SCALE).astype(target.dtype)
        target[:, HEAD_SIZE:] = dv_ref[:, span].T.astype(target.dtype)


def attention(chunk, first, lengths, queries, out_grad, far, near, own, done):
    rows = queries.shape[0]
    wide = GROUP * HEAD_SIZE
    pair = 2 * HEAD_SIZE
    heads = own.shape[1] // pair
    base = chunk * heads

    def query_block(h, *_):
        return (0, base + h)

    def block(h, *_):
        return (0, h)

    def far_block(h, *_):
        return (0, 0, h)

    in_specs = [
        pl.BlockSpec((rows, wide), query_block),
        pl.BlockSpec((rows, wide), query_block),
        pl.BlockSpec((2, rows, pair), far_block),
        pl.BlockSpec((rows, pair), block),
        pl.BlockSpec((rows, pair), block),
    ]
    operands = [first, lengths, queries, out_grad, far, near, own]
    aliases = {}
    if done is not None:
        in_specs += [pl.BlockSpec(memory_space=pl.ANY)] * 2
        aliases = {len(operands): 0, len(operands) + 1: 1}
        operands += list(done)
    return pl.pallas_call(
        attention_kernel,
        out_shape=(
            jax.ShapeDtypeStruct(queries.shape, jnp.bfloat16),
            jax.ShapeDtypeStruct(queries.shape, jnp.bfloat16),
            jax.ShapeDtypeStruct((2, rows, heads * pair), jnp.bfloat16),
            jax.ShapeDtypeStruct((rows, heads * pair), jnp.float32),
            jax.ShapeDtypeStruct((rows, heads * pair), jnp.float32),
        ),
        grid_spec=pltpu.PrefetchScalarGridSpec(
            num_scalar_prefetch=2,
            grid=(heads,),
            in_specs=in_specs,
            out_specs=(
                pl.BlockSpec((rows, wide), query_block),
                pl.BlockSpec((rows, wide), query_block),
                pl.BlockSpec((2, rows, pair), far_block),
                pl.BlockSpec((rows, pair), block),
                pl.BlockSpec((rows, pair), block),
            ),
            scratch_shapes=[
                pltpu.VMEM((rows, SPAN * rows), jnp.float32),
                pltpu.VMEM((HEAD_SIZE, SPAN * rows), jnp.float32),
                pltpu.VMEM((HEAD_SIZE, SPAN * rows), jnp.float32),
            ],
        ),
        input_output_aliases=aliases,
        compiler_params=pltpu.CompilerParams(vmem_limit_bytes=48 * 1024 * 1024),
        cost_estimate=pl.CostEstimate(
            flops=12 * rows * GROUP * heads * SPAN * rows * HEAD_SIZE * 2,
            bytes_accessed=heads * (4 * rows * wide * 2 + 14 * rows * pair),
            transcendentals=0,
        ),
        name="attention",
    )(*operands)


def local(queries, keys, values, out_grad, doc_lengths):
    rows = queries.shape[0]
    first = (lax.axis_index(AXES) * rows).astype(jnp.int32).reshape(1)
    chunks = KEY_VALUE_HEADS // CHUNK
    owns, nears, fars = [], [], []
    for chunk in range(chunks):
        parts = []
        for head in range(chunk * CHUNK, (chunk + 1) * CHUNK):
            span = slice(head * HEAD_SIZE, (head + 1) * HEAD_SIZE)
            parts += [keys[:, span], values[:, span]]
        owns.append(jnp.concatenate(parts, axis=1))
    for chunk in range(chunks):
        nears.append(passed_along(owns[chunk], 1))
    for chunk in range(chunks):
        fars.append(passed_along(jnp.stack([owns[chunk], nears[chunk]]), 2))
    done, totals = None, []
    for chunk in range(chunks):
        out, dq, dfar, dnear, down = attention(
            chunk, first, doc_lengths, queries, out_grad, fars[chunk], nears[chunk], owns[chunk], done
        )
        done = (out, dq)
        back = passed_along(dfar, -2).astype(jnp.float32)
        last = passed_along((dnear + back[1]).astype(jnp.bfloat16), -1)
        totals.append((down + back[0] + last.astype(jnp.float32)).astype(jnp.bfloat16))
    key_parts, value_parts = [], []
    for total in totals:
        for head in range(CHUNK):
            start = head * 2 * HEAD_SIZE
            key_parts.append(total[:, start : start + HEAD_SIZE])
            value_parts.append(total[:, start + HEAD_SIZE : start + 2 * HEAD_SIZE])
    return (
        done[0],
        done[1],
        jnp.concatenate(key_parts, axis=1),
        jnp.concatenate(value_parts, axis=1),
    )


def solution(mesh):
    spec = P(AXES, None)
    return jax.shard_map(
        local,
        mesh=mesh,
        in_specs=(spec, spec, spec, spec, P()),
        out_specs=(spec, spec, spec, spec),
        check_vma=False,
    )
```

profile of v0, /device:TPU:29, one launch (start us, length us, event | category | flops | bytes accessed | tf_op | source)
XLA Modules:
  0.0 113.6 jit_solution(9638036098493675742)
XLA Ops:
  0.6 1.1 fusion.14
  1.8 0.0 copy-start
  1.8 0.0 copy-start.1
  1.8 3.4 %collective-permute-start.2 = (bf16[256,512]{1,0:T(8,128)(2,1)S(1)}, bf16[256,512]{1,0:T(8,128)(2,1)S(1)}, u32[]{:S(2)}, u32[]{:S(2)}) collective-permute-start(bf16[256,512]{1,0:T(8,128)(2,1)S(1)} %get-tuple-element.33.own_ref), channel_id=1, source_target_pairs={{0,1},{1,2},{2,3},{3,4},{4,5},{5,6},{6,7},{7,8},{8,9},{9,10},{10,1... | collective-permute-start | bytes 786440 | tf_op jit(solution)/shard_map/ppermute | solution.py:35
  5.2 5.8 %collective-permute-done.2.near_ref = bf16[256,512]{1,0:T(8,128)(2,1)S(1)} collective-permute-done((bf16[256,512]{1,0:T(8,128)(2,1)S(1)}, bf16[256,512]{1,0:T(8,128)(2,1)S(1)}, u32[]{:S(2)}, u32[]{:S(2)}) %collective-permute-start.2) | collective-permute-done | bytes 262176 | tf_op jit(solution)/shard_map/ppermute | solution.py:35
  11.0 0.8 pad_maximum_fusion.1
  11.9 4.2 %collective-permute-start.3 = (bf16[2,256,512]{2,1,0:T(8,128)(2,1)}, bf16[2,256,512]{2,1,0:T(8,128)(2,1)}, u32[]{:S(2)}, u32[]{:S(2)}) collective-permute-start(bf16[2,256,512]{2,1,0:T(8,128)(2,1)} %pad_maximum_fusion.1), channel_id=1, source_target_pairs={{0,2},{1,3},{2,4},{3,5},{4,6},{5,7},{6,8},{7,9},{8,10},{9,11},{10,... | collective-permute-start | bytes 1572872 | tf_op jit(solution)/shard_map/ppermute | solution.py:35
  16.1 5.5 %collective-permute-start = (bf16[256,512]{1,0:T(8,128)(2,1)S(1)}, bf16[256,512]{1,0:T(8,128)(2,1)S(1)}, u32[]{:S(2)}, u32[]{:S(2)}) collective-permute-start(bf16[256,512]{1,0:T(8,128)(2,1)S(1)} %get-tuple-element.43.own_ref), channel_id=1, source_target_pairs={{0,1},{1,2},{2,3},{3,4},{4,5},{5,6},{6,7},{7,8},{8,9},{9,10},{10,1... | collective-permute-start | bytes 786440 | tf_op jit(solution)/shard_map/ppermute | solution.py:35
  21.7 11.4 %collective-permute-done.near_ref = bf16[256,512]{1,0:T(8,128)(2,1)S(1)} collective-permute-done((bf16[256,512]{1,0:T(8,128)(2,1)S(1)}, bf16[256,512]{1,0:T(8,128)(2,1)S(1)}, u32[]{:S(2)}, u32[]{:S(2)}) %collective-permute-start) | collective-permute-done | bytes 262176 | tf_op jit(solution)/shard_map/ppermute | solution.py:35
  33.1 0.1 pad_maximum_fusion
  33.1 2.6 %collective-permute-start.1 = (bf16[2,256,512]{2,1,0:T(8,128)(2,1)S(1)}, bf16[2,256,512]{2,1,0:T(8,128)(2,1)S(1)}, u32[]{:S(2)}, u32[]{:S(2)}) collective-permute-start(bf16[2,256,512]{2,1,0:T(8,128)(2,1)S(1)} %pad_maximum_fusion), channel_id=1, source_target_pairs={{0,2},{1,3},{2,4},{3,5},{4,6},{5,7},{6,8},{7,9},{8,10},{9,11},{10,... | collective-permute-start | bytes 1572872 | tf_op jit(solution)/shard_map/ppermute | solution.py:35
  35.7 0.0 collective-permute-done.3.far_ref
  35.7 0.0 copy-done
  35.8 20.7 %attention.2 = (bf16[256,4096]{1,0:T(8,128)(2,1)}, bf16[256,4096]{1,0:T(8,128)(2,1)}, bf16[2,256,512]{2,1,0:T(8,128)(2,1)S(1)}, f32[256,512]{1,0:T(8,128)S(1)}, f32[256,512]{1,0:T(8,128)S(1)}) custom-call(s32[1]{0:T(128)} %bitcast.first_ref, s32[16]{0:T(128)S(1)} %copy-done.1, bf16[256,4096]{1,0:T(8,128)(2,1)S(1)} %copy-done, bf16[256,4096]{1,0:T(8,128)(2,1)} %g_ref.3, ...), custom_call_target="tpu_custom_call" | custom-call | flops 12884901888 | bytes 6029312 | tf_op jit(solution)/shard_map/attention/pallas_call | solution.py:164
  56.5 2.7 %collective-permute-start.4 = (bf16[2,256,512]{2,1,0:T(8,128)(2,1)S(1)}, bf16[2,256,512]{2,1,0:T(8,128)(2,1)S(1)}, u32[]{:S(2)}, u32[]{:S(2)}) collective-permute-start(bf16[2,256,512]{2,1,0:T(8,128)(2,1)S(1)} %get-tuple-element.19), channel_id=1, source_target_pairs={{2,0},{3,1},{4,2},{5,3},{6,4},{7,5},{8,6},{9,7},{10,8},{11,9},{12,... | collective-permute-start | bytes 1572872 | tf_op jit(solution)/shard_map/ppermute | solution.py:35
  59.2 0.0 collective-permute-done.1.far_ref
  59.2 20.7 %attention.3 = (bf16[256,4096]{1,0:T(8,128)(2,1)}, bf16[256,4096]{1,0:T(8,128)(2,1)}, bf16[2,256,512]{2,1,0:T(8,128)(2,1)S(1)}, f32[256,512]{1,0:T(8,128)S(1)}, f32[256,512]{1,0:T(8,128)S(1)}) custom-call(s32[1]{0:T(128)} %bitcast.first_ref, s32[16]{0:T(128)S(1)} %copy-done.1, ...), custom_call_target="tpu_custom_call", output_to_operand_aliasing={{0}: (7, {}), {1}: (8, {})} | custom-call | flops 12884901888 | bytes 6029312 | tf_op jit(solution)/shard_map/attention/pallas_call | solution.py:164
  79.8 1.9 %collective-permute-start.6 = (bf16[2,256,512]{2,1,0:T(8,128)(2,1)S(1)}, bf16[2,256,512]{2,1,0:T(8,128)(2,1)S(1)}, u32[]{:S(2)}, u32[]{:S(2)}) collective-permute-start(bf16[2,256,512]{2,1,0:T(8,128)(2,1)S(1)} %get-tuple-element.22), channel_id=1, source_target_pairs={{2,0},{3,1},{4,2},{5,3},{6,4},{7,5},{8,6},{9,7},{10,8},{11,9},{12,... | collective-permute-start | bytes 1572872 | tf_op jit(solution)/shard_map/ppermute | solution.py:35
  81.8 0.0 collective-permute-done.4
  81.8 0.1 convert_element_type.24
  81.9 0.1 fusion.6
  82.0 6.8 %collective-permute-start.5 = (bf16[256,512]{1,0:T(8,128)(2,1)S(1)}, bf16[256,512]{1,0:T(8,128)(2,1)S(1)}, u32[]{:S(2)}, u32[]{:S(2)}) collective-permute-start(bf16[256,512]{1,0:T(8,128)(2,1)S(1)} %fusion.6), channel_id=1, source_target_pairs={{1,0},{2,1},{3,2},{4,3},{5,4},{6,5},{7,6},{8,7},{9,8},{10,9},{11,1... | collective-permute-start | bytes 786440 | tf_op jit(solution)/shard_map/ppermute | solution.py:35
  88.8 8.4 %collective-permute-done.6 = bf16[2,256,512]{2,1,0:T(8,128)(2,1)S(1)} collective-permute-done((bf16[2,256,512]{2,1,0:T(8,128)(2,1)S(1)}, bf16[2,256,512]{2,1,0:T(8,128)(2,1)S(1)}, u32[]{:S(2)}, u32[]{:S(2)}) %collective-permute-start.6) | collective-permute-done | bytes 524320 | tf_op jit(solution)/shard_map/ppermute | solution.py:35
  97.2 0.1 convert_element_type.28
  97.4 0.1 fusion.1
  97.5 8.2 %collective-permute-start.7 = (bf16[256,512]{1,0:T(8,128)(2,1)S(1)}, bf16[256,512]{1,0:T(8,128)(2,1)S(1)}, u32[]{:S(2)}, u32[]{:S(2)}) collective-permute-start(bf16[256,512]{1,0:T(8,128)(2,1)S(1)} %fusion.1), channel_id=1, source_target_pairs={{1,0},{2,1},{3,2},{4,3},{5,4},{6,5},{7,6},{8,7},{9,8},{10,9},{11,1... | collective-permute-start | bytes 786440 | tf_op jit(solution)/shard_map/ppermute | solution.py:35
  105.6 3.5 %collective-permute-done.5 = bf16[256,512]{1,0:T(8,128)(2,1)S(1)} collective-permute-done((bf16[256,512]{1,0:T(8,128)(2,1)S(1)}, bf16[256,512]{1,0:T(8,128)(2,1)S(1)}, u32[]{:S(2)}, u32[]{:S(2)}) %collective-permute-start.5) | collective-permute-done | bytes 262176 | tf_op jit(solution)/shard_map/ppermute | solution.py:35
  109.2 0.1 fusion.9
  109.4 2.6 %collective-permute-done.7 = bf16[256,512]{1,0:T(8,128)(2,1)S(1)} collective-permute-done((bf16[256,512]{1,0:T(8,128)(2,1)S(1)}, bf16[256,512]{1,0:T(8,128)(2,1)S(1)}, u32[]{:S(2)}, u32[]{:S(2)}) %collective-permute-start.7) | collective-permute-done | bytes 262176 | tf_op jit(solution)/shard_map/ppermute | solution.py:35
  112.0 0.1 fusion.4
  112.2 0.7 pad_maximum_fusion.5
  112.9 0.7 pad_maximum_fusion.4
  (5 shorter events, 0.2 us)
Async XLA Ops:
  1.8 34.0 %copy-start = (bf16[256,4096]{1,0:T(8,128)(2,1)S(1)}, bf16[256,4096]{1,0:T(8,128)(2,1)}, u32[]{:S(2)}) copy-start(bf16[256,4096]{1,0:T(8,128)(2,1)} %q_ref.3) | copy-start | bytes 6291460
  1.8 34.0 %copy-start.1 = (s32[16]{0:T(128)S(1)}, s32[16]{0:T(128)}, u32[]{:S(2)}) copy-start(s32[16]{0:T(128)} %lengths_ref.3) | copy-start | bytes 196
  1.8 9.2 %collective-permute-start.2 = (bf16[256,512]{1,0:T(8,128)(2,1)S(1)}, bf16[256,512]{1,0:T(8,128)(2,1)S(1)}, u32[]{:S(2)}, u32[]{:S(2)}) collective-permute-start(bf16[256,512]{1,0:T(8,128)(2,1)S(1)} %get-tuple-element.33.own_ref), channel_id=1, source_target_pairs={{0,1},{1,2},{2,3},{3,4},{4,5},{5,6},{6,7},{7,8},{8,9},{9,10},{10,1... | collective-permute-start | bytes 786440 | tf_op jit(solution)/shard_map/ppermute | solution.py:35
  11.9 23.9 %collective-permute-start.3 = (bf16[2,256,512]{2,1,0:T(8,128)(2,1)}, bf16[2,256,512]{2,1,0:T(8,128)(2,1)}, u32[]{:S(2)}, u32[]{:S(2)}) collective-permute-start(bf16[2,256,512]{2,1,0:T(8,128)(2,1)} %pad_maximum_fusion.1), channel_id=1, source_target_pairs={{0,2},{1,3},{2,4},{3,5},{4,6},{5,7},{6,8},{7,9},{8,10},{9,11},{10,... | collective-permute-start | bytes 1572872 | tf_op jit(solution)/shard_map/ppermute | solution.py:35
  16.1 16.9 %collective-permute-start = (bf16[256,512]{1,0:T(8,128)(2,1)S(1)}, bf16[256,512]{1,0:T(8,128)(2,1)S(1)}, u32[]{:S(2)}, u32[]{:S(2)}) collective-permute-start(bf16[256,512]{1,0:T(8,128)(2,1)S(1)} %get-tuple-element.43.own_ref), channel_id=1, source_target_pairs={{0,1},{1,2},{2,3},{3,4},{4,5},{5,6},{6,7},{7,8},{8,9},{9,10},{10,1... | collective-permute-start | bytes 786440 | tf_op jit(solution)/shard_map/ppermute | solution.py:35
  33.1 26.1 %collective-permute-start.1 = (bf16[2,256,512]{2,1,0:T(8,128)(2,1)S(1)}, bf16[2,256,512]{2,1,0:T(8,128)(2,1)S(1)}, u32[]{:S(2)}, u32[]{:S(2)}) collective-permute-start(bf16[2,256,512]{2,1,0:T(8,128)(2,1)S(1)} %pad_maximum_fusion), channel_id=1, source_target_pairs={{0,2},{1,3},{2,4},{3,5},{4,6},{5,7},{6,8},{7,9},{8,10},{9,11},{10,... | collective-permute-start | bytes 1572872 | tf_op jit(solution)/shard_map/ppermute | solution.py:35
  56.5 25.3 %collective-permute-start.4 = (bf16[2,256,512]{2,1,0:T(8,128)(2,1)S(1)}, bf16[2,256,512]{2,1,0:T(8,128)(2,1)S(1)}, u32[]{:S(2)}, u32[]{:S(2)}) collective-permute-start(bf16[2,256,512]{2,1,0:T(8,128)(2,1)S(1)} %get-tuple-element.19), channel_id=1, source_target_pairs={{2,0},{3,1},{4,2},{5,3},{6,4},{7,5},{8,6},{9,7},{10,8},{11,9},{12,... | collective-permute-start | bytes 1572872 | tf_op jit(solution)/shard_map/ppermute | solution.py:35
  79.8 17.4 %collective-permute-start.6 = (bf16[2,256,512]{2,1,0:T(8,128)(2,1)S(1)}, bf16[2,256,512]{2,1,0:T(8,128)(2,1)S(1)}, u32[]{:S(2)}, u32[]{:S(2)}) collective-permute-start(bf16[2,256,512]{2,1,0:T(8,128)(2,1)S(1)} %get-tuple-element.22), channel_id=1, source_target_pairs={{2,0},{3,1},{4,2},{5,3},{6,4},{7,5},{8,6},{9,7},{10,8},{11,9},{12,... | collective-permute-start | bytes 1572872 | tf_op jit(solution)/shard_map/ppermute | solution.py:35
  82.0 27.2 %collective-permute-start.5 = (bf16[256,512]{1,0:T(8,128)(2,1)S(1)}, bf16[256,512]{1,0:T(8,128)(2,1)S(1)}, u32[]{:S(2)}, u32[]{:S(2)}) collective-permute-start(bf16[256,512]{1,0:T(8,128)(2,1)S(1)} %fusion.6), channel_id=1, source_target_pairs={{1,0},{2,1},{3,2},{4,3},{5,4},{6,5},{7,6},{8,7},{9,8},{10,9},{11,1... | collective-permute-start | bytes 786440 | tf_op jit(solution)/shard_map/ppermute | solution.py:35
  97.5 14.5 %collective-permute-start.7 = (bf16[256,512]{1,0:T(8,128)(2,1)S(1)}, bf16[256,512]{1,0:T(8,128)(2,1)S(1)}, u32[]{:S(2)}, u32[]{:S(2)}) collective-permute-start(bf16[256,512]{1,0:T(8,128)(2,1)S(1)} %fusion.1), channel_id=1, source_target_pairs={{1,0},{2,1},{3,2},{4,3},{5,4},{6,5},{7,6},{8,7},{9,8},{10,9},{11,1... | collective-permute-start | bytes 786440 | tf_op jit(solution)/shard_map/ppermute | solution.py:35
where the time goes:
time: 115 us; the launch traced here: 114 us
  Pallas kernels  41.4 us (36%)
  starting transfers between devices  35.3 us (31%)
  waiting for transfers between devices  31.7 us (28%)
  other arithmetic  3.15 us (3%)
  local copies, waits for them, and re-layouts  1.22 us (1%)
    pallas_call x2, Pallas kernels, attention(): pl.pallas_call(attention_kernel, out_shape=(jax.ShapeDtypeStruct(queries....  41.4 us
    ppermute x8, starting transfers between devices, passed_along(): lax.ppermute(value, AXES, [(source, source + steps) for source in range(f...  35.3 us
    ppermute x8, waiting for transfers between devices, passed_along(): lax.ppermute(value, AXES, [(source, source + steps) for source in range(f...  31.7 us
  transfers between devices with their start and end apart: 8, of which 5 were waited for; matrix products, arithmetic and copies ran while one was open for 1% of the time, Pallas kernels for 36%

commit v1 on v0

v1 whole, which is shorter than its diff:
```python
import math

import jax
import jax.numpy as jnp
from jax import lax
from jax.experimental import pallas as pl
from jax.experimental.pallas import tpu as pltpu
from jax.sharding import PartitionSpec as P

HEAD_SIZE = 128
QUERY_HEADS = 32
KEY_VALUE_HEADS = 4
GROUP = QUERY_HEADS // KEY_VALUE_HEADS
SPAN = 4
AXES = ("blk", "inner")
CHUNK = 2
HALF = 128
UNITS = 2
MASKED = -1e30
SCALE = 1.0 / math.sqrt(HEAD_SIZE)
EXP2_SCALE = SCALE * math.log2(math.e)

NN = (((1,), (0,)), ((), ()))
NT = (((1,), (1,)), ((), ()))


def dot(a, b, dims=NN):
    return lax.dot_general(a, b, dims, preferred_element_type=jnp.float32)


def device_count():
    return lax.axis_size("blk") * lax.axis_size("inner")


def passed_along(value, steps):
    count = device_count()
    first, last = (max(0, -steps), min(count, count - steps))
    return lax.ppermute(value, AXES, [(source, source + steps) for source in range(first, last)])


def swapped(value):
    return lax.ppermute(value, AXES, [(source, source ^ 1) for source in range(device_count())])


def write_bias(bias_ref, lengths_ref, first_ref, rows, width):
    docs = lengths_ref.shape[0]
    for half in range(rows // HALF):
        first = first_ref[0] + half * HALF
        query_pos = first + lax.broadcasted_iota(jnp.int32, (8, HALF), 1)

        def step(doc, carry, query_pos=query_pos):
            end, start = carry
            end = end + lengths_ref[doc]
            return end, jnp.where(query_pos >= end, end, start)

        _, start = lax.fori_loop(0, docs, step, (jnp.int32(0), jnp.zeros((8, HALF), jnp.int32)))
        start = jnp.broadcast_to(start[:1], (width, HALF))
        query_pos = jnp.broadcast_to(query_pos[:1], (width, HALF))
        key_pos = first + HALF - width + lax.broadcasted_iota(jnp.int32, (width, HALF), 0)
        allowed = (key_pos >= start) & (key_pos <= query_pos)
        bias_ref[half] = jnp.where(allowed, 0.0, MASKED)


def attention_kernel(first_ref, lengths_ref, q_ref, g_ref, far_ref, mid_ref, near_ref, own_ref, *refs):
    (
        out_ref, dq_ref, dfar_ref, dmid_ref, dnear_ref, down_ref,
        bias_ref, key_ref, value_ref, key_t_ref, value_t_ref, p_ref, d_ref, dk_ref, dv_ref,
    ) = refs[-15:]
    rows = q_ref.shape[0]
    window = SPAN * rows
    width = window - HALF
    write_bias(bias_ref, lengths_ref, first_ref, rows, width)
    for j, block in enumerate((far_ref, mid_ref, near_ref, own_ref)):
        span = slice(j * rows, (j + 1) * rows)
        key_ref[span] = block[:, :HEAD_SIZE]
        value_ref[span] = block[:, HEAD_SIZE:]
        key_t_ref[:, span] = block[:, :HEAD_SIZE].T
        value_t_ref[:, span] = block[:, HEAD_SIZE:].T
    dk_ref[...] = jnp.zeros_like(dk_ref)
    dv_ref[...] = jnp.zeros_like(dv_ref)
    steps = GROUP // (2 * UNITS)

    def step(index, carry):
        half = index // steps
        start = pl.multiple_of(half * HALF, HALF)
        base = (index % steps) * 2 * UNITS
        queries = pl.ds(start, HALF)
        span = pl.ds(start, width)
        key, value = key_ref[span], value_ref[span]
        key_t, value_t = key_t_ref[:, span], value_t_ref[:, span]
        bias = bias_ref[half]
        bias = jnp.concatenate([bias, bias], axis=1)
        qs, gs = [], []
        for unit in range(UNITS):
            cols = [
                pl.ds(pl.multiple_of((base + 2 * unit + i) * HEAD_SIZE, HEAD_SIZE), HEAD_SIZE)
                for i in range(2)
            ]
            here = slice(unit * 2 * HALF, (unit + 1) * 2 * HALF)
            q = jnp.concatenate([q_ref[queries, c] for c in cols], axis=0)
            g_t = jnp.concatenate([g_ref[queries, c] for c in cols], axis=0).T.astype(jnp.float32)
            s = dot(key, q, NT) * EXP2_SCALE + bias
            e = jnp.exp2(s - jnp.max(s, axis=0, keepdims=True))
            inv = 1.0 / jnp.sum(e, axis=0, keepdims=True)
            p = e.astype(jnp.bfloat16)
            p_ref[:, here] = p
            out_t = (dot(value_t, p) * inv).astype(jnp.bfloat16)
            out = out_t.T
            for i in range(2):
                out_ref[queries, cols[i]] = out[i * HALF : (i + 1) * HALF]
            delta = jnp.sum(g_t * out_t.astype(jnp.float32), axis=0, keepdims=True) * inv
            g_t = (g_t * inv).astype(jnp.bfloat16)
            d = (p.astype(jnp.float32) * (dot(value, g_t) - delta)).astype(jnp.bfloat16)
            d_ref[:, here] = d
            dq = (dot(key_t, d) * SCALE).astype(jnp.bfloat16).T
            for i in range(2):
                dq_ref[queries, cols[i]] = dq[i * HALF : (i + 1) * HALF]
            qs.append(q)
            gs.append(g_t.T)
        dk_ref[span] += dot(d_ref[...], jnp.concatenate(qs, axis=0))
        dv_ref[span] += dot(p_ref[...], jnp.concatenate(gs, axis=0))
        return carry

    lax.fori_loop(0, (rows // HALF) * steps, step, 0)
    for j, target in enumerate((dfar_ref, dmid_ref, dnear_ref, down_ref)):
        span = slice(j * rows, (j + 1) * rows)
        target[:, :HEAD_SIZE] = (dk_ref[span] * SCALE).astype(target.dtype)
        target[:, HEAD_SIZE:] = dv_ref[span].astype(target.dtype)


def attention(head, first, lengths, queries, out_grad, blocks, grads, parts):
    rows = queries.shape[0]
    wide = GROUP * HEAD_SIZE
    pair = 2 * HEAD_SIZE
    window = SPAN * rows
    width = window - HALF
    place = head % CHUNK
    query_spec = pl.BlockSpec((rows, wide), lambda i, *_: (0, head))
    block_spec = pl.BlockSpec((rows, pair), lambda i, *_: (0, place))
    operands = [first, lengths, queries, out_grad, *blocks]
    in_specs = [query_spec] * 2 + [block_spec] * 4
    aliases = {}
    for at, array in enumerate((*grads, *parts)):
        if array is not None:
            aliases[len(operands)] = at
            operands.append(array)
            in_specs.append(pl.BlockSpec(memory_space=pl.ANY))
    bf16, f32 = jnp.bfloat16, jnp.float32
    results = pl.pallas_call(
        attention_kernel,
        out_shape=[jax.ShapeDtypeStruct(queries.shape, bf16)] * 2
        + [jax.ShapeDtypeStruct((rows, CHUNK * pair), kind) for kind in (bf16, f32, f32, f32)],
        grid_spec=pltpu.PrefetchScalarGridSpec(
            num_scalar_prefetch=2,
            grid=(1,),
            in_specs=in_specs,
            out_specs=[query_spec] * 2 + [block_spec] * 4,
            scratch_shapes=[
                pltpu.VMEM((rows // HALF, width, HALF), f32),
                pltpu.VMEM((window, HEAD_SIZE), bf16),
                pltpu.VMEM((window, HEAD_SIZE), bf16),
                pltpu.VMEM((HEAD_SIZE, window), bf16),
                pltpu.VMEM((HEAD_SIZE, window), bf16),
                pltpu.VMEM((width, UNITS * 2 * HALF), bf16),
                pltpu.VMEM((width, UNITS * 2 * HALF), bf16),
                pltpu.VMEM((window, HEAD_SIZE), f32),
                pltpu.VMEM((window, HEAD_SIZE), f32),
            ],
        ),
        input_output_aliases=aliases,
        compiler_params=pltpu.CompilerParams(vmem_limit_bytes=48 * 1024 * 1024),
        cost_estimate=pl.CostEstimate(
            flops=12 * rows * GROUP * window * HEAD_SIZE * 2,
            bytes_accessed=4 * rows * wide * 2 + 22 * rows * pair,
            transcendentals=0,
        ),
        name="attention",
    )(*operands)
    return results[:2], results[2:]


def local(queries, keys, values, out_grad, doc_lengths):
    rows = queries.shape[0]
    index = lax.axis_index(AXES)
    odd = index % 2 == 1
    first = (index * rows).astype(jnp.int32).reshape(1)
    bf16, f32 = jnp.bfloat16, jnp.float32
    chunks = range(KEY_VALUE_HEADS // CHUNK)
    owns, mids, nears, fars = [], [], [], []
    for chunk in chunks:
        parts = []
        for head in range(chunk * CHUNK, (chunk + 1) * CHUNK):
            span = slice(head * HEAD_SIZE, (head + 1) * HEAD_SIZE)
            parts += [keys[:, span], values[:, span]]
        owns.append(jnp.concatenate(parts, axis=1))
        mids.append(passed_along(owns[chunk], 2))
        nears.append(swapped(jnp.where(odd, mids[chunk], owns[chunk])))
        fars.append(passed_along(nears[chunk], 2))
    grads = (None, None)
    totals = []
    for chunk in chunks:
        parts = (None,) * 4
        for head in range(chunk * CHUNK, (chunk + 1) * CHUNK):
            blocks = (fars[chunk], mids[chunk], nears[chunk], owns[chunk])
            grads, parts = attention(head, first, doc_lengths, queries, out_grad, blocks, grads, parts)
        far, mid, near, own = parts
        near = (near + passed_along(far, -2).astype(f32)).astype(bf16)
        got = swapped(near).astype(f32)
        mid = (mid + jnp.where(odd, got, 0.0)).astype(bf16)
        own = own + jnp.where(odd, 0.0, got)
        totals.append((own + passed_along(mid, -2).astype(f32)).astype(bf16))
    key_parts, value_parts = [], []
    for total in totals:
        for head in range(CHUNK):
            start = head * 2 * HEAD_SIZE
            key_parts.append(total[:, start : start + HEAD_SIZE])
            value_parts.append(total[:, start + HEAD_SIZE : start + 2 * HEAD_SIZE])
    return (
        grads[0],
        grads[1],
        jnp.concatenate(key_parts, axis=1),
        jnp.concatenate(value_parts, axis=1),
    )


def solution(mesh):
    spec = P(AXES, None)
    return jax.shard_map(
        local,
        mesh=mesh,
        in_specs=(spec, spec, spec, spec, P()),
        out_specs=(spec, spec, spec, spec),
        check_vma=False,
    )
```

time: 115 us -> 124 us (1.078)
  Pallas kernels: 41.4 us -> 55.9 us
  starting transfers between devices: 35.3 us -> 28.9 us
    pallas_call x2 -> x4, Pallas kernels: 41.4 us -> 55.9 us  [attention(): pl.pallas_call(attention_kernel, out_shape=[jax.ShapeDtypeStruct(queries....]
    ppermute x8, starting transfers between devices: 35.3 us -> 27.7 us  [passed_along(): lax.ppermute(value, AXES, [(source, source + steps) for source in range(f...]
    ppermute x0 -> x4, waiting for transfers between devices: none -> 4 us  [swapped(): lax.ppermute(value, AXES, [(source, source ^ 1) for source in range(devic...]
    ppermute x8, waiting for transfers between devices: 31.7 us -> 27.8 us  [passed_along(): lax.ppermute(value, AXES, [(source, source + steps) for source in range(f...]
    select_n x0 -> x2, other arithmetic: none -> 1.72 us  [local(): nears.append(swapped(jnp.where(odd, mids[chunk], owns[chunk])))]
  transfers between devices with their start and end apart: 8 -> 12, of which waited for: 5 -> 8; matrix products, arithmetic and copies ran while one was open for 1% -> 2% of each run, Pallas kernels for 36% -> 45%
where the time goes in v1:
time: 124 us; the launch traced here: 123 us
  Pallas kernels  55.9 us (45%)
  waiting for transfers between devices  31.8 us (26%)
  starting transfers between devices  28.9 us (23%)
  other arithmetic  3.79 us (3%)
  local copies, waits for them, and re-layouts  2 us (2%)
    pallas_call x4, Pallas kernels, attention(): pl.pallas_call(attention_kernel, out_shape=[jax.ShapeDtypeStruct(queries....  55.9 us
    ppermute x8, waiting for transfers between devices, passed_along(): lax.ppermute(value, AXES, [(source, source + steps) for source in range(f...  27.8 us
    ppermute x8, starting transfers between devices, passed_along(): lax.ppermute(value, AXES, [(source, source + steps) for source in range(f...  27.7 us
    ppermute x4, waiting for transfers between devices, swapped(): lax.ppermute(value, AXES, [(source, source ^ 1) for source in range(devic...  4 us
  transfers between devices with their start and end apart: 12, of which 8 were waited for; matrix products, arithmetic and copies ran while one was open for 2% of the time, Pallas kernels for 45%

profile of v1, /device:TPU:29, one launch (start us, length us, event | category | flops | bytes accessed | tf_op | source)
XLA Modules:
  0.0 123.2 jit_solution(114803328170353162)
XLA Ops:
  0.7 1.3 %fusion.12 = (bf16[256,128]{1,0:T(8,128)(2,1)S(1)}, bf16[256,128]{1,0:T(8,128)(2,1)S(1)}, bf16[256,128]{1,0:T(8,128)(2,1)S(1)}, bf16[256,128]{1,0:T(8,128)(2,1)S...) fusion(bf16[256,512]{1,0:T(8,128)(2,1)} %param.6, ...), kind=kLoop, calls=%fused_computation.24 | loop fusion | bytes 1048576 | tf_op jit(solution)/shard_map/slice | solution.py:194
  1.9 0.6 copy-done.2
  2.6 3.3 %collective-permute-start.3 = (bf16[256,512]{1,0:T(8,128)(2,1)S(1)}, bf16[256,512]{1,0:T(8,128)(2,1)S(1)}, u32[]{:S(2)}, u32[]{:S(2)}) collective-permute-start(bf16[256,512]{1,0:T(8,128)(2,1)S(1)} %pad_maximum_fusion.1.own_ref), channel_id=1, source_target_pairs={{0,2},{1,3},{2,4},{3,5},{4,6},{5,7},{6,8},{7,9},{8,10},{9,11},{10,... | collective-permute-start | bytes 786440 | tf_op jit(solution)/shard_map/ppermute | solution.py:38
  6.0 3.5 %collective-permute-start = (bf16[256,512]{1,0:T(8,128)(2,1)S(1)}, bf16[256,512]{1,0:T(8,128)(2,1)S(1)}, u32[]{:S(2)}, u32[]{:S(2)}) collective-permute-start(bf16[256,512]{1,0:T(8,128)(2,1)S(1)} %pad_maximum_fusion.own_ref), channel_id=1, source_target_pairs={{0,2},{1,3},{2,4},{3,5},{4,6},{5,7},{6,8},{7,9},{8,10},{9,11},{10,... | collective-permute-start | bytes 786440 | tf_op jit(solution)/shard_map/ppermute | solution.py:38
  9.5 2.5 %collective-permute-done.3.mid_ref = bf16[256,512]{1,0:T(8,128)(2,1)S(1)} collective-permute-done((bf16[256,512]{1,0:T(8,128)(2,1)S(1)}, bf16[256,512]{1,0:T(8,128)(2,1)S(1)}, u32[]{:S(2)}, u32[]{:S(2)}) %collective-permute-start.3) | collective-permute-done | bytes 262176 | tf_op jit(solution)/shard_map/ppermute | solution.py:38
  12.0 0.9 broadcast_select_fusion
  12.9 0.3 collective-permute-start.4
  13.2 4.1 %collective-permute-done.mid_ref = bf16[256,512]{1,0:T(8,128)(2,1)S(1)} collective-permute-done((bf16[256,512]{1,0:T(8,128)(2,1)S(1)}, bf16[256,512]{1,0:T(8,128)(2,1)S(1)}, u32[]{:S(2)}, u32[]{:S(2)}) %collective-permute-start) | collective-permute-done | bytes 262176 | tf_op jit(solution)/shard_map/ppermute | solution.py:38
  17.3 0.8 broadcast_select_fusion.1
  18.1 0.2 collective-permute-start.1
  18.3 0.2 collective-permute-done.4.near_ref
  18.4 10.4 %collective-permute-start.5 = (bf16[256,512]{1,0:T(8,128)(2,1)}, bf16[256,512]{1,0:T(8,128)(2,1)}, u32[]{:S(2)}, u32[]{:S(2)}) collective-permute-start(bf16[256,512]{1,0:T(8,128)(2,1)} %collective-permute-done.4.near_ref), channel_id=1, source_target_pairs={{0,2},{1,3},{2,4},{3,5},{4,6},{5,7},{6,8},{7,9},{8,10},{9,11},{10,... | collective-permute-start | bytes 786440 | tf_op jit(solution)/shard_map/ppermute | solution.py:38
  28.9 2.7 %collective-permute-start.2 = (bf16[256,512]{1,0:T(8,128)(2,1)S(1)}, bf16[256,512]{1,0:T(8,128)(2,1)S(1)}, u32[]{:S(2)}, u32[]{:S(2)}) collective-permute-start(bf16[256,512]{1,0:T(8,128)(2,1)S(1)} %collective-permute-done.1.near_ref), channel_id=1, source_target_pairs={{0,2},{1,3},{2,4},{3,5},{4,6},{5,7},{6,8},{7,9},{8,10},{9,11},{10,... | collective-permute-start | bytes 786440 | tf_op jit(solution)/shard_map/ppermute | solution.py:38
  31.6 2.6 %collective-permute-done.5.far_ref = bf16[256,512]{1,0:T(8,128)(2,1)} collective-permute-done((bf16[256,512]{1,0:T(8,128)(2,1)}, bf16[256,512]{1,0:T(8,128)(2,1)}, u32[]{:S(2)}, u32[]{:S(2)}) %collective-permute-start.5) | collective-permute-done | bytes 262176 | tf_op jit(solution)/shard_map/ppermute | solution.py:38
  34.2 14.0 %attention.4 = (bf16[256,4096]{1,0:T(8,128)(2,1)}, bf16[256,4096]{1,0:T(8,128)(2,1)}, bf16[256,512]{1,0:T(8,128)(2,1)S(1)}, f32[256,512]{1,0:T(8,128)S(1)}, f32[...) custom-call(s32[1]{0:T(128)} %bitcast.first_ref, s32[16]{0:T(128)S(1)} %copy-done.1, bf16[256,4096]{1,0:T(8,128)(2,1)S(1)} %copy-done, ...), custom_call_target="tpu_custom_call" | custom-call | flops 6442450944 | bytes 3538944 | tf_op jit(solution)/shard_map/attention/pallas_call | solution.py:149
  48.1 14.0 %attention.5 = (bf16[256,4096]{1,0:T(8,128)(2,1)}, bf16[256,4096]{1,0:T(8,128)(2,1)}, bf16[256,512]{1,0:T(8,128)(2,1)S(1)}, f32[256,512]{1,0:T(8,128)S(1)}, f32[...) custom-call(s32[1]{0:T(128)} %bitcast.first_ref, ...), custom_call_target="tpu_custom_call", output_to_operand_aliasing={{0}: (8, {}), {1}: (9, {}), {2}: (10, {}), {3}: (11, {}), {... | custom-call | flops 6442450944 | bytes 3538944 | tf_op jit(solution)/shard_map/attention/pallas_call | solution.py:149
  62.1 2.1 %collective-permute-start.6 = (bf16[256,512]{1,0:T(8,128)(2,1)S(1)}, bf16[256,512]{1,0:T(8,128)(2,1)S(1)}, u32[]{:S(2)}, u32[]{:S(2)}) collective-permute-start(bf16[256,512]{1,0:T(8,128)(2,1)S(1)} %get-tuple-element.46), channel_id=1, source_target_pairs={{2,0},{3,1},{4,2},{5,3},{6,4},{7,5},{8,6},{9,7},{10,8},{11,9},{12,... | collective-permute-start | bytes 786440 | tf_op jit(solution)/shard_map/ppermute | solution.py:38
  64.3 13.9 %attention.6 = (bf16[256,4096]{1,0:T(8,128)(2,1)}, bf16[256,4096]{1,0:T(8,128)(2,1)}, bf16[256,512]{1,0:T(8,128)(2,1)S(1)}, f32[256,512]{1,0:T(8,128)S(1)}, f32[...) custom-call(s32[1]{0:T(128)} %bitcast.first_ref, s32[16]{0:T(128)S(1)} %copy-done.1, ...), custom_call_target="tpu_custom_call", output_to_operand_aliasing={{0}: (8, {}), {1}: (9, {})} | custom-call | flops 6442450944 | bytes 3538944 | tf_op jit(solution)/shard_map/attention/pallas_call | solution.py:149
  78.2 13.9 %attention.7 = (bf16[256,4096]{1,0:T(8,128)(2,1)}, bf16[256,4096]{1,0:T(8,128)(2,1)}, bf16[256,512]{1,0:T(8,128)(2,1)S(1)}, f32[256,512]{1,0:T(8,128)S(1)}, f32[...) custom-call(s32[1]{0:T(128)} %bitcast.first_ref, ...), custom_call_target="tpu_custom_call", output_to_operand_aliasing={{0}: (8, {}), {1}: (9, {}), {2}: (10, {}), {3}: (11, {}), {... | custom-call | flops 6442450944 | bytes 3538944 | tf_op jit(solution)/shard_map/attention/pallas_call | solution.py:149
  92.1 1.9 %collective-permute-start.9 = (bf16[256,512]{1,0:T(8,128)(2,1)S(1)}, bf16[256,512]{1,0:T(8,128)(2,1)S(1)}, u32[]{:S(2)}, u32[]{:S(2)}) collective-permute-start(bf16[256,512]{1,0:T(8,128)(2,1)S(1)} %get-tuple-element.50), channel_id=1, source_target_pairs={{2,0},{3,1},{4,2},{5,3},{6,4},{7,5},{8,6},{9,7},{10,8},{11,9},{12,... | collective-permute-start | bytes 786440 | tf_op jit(solution)/shard_map/ppermute | solution.py:38
  94.1 0.3 collective-permute-start.7
  94.4 8.8 %collective-permute-done.9 = bf16[256,512]{1,0:T(8,128)(2,1)S(1)} collective-permute-done((bf16[256,512]{1,0:T(8,128)(2,1)S(1)}, bf16[256,512]{1,0:T(8,128)(2,1)S(1)}, u32[]{:S(2)}, u32[]{:S(2)}) %collective-permute-start.9) | collective-permute-done | bytes 262176 | tf_op jit(solution)/shard_map/ppermute | solution.py:38
  103.3 0.3 collective-permute-start.10
  103.7 1.9 %collective-permute-start.8 = (bf16[256,512]{1,0:T(8,128)(2,1)S(1)}, bf16[256,512]{1,0:T(8,128)(2,1)S(1)}, u32[]{:S(2)}, u32[]{:S(2)}) collective-permute-start(bf16[256,512]{1,0:T(8,128)(2,1)S(1)} %fusion.4), channel_id=1, source_target_pairs={{2,0},{3,1},{4,2},{5,3},{6,4},{7,5},{8,6},{9,7},{10,8},{11,9},{12,... | collective-permute-start | bytes 786440 | tf_op jit(solution)/shard_map/ppermute | solution.py:38
  105.6 3.8 %collective-permute-done.10 = bf16[256,512]{1,0:T(8,128)(2,1)S(1)} collective-permute-done((bf16[256,512]{1,0:T(8,128)(2,1)S(1)}, bf16[256,512]{1,0:T(8,128)(2,1)S(1)}, u32[]{:S(2)}, u32[]{:S(2)}) %collective-permute-start.10) | collective-permute-done | bytes 262176 | tf_op jit(solution)/shard_map/ppermute | solution.py:42
  109.5 1.9 %collective-permute-start.11 = (bf16[256,512]{1,0:T(8,128)(2,1)S(1)}, bf16[256,512]{1,0:T(8,128)(2,1)S(1)}, u32[]{:S(2)}, u32[]{:S(2)}) collective-permute-start(bf16[256,512]{1,0:T(8,128)(2,1)S(1)} %fusion.9), channel_id=1, source_target_pairs={{2,0},{3,1},{4,2},{5,3},{6,4},{7,5},{8,6},{9,7},{10,8},{11,9},{12,... | collective-permute-start | bytes 786440 | tf_op jit(solution)/shard_map/ppermute | solution.py:38
  111.5 4.9 %collective-permute-done.8 = bf16[256,512]{1,0:T(8,128)(2,1)S(1)} collective-permute-done((bf16[256,512]{1,0:T(8,128)(2,1)S(1)}, bf16[256,512]{1,0:T(8,128)(2,1)S(1)}, u32[]{:S(2)}, u32[]{:S(2)}) %collective-permute-start.8) | collective-permute-done | bytes 262176 | tf_op jit(solution)/shard_map/ppermute | solution.py:38
  116.4 0.1 fusion.2
  116.6 4.9 %collective-permute-done.11 = bf16[256,512]{1,0:T(8,128)(2,1)S(1)} collective-permute-done((bf16[256,512]{1,0:T(8,128)(2,1)S(1)}, bf16[256,512]{1,0:T(8,128)(2,1)S(1)}, u32[]{:S(2)}, u32[]{:S(2)}) %collective-permute-start.11) | collective-permute-done | bytes 262176 | tf_op jit(solution)/shard_map/ppermute | solution.py:38
  121.5 0.1 fusion.7
  121.7 0.7 pad_maximum_fusion.3
  122.4 0.7 pad_maximum_fusion.2
  (19 shorter events, 0.5 us)
Async XLA Ops:
  0.6 33.5 %copy-start = (bf16[256,4096]{1,0:T(8,128)(2,1)S(1)}, bf16[256,4096]{1,0:T(8,128)(2,1)}, u32[]{:S(2)}) copy-start(bf16[256,4096]{1,0:T(8,128)(2,1)} %q_ref.7) | copy-start | bytes 6291460
  0.6 33.5 %copy-start.1 = (s32[16]{0:T(128)S(1)}, s32[16]{0:T(128)}, u32[]{:S(2)}) copy-start(s32[16]{0:T(128)} %lengths_ref.7) | copy-start | bytes 196
  1.9 0.6 copy-start.2
  1.9 0.6 copy-start.3
  2.6 9.4 %collective-permute-start.3 = (bf16[256,512]{1,0:T(8,128)(2,1)S(1)}, bf16[256,512]{1,0:T(8,128)(2,1)S(1)}, u32[]{:S(2)}, u32[]{:S(2)}) collective-permute-start(bf16[256,512]{1,0:T(8,128)(2,1)S(1)} %pad_maximum_fusion.1.own_ref), channel_id=1, source_target_pairs={{0,2},{1,3},{2,4},{3,5},{4,6},{5,7},{6,8},{7,9},{8,10},{9,11},{10,... | collective-permute-start | bytes 786440 | tf_op jit(solution)/shard_map/ppermute | solution.py:38
  6.0 11.3 %collective-permute-start = (bf16[256,512]{1,0:T(8,128)(2,1)S(1)}, bf16[256,512]{1,0:T(8,128)(2,1)S(1)}, u32[]{:S(2)}, u32[]{:S(2)}) collective-permute-start(bf16[256,512]{1,0:T(8,128)(2,1)S(1)} %pad_maximum_fusion.own_ref), channel_id=1, source_target_pairs={{0,2},{1,3},{2,4},{3,5},{4,6},{5,7},{6,8},{7,9},{8,10},{9,11},{10,... | collective-permute-start | bytes 786440 | tf_op jit(solution)/shard_map/ppermute | solution.py:38
  12.9 5.5 %collective-permute-start.4 = (bf16[256,512]{1,0:T(8,128)(2,1)S(1)}, bf16[256,512]{1,0:T(8,128)(2,1)}, u32[]{:S(2)}, u32[]{:S(2)}) collective-permute-start(bf16[256,512]{1,0:T(8,128)(2,1)S(1)} %broadcast_select_fusion), channel_id=1, source_target_pairs={{0,1},{1,0},{2,3},{3,2},{4,5},{5,4},{6,7},{7,6},{8,9},{9,8},{10,11... | collective-permute-start | bytes 786440 | tf_op jit(solution)/shard_map/ppermute | solution.py:42
  18.1 10.8 %collective-permute-start.1 = (bf16[256,512]{1,0:T(8,128)(2,1)}, bf16[256,512]{1,0:T(8,128)(2,1)S(1)}, u32[]{:S(2)}, u32[]{:S(2)}) collective-permute-start(bf16[256,512]{1,0:T(8,128)(2,1)} %broadcast_select_fusion.1), channel_id=1, source_target_pairs={{0,1},{1,0},{2,3},{3,2},{4,5},{5,4},{6,7},{7,6},{8,9},{9,8},{10,11... | collective-permute-start | bytes 786440 | tf_op jit(solution)/shard_map/ppermute | solution.py:42
  18.4 15.7 %collective-permute-start.5 = (bf16[256,512]{1,0:T(8,128)(2,1)}, bf16[256,512]{1,0:T(8,128)(2,1)}, u32[]{:S(2)}, u32[]{:S(2)}) collective-permute-start(bf16[256,512]{1,0:T(8,128)(2,1)} %collective-permute-done.4.near_ref), channel_id=1, source_target_pairs={{0,2},{1,3},{2,4},{3,5},{4,6},{5,7},{6,8},{7,9},{8,10},{9,11},{10,... | collective-permute-start | bytes 786440 | tf_op jit(solution)/shard_map/ppermute | solution.py:38
  28.9 35.4 %collective-permute-start.2 = (bf16[256,512]{1,0:T(8,128)(2,1)S(1)}, bf16[256,512]{1,0:T(8,128)(2,1)S(1)}, u32[]{:S(2)}, u32[]{:S(2)}) collective-permute-start(bf16[256,512]{1,0:T(8,128)(2,1)S(1)} %collective-permute-done.1.near_ref), channel_id=1, source_target_pairs={{0,2},{1,3},{2,4},{3,5},{4,6},{5,7},{6,8},{7,9},{8,10},{9,11},{10,... | collective-permute-start | bytes 786440 | tf_op jit(solution)/shard_map/ppermute | solution.py:38
  62.1 31.9 %collective-permute-start.6 = (bf16[256,512]{1,0:T(8,128)(2,1)S(1)}, bf16[256,512]{1,0:T(8,128)(2,1)S(1)}, u32[]{:S(2)}, u32[]{:S(2)}) collective-permute-start(bf16[256,512]{1,0:T(8,128)(2,1)S(1)} %get-tuple-element.46), channel_id=1, source_target_pairs={{2,0},{3,1},{4,2},{5,3},{6,4},{7,5},{8,6},{9,7},{10,8},{11,9},{12,... | collective-permute-start | bytes 786440 | tf_op jit(solution)/shard_map/ppermute | solution.py:38
  92.1 11.1 %collective-permute-start.9 = (bf16[256,512]{1,0:T(8,128)(2,1)S(1)}, bf16[256,512]{1,0:T(8,128)(2,1)S(1)}, u32[]{:S(2)}, u32[]{:S(2)}) collective-permute-start(bf16[256,512]{1,0:T(8,128)(2,1)S(1)} %get-tuple-element.50), channel_id=1, source_target_pairs={{2,0},{3,1},{4,2},{5,3},{6,4},{7,5},{8,6},{9,7},{10,8},{11,9},{12,... | collective-permute-start | bytes 786440 | tf_op jit(solution)/shard_map/ppermute | solution.py:38
  94.1 9.5 %collective-permute-start.7 = (bf16[256,512]{1,0:T(8,128)(2,1)S(1)}, bf16[256,512]{1,0:T(8,128)(2,1)S(1)}, u32[]{:S(2)}, u32[]{:S(2)}) collective-permute-start(bf16[256,512]{1,0:T(8,128)(2,1)S(1)} %add_convert_fusion.1), channel_id=1, source_target_pairs={{0,1},{1,0},{2,3},{3,2},{4,5},{5,4},{6,7},{7,6},{8,9},{9,8},{10,11... | collective-permute-start | bytes 786440 | tf_op jit(solution)/shard_map/ppermute | solution.py:42
  103.3 6.1 %collective-permute-start.10 = (bf16[256,512]{1,0:T(8,128)(2,1)S(1)}, bf16[256,512]{1,0:T(8,128)(2,1)S(1)}, u32[]{:S(2)}, u32[]{:S(2)}) collective-permute-start(bf16[256,512]{1,0:T(8,128)(2,1)S(1)} %add_convert_fusion), channel_id=1, source_target_pairs={{0,1},{1,0},{2,3},{3,2},{4,5},{5,4},{6,7},{7,6},{8,9},{9,8},{10,11... | collective-permute-start | bytes 786440 | tf_op jit(solution)/shard_map/ppermute | solution.py:42
  103.7 12.7 %collective-permute-start.8 = (bf16[256,512]{1,0:T(8,128)(2,1)S(1)}, bf16[256,512]{1,0:T(8,128)(2,1)S(1)}, u32[]{:S(2)}, u32[]{:S(2)}) collective-permute-start(bf16[256,512]{1,0:T(8,128)(2,1)S(1)} %fusion.4), channel_id=1, source_target_pairs={{2,0},{3,1},{4,2},{5,3},{6,4},{7,5},{8,6},{9,7},{10,8},{11,9},{12,... | collective-permute-start | bytes 786440 | tf_op jit(solution)/shard_map/ppermute | solution.py:38
  109.5 12.0 %collective-permute-start.11 = (bf16[256,512]{1,0:T(8,128)(2,1)S(1)}, bf16[256,512]{1,0:T(8,128)(2,1)S(1)}, u32[]{:S(2)}, u32[]{:S(2)}) collective-permute-start(bf16[256,512]{1,0:T(8,128)(2,1)S(1)} %fusion.9), channel_id=1, source_target_pairs={{2,0},{3,1},{4,2},{5,3},{6,4},{7,5},{8,6},{9,7},{10,8},{11,9},{12,... | collective-permute-start | bytes 786440 | tf_op jit(solution)/shard_map/ppermute | solution.py:38

commit v2 on v1

v2 whole, which is shorter than its diff:
```python
import math

import jax
import jax.numpy as jnp
from jax import lax
from jax.experimental import pallas as pl
from jax.experimental.pallas import tpu as pltpu
from jax.sharding import PartitionSpec as P

HEAD_SIZE = 128
QUERY_HEADS = 32
KEY_VALUE_HEADS = 4
GROUP = QUERY_HEADS // KEY_VALUE_HEADS
SPAN = 4
AXES = ("blk", "inner")
CHUNK = 2
UNITS = 2
MASKED = -1e30
SCALE = 1.0 / math.sqrt(HEAD_SIZE)
EXP2_SCALE = SCALE * math.log2(math.e)

NN = (((1,), (0,)), ((), ()))


def dot(a, b, dims=NN):
    return lax.dot_general(a, b, dims, preferred_element_type=jnp.float32)


def device_count():
    return lax.axis_size("blk") * lax.axis_size("inner")


def passed_along(value, steps):
    count = device_count()
    first, last = (max(0, -steps), min(count, count - steps))
    return lax.ppermute(value, AXES, [(source, source + steps) for source in range(first, last)])


def swapped(value):
    return lax.ppermute(value, AXES, [(source, source ^ 1) for source in range(device_count())])


def write_bias(bias_ref, lengths_ref, first_ref, rows):
    docs = lengths_ref.shape[0]
    first = first_ref[0]
    query_pos = first + lax.broadcasted_iota(jnp.int32, (rows, 128), 0)

    def step(doc, carry):
        end, start = carry
        end = end + lengths_ref[doc]
        return end, jnp.where(query_pos >= end, end, start)

    _, start = lax.fori_loop(0, docs, step, (jnp.int32(0), jnp.zeros((rows, 128), jnp.int32)))
    lane = lax.broadcasted_iota(jnp.int32, (rows, 128), 1)
    for part in range(SPAN * rows // 128):
        key_pos = first - (SPAN - 1) * rows + part * 128 + lane
        allowed = (key_pos >= start) & (key_pos <= query_pos)
        bias_ref[:, part * 128 : (part + 1) * 128] = jnp.where(allowed, 0.0, MASKED)


def attention_kernel(first_ref, lengths_ref, q_ref, g_ref, far_ref, mid_ref, near_ref, own_ref, *refs):
    (
        out_ref, dq_ref, dfar_ref, dmid_ref, dnear_ref, down_ref,
        bias_ref, key_ref, value_ref, key_t_ref, value_t_ref, p_ref, d_ref, dk_ref, dv_ref,
    ) = refs[-15:]
    rows = q_ref.shape[0]

    @pl.when(pl.program_id(0) == 0)
    def _():
        write_bias(bias_ref, lengths_ref, first_ref, rows)
        value_ref[:, HEAD_SIZE:] = jnp.ones((SPAN * rows, HEAD_SIZE), jnp.bfloat16)

    for j, block in enumerate((far_ref, mid_ref, near_ref, own_ref)):
        span = slice(j * rows, (j + 1) * rows)
        key_ref[span] = block[:, :HEAD_SIZE]
        value_ref[span, :HEAD_SIZE] = block[:, HEAD_SIZE:]
        key_t_ref[:, span] = block[:, :HEAD_SIZE].T
        value_t_ref[:, span] = block[:, HEAD_SIZE:].T
    dk_ref[...] = jnp.zeros_like(dk_ref)
    dv_ref[...] = jnp.zeros_like(dv_ref)

    def step(index, carry):
        qs, gs = [], []
        for unit in range(UNITS):
            cols = pl.ds(pl.multiple_of((index * UNITS + unit) * HEAD_SIZE, HEAD_SIZE), HEAD_SIZE)
            here = slice(unit * rows, (unit + 1) * rows)
            q = q_ref[:, cols]
            g = g_ref[:, cols].astype(jnp.float32)
            s = dot(q, key_t_ref[...]) * EXP2_SCALE + bias_ref[...]
            p = jnp.exp2(s - jnp.max(s, axis=1, keepdims=True)).astype(jnp.bfloat16)
            p_ref[here] = p
            mixed = dot(p, value_ref[...])
            inv = 1.0 / mixed[:, HEAD_SIZE:]
            out = (mixed[:, :HEAD_SIZE] * inv).astype(jnp.bfloat16)
            out_ref[:, cols] = out
            g = g * inv
            delta = jnp.sum(g * out.astype(jnp.float32), axis=1, keepdims=True)
            g = g.astype(jnp.bfloat16)
            d = (p.astype(jnp.float32) * (dot(g, value_t_ref[...]) - delta)).astype(jnp.bfloat16)
            d_ref[here] = d
            dq_ref[:, cols] = (dot(d, key_ref[...]) * SCALE).astype(jnp.bfloat16)
            qs.append(q.T)
            gs.append(g.T)
        dk_ref[...] += dot(jnp.concatenate(qs, axis=1), d_ref[...])
        dv_ref[...] += dot(jnp.concatenate(gs, axis=1), p_ref[...])
        return carry

    lax.fori_loop(0, GROUP // UNITS, step, 0)
    for j, target in enumerate((dfar_ref, dmid_ref, dnear_ref, down_ref)):
        span = slice(j * rows, (j + 1) * rows)
        target[:, :HEAD_SIZE] = (dk_ref[:, span].T * SCALE).astype(target.dtype)
        target[:, HEAD_SIZE:] = dv_ref[:, span].T.astype(target.dtype)


def attention(chunk, first, lengths, queries, out_grad, blocks, grads):
    rows = queries.shape[0]
    wide = GROUP * HEAD_SIZE
    pair = 2 * HEAD_SIZE
    window = SPAN * rows
    query_spec = pl.BlockSpec((rows, wide), lambda i, *_: (0, chunk * CHUNK + i))
    block_spec = pl.BlockSpec((rows, pair), lambda i, *_: (0, i))
    operands = [first, lengths, queries, out_grad, *blocks]
    in_specs = [query_spec] * 2 + [block_spec] * 4
    aliases = {}
    for at, array in enumerate(grads):
        if array is not None:
            aliases[len(operands)] = at
            operands.append(array)
            in_specs.append(pl.BlockSpec(memory_space=pl.ANY))
    bf16, f32 = jnp.bfloat16, jnp.float32
    results = pl.pallas_call(
        attention_kernel,
        out_shape=[jax.ShapeDtypeStruct(queries.shape, bf16)] * 2
        + [jax.ShapeDtypeStruct((rows, CHUNK * pair), kind) for kind in (bf16, f32, f32, f32)],
        grid_spec=pltpu.PrefetchScalarGridSpec(
            num_scalar_prefetch=2,
            grid=(CHUNK,),
            in_specs=in_specs,
            out_specs=[query_spec] * 2 + [block_spec] * 4,
            scratch_shapes=[
                pltpu.VMEM((rows, window), f32),
                pltpu.VMEM((window, HEAD_SIZE), bf16),
                pltpu.VMEM((window, 2 * HEAD_SIZE), bf16),
                pltpu.VMEM((HEAD_SIZE, window), bf16),
                pltpu.VMEM((HEAD_SIZE, window), bf16),
                pltpu.VMEM((UNITS * rows, window), bf16),
                pltpu.VMEM((UNITS * rows, window), bf16),
                pltpu.VMEM((HEAD_SIZE, window), f32),
                pltpu.VMEM((HEAD_SIZE, window), f32),
            ],
        ),
        input_output_aliases=aliases,
        compiler_params=pltpu.CompilerParams(vmem_limit_bytes=48 * 1024 * 1024),
        cost_estimate=pl.CostEstimate(
            flops=12 * CHUNK * rows * GROUP * window * HEAD_SIZE * 2,
            bytes_accessed=CHUNK * (4 * rows * wide * 2 + 22 * rows * pair),
            transcendentals=0,
        ),
        name="attention",
    )(*operands)
    return results[:2], results[2:]


def local(queries, keys, values, out_grad, doc_lengths):
    rows = queries.shape[0]
    index = lax.axis_index(AXES)
    odd = index % 2 == 1
    first = (index * rows).astype(jnp.int32).reshape(1)
    bf16, f32 = jnp.bfloat16, jnp.float32
    chunks = range(KEY_VALUE_HEADS // CHUNK)
    owns, mids, nears, fars = [], [], [], []
    for chunk in chunks:
        parts = []
        for head in range(chunk * CHUNK, (chunk + 1) * CHUNK):
            span = slice(head * HEAD_SIZE, (head + 1) * HEAD_SIZE)
            parts += [keys[:, span], values[:, span]]
        owns.append(jnp.concatenate(parts, axis=1))
        mids.append(passed_along(owns[chunk], 2))
        nears.append(swapped(jnp.where(odd, mids[chunk], owns[chunk])))
        fars.append(passed_along(nears[chunk], 2))
    grads = (None, None)
    totals = []
    for chunk in chunks:
        blocks = (fars[chunk], mids[chunk], nears[chunk], owns[chunk])
        grads, parts = attention(chunk, first, doc_lengths, queries, out_grad, blocks, grads)
        far, mid, near, own = parts
        near = (near + passed_along(far, -2).astype(f32)).astype(bf16)
        got = swapped(near).astype(f32)
        mid = (mid + jnp.where(odd, got, 0.0)).astype(bf16)
        own = own + jnp.where(odd, 0.0, got)
        totals.append((own + passed_along(mid, -2).astype(f32)).astype(bf16))
    key_parts, value_parts = [], []
    for total in totals:
        for head in range(CHUNK):
            start = head * 2 * HEAD_SIZE
            key_parts.append(total[:, start : start + HEAD_SIZE])
            value_parts.append(total[:, start + HEAD_SIZE : start + 2 * HEAD_SIZE])
    return (
        grads[0],
        grads[1],
        jnp.concatenate(key_parts, axis=1),
        jnp.concatenate(value_parts, axis=1),
    )


def solution(mesh):
    spec = P(AXES, None)
    return jax.shard_map(
        local,
        mesh=mesh,
        in_specs=(spec, spec, spec, spec, P()),
        out_specs=(spec, spec, spec, spec),
        check_vma=False,
    )
```

time: 124 us -> 116 us (0.935)
  Pallas kernels: 55.9 us -> 48.6 us
    pallas_call x4 -> x2, Pallas kernels: 55.9 us -> 48.6 us  [attention(): pl.pallas_call(attention_kernel, out_shape=[jax.ShapeDtypeStruct(queries....]
  transfers between devices with their start and end apart: 12 -> 12, of which waited for: 8 -> 8; matrix products, arithmetic and copies ran while one was open for 2% -> 2% of each run, Pallas kernels for 45% -> 42%
where the time goes in v2:
time: 116 us; the launch traced here: 115 us
  Pallas kernels  48.6 us (42%)
  waiting for transfers between devices  31.8 us (27%)
  starting transfers between devices  28.7 us (25%)
  other arithmetic  3.83 us (3%)
  local copies, waits for them, and re-layouts  1.38 us (1%)
    pallas_call x2, Pallas kernels, attention(): pl.pallas_call(attention_kernel, out_shape=[jax.ShapeDtypeStruct(queries....  48.6 us
    ppermute x8, waiting for transfers between devices, passed_along(): lax.ppermute(value, AXES, [(source, source + steps) for source in range(f...  27.8 us
    ppermute x8, starting transfers between devices, passed_along(): lax.ppermute(value, AXES, [(source, source + steps) for source in range(f...  27.6 us
    ppermute x4, waiting for transfers between devices, swapped(): lax.ppermute(value, AXES, [(source, source ^ 1) for source in range(devic...  3.99 us
  transfers between devices with their start and end apart: 12, of which 8 were waited for; matrix products, arithmetic and copies ran while one was open for 2% of the time, Pallas kernels for 42%

profile of v2, /device:TPU:29, one launch (start us, length us, event | category | flops | bytes accessed | tf_op | source)
XLA Modules:
  0.0 115.2 jit_solution(9561581357339624529)
XLA Ops:
  0.7 1.3 %fusion.12 = (bf16[256,128]{1,0:T(8,128)(2,1)S(1)}, bf16[256,128]{1,0:T(8,128)(2,1)S(1)}, bf16[256,128]{1,0:T(8,128)(2,1)S(1)}, bf16[256,128]{1,0:T(8,128)(2,1)S...) fusion(bf16[256,512]{1,0:T(8,128)(2,1)} %param.6, ...), kind=kLoop, calls=%fused_computation.24 | loop fusion | bytes 1048576 | tf_op jit(solution)/shard_map/slice | solution.py:176
  2.0 3.3 %collective-permute-start.3 = (bf16[256,512]{1,0:T(8,128)(2,1)S(1)}, bf16[256,512]{1,0:T(8,128)(2,1)S(1)}, u32[]{:S(2)}, u32[]{:S(2)}) collective-permute-start(bf16[256,512]{1,0:T(8,128)(2,1)S(1)} %pad_maximum_fusion.1.own_ref), channel_id=1, source_target_pairs={{0,2},{1,3},{2,4},{3,5},{4,6},{5,7},{6,8},{7,9},{8,10},{9,11},{10,... | collective-permute-start | bytes 786440 | tf_op jit(solution)/shard_map/ppermute | solution.py:36
  5.4 3.5 %collective-permute-start = (bf16[256,512]{1,0:T(8,128)(2,1)S(1)}, bf16[256,512]{1,0:T(8,128)(2,1)S(1)}, u32[]{:S(2)}, u32[]{:S(2)}) collective-permute-start(bf16[256,512]{1,0:T(8,128)(2,1)S(1)} %pad_maximum_fusion.own_ref), channel_id=1, source_target_pairs={{0,2},{1,3},{2,4},{3,5},{4,6},{5,7},{6,8},{7,9},{8,10},{9,11},{10,... | collective-permute-start | bytes 786440 | tf_op jit(solution)/shard_map/ppermute | solution.py:36
  8.9 2.5 %collective-permute-done.3.mid_ref = bf16[256,512]{1,0:T(8,128)(2,1)S(1)} collective-permute-done((bf16[256,512]{1,0:T(8,128)(2,1)S(1)}, bf16[256,512]{1,0:T(8,128)(2,1)S(1)}, u32[]{:S(2)}, u32[]{:S(2)}) %collective-permute-start.3) | collective-permute-done | bytes 262176 | tf_op jit(solution)/shard_map/ppermute | solution.py:36
  11.4 1.0 broadcast_select_fusion
  12.3 0.3 collective-permute-start.4
  12.6 4.1 %collective-permute-done.mid_ref = bf16[256,512]{1,0:T(8,128)(2,1)S(1)} collective-permute-done((bf16[256,512]{1,0:T(8,128)(2,1)S(1)}, bf16[256,512]{1,0:T(8,128)(2,1)S(1)}, u32[]{:S(2)}, u32[]{:S(2)}) %collective-permute-start) | collective-permute-done | bytes 262176 | tf_op jit(solution)/shard_map/ppermute | solution.py:36
  16.7 0.8 broadcast_select_fusion.1
  17.4 0.2 collective-permute-start.1
  17.7 0.2 collective-permute-done.4.near_ref
  17.8 10.4 %collective-permute-start.5 = (bf16[256,512]{1,0:T(8,128)(2,1)}, bf16[256,512]{1,0:T(8,128)(2,1)}, u32[]{:S(2)}, u32[]{:S(2)}) collective-permute-start(bf16[256,512]{1,0:T(8,128)(2,1)} %collective-permute-done.4.near_ref), channel_id=1, source_target_pairs={{0,2},{1,3},{2,4},{3,5},{4,6},{5,7},{6,8},{7,9},{8,10},{9,11},{10,... | collective-permute-start | bytes 786440 | tf_op jit(solution)/shard_map/ppermute | solution.py:36
  28.2 2.7 %collective-permute-start.2 = (bf16[256,512]{1,0:T(8,128)(2,1)S(1)}, bf16[256,512]{1,0:T(8,128)(2,1)S(1)}, u32[]{:S(2)}, u32[]{:S(2)}) collective-permute-start(bf16[256,512]{1,0:T(8,128)(2,1)S(1)} %collective-permute-done.1.near_ref), channel_id=1, source_target_pairs={{0,2},{1,3},{2,4},{3,5},{4,6},{5,7},{6,8},{7,9},{8,10},{9,11},{10,... | collective-permute-start | bytes 786440 | tf_op jit(solution)/shard_map/ppermute | solution.py:36
  30.9 2.6 %collective-permute-done.5.far_ref = bf16[256,512]{1,0:T(8,128)(2,1)} collective-permute-done((bf16[256,512]{1,0:T(8,128)(2,1)}, bf16[256,512]{1,0:T(8,128)(2,1)}, u32[]{:S(2)}, u32[]{:S(2)}) %collective-permute-start.5) | collective-permute-done | bytes 262176 | tf_op jit(solution)/shard_map/ppermute | solution.py:36
  33.5 24.3 %attention.2 = (bf16[256,4096]{1,0:T(8,128)(2,1)}, bf16[256,4096]{1,0:T(8,128)(2,1)}, bf16[256,512]{1,0:T(8,128)(2,1)S(1)}, f32[256,512]{1,0:T(8,128)S(1)}, f32[...) custom-call(s32[1]{0:T(128)} %bitcast.first_ref, s32[16]{0:T(128)S(1)} %copy-done.1, bf16[256,4096]{1,0:T(8,128)(2,1)S(1)} %copy-done, ...), custom_call_target="tpu_custom_call" | custom-call | flops 12884901888 | bytes 7077888 | tf_op jit(solution)/shard_map/attention/pallas_call | solution.py:131
  57.9 1.9 %collective-permute-start.6 = (bf16[256,512]{1,0:T(8,128)(2,1)S(1)}, bf16[256,512]{1,0:T(8,128)(2,1)S(1)}, u32[]{:S(2)}, u32[]{:S(2)}) collective-permute-start(bf16[256,512]{1,0:T(8,128)(2,1)S(1)} %get-tuple-element.22), channel_id=1, source_target_pairs={{2,0},{3,1},{4,2},{5,3},{6,4},{7,5},{8,6},{9,7},{10,8},{11,9},{12,... | collective-permute-start | bytes 786440 | tf_op jit(solution)/shard_map/ppermute | solution.py:36
  59.8 24.3 %attention.3 = (bf16[256,4096]{1,0:T(8,128)(2,1)}, bf16[256,4096]{1,0:T(8,128)(2,1)}, bf16[256,512]{1,0:T(8,128)(2,1)S(1)}, f32[256,512]{1,0:T(8,128)S(1)}, f32[...) custom-call(s32[1]{0:T(128)} %bitcast.first_ref, s32[16]{0:T(128)S(1)} %copy-done.1, ...), custom_call_target="tpu_custom_call", output_to_operand_aliasing={{0}: (8, {}), {1}: (9, {})} | custom-call | flops 12884901888 | bytes 7077888 | tf_op jit(solution)/shard_map/attention/pallas_call | solution.py:131
  84.1 1.9 %collective-permute-start.9 = (bf16[256,512]{1,0:T(8,128)(2,1)S(1)}, bf16[256,512]{1,0:T(8,128)(2,1)S(1)}, u32[]{:S(2)}, u32[]{:S(2)}) collective-permute-start(bf16[256,512]{1,0:T(8,128)(2,1)S(1)} %get-tuple-element.26), channel_id=1, source_target_pairs={{2,0},{3,1},{4,2},{5,3},{6,4},{7,5},{8,6},{9,7},{10,8},{11,9},{12,... | collective-permute-start | bytes 786440 | tf_op jit(solution)/shard_map/ppermute | solution.py:36
  86.1 0.3 collective-permute-start.7
  86.4 8.8 %collective-permute-done.9 = bf16[256,512]{1,0:T(8,128)(2,1)S(1)} collective-permute-done((bf16[256,512]{1,0:T(8,128)(2,1)S(1)}, bf16[256,512]{1,0:T(8,128)(2,1)S(1)}, u32[]{:S(2)}, u32[]{:S(2)}) %collective-permute-start.9) | collective-permute-done | bytes 262176 | tf_op jit(solution)/shard_map/ppermute | solution.py:36
  95.2 0.1 add_convert_fusion
  95.3 0.3 collective-permute-start.10
  95.6 0.1 fusion.4
  95.7 1.9 %collective-permute-start.8 = (bf16[256,512]{1,0:T(8,128)(2,1)S(1)}, bf16[256,512]{1,0:T(8,128)(2,1)S(1)}, u32[]{:S(2)}, u32[]{:S(2)}) collective-permute-start(bf16[256,512]{1,0:T(8,128)(2,1)S(1)} %fusion.4), channel_id=1, source_target_pairs={{2,0},{3,1},{4,2},{5,3},{6,4},{7,5},{8,6},{9,7},{10,8},{11,9},{12,... | collective-permute-start | bytes 786440 | tf_op jit(solution)/shard_map/ppermute | solution.py:36
  97.6 3.8 %collective-permute-done.10 = bf16[256,512]{1,0:T(8,128)(2,1)S(1)} collective-permute-done((bf16[256,512]{1,0:T(8,128)(2,1)S(1)}, bf16[256,512]{1,0:T(8,128)(2,1)S(1)}, u32[]{:S(2)}, u32[]{:S(2)}) %collective-permute-start.10) | collective-permute-done | bytes 262176 | tf_op jit(solution)/shard_map/ppermute | solution.py:40
  101.4 0.1 fusion.9
  101.5 1.9 %collective-permute-start.11 = (bf16[256,512]{1,0:T(8,128)(2,1)S(1)}, bf16[256,512]{1,0:T(8,128)(2,1)S(1)}, u32[]{:S(2)}, u32[]{:S(2)}) collective-permute-start(bf16[256,512]{1,0:T(8,128)(2,1)S(1)} %fusion.9), channel_id=1, source_target_pairs={{2,0},{3,1},{4,2},{5,3},{6,4},{7,5},{8,6},{9,7},{10,8},{11,9},{12,... | collective-permute-start | bytes 786440 | tf_op jit(solution)/shard_map/ppermute | solution.py:36
  103.4 4.9 %collective-permute-done.8 = bf16[256,512]{1,0:T(8,128)(2,1)S(1)} collective-permute-done((bf16[256,512]{1,0:T(8,128)(2,1)S(1)}, bf16[256,512]{1,0:T(8,128)(2,1)S(1)}, u32[]{:S(2)}, u32[]{:S(2)}) %collective-permute-start.8) | collective-permute-done | bytes 262176 | tf_op jit(solution)/shard_map/ppermute | solution.py:36
  108.4 0.1 fusion.2
  108.6 4.9 %collective-permute-done.11 = bf16[256,512]{1,0:T(8,128)(2,1)S(1)} collective-permute-done((bf16[256,512]{1,0:T(8,128)(2,1)S(1)}, bf16[256,512]{1,0:T(8,128)(2,1)S(1)}, u32[]{:S(2)}, u32[]{:S(2)}) %collective-permute-start.11) | collective-permute-done | bytes 262176 | tf_op jit(solution)/shard_map/ppermute | solution.py:36
  113.5 0.1 fusion.7
  113.7 0.7 pad_maximum_fusion.3
  114.4 0.7 pad_maximum_fusion.2
  (17 shorter events, 0.3 us)
Async XLA Ops:
  0.6 32.9 %copy-start.1 = (s32[16]{0:T(128)S(1)}, s32[16]{0:T(128)}, u32[]{:S(2)}) copy-start(s32[16]{0:T(128)} %lengths_ref.3) | copy-start | bytes 196
  0.6 32.9 %copy-start = (bf16[256,4096]{1,0:T(8,128)(2,1)S(1)}, bf16[256,4096]{1,0:T(8,128)(2,1)}, u32[]{:S(2)}) copy-start(bf16[256,4096]{1,0:T(8,128)(2,1)} %q_ref.3) | copy-start | bytes 6291460
  1.9 3.4 %copy-start.2 = (bf16[256,128]{1,0:T(8,128)(2,1)}, bf16[256,128]{1,0:T(8,128)(2,1)S(1)}, u32[]{:S(2)}) copy-start(bf16[256,128]{1,0:T(8,128)(2,1)S(1)} %get-tuple-element.44) | copy-start | bytes 196612
  1.9 3.4 %copy-start.3 = (bf16[256,128]{1,0:T(8,128)(2,1)}, bf16[256,128]{1,0:T(8,128)(2,1)S(1)}, u32[]{:S(2)}) copy-start(bf16[256,128]{1,0:T(8,128)(2,1)S(1)} %get-tuple-element.47) | copy-start | bytes 196612
  2.0 9.4 %collective-permute-start.3 = (bf16[256,512]{1,0:T(8,128)(2,1)S(1)}, bf16[256,512]{1,0:T(8,128)(2,1)S(1)}, u32[]{:S(2)}, u32[]{:S(2)}) collective-permute-start(bf16[256,512]{1,0:T(8,128)(2,1)S(1)} %pad_maximum_fusion.1.own_ref), channel_id=1, source_target_pairs={{0,2},{1,3},{2,4},{3,5},{4,6},{5,7},{6,8},{7,9},{8,10},{9,11},{10,... | collective-permute-start | bytes 786440 | tf_op jit(solution)/shard_map/ppermute | solution.py:36
  5.4 11.3 %collective-permute-start = (bf16[256,512]{1,0:T(8,128)(2,1)S(1)}, bf16[256,512]{1,0:T(8,128)(2,1)S(1)}, u32[]{:S(2)}, u32[]{:S(2)}) collective-permute-start(bf16[256,512]{1,0:T(8,128)(2,1)S(1)} %pad_maximum_fusion.own_ref), channel_id=1, source_target_pairs={{0,2},{1,3},{2,4},{3,5},{4,6},{5,7},{6,8},{7,9},{8,10},{9,11},{10,... | collective-permute-start | bytes 786440 | tf_op jit(solution)/shard_map/ppermute | solution.py:36
  12.3 5.5 %collective-permute-start.4 = (bf16[256,512]{1,0:T(8,128)(2,1)S(1)}, bf16[256,512]{1,0:T(8,128)(2,1)}, u32[]{:S(2)}, u32[]{:S(2)}) collective-permute-start(bf16[256,512]{1,0:T(8,128)(2,1)S(1)} %broadcast_select_fusion), channel_id=1, source_target_pairs={{0,1},{1,0},{2,3},{3,2},{4,5},{5,4},{6,7},{7,6},{8,9},{9,8},{10,11... | collective-permute-start | bytes 786440 | tf_op jit(solution)/shard_map/ppermute | solution.py:40
  17.4 10.8 %collective-permute-start.1 = (bf16[256,512]{1,0:T(8,128)(2,1)}, bf16[256,512]{1,0:T(8,128)(2,1)S(1)}, u32[]{:S(2)}, u32[]{:S(2)}) collective-permute-start(bf16[256,512]{1,0:T(8,128)(2,1)} %broadcast_select_fusion.1), channel_id=1, source_target_pairs={{0,1},{1,0},{2,3},{3,2},{4,5},{5,4},{6,7},{7,6},{8,9},{9,8},{10,11... | collective-permute-start | bytes 786440 | tf_op jit(solution)/shard_map/ppermute | solution.py:40
  17.8 15.7 %collective-permute-start.5 = (bf16[256,512]{1,0:T(8,128)(2,1)}, bf16[256,512]{1,0:T(8,128)(2,1)}, u32[]{:S(2)}, u32[]{:S(2)}) collective-permute-start(bf16[256,512]{1,0:T(8,128)(2,1)} %collective-permute-done.4.near_ref), channel_id=1, source_target_pairs={{0,2},{1,3},{2,4},{3,5},{4,6},{5,7},{6,8},{7,9},{8,10},{9,11},{10,... | collective-permute-start | bytes 786440 | tf_op jit(solution)/shard_map/ppermute | solution.py:36
  28.2 31.5 %collective-permute-start.2 = (bf16[256,512]{1,0:T(8,128)(2,1)S(1)}, bf16[256,512]{1,0:T(8,128)(2,1)S(1)}, u32[]{:S(2)}, u32[]{:S(2)}) collective-permute-start(bf16[256,512]{1,0:T(8,128)(2,1)S(1)} %collective-permute-done.1.near_ref), channel_id=1, source_target_pairs={{0,2},{1,3},{2,4},{3,5},{4,6},{5,7},{6,8},{7,9},{8,10},{9,11},{10,... | collective-permute-start | bytes 786440 | tf_op jit(solution)/shard_map/ppermute | solution.py:36
  57.9 28.1 %collective-permute-start.6 = (bf16[256,512]{1,0:T(8,128)(2,1)S(1)}, bf16[256,512]{1,0:T(8,128)(2,1)S(1)}, u32[]{:S(2)}, u32[]{:S(2)}) collective-permute-start(bf16[256,512]{1,0:T(8,128)(2,1)S(1)} %get-tuple-element.22), channel_id=1, source_target_pairs={{2,0},{3,1},{4,2},{5,3},{6,4},{7,5},{8,6},{9,7},{10,8},{11,9},{12,... | collective-permute-start | bytes 786440 | tf_op jit(solution)/shard_map/ppermute | solution.py:36
  84.1 11.1 %collective-permute-start.9 = (bf16[256,512]{1,0:T(8,128)(2,1)S(1)}, bf16[256,512]{1,0:T(8,128)(2,1)S(1)}, u32[]{:S(2)}, u32[]{:S(2)}) collective-permute-start(bf16[256,512]{1,0:T(8,128)(2,1)S(1)} %get-tuple-element.26), channel_id=1, source_target_pairs={{2,0},{3,1},{4,2},{5,3},{6,4},{7,5},{8,6},{9,7},{10,8},{11,9},{12,... | collective-permute-start | bytes 786440 | tf_op jit(solution)/shard_map/ppermute | solution.py:36
  86.1 9.5 %collective-permute-start.7 = (bf16[256,512]{1,0:T(8,128)(2,1)S(1)}, bf16[256,512]{1,0:T(8,128)(2,1)S(1)}, u32[]{:S(2)}, u32[]{:S(2)}) collective-permute-start(bf16[256,512]{1,0:T(8,128)(2,1)S(1)} %add_convert_fusion.1), channel_id=1, source_target_pairs={{0,1},{1,0},{2,3},{3,2},{4,5},{5,4},{6,7},{7,6},{8,9},{9,8},{10,11... | collective-permute-start | bytes 786440 | tf_op jit(solution)/shard_map/ppermute | solution.py:40
  95.3 6.1 %collective-permute-start.10 = (bf16[256,512]{1,0:T(8,128)(2,1)S(1)}, bf16[256,512]{1,0:T(8,128)(2,1)S(1)}, u32[]{:S(2)}, u32[]{:S(2)}) collective-permute-start(bf16[256,512]{1,0:T(8,128)(2,1)S(1)} %add_convert_fusion), channel_id=1, source_target_pairs={{0,1},{1,0},{2,3},{3,2},{4,5},{5,4},{6,7},{7,6},{8,9},{9,8},{10,11... | collective-permute-start | bytes 786440 | tf_op jit(solution)/shard_map/ppermute | solution.py:40
  95.7 12.7 %collective-permute-start.8 = (bf16[256,512]{1,0:T(8,128)(2,1)S(1)}, bf16[256,512]{1,0:T(8,128)(2,1)S(1)}, u32[]{:S(2)}, u32[]{:S(2)}) collective-permute-start(bf16[256,512]{1,0:T(8,128)(2,1)S(1)} %fusion.4), channel_id=1, source_target_pairs={{2,0},{3,1},{4,2},{5,3},{6,4},{7,5},{8,6},{9,7},{10,8},{11,9},{12,... | collective-permute-start | bytes 786440 | tf_op jit(solution)/shard_map/ppermute | solution.py:36
  101.5 12.0 %collective-permute-start.11 = (bf16[256,512]{1,0:T(8,128)(2,1)S(1)}, bf16[256,512]{1,0:T(8,128)(2,1)S(1)}, u32[]{:S(2)}, u32[]{:S(2)}) collective-permute-start(bf16[256,512]{1,0:T(8,128)(2,1)S(1)} %fusion.9), channel_id=1, source_target_pairs={{2,0},{3,1},{4,2},{5,3},{6,4},{7,5},{8,6},{9,7},{10,8},{11,9},{12,... | collective-permute-start | bytes 786440 | tf_op jit(solution)/shard_map/ppermute | solution.py:36

commit v3 on v2

--- a/solution.py
+++ b/solution.py
@@ -14,7 +14,7 @@
 SPAN = 4
 AXES = ("blk", "inner")
 CHUNK = 2
-UNITS = 2
+ROWS = 32
 MASKED = -1e30
 SCALE = 1.0 / math.sqrt(HEAD_SIZE)
 EXP2_SCALE = SCALE * math.log2(math.e)
@@ -61,51 +61,91 @@
 def attention_kernel(first_ref, lengths_ref, q_ref, g_ref, far_ref, mid_ref, near_ref, own_ref, *refs):
     (
         out_ref, dq_ref, dfar_ref, dmid_ref, dnear_ref, down_ref,
-        bias_ref, key_ref, value_ref, key_t_ref, value_t_ref, p_ref, d_ref, dk_ref, dv_ref,
-    ) = refs[-15:]
+        bias_ref, key_ref, value_ref, key_t_ref, value_t_ref, dk_ref, dv_ref, inv_ref, *slots,
+    ) = refs[-26:]
+    s_refs, p_refs, dp_refs, d_refs, g_refs, delta_refs = (slots[i : i + 2] for i in range(0, 12, 2))
     rows = q_ref.shape[0]
+    window = SPAN * rows
 
     @pl.when(pl.program_id(0) == 0)
     def _():
         write_bias(bias_ref, lengths_ref, first_ref, rows)
-        value_ref[:, HEAD_SIZE:] = jnp.ones((SPAN * rows, HEAD_SIZE), jnp.bfloat16)
+        for ref in (*p_refs, *d_refs):
+            ref[...] = jnp.zeros_like(ref)
 
     for j, block in enumerate((far_ref, mid_ref, near_ref, own_ref)):
         span = slice(j * rows, (j + 1) * rows)
         key_ref[span] = block[:, :HEAD_SIZE]
-        value_ref[span, :HEAD_SIZE] = block[:, HEAD_SIZE:]
+        value_ref[span] = block[:, HEAD_SIZE:]
         key_t_ref[:, span] = block[:, :HEAD_SIZE].T
         value_t_ref[:, span] = block[:, HEAD_SIZE:].T
     dk_ref[...] = jnp.zeros_like(dk_ref)
     dv_ref[...] = jnp.zeros_like(dv_ref)
+    p_refs[1][...] = jnp.zeros_like(p_refs[1])
+    dp_refs[1][...] = jnp.zeros_like(dp_refs[1])
+    g_refs[1][...] = jnp.zeros_like(g_refs[1])
+    delta_refs[1][...] = jnp.zeros_like(delta_refs[1])
+
+    chunks = [
+        (slice(r, r + ROWS), slice((r + 1) // 128 * 128, -(-(window - rows + r + ROWS) // 128) * 128))
+        for r in range(0, rows, ROWS)
+    ]
+
+    def columns(head):
+        return pl.ds(pl.multiple_of(head * HEAD_SIZE, HEAD_SIZE), HEAD_SIZE)
+
+    def scores(head, slot):
+        s_refs[slot][...] = dot(q_ref[:, columns(head)], key_t_ref[...])
+
+    def softmax(slot):
+        for here, keys in chunks:
+            s = s_refs[slot][here, keys] * EXP2_SCALE + bias_ref[here, keys]
+            e = jnp.exp2(s - jnp.max(s, axis=1, keepdims=True))
+            inv = 1.0 / jnp.sum(e, axis=1, keepdims=True)
+            inv_ref[here] = jnp.broadcast_to(inv, (ROWS, HEAD_SIZE))
+            p_refs[slot][here, keys] = e.astype(jnp.bfloat16)
+
+    def mix(head, slot):
+        cols = columns(head)
+        mixed = dot(p_refs[slot][...], value_ref[...])
+        inv = inv_ref[...]
+        out = (mixed * inv).astype(jnp.bfloat16)
+        out_ref[:, cols] = out
+        g = g_ref[:, cols].astype(jnp.float32) * inv
+        delta = jnp.sum(g * out.astype(jnp.float32), axis=1, keepdims=True)
+        delta_refs[slot][...] = jnp.broadcast_to(delta, (rows, HEAD_SIZE))
+        g_refs[slot][...] = g.astype(jnp.bfloat16)
+        dp_refs[slot][...] = dot(g_refs[slot][...], value_t_ref[...])
+
+    def score_grad(slot):
+        for here, keys in chunks:
+            repeat = (keys.stop - keys.start) // HEAD_SIZE
+            delta = jnp.concatenate([delta_refs[slot][here]] * repeat, axis=1)
+            p = p_refs[slot][here, keys].astype(jnp.float32)
+            d_refs[slot][here, keys] = (p * (dp_refs[slot][here, keys] - delta)).astype(jnp.bfloat16)
+
+    def spread(head, slot):
+        cols = columns(head)
+        dq_ref[:, cols] = (dot(d_refs[slot][...], key_ref[...]) * SCALE).astype(jnp.bfloat16)
+        dk_ref[...] += dot(q_ref[:, cols].T, d_refs[slot][...])
+        dv_ref[...] += dot(g_refs[slot][...].T, p_refs[slot][...])
+
+    scores(0, 0)
 
     def step(index, carry):
-        qs, gs = [], []
-        for unit in range(UNITS):
-            cols = pl.ds(pl.multiple_of((index * UNITS + unit) * HEAD_SIZE, HEAD_SIZE), HEAD_SIZE)
-            here = slice(unit * rows, (unit + 1) * rows)
-            q = q_ref[:, cols]
-            g = g_ref[:, cols].astype(jnp.float32)
-            s = dot(q, key_t_ref[...]) * EXP2_SCALE + bias_ref[...]
-            p = jnp.exp2(s - jnp.max(s, axis=1, keepdims=True)).astype(jnp.bfloat16)
-            p_ref[here] = p
-            mixed = dot(p, value_ref[...])
-            inv = 1.0 / mixed[:, HEAD_SIZE:]
-            out = (mixed[:, :HEAD_SIZE] * inv).astype(jnp.bfloat16)
-            out_ref[:, cols] = out
-            g = g * inv
-            delta = jnp.sum(g * out.astype(jnp.float32), axis=1, keepdims=True)
-            g = g.astype(jnp.bfloat16)
-            d = (p.astype(jnp.float32) * (dot(g, value_t_ref[...]) - delta)).astype(jnp.bfloat16)
-            d_ref[here] = d
-            dq_ref[:, cols] = (dot(d, key_ref[...]) * SCALE).astype(jnp.bfloat16)
-            qs.append(q.T)
-            gs.append(g.T)
-        dk_ref[...] += dot(jnp.concatenate(qs, axis=1), d_ref[...])
-        dv_ref[...] += dot(jnp.concatenate(gs, axis=1), p_ref[...])
+        for slot in range(2):
+            head = 2 * index + slot
+            before = jnp.maximum(head - 1, 0)
+            scores(jnp.minimum(head + 1, GROUP - 1), 1 - slot)
+            score_grad(1 - slot)
+            softmax(slot)
+            spread(before, 1 - slot)
+            mix(head, slot)
         return carry
 
-    lax.fori_loop(0, GROUP // UNITS, step, 0)
+    lax.fori_loop(0, GROUP // 2, step, 0)
+    score_grad(1)
+    spread(GROUP - 1, 1)
     for j, target in enumerate((dfar_ref, dmid_ref, dnear_ref, down_ref)):
         span = slice(j * rows, (j + 1) * rows)
         target[:, :HEAD_SIZE] = (dk_ref[:, span].T * SCALE).astype(target.dtype)
@@ -140,13 +180,24 @@
             scratch_shapes=[
                 pltpu.VMEM((rows, window), f32),
                 pltpu.VMEM((window, HEAD_SIZE), bf16),
-                pltpu.VMEM((window, 2 * HEAD_SIZE), bf16),
+                pltpu.VMEM((window, HEAD_SIZE), bf16),
                 pltpu.VMEM((HEAD_SIZE, window), bf16),
                 pltpu.VMEM((HEAD_SIZE, window), bf16),
-                pltpu.VMEM((UNITS * rows, window), bf16),
-                pltpu.VMEM((UNITS * rows, window), bf16),
                 pltpu.VMEM((HEAD_SIZE, window), f32),
                 pltpu.VMEM((HEAD_SIZE, window), f32),
+                pltpu.VMEM((rows, HEAD_SIZE), f32),
+            ]
+            + [
+                pltpu.VMEM((rows, columns), kind)
+                for columns, kind in (
+                    (window, f32),
+                    (window, bf16),
+                    (window, f32),
+                    (window, bf16),
+                    (HEAD_SIZE, bf16),
+                    (HEAD_SIZE, f32),
+                )
+                for _ in range(2)
             ],
         ),
         input_output_aliases=aliases,

time: 116 us -> 107 us (0.922)
  Pallas kernels: 48.6 us -> 39.9 us
    pallas_call x2, Pallas kernels: 48.6 us -> 39.9 us  [attention(): pl.pallas_call(attention_kernel, out_shape=[jax.ShapeDtypeStruct(queries....]
  transfers between devices with their start and end apart: 12 -> 12, of which waited for: 8 -> 8; matrix products, arithmetic and copies ran while one was open for 2% -> 2% of each run, Pallas kernels for 42% -> 37%
where the time goes in v3:
time: 107 us; the launch traced here: 106 us
  Pallas kernels  39.9 us (37%)
  waiting for transfers between devices  31.8 us (30%)
  starting transfers between devices  28.7 us (27%)
  other arithmetic  3.83 us (4%)
  local copies, waits for them, and re-layouts  1.38 us (1%)
    pallas_call x2, Pallas kernels, attention(): pl.pallas_call(attention_kernel, out_shape=[jax.ShapeDtypeStruct(queries....  39.9 us
    ppermute x8, waiting for transfers between devices, passed_along(): lax.ppermute(value, AXES, [(source, source + steps) for source in range(f...  27.8 us
    ppermute x8, starting transfers between devices, passed_along(): lax.ppermute(value, AXES, [(source, source + steps) for source in range(f...  27.6 us
    ppermute x4, waiting for transfers between devices, swapped(): lax.ppermute(value, AXES, [(source, source ^ 1) for source in range(devic...  3.99 us
  transfers between devices with their start and end apart: 12, of which 8 were waited for; matrix products, arithmetic and copies ran while one was open for 2% of the time, Pallas kernels for 37%

profile of v3, /device:TPU:29, one launch (start us, length us, event | category | flops | bytes accessed | tf_op | source)
XLA Modules:
  0.0 106.4 jit_solution(18048195994790012150)
XLA Ops:
  0.7 1.3 %fusion.12 = (bf16[256,128]{1,0:T(8,128)(2,1)S(1)}, bf16[256,128]{1,0:T(8,128)(2,1)S(1)}, bf16[256,128]{1,0:T(8,128)(2,1)S(1)}, bf16[256,128]{1,0:T(8,128)(2,1)S...) fusion(bf16[256,512]{1,0:T(8,128)(2,1)} %param.6, ...), kind=kLoop, calls=%fused_computation.24 | loop fusion | bytes 1048576 | tf_op jit(solution)/shard_map/slice | solution.py:227
  2.0 3.3 %collective-permute-start.3 = (bf16[256,512]{1,0:T(8,128)(2,1)S(1)}, bf16[256,512]{1,0:T(8,128)(2,1)S(1)}, u32[]{:S(2)}, u32[]{:S(2)}) collective-permute-start(bf16[256,512]{1,0:T(8,128)(2,1)S(1)} %pad_maximum_fusion.1.own_ref), channel_id=1, source_target_pairs={{0,2},{1,3},{2,4},{3,5},{4,6},{5,7},{6,8},{7,9},{8,10},{9,11},{10,... | collective-permute-start | bytes 786440 | tf_op jit(solution)/shard_map/ppermute | solution.py:36
  5.4 3.5 %collective-permute-start = (bf16[256,512]{1,0:T(8,128)(2,1)S(1)}, bf16[256,512]{1,0:T(8,128)(2,1)S(1)}, u32[]{:S(2)}, u32[]{:S(2)}) collective-permute-start(bf16[256,512]{1,0:T(8,128)(2,1)S(1)} %pad_maximum_fusion.own_ref), channel_id=1, source_target_pairs={{0,2},{1,3},{2,4},{3,5},{4,6},{5,7},{6,8},{7,9},{8,10},{9,11},{10,... | collective-permute-start | bytes 786440 | tf_op jit(solution)/shard_map/ppermute | solution.py:36
  8.9 2.5 %collective-permute-done.3.mid_ref = bf16[256,512]{1,0:T(8,128)(2,1)S(1)} collective-permute-done((bf16[256,512]{1,0:T(8,128)(2,1)S(1)}, bf16[256,512]{1,0:T(8,128)(2,1)S(1)}, u32[]{:S(2)}, u32[]{:S(2)}) %collective-permute-start.3) | collective-permute-done | bytes 262176 | tf_op jit(solution)/shard_map/ppermute | solution.py:36
  11.4 1.0 broadcast_select_fusion
  12.3 0.3 collective-permute-start.4
  12.6 4.1 %collective-permute-done.mid_ref = bf16[256,512]{1,0:T(8,128)(2,1)S(1)} collective-permute-done((bf16[256,512]{1,0:T(8,128)(2,1)S(1)}, bf16[256,512]{1,0:T(8,128)(2,1)S(1)}, u32[]{:S(2)}, u32[]{:S(2)}) %collective-permute-start) | collective-permute-done | bytes 262176 | tf_op jit(solution)/shard_map/ppermute | solution.py:36
  16.7 0.8 broadcast_select_fusion.1
  17.4 0.2 collective-permute-start.1
  17.7 0.2 collective-permute-done.4.near_ref
  17.8 10.4 %collective-permute-start.5 = (bf16[256,512]{1,0:T(8,128)(2,1)}, bf16[256,512]{1,0:T(8,128)(2,1)}, u32[]{:S(2)}, u32[]{:S(2)}) collective-permute-start(bf16[256,512]{1,0:T(8,128)(2,1)} %collective-permute-done.4.near_ref), channel_id=1, source_target_pairs={{0,2},{1,3},{2,4},{3,5},{4,6},{5,7},{6,8},{7,9},{8,10},{9,11},{10,... | collective-permute-start | bytes 786440 | tf_op jit(solution)/shard_map/ppermute | solution.py:36
  28.2 2.7 %collective-permute-start.2 = (bf16[256,512]{1,0:T(8,128)(2,1)S(1)}, bf16[256,512]{1,0:T(8,128)(2,1)S(1)}, u32[]{:S(2)}, u32[]{:S(2)}) collective-permute-start(bf16[256,512]{1,0:T(8,128)(2,1)S(1)} %collective-permute-done.1.near_ref), channel_id=1, source_target_pairs={{0,2},{1,3},{2,4},{3,5},{4,6},{5,7},{6,8},{7,9},{8,10},{9,11},{10,... | collective-permute-start | bytes 786440 | tf_op jit(solution)/shard_map/ppermute | solution.py:36
  30.9 2.6 %collective-permute-done.5.far_ref = bf16[256,512]{1,0:T(8,128)(2,1)} collective-permute-done((bf16[256,512]{1,0:T(8,128)(2,1)}, bf16[256,512]{1,0:T(8,128)(2,1)}, u32[]{:S(2)}, u32[]{:S(2)}) %collective-permute-start.5) | collective-permute-done | bytes 262176 | tf_op jit(solution)/shard_map/ppermute | solution.py:36
  33.5 19.9 %attention.2 = (bf16[256,4096]{1,0:T(8,128)(2,1)}, bf16[256,4096]{1,0:T(8,128)(2,1)}, bf16[256,512]{1,0:T(8,128)(2,1)S(1)}, f32[256,512]{1,0:T(8,128)S(1)}, f32[...) custom-call(s32[1]{0:T(128)} %bitcast.first_ref, s32[16]{0:T(128)S(1)} %copy-done.1, bf16[256,4096]{1,0:T(8,128)(2,1)S(1)} %copy-done, ...), custom_call_target="tpu_custom_call" | custom-call | flops 12884901888 | bytes 7077888 | tf_op jit(solution)/shard_map/attention/pallas_call | solution.py:171
  53.5 1.9 %collective-permute-start.6 = (bf16[256,512]{1,0:T(8,128)(2,1)S(1)}, bf16[256,512]{1,0:T(8,128)(2,1)S(1)}, u32[]{:S(2)}, u32[]{:S(2)}) collective-permute-start(bf16[256,512]{1,0:T(8,128)(2,1)S(1)} %get-tuple-element.22), channel_id=1, source_target_pairs={{2,0},{3,1},{4,2},{5,3},{6,4},{7,5},{8,6},{9,7},{10,8},{11,9},{12,... | collective-permute-start | bytes 786440 | tf_op jit(solution)/shard_map/ppermute | solution.py:36
  55.4 19.9 %attention.3 = (bf16[256,4096]{1,0:T(8,128)(2,1)}, bf16[256,4096]{1,0:T(8,128)(2,1)}, bf16[256,512]{1,0:T(8,128)(2,1)S(1)}, f32[256,512]{1,0:T(8,128)S(1)}, f32[...) custom-call(s32[1]{0:T(128)} %bitcast.first_ref, s32[16]{0:T(128)S(1)} %copy-done.1, ...), custom_call_target="tpu_custom_call", output_to_operand_aliasing={{0}: (8, {}), {1}: (9, {})} | custom-call | flops 12884901888 | bytes 7077888 | tf_op jit(solution)/shard_map/attention/pallas_call | solution.py:171
  75.3 1.9 %collective-permute-start.9 = (bf16[256,512]{1,0:T(8,128)(2,1)S(1)}, bf16[256,512]{1,0:T(8,128)(2,1)S(1)}, u32[]{:S(2)}, u32[]{:S(2)}) collective-permute-start(bf16[256,512]{1,0:T(8,128)(2,1)S(1)} %get-tuple-element.26), channel_id=1, source_target_pairs={{2,0},{3,1},{4,2},{5,3},{6,4},{7,5},{8,6},{9,7},{10,8},{11,9},{12,... | collective-permute-start | bytes 786440 | tf_op jit(solution)/shard_map/ppermute | solution.py:36
  77.3 0.3 collective-permute-start.7
  77.6 8.8 %collective-permute-done.9 = bf16[256,512]{1,0:T(8,128)(2,1)S(1)} collective-permute-done((bf16[256,512]{1,0:T(8,128)(2,1)S(1)}, bf16[256,512]{1,0:T(8,128)(2,1)S(1)}, u32[]{:S(2)}, u32[]{:S(2)}) %collective-permute-start.9) | collective-permute-done | bytes 262176 | tf_op jit(solution)/shard_map/ppermute | solution.py:36
  86.5 0.1 add_convert_fusion
  86.5 0.3 collective-permute-start.10
  86.8 0.1 fusion.4
  86.9 1.9 %collective-permute-start.8 = (bf16[256,512]{1,0:T(8,128)(2,1)S(1)}, bf16[256,512]{1,0:T(8,128)(2,1)S(1)}, u32[]{:S(2)}, u32[]{:S(2)}) collective-permute-start(bf16[256,512]{1,0:T(8,128)(2,1)S(1)} %fusion.4), channel_id=1, source_target_pairs={{2,0},{3,1},{4,2},{5,3},{6,4},{7,5},{8,6},{9,7},{10,8},{11,9},{12,... | collective-permute-start | bytes 786440 | tf_op jit(solution)/shard_map/ppermute | solution.py:36
  88.8 3.8 %collective-permute-done.10 = bf16[256,512]{1,0:T(8,128)(2,1)S(1)} collective-permute-done((bf16[256,512]{1,0:T(8,128)(2,1)S(1)}, bf16[256,512]{1,0:T(8,128)(2,1)S(1)}, u32[]{:S(2)}, u32[]{:S(2)}) %collective-permute-start.10) | collective-permute-done | bytes 262176 | tf_op jit(solution)/shard_map/ppermute | solution.py:40
  92.7 0.1 fusion.9
  92.8 1.9 %collective-permute-start.11 = (bf16[256,512]{1,0:T(8,128)(2,1)S(1)}, bf16[256,512]{1,0:T(8,128)(2,1)S(1)}, u32[]{:S(2)}, u32[]{:S(2)}) collective-permute-start(bf16[256,512]{1,0:T(8,128)(2,1)S(1)} %fusion.9), channel_id=1, source_target_pairs={{2,0},{3,1},{4,2},{5,3},{6,4},{7,5},{8,6},{9,7},{10,8},{11,9},{12,... | collective-permute-start | bytes 786440 | tf_op jit(solution)/shard_map/ppermute | solution.py:36
  94.7 4.9 %collective-permute-done.8 = bf16[256,512]{1,0:T(8,128)(2,1)S(1)} collective-permute-done((bf16[256,512]{1,0:T(8,128)(2,1)S(1)}, bf16[256,512]{1,0:T(8,128)(2,1)S(1)}, u32[]{:S(2)}, u32[]{:S(2)}) %collective-permute-start.8) | collective-permute-done | bytes 262176 | tf_op jit(solution)/shard_map/ppermute | solution.py:36
  99.6 0.1 fusion.2
  99.8 4.9 %collective-permute-done.11 = bf16[256,512]{1,0:T(8,128)(2,1)S(1)} collective-permute-done((bf16[256,512]{1,0:T(8,128)(2,1)S(1)}, bf16[256,512]{1,0:T(8,128)(2,1)S(1)}, u32[]{:S(2)}, u32[]{:S(2)}) %collective-permute-start.11) | collective-permute-done | bytes 262176 | tf_op jit(solution)/shard_map/ppermute | solution.py:36
  104.7 0.1 fusion.7
  104.9 0.7 pad_maximum_fusion.3
  105.6 0.7 pad_maximum_fusion.2
  (17 shorter events, 0.3 us)
Async XLA Ops:
  0.6 32.9 %copy-start.1 = (s32[16]{0:T(128)S(1)}, s32[16]{0:T(128)}, u32[]{:S(2)}) copy-start(s32[16]{0:T(128)} %lengths_ref.3) | copy-start | bytes 196
  0.6 32.9 %copy-start = (bf16[256,4096]{1,0:T(8,128)(2,1)S(1)}, bf16[256,4096]{1,0:T(8,128)(2,1)}, u32[]{:S(2)}) copy-start(bf16[256,4096]{1,0:T(8,128)(2,1)} %q_ref.3) | copy-start | bytes 6291460
  1.9 3.4 %copy-start.2 = (bf16[256,128]{1,0:T(8,128)(2,1)}, bf16[256,128]{1,0:T(8,128)(2,1)S(1)}, u32[]{:S(2)}) copy-start(bf16[256,128]{1,0:T(8,128)(2,1)S(1)} %get-tuple-element.44) | copy-start | bytes 196612
  1.9 3.4 %copy-start.3 = (bf16[256,128]{1,0:T(8,128)(2,1)}, bf16[256,128]{1,0:T(8,128)(2,1)S(1)}, u32[]{:S(2)}) copy-start(bf16[256,128]{1,0:T(8,128)(2,1)S(1)} %get-tuple-element.47) | copy-start | bytes 196612
  2.0 9.4 %collective-permute-start.3 = (bf16[256,512]{1,0:T(8,128)(2,1)S(1)}, bf16[256,512]{1,0:T(8,128)(2,1)S(1)}, u32[]{:S(2)}, u32[]{:S(2)}) collective-permute-start(bf16[256,512]{1,0:T(8,128)(2,1)S(1)} %pad_maximum_fusion.1.own_ref), channel_id=1, source_target_pairs={{0,2},{1,3},{2,4},{3,5},{4,6},{5,7},{6,8},{7,9},{8,10},{9,11},{10,... | collective-permute-start | bytes 786440 | tf_op jit(solution)/shard_map/ppermute | solution.py:36
  5.4 11.3 %collective-permute-start = (bf16[256,512]{1,0:T(8,128)(2,1)S(1)}, bf16[256,512]{1,0:T(8,128)(2,1)S(1)}, u32[]{:S(2)}, u32[]{:S(2)}) collective-permute-start(bf16[256,512]{1,0:T(8,128)(2,1)S(1)} %pad_maximum_fusion.own_ref), channel_id=1, source_target_pairs={{0,2},{1,3},{2,4},{3,5},{4,6},{5,7},{6,8},{7,9},{8,10},{9,11},{10,... | collective-permute-start | bytes 786440 | tf_op jit(solution)/shard_map/ppermute | solution.py:36
  12.3 5.5 %collective-permute-start.4 = (bf16[256,512]{1,0:T(8,128)(2,1)S(1)}, bf16[256,512]{1,0:T(8,128)(2,1)}, u32[]{:S(2)}, u32[]{:S(2)}) collective-permute-start(bf16[256,512]{1,0:T(8,128)(2,1)S(1)} %broadcast_select_fusion), channel_id=1, source_target_pairs={{0,1},{1,0},{2,3},{3,2},{4,5},{5,4},{6,7},{7,6},{8,9},{9,8},{10,11... | collective-permute-start | bytes 786440 | tf_op jit(solution)/shard_map/ppermute | solution.py:40
  17.4 10.8 %collective-permute-start.1 = (bf16[256,512]{1,0:T(8,128)(2,1)}, bf16[256,512]{1,0:T(8,128)(2,1)S(1)}, u32[]{:S(2)}, u32[]{:S(2)}) collective-permute-start(bf16[256,512]{1,0:T(8,128)(2,1)} %broadcast_select_fusion.1), channel_id=1, source_target_pairs={{0,1},{1,0},{2,3},{3,2},{4,5},{5,4},{6,7},{7,6},{8,9},{9,8},{10,11... | collective-permute-start | bytes 786440 | tf_op jit(solution)/shard_map/ppermute | solution.py:40
  17.8 15.7 %collective-permute-start.5 = (bf16[256,512]{1,0:T(8,128)(2,1)}, bf16[256,512]{1,0:T(8,128)(2,1)}, u32[]{:S(2)}, u32[]{:S(2)}) collective-permute-start(bf16[256,512]{1,0:T(8,128)(2,1)} %collective-permute-done.4.near_ref), channel_id=1, source_target_pairs={{0,2},{1,3},{2,4},{3,5},{4,6},{5,7},{6,8},{7,9},{8,10},{9,11},{10,... | collective-permute-start | bytes 786440 | tf_op jit(solution)/shard_map/ppermute | solution.py:36
  28.2 27.2 %collective-permute-start.2 = (bf16[256,512]{1,0:T(8,128)(2,1)S(1)}, bf16[256,512]{1,0:T(8,128)(2,1)S(1)}, u32[]{:S(2)}, u32[]{:S(2)}) collective-permute-start(bf16[256,512]{1,0:T(8,128)(2,1)S(1)} %collective-permute-done.1.near_ref), channel_id=1, source_target_pairs={{0,2},{1,3},{2,4},{3,5},{4,6},{5,7},{6,8},{7,9},{8,10},{9,11},{10,... | collective-permute-start | bytes 786440 | tf_op jit(solution)/shard_map/ppermute | solution.py:36
  53.5 23.8 %collective-permute-start.6 = (bf16[256,512]{1,0:T(8,128)(2,1)S(1)}, bf16[256,512]{1,0:T(8,128)(2,1)S(1)}, u32[]{:S(2)}, u32[]{:S(2)}) collective-permute-start(bf16[256,512]{1,0:T(8,128)(2,1)S(1)} %get-tuple-element.22), channel_id=1, source_target_pairs={{2,0},{3,1},{4,2},{5,3},{6,4},{7,5},{8,6},{9,7},{10,8},{11,9},{12,... | collective-permute-start | bytes 786440 | tf_op jit(solution)/shard_map/ppermute | solution.py:36
  75.3 11.1 %collective-permute-start.9 = (bf16[256,512]{1,0:T(8,128)(2,1)S(1)}, bf16[256,512]{1,0:T(8,128)(2,1)S(1)}, u32[]{:S(2)}, u32[]{:S(2)}) collective-permute-start(bf16[256,512]{1,0:T(8,128)(2,1)S(1)} %get-tuple-element.26), channel_id=1, source_target_pairs={{2,0},{3,1},{4,2},{5,3},{6,4},{7,5},{8,6},{9,7},{10,8},{11,9},{12,... | collective-permute-start | bytes 786440 | tf_op jit(solution)/shard_map/ppermute | solution.py:36
  77.3 9.5 %collective-permute-start.7 = (bf16[256,512]{1,0:T(8,128)(2,1)S(1)}, bf16[256,512]{1,0:T(8,128)(2,1)S(1)}, u32[]{:S(2)}, u32[]{:S(2)}) collective-permute-start(bf16[256,512]{1,0:T(8,128)(2,1)S(1)} %add_convert_fusion.1), channel_id=1, source_target_pairs={{0,1},{1,0},{2,3},{3,2},{4,5},{5,4},{6,7},{7,6},{8,9},{9,8},{10,11... | collective-permute-start | bytes 786440 | tf_op jit(solution)/shard_map/ppermute | solution.py:40
  86.5 6.1 %collective-permute-start.10 = (bf16[256,512]{1,0:T(8,128)(2,1)S(1)}, bf16[256,512]{1,0:T(8,128)(2,1)S(1)}, u32[]{:S(2)}, u32[]{:S(2)}) collective-permute-start(bf16[256,512]{1,0:T(8,128)(2,1)S(1)} %add_convert_fusion), channel_id=1, source_target_pairs={{0,1},{1,0},{2,3},{3,2},{4,5},{5,4},{6,7},{7,6},{8,9},{9,8},{10,11... | collective-permute-start | bytes 786440 | tf_op jit(solution)/shard_map/ppermute | solution.py:40
  86.9 12.7 %collective-permute-start.8 = (bf16[256,512]{1,0:T(8,128)(2,1)S(1)}, bf16[256,512]{1,0:T(8,128)(2,1)S(1)}, u32[]{:S(2)}, u32[]{:S(2)}) collective-permute-start(bf16[256,512]{1,0:T(8,128)(2,1)S(1)} %fusion.4), channel_id=1, source_target_pairs={{2,0},{3,1},{4,2},{5,3},{6,4},{7,5},{8,6},{9,7},{10,8},{11,9},{12,... | collective-permute-start | bytes 786440 | tf_op jit(solution)/shard_map/ppermute | solution.py:36
  92.8 12.0 %collective-permute-start.11 = (bf16[256,512]{1,0:T(8,128)(2,1)S(1)}, bf16[256,512]{1,0:T(8,128)(2,1)S(1)}, u32[]{:S(2)}, u32[]{:S(2)}) collective-permute-start(bf16[256,512]{1,0:T(8,128)(2,1)S(1)} %fusion.9), channel_id=1, source_target_pairs={{2,0},{3,1},{4,2},{5,3},{6,4},{7,5},{8,6},{9,7},{10,8},{11,9},{12,... | collective-permute-start | bytes 786440 | tf_op jit(solution)/shard_map/ppermute | solution.py:36

commit v4 on v3

--- a/solution.py
+++ b/solution.py
@@ -1,3 +1,4 @@
+import functools
 import math
 
 import jax
@@ -40,6 +41,15 @@
     return lax.ppermute(value, AXES, [(source, source ^ 1) for source in range(device_count())])
 
 
+def run(first, second):
+    order = sorted(
+        [((i + 0.5) / len(part), k, piece) for k, part in enumerate((second, first)) for i, piece in enumerate(part)],
+        key=lambda entry: entry[:2],
+    )
+    for entry in order:
+        entry[2]()
+
+
 def write_bias(bias_ref, lengths_ref, first_ref, rows):
     docs = lengths_ref.shape[0]
     first = first_ref[0]
@@ -70,7 +80,7 @@
     @pl.when(pl.program_id(0) == 0)
     def _():
         write_bias(bias_ref, lengths_ref, first_ref, rows)
-        for ref in (*p_refs, *d_refs):
+        for ref in p_refs:
             ref[...] = jnp.zeros_like(ref)
 
     for j, block in enumerate((far_ref, mid_ref, near_ref, own_ref)):
@@ -82,6 +92,8 @@
     dk_ref[...] = jnp.zeros_like(dk_ref)
     dv_ref[...] = jnp.zeros_like(dv_ref)
     p_refs[1][...] = jnp.zeros_like(p_refs[1])
+    for ref in d_refs:
+        ref[...] = jnp.zeros_like(ref)
     dp_refs[1][...] = jnp.zeros_like(dp_refs[1])
     g_refs[1][...] = jnp.zeros_like(g_refs[1])
     delta_refs[1][...] = jnp.zeros_like(delta_refs[1])
@@ -94,16 +106,23 @@
     def columns(head):
         return pl.ds(pl.multiple_of(head * HEAD_SIZE, HEAD_SIZE), HEAD_SIZE)
 
+    tiles = [slice(j * rows, (j + 1) * rows) for j in range(SPAN)]
+
     def scores(head, slot):
-        s_refs[slot][...] = dot(q_ref[:, columns(head)], key_t_ref[...])
+        def piece(tile):
+            s_refs[slot][:, tile] = dot(q_ref[:, columns(head)], key_t_ref[:, tile])
+
+        return [functools.partial(piece, tile) for tile in tiles]
 
     def softmax(slot):
-        for here, keys in chunks:
+        def piece(here, keys):
             s = s_refs[slot][here, keys] * EXP2_SCALE + bias_ref[here, keys]
             e = jnp.exp2(s - jnp.max(s, axis=1, keepdims=True))
             inv = 1.0 / jnp.sum(e, axis=1, keepdims=True)
             inv_ref[here] = jnp.broadcast_to(inv, (ROWS, HEAD_SIZE))
             p_refs[slot][here, keys] = e.astype(jnp.bfloat16)
+
+        return [functools.partial(piece, *chunk) for chunk in chunks]
 
     def mix(head, slot):
         cols = columns(head)
@@ -115,37 +134,64 @@
         delta = jnp.sum(g * out.astype(jnp.float32), axis=1, keepdims=True)
         delta_refs[slot][...] = jnp.broadcast_to(delta, (rows, HEAD_SIZE))
         g_refs[slot][...] = g.astype(jnp.bfloat16)
-        dp_refs[slot][...] = dot(g_refs[slot][...], value_t_ref[...])
+
+    def prob_grad(slot):
+        def piece(tile):
+            dp_refs[slot][:, tile] = dot(g_refs[slot][...], value_t_ref[:, tile])
+
+        return [functools.partial(piece, tile) for tile in tiles]
 
     def score_grad(slot):
-        for here, keys in chunks:
+        def piece(here, keys):
             repeat = (keys.stop - keys.start) // HEAD_SIZE
             delta = jnp.concatenate([delta_refs[slot][here]] * repeat, axis=1)
             p = p_refs[slot][here, keys].astype(jnp.float32)
             d_refs[slot][here, keys] = (p * (dp_refs[slot][here, keys] - delta)).astype(jnp.bfloat16)
 
-    def spread(head, slot):
-        cols = columns(head)
-        dq_ref[:, cols] = (dot(d_refs[slot][...], key_ref[...]) * SCALE).astype(jnp.bfloat16)
-        dk_ref[...] += dot(q_ref[:, cols].T, d_refs[slot][...])
-        dv_ref[...] += dot(g_refs[slot][...].T, p_refs[slot][...])
-
-    scores(0, 0)
+        return [functools.partial(piece, *chunk) for chunk in chunks]
+
+    def query_grad(head, slot):
+        dq = dot(d_refs[slot][...], key_ref[...]) * SCALE
+        dq_ref[:, columns(head)] = dq.astype(jnp.bfloat16)
+
+    def key_grad(head, slot):
+        def piece(tile):
+            dk_ref[:, tile] += dot(q_ref[:, columns(head)].T, d_refs[slot][:, tile])
+
+        return [functools.partial(piece, tile) for tile in tiles]
+
+    def value_grad(slot):
+        def piece(tile):
+            dv_ref[:, tile] += dot(g_refs[slot][...].T, p_refs[slot][:, tile])
+
+        return [functools.partial(piece, tile) for tile in tiles]
+
+    run([], scores(0, 0))
 
     def step(index, carry):
         for slot in range(2):
             head = 2 * index + slot
-            before = jnp.maximum(head - 1, 0)
-            scores(jnp.minimum(head + 1, GROUP - 1), 1 - slot)
-            score_grad(1 - slot)
-            softmax(slot)
-            spread(before, 1 - slot)
-            mix(head, slot)
+            older = jnp.maximum(head - 2, 0)
+            run(
+                softmax(slot),
+                scores(jnp.minimum(head + 1, GROUP - 1), 1 - slot) + value_grad(1 - slot),
+            )
+            run(
+                score_grad(1 - slot),
+                [functools.partial(mix, head, slot)]
+                + [functools.partial(query_grad, older, slot)]
+                + key_grad(older, slot)
+                + prob_grad(slot),
+            )
         return carry
 
     lax.fori_loop(0, GROUP // 2, step, 0)
-    score_grad(1)
-    spread(GROUP - 1, 1)
+    run(
+        score_grad(1),
+        value_grad(1) + [functools.partial(query_grad, GROUP - 2, 0)] + key_grad(GROUP - 2, 0),
+    )
+    query_grad(GROUP - 1, 1)
+    run([], key_grad(GROUP - 1, 1))
     for j, target in enumerate((dfar_ref, dmid_ref, dnear_ref, down_ref)):
         span = slice(j * rows, (j + 1) * rows)
         target[:, :HEAD_SIZE] = (dk_ref[:, span].T * SCALE).astype(target.dtype)

time: 107 us -> 111 us (1.037)
  Pallas kernels: 39.9 us -> 43.7 us
    pallas_call x2, Pallas kernels: 39.9 us -> 43.7 us  [attention(): pl.pallas_call(attention_kernel, out_shape=[jax.ShapeDtypeStruct(queries....]
  transfers between devices with their start and end apart: 12 -> 12, of which waited for: 8 -> 8; matrix products, arithmetic and copies ran while one was open for 2% -> 2% of each run, Pallas kernels for 37% -> 40%
where the time goes in v4:
time: 111 us; the launch traced here: 110 us
  Pallas kernels  43.7 us (39%)
  waiting for transfers between devices  31.8 us (29%)
  starting transfers between devices  28.7 us (26%)
  other arithmetic  3.83 us (3%)
  local copies, waits for them, and re-layouts  1.38 us (1%)
    pallas_call x2, Pallas kernels, attention(): pl.pallas_call(attention_kernel, out_shape=[jax.ShapeDtypeStruct(queries....  43.7 us
    ppermute x8, waiting for transfers between devices, passed_along(): lax.ppermute(value, AXES, [(source, source + steps) for source in range(f...  27.8 us
    ppermute x8, starting transfers between devices, passed_along(): lax.ppermute(value, AXES, [(source, source + steps) for source in range(f...  27.6 us
    ppermute x4, waiting for transfers between devices, swapped(): lax.ppermute(value, AXES, [(source, source ^ 1) for source in range(devic...  3.99 us
  transfers between devices with their start and end apart: 12, of which 8 were waited for; matrix products, arithmetic and copies ran while one was open for 2% of the time, Pallas kernels for 40%

profile of v4, /device:TPU:29, one launch (start us, length us, event | category | flops | bytes accessed | tf_op | source)
XLA Modules:
  0.0 110.2 jit_solution(1784317008029794302)
XLA Ops:
  0.7 1.3 %fusion.12 = (bf16[256,128]{1,0:T(8,128)(2,1)S(1)}, bf16[256,128]{1,0:T(8,128)(2,1)S(1)}, bf16[256,128]{1,0:T(8,128)(2,1)S(1)}, bf16[256,128]{1,0:T(8,128)(2,1)S...) fusion(bf16[256,512]{1,0:T(8,128)(2,1)} %param.6, ...), kind=kLoop, calls=%fused_computation.24 | loop fusion | bytes 1048576 | tf_op jit(solution)/shard_map/slice | solution.py:273
  2.0 3.3 %collective-permute-start.3 = (bf16[256,512]{1,0:T(8,128)(2,1)S(1)}, bf16[256,512]{1,0:T(8,128)(2,1)S(1)}, u32[]{:S(2)}, u32[]{:S(2)}) collective-permute-start(bf16[256,512]{1,0:T(8,128)(2,1)S(1)} %pad_maximum_fusion.1.own_ref), channel_id=1, source_target_pairs={{0,2},{1,3},{2,4},{3,5},{4,6},{5,7},{6,8},{7,9},{8,10},{9,11},{10,... | collective-permute-start | bytes 786440 | tf_op jit(solution)/shard_map/ppermute | solution.py:37
  5.4 3.5 %collective-permute-start = (bf16[256,512]{1,0:T(8,128)(2,1)S(1)}, bf16[256,512]{1,0:T(8,128)(2,1)S(1)}, u32[]{:S(2)}, u32[]{:S(2)}) collective-permute-start(bf16[256,512]{1,0:T(8,128)(2,1)S(1)} %pad_maximum_fusion.own_ref), channel_id=1, source_target_pairs={{0,2},{1,3},{2,4},{3,5},{4,6},{5,7},{6,8},{7,9},{8,10},{9,11},{10,... | collective-permute-start | bytes 786440 | tf_op jit(solution)/shard_map/ppermute | solution.py:37
  8.9 2.5 %collective-permute-done.3.mid_ref = bf16[256,512]{1,0:T(8,128)(2,1)S(1)} collective-permute-done((bf16[256,512]{1,0:T(8,128)(2,1)S(1)}, bf16[256,512]{1,0:T(8,128)(2,1)S(1)}, u32[]{:S(2)}, u32[]{:S(2)}) %collective-permute-start.3) | collective-permute-done | bytes 262176 | tf_op jit(solution)/shard_map/ppermute | solution.py:37
  11.4 1.0 broadcast_select_fusion
  12.3 0.3 collective-permute-start.4
  12.6 4.1 %collective-permute-done.mid_ref = bf16[256,512]{1,0:T(8,128)(2,1)S(1)} collective-permute-done((bf16[256,512]{1,0:T(8,128)(2,1)S(1)}, bf16[256,512]{1,0:T(8,128)(2,1)S(1)}, u32[]{:S(2)}, u32[]{:S(2)}) %collective-permute-start) | collective-permute-done | bytes 262176 | tf_op jit(solution)/shard_map/ppermute | solution.py:37
  16.7 0.8 broadcast_select_fusion.1
  17.4 0.2 collective-permute-start.1
  17.7 0.2 collective-permute-done.4.near_ref
  17.8 10.4 %collective-permute-start.5 = (bf16[256,512]{1,0:T(8,128)(2,1)}, bf16[256,512]{1,0:T(8,128)(2,1)}, u32[]{:S(2)}, u32[]{:S(2)}) collective-permute-start(bf16[256,512]{1,0:T(8,128)(2,1)} %collective-permute-done.4.near_ref), channel_id=1, source_target_pairs={{0,2},{1,3},{2,4},{3,5},{4,6},{5,7},{6,8},{7,9},{8,10},{9,11},{10,... | collective-permute-start | bytes 786440 | tf_op jit(solution)/shard_map/ppermute | solution.py:37
  28.2 2.7 %collective-permute-start.2 = (bf16[256,512]{1,0:T(8,128)(2,1)S(1)}, bf16[256,512]{1,0:T(8,128)(2,1)S(1)}, u32[]{:S(2)}, u32[]{:S(2)}) collective-permute-start(bf16[256,512]{1,0:T(8,128)(2,1)S(1)} %collective-permute-done.1.near_ref), channel_id=1, source_target_pairs={{0,2},{1,3},{2,4},{3,5},{4,6},{5,7},{6,8},{7,9},{8,10},{9,11},{10,... | collective-permute-start | bytes 786440 | tf_op jit(solution)/shard_map/ppermute | solution.py:37
  30.9 2.6 %collective-permute-done.5.far_ref = bf16[256,512]{1,0:T(8,128)(2,1)} collective-permute-done((bf16[256,512]{1,0:T(8,128)(2,1)}, bf16[256,512]{1,0:T(8,128)(2,1)}, u32[]{:S(2)}, u32[]{:S(2)}) %collective-permute-start.5) | collective-permute-done | bytes 262176 | tf_op jit(solution)/shard_map/ppermute | solution.py:37
  33.5 21.9 %attention.2 = (bf16[256,4096]{1,0:T(8,128)(2,1)}, bf16[256,4096]{1,0:T(8,128)(2,1)}, bf16[256,512]{1,0:T(8,128)(2,1)S(1)}, f32[256,512]{1,0:T(8,128)S(1)}, f32[...) custom-call(s32[1]{0:T(128)} %bitcast.first_ref, s32[16]{0:T(128)S(1)} %copy-done.1, bf16[256,4096]{1,0:T(8,128)(2,1)S(1)} %copy-done, ...), custom_call_target="tpu_custom_call" | custom-call | flops 12884901888 | bytes 7077888 | tf_op jit(solution)/shard_map/attention/pallas_call | solution.py:217
  55.4 1.9 %collective-permute-start.6 = (bf16[256,512]{1,0:T(8,128)(2,1)S(1)}, bf16[256,512]{1,0:T(8,128)(2,1)S(1)}, u32[]{:S(2)}, u32[]{:S(2)}) collective-permute-start(bf16[256,512]{1,0:T(8,128)(2,1)S(1)} %get-tuple-element.22), channel_id=1, source_target_pairs={{2,0},{3,1},{4,2},{5,3},{6,4},{7,5},{8,6},{9,7},{10,8},{11,9},{12,... | collective-permute-start | bytes 786440 | tf_op jit(solution)/shard_map/ppermute | solution.py:37
  57.3 21.8 %attention.3 = (bf16[256,4096]{1,0:T(8,128)(2,1)}, bf16[256,4096]{1,0:T(8,128)(2,1)}, bf16[256,512]{1,0:T(8,128)(2,1)S(1)}, f32[256,512]{1,0:T(8,128)S(1)}, f32[...) custom-call(s32[1]{0:T(128)} %bitcast.first_ref, s32[16]{0:T(128)S(1)} %copy-done.1, ...), custom_call_target="tpu_custom_call", output_to_operand_aliasing={{0}: (8, {}), {1}: (9, {})} | custom-call | flops 12884901888 | bytes 7077888 | tf_op jit(solution)/shard_map/attention/pallas_call | solution.py:217
  79.2 1.9 %collective-permute-start.9 = (bf16[256,512]{1,0:T(8,128)(2,1)S(1)}, bf16[256,512]{1,0:T(8,128)(2,1)S(1)}, u32[]{:S(2)}, u32[]{:S(2)}) collective-permute-start(bf16[256,512]{1,0:T(8,128)(2,1)S(1)} %get-tuple-element.26), channel_id=1, source_target_pairs={{2,0},{3,1},{4,2},{5,3},{6,4},{7,5},{8,6},{9,7},{10,8},{11,9},{12,... | collective-permute-start | bytes 786440 | tf_op jit(solution)/shard_map/ppermute | solution.py:37
  81.2 0.3 collective-permute-start.7
  81.5 8.8 %collective-permute-done.9 = bf16[256,512]{1,0:T(8,128)(2,1)S(1)} collective-permute-done((bf16[256,512]{1,0:T(8,128)(2,1)S(1)}, bf16[256,512]{1,0:T(8,128)(2,1)S(1)}, u32[]{:S(2)}, u32[]{:S(2)}) %collective-permute-start.9) | collective-permute-done | bytes 262176 | tf_op jit(solution)/shard_map/ppermute | solution.py:37
  90.3 0.1 add_convert_fusion
  90.4 0.3 collective-permute-start.10
  90.7 0.1 fusion.4
  90.7 1.9 %collective-permute-start.8 = (bf16[256,512]{1,0:T(8,128)(2,1)S(1)}, bf16[256,512]{1,0:T(8,128)(2,1)S(1)}, u32[]{:S(2)}, u32[]{:S(2)}) collective-permute-start(bf16[256,512]{1,0:T(8,128)(2,1)S(1)} %fusion.4), channel_id=1, source_target_pairs={{2,0},{3,1},{4,2},{5,3},{6,4},{7,5},{8,6},{9,7},{10,8},{11,9},{12,... | collective-permute-start | bytes 786440 | tf_op jit(solution)/shard_map/ppermute | solution.py:37
  92.7 3.8 %collective-permute-done.10 = bf16[256,512]{1,0:T(8,128)(2,1)S(1)} collective-permute-done((bf16[256,512]{1,0:T(8,128)(2,1)S(1)}, bf16[256,512]{1,0:T(8,128)(2,1)S(1)}, u32[]{:S(2)}, u32[]{:S(2)}) %collective-permute-start.10) | collective-permute-done | bytes 262176 | tf_op jit(solution)/shard_map/ppermute | solution.py:41
  96.5 0.1 fusion.9
  96.6 1.9 %collective-permute-start.11 = (bf16[256,512]{1,0:T(8,128)(2,1)S(1)}, bf16[256,512]{1,0:T(8,128)(2,1)S(1)}, u32[]{:S(2)}, u32[]{:S(2)}) collective-permute-start(bf16[256,512]{1,0:T(8,128)(2,1)S(1)} %fusion.9), channel_id=1, source_target_pairs={{2,0},{3,1},{4,2},{5,3},{6,4},{7,5},{8,6},{9,7},{10,8},{11,9},{12,... | collective-permute-start | bytes 786440 | tf_op jit(solution)/shard_map/ppermute | solution.py:37
  98.5 4.9 %collective-permute-done.8 = bf16[256,512]{1,0:T(8,128)(2,1)S(1)} collective-permute-done((bf16[256,512]{1,0:T(8,128)(2,1)S(1)}, bf16[256,512]{1,0:T(8,128)(2,1)S(1)}, u32[]{:S(2)}, u32[]{:S(2)}) %collective-permute-start.8) | collective-permute-done | bytes 262176 | tf_op jit(solution)/shard_map/ppermute | solution.py:37
  103.5 0.1 fusion.2
  103.6 4.9 %collective-permute-done.11 = bf16[256,512]{1,0:T(8,128)(2,1)S(1)} collective-permute-done((bf16[256,512]{1,0:T(8,128)(2,1)S(1)}, bf16[256,512]{1,0:T(8,128)(2,1)S(1)}, u32[]{:S(2)}, u32[]{:S(2)}) %collective-permute-start.11) | collective-permute-done | bytes 262176 | tf_op jit(solution)/shard_map/ppermute | solution.py:37
  108.6 0.1 fusion.7
  108.8 0.7 pad_maximum_fusion.3
  109.5 0.7 pad_maximum_fusion.2
  (17 shorter events, 0.3 us)
Async XLA Ops:
  0.6 32.9 %copy-start.1 = (s32[16]{0:T(128)S(1)}, s32[16]{0:T(128)}, u32[]{:S(2)}) copy-start(s32[16]{0:T(128)} %lengths_ref.3) | copy-start | bytes 196
  0.6 32.9 %copy-start = (bf16[256,4096]{1,0:T(8,128)(2,1)S(1)}, bf16[256,4096]{1,0:T(8,128)(2,1)}, u32[]{:S(2)}) copy-start(bf16[256,4096]{1,0:T(8,128)(2,1)} %q_ref.3) | copy-start | bytes 6291460
  1.9 3.4 %copy-start.2 = (bf16[256,128]{1,0:T(8,128)(2,1)}, bf16[256,128]{1,0:T(8,128)(2,1)S(1)}, u32[]{:S(2)}) copy-start(bf16[256,128]{1,0:T(8,128)(2,1)S(1)} %get-tuple-element.44) | copy-start | bytes 196612
  1.9 3.4 %copy-start.3 = (bf16[256,128]{1,0:T(8,128)(2,1)}, bf16[256,128]{1,0:T(8,128)(2,1)S(1)}, u32[]{:S(2)}) copy-start(bf16[256,128]{1,0:T(8,128)(2,1)S(1)} %get-tuple-element.47) | copy-start | bytes 196612
  2.0 9.4 %collective-permute-start.3 = (bf16[256,512]{1,0:T(8,128)(2,1)S(1)}, bf16[256,512]{1,0:T(8,128)(2,1)S(1)}, u32[]{:S(2)}, u32[]{:S(2)}) collective-permute-start(bf16[256,512]{1,0:T(8,128)(2,1)S(1)} %pad_maximum_fusion.1.own_ref), channel_id=1, source_target_pairs={{0,2},{1,3},{2,4},{3,5},{4,6},{5,7},{6,8},{7,9},{8,10},{9,11},{10,... | collective-permute-start | bytes 786440 | tf_op jit(solution)/shard_map/ppermute | solution.py:37
  5.4 11.3 %collective-permute-start = (bf16[256,512]{1,0:T(8,128)(2,1)S(1)}, bf16[256,512]{1,0:T(8,128)(2,1)S(1)}, u32[]{:S(2)}, u32[]{:S(2)}) collective-permute-start(bf16[256,512]{1,0:T(8,128)(2,1)S(1)} %pad_maximum_fusion.own_ref), channel_id=1, source_target_pairs={{0,2},{1,3},{2,4},{3,5},{4,6},{5,7},{6,8},{7,9},{8,10},{9,11},{10,... | collective-permute-start | bytes 786440 | tf_op jit(solution)/shard_map/ppermute | solution.py:37
  12.3 5.5 %collective-permute-start.4 = (bf16[256,512]{1,0:T(8,128)(2,1)S(1)}, bf16[256,512]{1,0:T(8,128)(2,1)}, u32[]{:S(2)}, u32[]{:S(2)}) collective-permute-start(bf16[256,512]{1,0:T(8,128)(2,1)S(1)} %broadcast_select_fusion), channel_id=1, source_target_pairs={{0,1},{1,0},{2,3},{3,2},{4,5},{5,4},{6,7},{7,6},{8,9},{9,8},{10,11... | collective-permute-start | bytes 786440 | tf_op jit(solution)/shard_map/ppermute | solution.py:41
  17.4 10.8 %collective-permute-start.1 = (bf16[256,512]{1,0:T(8,128)(2,1)}, bf16[256,512]{1,0:T(8,128)(2,1)S(1)}, u32[]{:S(2)}, u32[]{:S(2)}) collective-permute-start(bf16[256,512]{1,0:T(8,128)(2,1)} %broadcast_select_fusion.1), channel_id=1, source_target_pairs={{0,1},{1,0},{2,3},{3,2},{4,5},{5,4},{6,7},{7,6},{8,9},{9,8},{10,11... | collective-permute-start | bytes 786440 | tf_op jit(solution)/shard_map/ppermute | solution.py:41
  17.8 15.7 %collective-permute-start.5 = (bf16[256,512]{1,0:T(8,128)(2,1)}, bf16[256,512]{1,0:T(8,128)(2,1)}, u32[]{:S(2)}, u32[]{:S(2)}) collective-permute-start(bf16[256,512]{1,0:T(8,128)(2,1)} %collective-permute-done.4.near_ref), channel_id=1, source_target_pairs={{0,2},{1,3},{2,4},{3,5},{4,6},{5,7},{6,8},{7,9},{8,10},{9,11},{10,... | collective-permute-start | bytes 786440 | tf_op jit(solution)/shard_map/ppermute | solution.py:37
  28.2 29.1 %collective-permute-start.2 = (bf16[256,512]{1,0:T(8,128)(2,1)S(1)}, bf16[256,512]{1,0:T(8,128)(2,1)S(1)}, u32[]{:S(2)}, u32[]{:S(2)}) collective-permute-start(bf16[256,512]{1,0:T(8,128)(2,1)S(1)} %collective-permute-done.1.near_ref), channel_id=1, source_target_pairs={{0,2},{1,3},{2,4},{3,5},{4,6},{5,7},{6,8},{7,9},{8,10},{9,11},{10,... | collective-permute-start | bytes 786440 | tf_op jit(solution)/shard_map/ppermute | solution.py:37
  55.4 25.7 %collective-permute-start.6 = (bf16[256,512]{1,0:T(8,128)(2,1)S(1)}, bf16[256,512]{1,0:T(8,128)(2,1)S(1)}, u32[]{:S(2)}, u32[]{:S(2)}) collective-permute-start(bf16[256,512]{1,0:T(8,128)(2,1)S(1)} %get-tuple-element.22), channel_id=1, source_target_pairs={{2,0},{3,1},{4,2},{5,3},{6,4},{7,5},{8,6},{9,7},{10,8},{11,9},{12,... | collective-permute-start | bytes 786440 | tf_op jit(solution)/shard_map/ppermute | solution.py:37
  79.2 11.1 %collective-permute-start.9 = (bf16[256,512]{1,0:T(8,128)(2,1)S(1)}, bf16[256,512]{1,0:T(8,128)(2,1)S(1)}, u32[]{:S(2)}, u32[]{:S(2)}) collective-permute-start(bf16[256,512]{1,0:T(8,128)(2,1)S(1)} %get-tuple-element.26), channel_id=1, source_target_pairs={{2,0},{3,1},{4,2},{5,3},{6,4},{7,5},{8,6},{9,7},{10,8},{11,9},{12,... | collective-permute-start | bytes 786440 | tf_op jit(solution)/shard_map/ppermute | solution.py:37
  81.2 9.5 %collective-permute-start.7 = (bf16[256,512]{1,0:T(8,128)(2,1)S(1)}, bf16[256,512]{1,0:T(8,128)(2,1)S(1)}, u32[]{:S(2)}, u32[]{:S(2)}) collective-permute-start(bf16[256,512]{1,0:T(8,128)(2,1)S(1)} %add_convert_fusion.1), channel_id=1, source_target_pairs={{0,1},{1,0},{2,3},{3,2},{4,5},{5,4},{6,7},{7,6},{8,9},{9,8},{10,11... | collective-permute-start | bytes 786440 | tf_op jit(solution)/shard_map/ppermute | solution.py:41
  90.4 6.1 %collective-permute-start.10 = (bf16[256,512]{1,0:T(8,128)(2,1)S(1)}, bf16[256,512]{1,0:T(8,128)(2,1)S(1)}, u32[]{:S(2)}, u32[]{:S(2)}) collective-permute-start(bf16[256,512]{1,0:T(8,128)(2,1)S(1)} %add_convert_fusion), channel_id=1, source_target_pairs={{0,1},{1,0},{2,3},{3,2},{4,5},{5,4},{6,7},{7,6},{8,9},{9,8},{10,11... | collective-permute-start | bytes 786440 | tf_op jit(solution)/shard_map/ppermute | solution.py:41
  90.7 12.7 %collective-permute-start.8 = (bf16[256,512]{1,0:T(8,128)(2,1)S(1)}, bf16[256,512]{1,0:T(8,128)(2,1)S(1)}, u32[]{:S(2)}, u32[]{:S(2)}) collective-permute-start(bf16[256,512]{1,0:T(8,128)(2,1)S(1)} %fusion.4), channel_id=1, source_target_pairs={{2,0},{3,1},{4,2},{5,3},{6,4},{7,5},{8,6},{9,7},{10,8},{11,9},{12,... | collective-permute-start | bytes 786440 | tf_op jit(solution)/shard_map/ppermute | solution.py:37
  96.6 12.0 %collective-permute-start.11 = (bf16[256,512]{1,0:T(8,128)(2,1)S(1)}, bf16[256,512]{1,0:T(8,128)(2,1)S(1)}, u32[]{:S(2)}, u32[]{:S(2)}) collective-permute-start(bf16[256,512]{1,0:T(8,128)(2,1)S(1)} %fusion.9), channel_id=1, source_target_pairs={{2,0},{3,1},{4,2},{5,3},{6,4},{7,5},{8,6},{9,7},{10,8},{11,9},{12,... | collective-permute-start | bytes 786440 | tf_op jit(solution)/shard_map/ppermute | solution.py:37

commit v5 on v3

--- a/solution.py
+++ b/solution.py
@@ -15,11 +15,13 @@
 AXES = ("blk", "inner")
 CHUNK = 2
 ROWS = 32
+UNIT = 2
 MASKED = -1e30
 SCALE = 1.0 / math.sqrt(HEAD_SIZE)
 EXP2_SCALE = SCALE * math.log2(math.e)
 
 NN = (((1,), (0,)), ((), ()))
+TN = (((0,), (0,)), ((), ()))
 
 
 def dot(a, b, dims=NN):
@@ -61,11 +63,12 @@
 def attention_kernel(first_ref, lengths_ref, q_ref, g_ref, far_ref, mid_ref, near_ref, own_ref, *refs):
     (
         out_ref, dq_ref, dfar_ref, dmid_ref, dnear_ref, down_ref,
-        bias_ref, key_ref, value_ref, key_t_ref, value_t_ref, dk_ref, dv_ref, inv_ref, *slots,
-    ) = refs[-26:]
+        bias_ref, key_ref, value_ref, key_t_ref, value_t_ref, dk_ref, dv_ref, inv_ref, q_all_ref, *slots,
+    ) = refs[-27:]
     s_refs, p_refs, dp_refs, d_refs, g_refs, delta_refs = (slots[i : i + 2] for i in range(0, 12, 2))
     rows = q_ref.shape[0]
     window = SPAN * rows
+    stack = UNIT * rows
 
     @pl.when(pl.program_id(0) == 0)
     def _():
@@ -79,6 +82,8 @@
         value_ref[span] = block[:, HEAD_SIZE:]
         key_t_ref[:, span] = block[:, :HEAD_SIZE].T
         value_t_ref[:, span] = block[:, HEAD_SIZE:].T
+    for head in range(GROUP):
+        q_all_ref[head * rows : (head + 1) * rows] = q_ref[:, head * HEAD_SIZE : (head + 1) * HEAD_SIZE]
     dk_ref[...] = jnp.zeros_like(dk_ref)
     dv_ref[...] = jnp.zeros_like(dv_ref)
     p_refs[1][...] = jnp.zeros_like(p_refs[1])
@@ -87,69 +92,85 @@
     delta_refs[1][...] = jnp.zeros_like(delta_refs[1])
 
     chunks = [
-        (slice(r, r + ROWS), slice((r + 1) // 128 * 128, -(-(window - rows + r + ROWS) // 128) * 128))
+        (
+            slice(r, r + ROWS),
+            slice(h * rows + r, h * rows + r + ROWS),
+            slice((r + 1) // 128 * 128, -(-(window - rows + r + ROWS) // 128) * 128),
+        )
+        for h in range(UNIT)
         for r in range(0, rows, ROWS)
     ]
 
-    def columns(head):
-        return pl.ds(pl.multiple_of(head * HEAD_SIZE, HEAD_SIZE), HEAD_SIZE)
-
-    def scores(head, slot):
-        s_refs[slot][...] = dot(q_ref[:, columns(head)], key_t_ref[...])
+    def queries(unit):
+        return q_all_ref[pl.ds(pl.multiple_of(unit * stack, stack), stack)]
+
+    def heads(unit):
+        return [
+            (
+                slice(i * rows, (i + 1) * rows),
+                pl.ds(pl.multiple_of((unit * UNIT + i) * HEAD_SIZE, HEAD_SIZE), HEAD_SIZE),
+            )
+            for i in range(UNIT)
+        ]
+
+    def scores(unit, slot):
+        s_refs[slot][...] = dot(queries(unit), key_t_ref[...])
 
     def softmax(slot):
-        for here, keys in chunks:
-            s = s_refs[slot][here, keys] * EXP2_SCALE + bias_ref[here, keys]
+        for row, here, keys in chunks:
+            s = s_refs[slot][here, keys] * EXP2_SCALE + bias_ref[row, keys]
             e = jnp.exp2(s - jnp.max(s, axis=1, keepdims=True))
             inv = 1.0 / jnp.sum(e, axis=1, keepdims=True)
             inv_ref[here] = jnp.broadcast_to(inv, (ROWS, HEAD_SIZE))
             p_refs[slot][here, keys] = e.astype(jnp.bfloat16)
 
-    def mix(head, slot):
-        cols = columns(head)
+    def mix(unit, slot):
         mixed = dot(p_refs[slot][...], value_ref[...])
-        inv = inv_ref[...]
-        out = (mixed * inv).astype(jnp.bfloat16)
-        out_ref[:, cols] = out
-        g = g_ref[:, cols].astype(jnp.float32) * inv
-        delta = jnp.sum(g * out.astype(jnp.float32), axis=1, keepdims=True)
-        delta_refs[slot][...] = jnp.broadcast_to(delta, (rows, HEAD_SIZE))
-        g_refs[slot][...] = g.astype(jnp.bfloat16)
+        for here, cols in heads(unit):
+            inv = inv_ref[here]
+            out = (mixed[here] * inv).astype(jnp.bfloat16)
+            out_ref[:, cols] = out
+            g = g_ref[:, cols].astype(jnp.float32) * inv
+            delta = jnp.sum(g * out.astype(jnp.float32), axis=1, keepdims=True)
+            delta_refs[slot][here] = jnp.broadcast_to(delta, (rows, HEAD_SIZE))
+            g_refs[slot][here] = g.astype(jnp.bfloat16)
         dp_refs[slot][...] = dot(g_refs[slot][...], value_t_ref[...])
 
     def score_grad(slot):
-        for here, keys in chunks:
+        for row, here, keys in chunks:
             repeat = (keys.stop - keys.start) // HEAD_SIZE
             delta = jnp.concatenate([delta_refs[slot][here]] * repeat, axis=1)
             p = p_refs[slot][here, keys].astype(jnp.float32)
             d_refs[slot][here, keys] = (p * (dp_refs[slot][here, keys] - delta)).astype(jnp.bfloat16)
 
-    def spread(head, slot):
-        cols = columns(head)
-        dq_ref[:, cols] = (dot(d_refs[slot][...], key_ref[...]) * SCALE).astype(jnp.bfloat16)
-        dk_ref[...] += dot(q_ref[:, cols].T, d_refs[slot][...])
-        dv_ref[...] += dot(g_refs[slot][...].T, p_refs[slot][...])
+    def spread(unit, slot):
+        dq = (dot(d_refs[slot][...], key_ref[...]) * SCALE).astype(jnp.bfloat16)
+        for here, cols in heads(unit):
+            dq_ref[:, cols] = dq[here]
+        dk_ref[...] += dot(d_refs[slot][...], queries(unit), TN)
+        dv_ref[...] += dot(p_refs[slot][...], g_refs[slot][...], TN)
 
     scores(0, 0)
+    units = GROUP // UNIT
 
     def step(index, carry):
         for slot in range(2):
-            head = 2 * index + slot
-            before = jnp.maximum(head - 1, 0)
-            scores(jnp.minimum(head + 1, GROUP - 1), 1 - slot)
+            unit = 2 * index + slot
+            before = jnp.maximum(unit - 1, 0)
+            scores(jnp.minimum(unit + 1, units - 1), 1 - slot)
             score_grad(1 - slot)
             softmax(slot)
             spread(before, 1 - slot)
-            mix(head, slot)
+            mix(unit, slot)
         return carry
 
-    lax.fori_loop(0, GROUP // 2, step, 0)
+    lax.fori_loop(0, units // 2, step, 0)
     score_grad(1)
-    spread(GROUP - 1, 1)
+    spread(units - 1, 1)
     for j, target in enumerate((dfar_ref, dmid_ref, dnear_ref, down_ref)):
         span = slice(j * rows, (j + 1) * rows)
-        target[:, :HEAD_SIZE] = (dk_ref[:, span].T * SCALE).astype(target.dtype)
-        target[:, HEAD_SIZE:] = dv_ref[:, span].T.astype(target.dtype)
+        target[:, :HEAD_SIZE] = (dk_ref[span] * SCALE).astype(target.dtype)
+        target[:, HEAD_SIZE:] = dv_ref[span].astype(target.dtype)
 
 
 def attention(chunk, first, lengths, queries, out_grad, blocks, grads):
@@ -183,12 +204,13 @@
                 pltpu.VMEM((window, HEAD_SIZE), bf16),
                 pltpu.VMEM((HEAD_SIZE, window), bf16),
                 pltpu.VMEM((HEAD_SIZE, window), bf16),
-                pltpu.VMEM((HEAD_SIZE, window), f32),
-                pltpu.VMEM((HEAD_SIZE, window), f32),
-                pltpu.VMEM((rows, HEAD_SIZE), f32),
+                pltpu.VMEM((window, HEAD_SIZE), f32),
+                pltpu.VMEM((window, HEAD_SIZE), f32),
+                pltpu.VMEM((UNIT * rows, HEAD_SIZE), f32),
+                pltpu.VMEM((GROUP * rows, HEAD_SIZE), bf16),
             ]
             + [
-                pltpu.VMEM((rows, columns), kind)
+                pltpu.VMEM((UNIT * rows, columns), kind)
                 for columns, kind in (
                     (window, f32),
                     (window, bf16),

time: 107 us -> 113 us (1.056)
  Pallas kernels: 39.9 us -> 45.8 us
    pallas_call x2, Pallas kernels: 39.9 us -> 45.8 us  [attention(): pl.pallas_call(attention_kernel, out_shape=[jax.ShapeDtypeStruct(queries....]
  transfers between devices with their start and end apart: 12 -> 12, of which waited for: 8 -> 8; matrix products, arithmetic and copies ran while one was open for 2% -> 2% of each run, Pallas kernels for 37% -> 41%
where the time goes in v5:
time: 113 us
  Pallas kernels  45.8 us (41%)
  waiting for transfers between devices  31.8 us (28%)
  starting transfers between devices  28.8 us (25%)
  other arithmetic  3.83 us (3%)
  local copies, waits for them, and re-layouts  1.38 us (1%)
    pallas_call x2, Pallas kernels, attention(): pl.pallas_call(attention_kernel, out_shape=[jax.ShapeDtypeStruct(queries....  45.8 us
    ppermute x8, waiting for transfers between devices, passed_along(): lax.ppermute(value, AXES, [(source, source + steps) for source in range(f...  27.8 us
    ppermute x8, starting transfers between devices, passed_along(): lax.ppermute(value, AXES, [(source, source + steps) for source in range(f...  27.8 us
    ppermute x4, waiting for transfers between devices, swapped(): lax.ppermute(value, AXES, [(source, source ^ 1) for source in range(devic...  4 us
  transfers between devices with their start and end apart: 12, of which 8 were waited for; matrix products, arithmetic and copies ran while one was open for 2% of the time, Pallas kernels for 41%

profile of v5, /device:TPU:29, one launch (start us, length us, event | category | flops | bytes accessed | tf_op | source)
XLA Modules:
  0.0 112.5 jit_solution(5392333500610345532)
XLA Ops:
  0.7 1.3 %fusion.12 = (bf16[256,128]{1,0:T(8,128)(2,1)S(1)}, bf16[256,128]{1,0:T(8,128)(2,1)S(1)}, bf16[256,128]{1,0:T(8,128)(2,1)S(1)}, bf16[256,128]{1,0:T(8,128)(2,1)S...) fusion(bf16[256,512]{1,0:T(8,128)(2,1)} %param.6, ...), kind=kLoop, calls=%fused_computation.24 | loop fusion | bytes 1048576 | tf_op jit(solution)/shard_map/slice | solution.py:249
  2.0 3.3 %collective-permute-start.3 = (bf16[256,512]{1,0:T(8,128)(2,1)S(1)}, bf16[256,512]{1,0:T(8,128)(2,1)S(1)}, u32[]{:S(2)}, u32[]{:S(2)}) collective-permute-start(bf16[256,512]{1,0:T(8,128)(2,1)S(1)} %pad_maximum_fusion.1.own_ref), channel_id=1, source_target_pairs={{0,2},{1,3},{2,4},{3,5},{4,6},{5,7},{6,8},{7,9},{8,10},{9,11},{10,... | collective-permute-start | bytes 786440 | tf_op jit(solution)/shard_map/ppermute | solution.py:38
  5.4 3.5 %collective-permute-start = (bf16[256,512]{1,0:T(8,128)(2,1)S(1)}, bf16[256,512]{1,0:T(8,128)(2,1)S(1)}, u32[]{:S(2)}, u32[]{:S(2)}) collective-permute-start(bf16[256,512]{1,0:T(8,128)(2,1)S(1)} %pad_maximum_fusion.own_ref), channel_id=1, source_target_pairs={{0,2},{1,3},{2,4},{3,5},{4,6},{5,7},{6,8},{7,9},{8,10},{9,11},{10,... | collective-permute-start | bytes 786440 | tf_op jit(solution)/shard_map/ppermute | solution.py:38
  8.9 2.5 %collective-permute-done.3.mid_ref = bf16[256,512]{1,0:T(8,128)(2,1)S(1)} collective-permute-done((bf16[256,512]{1,0:T(8,128)(2,1)S(1)}, bf16[256,512]{1,0:T(8,128)(2,1)S(1)}, u32[]{:S(2)}, u32[]{:S(2)}) %collective-permute-start.3) | collective-permute-done | bytes 262176 | tf_op jit(solution)/shard_map/ppermute | solution.py:38
  11.4 1.0 broadcast_select_fusion
  12.3 0.3 collective-permute-start.4
  12.6 4.1 %collective-permute-done.mid_ref = bf16[256,512]{1,0:T(8,128)(2,1)S(1)} collective-permute-done((bf16[256,512]{1,0:T(8,128)(2,1)S(1)}, bf16[256,512]{1,0:T(8,128)(2,1)S(1)}, u32[]{:S(2)}, u32[]{:S(2)}) %collective-permute-start) | collective-permute-done | bytes 262176 | tf_op jit(solution)/shard_map/ppermute | solution.py:38
  16.7 0.8 broadcast_select_fusion.1
  17.4 0.2 collective-permute-start.1
  17.7 0.2 collective-permute-done.4.near_ref
  17.8 10.4 %collective-permute-start.5 = (bf16[256,512]{1,0:T(8,128)(2,1)}, bf16[256,512]{1,0:T(8,128)(2,1)}, u32[]{:S(2)}, u32[]{:S(2)}) collective-permute-start(bf16[256,512]{1,0:T(8,128)(2,1)} %collective-permute-done.4.near_ref), channel_id=1, source_target_pairs={{0,2},{1,3},{2,4},{3,5},{4,6},{5,7},{6,8},{7,9},{8,10},{9,11},{10,... | collective-permute-start | bytes 786440 | tf_op jit(solution)/shard_map/ppermute | solution.py:38
  28.2 2.7 %collective-permute-start.2 = (bf16[256,512]{1,0:T(8,128)(2,1)S(1)}, bf16[256,512]{1,0:T(8,128)(2,1)S(1)}, u32[]{:S(2)}, u32[]{:S(2)}) collective-permute-start(bf16[256,512]{1,0:T(8,128)(2,1)S(1)} %collective-permute-done.1.near_ref), channel_id=1, source_target_pairs={{0,2},{1,3},{2,4},{3,5},{4,6},{5,7},{6,8},{7,9},{8,10},{9,11},{10,... | collective-permute-start | bytes 786440 | tf_op jit(solution)/shard_map/ppermute | solution.py:38
  30.9 2.6 %collective-permute-done.5.far_ref = bf16[256,512]{1,0:T(8,128)(2,1)} collective-permute-done((bf16[256,512]{1,0:T(8,128)(2,1)}, bf16[256,512]{1,0:T(8,128)(2,1)}, u32[]{:S(2)}, u32[]{:S(2)}) %collective-permute-start.5) | collective-permute-done | bytes 262176 | tf_op jit(solution)/shard_map/ppermute | solution.py:38
  33.5 22.9 %attention.2 = (bf16[256,4096]{1,0:T(8,128)(2,1)}, bf16[256,4096]{1,0:T(8,128)(2,1)}, bf16[256,512]{1,0:T(8,128)(2,1)S(1)}, f32[256,512]{1,0:T(8,128)S(1)}, f32[...) custom-call(s32[1]{0:T(128)} %bitcast.first_ref, s32[16]{0:T(128)S(1)} %copy-done.1, bf16[256,4096]{1,0:T(8,128)(2,1)S(1)} %copy-done, ...), custom_call_target="tpu_custom_call" | custom-call | flops 12884901888 | bytes 7077888 | tf_op jit(solution)/shard_map/attention/pallas_call | solution.py:192
  56.5 2.1 %collective-permute-start.6 = (bf16[256,512]{1,0:T(8,128)(2,1)S(1)}, bf16[256,512]{1,0:T(8,128)(2,1)S(1)}, u32[]{:S(2)}, u32[]{:S(2)}) collective-permute-start(bf16[256,512]{1,0:T(8,128)(2,1)S(1)} %get-tuple-element.22), channel_id=1, source_target_pairs={{2,0},{3,1},{4,2},{5,3},{6,4},{7,5},{8,6},{9,7},{10,8},{11,9},{12,... | collective-permute-start | bytes 786440 | tf_op jit(solution)/shard_map/ppermute | solution.py:38
  58.6 22.9 %attention.3 = (bf16[256,4096]{1,0:T(8,128)(2,1)}, bf16[256,4096]{1,0:T(8,128)(2,1)}, bf16[256,512]{1,0:T(8,128)(2,1)S(1)}, f32[256,512]{1,0:T(8,128)S(1)}, f32[...) custom-call(s32[1]{0:T(128)} %bitcast.first_ref, s32[16]{0:T(128)S(1)} %copy-done.1, ...), custom_call_target="tpu_custom_call", output_to_operand_aliasing={{0}: (8, {}), {1}: (9, {})} | custom-call | flops 12884901888 | bytes 7077888 | tf_op jit(solution)/shard_map/attention/pallas_call | solution.py:192
  81.5 1.9 %collective-permute-start.9 = (bf16[256,512]{1,0:T(8,128)(2,1)S(1)}, bf16[256,512]{1,0:T(8,128)(2,1)S(1)}, u32[]{:S(2)}, u32[]{:S(2)}) collective-permute-start(bf16[256,512]{1,0:T(8,128)(2,1)S(1)} %get-tuple-element.26), channel_id=1, source_target_pairs={{2,0},{3,1},{4,2},{5,3},{6,4},{7,5},{8,6},{9,7},{10,8},{11,9},{12,... | collective-permute-start | bytes 786440 | tf_op jit(solution)/shard_map/ppermute | solution.py:38
  83.5 0.3 collective-permute-start.7
  83.8 8.8 %collective-permute-done.9 = bf16[256,512]{1,0:T(8,128)(2,1)S(1)} collective-permute-done((bf16[256,512]{1,0:T(8,128)(2,1)S(1)}, bf16[256,512]{1,0:T(8,128)(2,1)S(1)}, u32[]{:S(2)}, u32[]{:S(2)}) %collective-permute-start.9) | collective-permute-done | bytes 262176 | tf_op jit(solution)/shard_map/ppermute | solution.py:38
  92.6 0.1 add_convert_fusion
  92.7 0.3 collective-permute-start.10
  93.0 0.1 fusion.4
  93.0 1.9 %collective-permute-start.8 = (bf16[256,512]{1,0:T(8,128)(2,1)S(1)}, bf16[256,512]{1,0:T(8,128)(2,1)S(1)}, u32[]{:S(2)}, u32[]{:S(2)}) collective-permute-start(bf16[256,512]{1,0:T(8,128)(2,1)S(1)} %fusion.4), channel_id=1, source_target_pairs={{2,0},{3,1},{4,2},{5,3},{6,4},{7,5},{8,6},{9,7},{10,8},{11,9},{12,... | collective-permute-start | bytes 786440 | tf_op jit(solution)/shard_map/ppermute | solution.py:38
  95.0 3.8 %collective-permute-done.10 = bf16[256,512]{1,0:T(8,128)(2,1)S(1)} collective-permute-done((bf16[256,512]{1,0:T(8,128)(2,1)S(1)}, bf16[256,512]{1,0:T(8,128)(2,1)S(1)}, u32[]{:S(2)}, u32[]{:S(2)}) %collective-permute-start.10) | collective-permute-done | bytes 262176 | tf_op jit(solution)/shard_map/ppermute | solution.py:42
  98.8 0.1 fusion.9
  98.9 1.9 %collective-permute-start.11 = (bf16[256,512]{1,0:T(8,128)(2,1)S(1)}, bf16[256,512]{1,0:T(8,128)(2,1)S(1)}, u32[]{:S(2)}, u32[]{:S(2)}) collective-permute-start(bf16[256,512]{1,0:T(8,128)(2,1)S(1)} %fusion.9), channel_id=1, source_target_pairs={{2,0},{3,1},{4,2},{5,3},{6,4},{7,5},{8,6},{9,7},{10,8},{11,9},{12,... | collective-permute-start | bytes 786440 | tf_op jit(solution)/shard_map/ppermute | solution.py:38
  100.8 4.9 %collective-permute-done.8 = bf16[256,512]{1,0:T(8,128)(2,1)S(1)} collective-permute-done((bf16[256,512]{1,0:T(8,128)(2,1)S(1)}, bf16[256,512]{1,0:T(8,128)(2,1)S(1)}, u32[]{:S(2)}, u32[]{:S(2)}) %collective-permute-start.8) | collective-permute-done | bytes 262176 | tf_op jit(solution)/shard_map/ppermute | solution.py:38
  105.8 0.1 fusion.2
  105.9 4.9 %collective-permute-done.11 = bf16[256,512]{1,0:T(8,128)(2,1)S(1)} collective-permute-done((bf16[256,512]{1,0:T(8,128)(2,1)S(1)}, bf16[256,512]{1,0:T(8,128)(2,1)S(1)}, u32[]{:S(2)}, u32[]{:S(2)}) %collective-permute-start.11) | collective-permute-done | bytes 262176 | tf_op jit(solution)/shard_map/ppermute | solution.py:38
  110.9 0.1 fusion.7
  111.1 0.7 pad_maximum_fusion.3
  111.8 0.7 pad_maximum_fusion.2
  (17 shorter events, 0.3 us)
Async XLA Ops:
  0.6 32.9 %copy-start.1 = (s32[16]{0:T(128)S(1)}, s32[16]{0:T(128)}, u32[]{:S(2)}) copy-start(s32[16]{0:T(128)} %lengths_ref.3) | copy-start | bytes 196
  0.6 32.9 %copy-start = (bf16[256,4096]{1,0:T(8,128)(2,1)S(1)}, bf16[256,4096]{1,0:T(8,128)(2,1)}, u32[]{:S(2)}) copy-start(bf16[256,4096]{1,0:T(8,128)(2,1)} %q_ref.3) | copy-start | bytes 6291460
  1.9 3.4 %copy-start.2 = (bf16[256,128]{1,0:T(8,128)(2,1)}, bf16[256,128]{1,0:T(8,128)(2,1)S(1)}, u32[]{:S(2)}) copy-start(bf16[256,128]{1,0:T(8,128)(2,1)S(1)} %get-tuple-element.44) | copy-start | bytes 196612
  1.9 3.4 %copy-start.3 = (bf16[256,128]{1,0:T(8,128)(2,1)}, bf16[256,128]{1,0:T(8,128)(2,1)S(1)}, u32[]{:S(2)}) copy-start(bf16[256,128]{1,0:T(8,128)(2,1)S(1)} %get-tuple-element.47) | copy-start | bytes 196612
  2.0 9.4 %collective-permute-start.3 = (bf16[256,512]{1,0:T(8,128)(2,1)S(1)}, bf16[256,512]{1,0:T(8,128)(2,1)S(1)}, u32[]{:S(2)}, u32[]{:S(2)}) collective-permute-start(bf16[256,512]{1,0:T(8,128)(2,1)S(1)} %pad_maximum_fusion.1.own_ref), channel_id=1, source_target_pairs={{0,2},{1,3},{2,4},{3,5},{4,6},{5,7},{6,8},{7,9},{8,10},{9,11},{10,... | collective-permute-start | bytes 786440 | tf_op jit(solution)/shard_map/ppermute | solution.py:38
  5.4 11.3 %collective-permute-start = (bf16[256,512]{1,0:T(8,128)(2,1)S(1)}, bf16[256,512]{1,0:T(8,128)(2,1)S(1)}, u32[]{:S(2)}, u32[]{:S(2)}) collective-permute-start(bf16[256,512]{1,0:T(8,128)(2,1)S(1)} %pad_maximum_fusion.own_ref), channel_id=1, source_target_pairs={{0,2},{1,3},{2,4},{3,5},{4,6},{5,7},{6,8},{7,9},{8,10},{9,11},{10,... | collective-permute-start | bytes 786440 | tf_op jit(solution)/shard_map/ppermute | solution.py:38
  12.3 5.5 %collective-permute-start.4 = (bf16[256,512]{1,0:T(8,128)(2,1)S(1)}, bf16[256,512]{1,0:T(8,128)(2,1)}, u32[]{:S(2)}, u32[]{:S(2)}) collective-permute-start(bf16[256,512]{1,0:T(8,128)(2,1)S(1)} %broadcast_select_fusion), channel_id=1, source_target_pairs={{0,1},{1,0},{2,3},{3,2},{4,5},{5,4},{6,7},{7,6},{8,9},{9,8},{10,11... | collective-permute-start | bytes 786440 | tf_op jit(solution)/shard_map/ppermute | solution.py:42
  17.4 10.8 %collective-permute-start.1 = (bf16[256,512]{1,0:T(8,128)(2,1)}, bf16[256,512]{1,0:T(8,128)(2,1)S(1)}, u32[]{:S(2)}, u32[]{:S(2)}) collective-permute-start(bf16[256,512]{1,0:T(8,128)(2,1)} %broadcast_select_fusion.1), channel_id=1, source_target_pairs={{0,1},{1,0},{2,3},{3,2},{4,5},{5,4},{6,7},{7,6},{8,9},{9,8},{10,11... | collective-permute-start | bytes 786440 | tf_op jit(solution)/shard_map/ppermute | solution.py:42
  17.8 15.7 %collective-permute-start.5 = (bf16[256,512]{1,0:T(8,128)(2,1)}, bf16[256,512]{1,0:T(8,128)(2,1)}, u32[]{:S(2)}, u32[]{:S(2)}) collective-permute-start(bf16[256,512]{1,0:T(8,128)(2,1)} %collective-permute-done.4.near_ref), channel_id=1, source_target_pairs={{0,2},{1,3},{2,4},{3,5},{4,6},{5,7},{6,8},{7,9},{8,10},{9,11},{10,... | collective-permute-start | bytes 786440 | tf_op jit(solution)/shard_map/ppermute | solution.py:38
  28.2 30.3 %collective-permute-start.2 = (bf16[256,512]{1,0:T(8,128)(2,1)S(1)}, bf16[256,512]{1,0:T(8,128)(2,1)S(1)}, u32[]{:S(2)}, u32[]{:S(2)}) collective-permute-start(bf16[256,512]{1,0:T(8,128)(2,1)S(1)} %collective-permute-done.1.near_ref), channel_id=1, source_target_pairs={{0,2},{1,3},{2,4},{3,5},{4,6},{5,7},{6,8},{7,9},{8,10},{9,11},{10,... | collective-permute-start | bytes 786440 | tf_op jit(solution)/shard_map/ppermute | solution.py:38
  56.5 26.9 %collective-permute-start.6 = (bf16[256,512]{1,0:T(8,128)(2,1)S(1)}, bf16[256,512]{1,0:T(8,128)(2,1)S(1)}, u32[]{:S(2)}, u32[]{:S(2)}) collective-permute-start(bf16[256,512]{1,0:T(8,128)(2,1)S(1)} %get-tuple-element.22), channel_id=1, source_target_pairs={{2,0},{3,1},{4,2},{5,3},{6,4},{7,5},{8,6},{9,7},{10,8},{11,9},{12,... | collective-permute-start | bytes 786440 | tf_op jit(solution)/shard_map/ppermute | solution.py:38
  81.5 11.1 %collective-permute-start.9 = (bf16[256,512]{1,0:T(8,128)(2,1)S(1)}, bf16[256,512]{1,0:T(8,128)(2,1)S(1)}, u32[]{:S(2)}, u32[]{:S(2)}) collective-permute-start(bf16[256,512]{1,0:T(8,128)(2,1)S(1)} %get-tuple-element.26), channel_id=1, source_target_pairs={{2,0},{3,1},{4,2},{5,3},{6,4},{7,5},{8,6},{9,7},{10,8},{11,9},{12,... | collective-permute-start | bytes 786440 | tf_op jit(solution)/shard_map/ppermute | solution.py:38
  83.5 9.5 %collective-permute-start.7 = (bf16[256,512]{1,0:T(8,128)(2,1)S(1)}, bf16[256,512]{1,0:T(8,128)(2,1)S(1)}, u32[]{:S(2)}, u32[]{:S(2)}) collective-permute-start(bf16[256,512]{1,0:T(8,128)(2,1)S(1)} %add_convert_fusion.1), channel_id=1, source_target_pairs={{0,1},{1,0},{2,3},{3,2},{4,5},{5,4},{6,7},{7,6},{8,9},{9,8},{10,11... | collective-permute-start | bytes 786440 | tf_op jit(solution)/shard_map/ppermute | solution.py:42
  92.7 6.1 %collective-permute-start.10 = (bf16[256,512]{1,0:T(8,128)(2,1)S(1)}, bf16[256,512]{1,0:T(8,128)(2,1)S(1)}, u32[]{:S(2)}, u32[]{:S(2)}) collective-permute-start(bf16[256,512]{1,0:T(8,128)(2,1)S(1)} %add_convert_fusion), channel_id=1, source_target_pairs={{0,1},{1,0},{2,3},{3,2},{4,5},{5,4},{6,7},{7,6},{8,9},{9,8},{10,11... | collective-permute-start | bytes 786440 | tf_op jit(solution)/shard_map/ppermute | solution.py:42
  93.0 12.7 %collective-permute-start.8 = (bf16[256,512]{1,0:T(8,128)(2,1)S(1)}, bf16[256,512]{1,0:T(8,128)(2,1)S(1)}, u32[]{:S(2)}, u32[]{:S(2)}) collective-permute-start(bf16[256,512]{1,0:T(8,128)(2,1)S(1)} %fusion.4), channel_id=1, source_target_pairs={{2,0},{3,1},{4,2},{5,3},{6,4},{7,5},{8,6},{9,7},{10,8},{11,9},{12,... | collective-permute-start | bytes 786440 | tf_op jit(solution)/shard_map/ppermute | solution.py:38
  98.9 12.0 %collective-permute-start.11 = (bf16[256,512]{1,0:T(8,128)(2,1)S(1)}, bf16[256,512]{1,0:T(8,128)(2,1)S(1)}, u32[]{:S(2)}, u32[]{:S(2)}) collective-permute-start(bf16[256,512]{1,0:T(8,128)(2,1)S(1)} %fusion.9), channel_id=1, source_target_pairs={{2,0},{3,1},{4,2},{5,3},{6,4},{7,5},{8,6},{9,7},{10,8},{11,9},{12,... | collective-permute-start | bytes 786440 | tf_op jit(solution)/shard_map/ppermute | solution.py:38

commit v6 on v3

--- a/solution.py
+++ b/solution.py
@@ -40,10 +40,11 @@
     return lax.ppermute(value, AXES, [(source, source ^ 1) for source in range(device_count())])
 
 
-def write_bias(bias_ref, lengths_ref, first_ref, rows):
+def write_masks(bias_ref, old_ref, cut_ref, lengths_ref, first_ref, rows):
     docs = lengths_ref.shape[0]
     first = first_ref[0]
-    query_pos = first + lax.broadcasted_iota(jnp.int32, (rows, 128), 0)
+    row = lax.broadcasted_iota(jnp.int32, (rows, 128), 0)
+    query_pos = first + row
 
     def step(doc, carry):
         end, start = carry
@@ -52,83 +53,110 @@
 
     _, start = lax.fori_loop(0, docs, step, (jnp.int32(0), jnp.zeros((rows, 128), jnp.int32)))
     lane = lax.broadcasted_iota(jnp.int32, (rows, 128), 1)
-    for part in range(SPAN * rows // 128):
-        key_pos = first - (SPAN - 1) * rows + part * 128 + lane
-        allowed = (key_pos >= start) & (key_pos <= query_pos)
+    old = start < first - (SPAN - 2) * rows
+    old_ref[...] = jnp.where(old, 1.0, 0.0)
+    cut = jnp.min(jnp.where(old, start - (first - (SPAN - 1) * rows), rows), axis=0, keepdims=True)
+    cut_ref[...] = jnp.broadcast_to(cut, cut_ref.shape)
+    cut = jnp.broadcast_to(cut, (rows, 128))
+    for part in range((SPAN - 1) * rows // 128):
+        offset = part * 128 + lane
+        if part < rows // 128:
+            own = (offset <= row) & ((first + offset >= start) | (old & (offset < cut)))
+            allowed = own | (old & (offset >= cut))
+        else:
+            allowed = first - (SPAN - 1) * rows + offset >= start
         bias_ref[:, part * 128 : (part + 1) * 128] = jnp.where(allowed, 0.0, MASKED)
 
 
 def attention_kernel(first_ref, lengths_ref, q_ref, g_ref, far_ref, mid_ref, near_ref, own_ref, *refs):
     (
         out_ref, dq_ref, dfar_ref, dmid_ref, dnear_ref, down_ref,
-        bias_ref, key_ref, value_ref, key_t_ref, value_t_ref, dk_ref, dv_ref, inv_ref, *slots,
-    ) = refs[-26:]
+        bias_ref, old_ref, cut_ref,
+        key_ref, value_ref, key_t_ref, value_t_ref, key2_ref, value2_ref, key2_t_ref, value2_t_ref,
+        dk_ref, dv_ref, dk2_ref, dv2_ref, inv_ref, *slots,
+    ) = refs[-34:]
     s_refs, p_refs, dp_refs, d_refs, g_refs, delta_refs = (slots[i : i + 2] for i in range(0, 12, 2))
     rows = q_ref.shape[0]
-    window = SPAN * rows
+    window = (SPAN - 1) * rows
+    two = slice(0, rows)
+    rest = slice(rows, window)
 
     @pl.when(pl.program_id(0) == 0)
     def _():
-        write_bias(bias_ref, lengths_ref, first_ref, rows)
-        for ref in (*p_refs, *d_refs):
-            ref[...] = jnp.zeros_like(ref)
-
-    for j, block in enumerate((far_ref, mid_ref, near_ref, own_ref)):
+        write_masks(bias_ref, old_ref, cut_ref, lengths_ref, first_ref, rows)
+
+    for j, block in enumerate((mid_ref, near_ref)):
         span = slice(j * rows, (j + 1) * rows)
         key_ref[span] = block[:, :HEAD_SIZE]
         value_ref[span] = block[:, HEAD_SIZE:]
         key_t_ref[:, span] = block[:, :HEAD_SIZE].T
         value_t_ref[:, span] = block[:, HEAD_SIZE:].T
-    dk_ref[...] = jnp.zeros_like(dk_ref)
-    dv_ref[...] = jnp.zeros_like(dv_ref)
-    p_refs[1][...] = jnp.zeros_like(p_refs[1])
-    dp_refs[1][...] = jnp.zeros_like(dp_refs[1])
-    g_refs[1][...] = jnp.zeros_like(g_refs[1])
-    delta_refs[1][...] = jnp.zeros_like(delta_refs[1])
-
-    chunks = [
-        (slice(r, r + ROWS), slice((r + 1) // 128 * 128, -(-(window - rows + r + ROWS) // 128) * 128))
-        for r in range(0, rows, ROWS)
-    ]
+    from_far = lax.broadcasted_iota(jnp.int32, (rows, 2 * HEAD_SIZE), 0) >= cut_ref[0, 0]
+    mixed = jnp.where(from_far, far_ref[...].astype(jnp.float32), own_ref[...].astype(jnp.float32))
+    mixed = mixed.astype(jnp.bfloat16)
+    for j, block in enumerate((mixed, own_ref)):
+        span = slice(j * HEAD_SIZE, (j + 1) * HEAD_SIZE)
+        key2_ref[:, span] = block[:, :HEAD_SIZE]
+        value2_ref[:, span] = block[:, HEAD_SIZE:]
+        key2_t_ref[span] = block[:, :HEAD_SIZE].T
+        value2_t_ref[span] = block[:, HEAD_SIZE:].T
+    for ref in (dk_ref, dv_ref, dk2_ref, dv2_ref, p_refs[1], dp_refs[1], g_refs[1], delta_refs[1]):
+        ref[...] = jnp.zeros_like(ref)
 
     def columns(head):
         return pl.ds(pl.multiple_of(head * HEAD_SIZE, HEAD_SIZE), HEAD_SIZE)
 
+    def doubled(x):
+        old = old_ref[...].astype(jnp.bfloat16)
+        return jnp.concatenate([x * old, x * (1 - old)], axis=1)
+
+    def picked(x):
+        return jnp.where(old_ref[...] > 0.5, x[:, :HEAD_SIZE], x[:, HEAD_SIZE:])
+
     def scores(head, slot):
-        s_refs[slot][...] = dot(q_ref[:, columns(head)], key_t_ref[...])
+        q = q_ref[:, columns(head)]
+        s_refs[slot][:, two] = dot(doubled(q), key2_t_ref[...])
+        s_refs[slot][:, rest] = dot(q, key_t_ref[...])
 
     def softmax(slot):
-        for here, keys in chunks:
-            s = s_refs[slot][here, keys] * EXP2_SCALE + bias_ref[here, keys]
+        for r in range(0, rows, ROWS):
+            here = slice(r, r + ROWS)
+            s = s_refs[slot][here] * EXP2_SCALE + bias_ref[here]
             e = jnp.exp2(s - jnp.max(s, axis=1, keepdims=True))
             inv = 1.0 / jnp.sum(e, axis=1, keepdims=True)
             inv_ref[here] = jnp.broadcast_to(inv, (ROWS, HEAD_SIZE))
-            p_refs[slot][here, keys] = e.astype(jnp.bfloat16)
+            p_refs[slot][here] = e.astype(jnp.bfloat16)
 
     def mix(head, slot):
         cols = columns(head)
-        mixed = dot(p_refs[slot][...], value_ref[...])
+        total = picked(dot(p_refs[slot][:, two], value2_ref[...])) + dot(p_refs[slot][:, rest], value_ref[...])
         inv = inv_ref[...]
-        out = (mixed * inv).astype(jnp.bfloat16)
+        out = (total * inv).astype(jnp.bfloat16)
         out_ref[:, cols] = out
         g = g_ref[:, cols].astype(jnp.float32) * inv
         delta = jnp.sum(g * out.astype(jnp.float32), axis=1, keepdims=True)
         delta_refs[slot][...] = jnp.broadcast_to(delta, (rows, HEAD_SIZE))
-        g_refs[slot][...] = g.astype(jnp.bfloat16)
-        dp_refs[slot][...] = dot(g_refs[slot][...], value_t_ref[...])
+        g = g.astype(jnp.bfloat16)
+        g_refs[slot][...] = g
+        dp_refs[slot][:, two] = dot(doubled(g), value2_t_ref[...])
+        dp_refs[slot][:, rest] = dot(g, value_t_ref[...])
 
     def score_grad(slot):
-        for here, keys in chunks:
-            repeat = (keys.stop - keys.start) // HEAD_SIZE
-            delta = jnp.concatenate([delta_refs[slot][here]] * repeat, axis=1)
-            p = p_refs[slot][here, keys].astype(jnp.float32)
-            d_refs[slot][here, keys] = (p * (dp_refs[slot][here, keys] - delta)).astype(jnp.bfloat16)
+        for r in range(0, rows, ROWS):
+            here = slice(r, r + ROWS)
+            delta = jnp.concatenate([delta_refs[slot][here]] * (window // HEAD_SIZE), axis=1)
+            d_refs[slot][here] = p_refs[slot][here] * (dp_refs[slot][here] - delta).astype(jnp.bfloat16)
 
     def spread(head, slot):
         cols = columns(head)
-        dq_ref[:, cols] = (dot(d_refs[slot][...], key_ref[...]) * SCALE).astype(jnp.bfloat16)
-        dk_ref[...] += dot(q_ref[:, cols].T, d_refs[slot][...])
-        dv_ref[...] += dot(g_refs[slot][...].T, p_refs[slot][...])
+        total = picked(dot(d_refs[slot][:, two], key2_ref[...])) + dot(d_refs[slot][:, rest], key_ref[...])
+        dq_ref[:, cols] = (total * SCALE).astype(jnp.bfloat16)
+        q = q_ref[:, cols]
+        g = g_refs[slot][...]
+        dk2_ref[...] += dot(doubled(q).T, d_refs[slot][:, two])
+        dk_ref[...] += dot(q.T, d_refs[slot][:, rest])
+        dv2_ref[...] += dot(doubled(g).T, p_refs[slot][:, two])
+        dv_ref[...] += dot(g.T, p_refs[slot][:, rest])
 
     scores(0, 0)
 
@@ -146,17 +174,22 @@
     lax.fori_loop(0, GROUP // 2, step, 0)
     score_grad(1)
     spread(GROUP - 1, 1)
-    for j, target in enumerate((dfar_ref, dmid_ref, dnear_ref, down_ref)):
-        span = slice(j * rows, (j + 1) * rows)
-        target[:, :HEAD_SIZE] = (dk_ref[:, span].T * SCALE).astype(target.dtype)
-        target[:, HEAD_SIZE:] = dv_ref[:, span].T.astype(target.dtype)
+    from_far = from_far[:, :HEAD_SIZE]
+    for part, grad, grad2, scale in ((0, dk_ref, dk2_ref, SCALE), (1, dv_ref, dv2_ref, 1.0)):
+        span = slice(part * HEAD_SIZE, (part + 1) * HEAD_SIZE)
+        either = grad2[:HEAD_SIZE].T * scale
+        own = grad2[HEAD_SIZE:].T * scale
+        dfar_ref[:, span] = jnp.where(from_far, either, 0.0).astype(dfar_ref.dtype)
+        down_ref[:, span] = own + jnp.where(from_far, 0.0, either)
+        dmid_ref[:, span] = grad[:, :rows].T * scale
+        dnear_ref[:, span] = grad[:, rows:].T * scale
 
 
 def attention(chunk, first, lengths, queries, out_grad, blocks, grads):
     rows = queries.shape[0]
     wide = GROUP * HEAD_SIZE
     pair = 2 * HEAD_SIZE
-    window = SPAN * rows
+    window = (SPAN - 1) * rows
     query_spec = pl.BlockSpec((rows, wide), lambda i, *_: (0, chunk * CHUNK + i))
     block_spec = pl.BlockSpec((rows, pair), lambda i, *_: (0, i))
     operands = [first, lengths, queries, out_grad, *blocks]
@@ -178,26 +211,26 @@
             in_specs=in_specs,
             out_specs=[query_spec] * 2 + [block_spec] * 4,
             scratch_shapes=[
-                pltpu.VMEM((rows, window), f32),
-                pltpu.VMEM((window, HEAD_SIZE), bf16),
-                pltpu.VMEM((window, HEAD_SIZE), bf16),
-                pltpu.VMEM((HEAD_SIZE, window), bf16),
-                pltpu.VMEM((HEAD_SIZE, window), bf16),
-                pltpu.VMEM((HEAD_SIZE, window), f32),
-                pltpu.VMEM((HEAD_SIZE, window), f32),
-                pltpu.VMEM((rows, HEAD_SIZE), f32),
-            ]
-            + [
-                pltpu.VMEM((rows, columns), kind)
-                for columns, kind in (
-                    (window, f32),
-                    (window, bf16),
-                    (window, f32),
-                    (window, bf16),
-                    (HEAD_SIZE, bf16),
-                    (HEAD_SIZE, f32),
+                pltpu.VMEM(shape, kind)
+                for shape, kind, count in (
+                    ((rows, window), f32, 1),
+                    ((rows, HEAD_SIZE), f32, 1),
+                    ((8, HEAD_SIZE), jnp.int32, 1),
+                    ((2 * rows, HEAD_SIZE), bf16, 2),
+                    ((HEAD_SIZE, 2 * rows), bf16, 2),
+                    ((rows, pair), bf16, 2),
+                    ((pair, rows), bf16, 2),
+                    ((HEAD_SIZE, 2 * rows), f32, 2),
+                    ((pair, rows), f32, 2),
+                    ((rows, HEAD_SIZE), f32, 1),
+                    ((rows, window), f32, 2),
+                    ((rows, window), bf16, 2),
+                    ((rows, window), f32, 2),
+                    ((rows, window), bf16, 2),
+                    ((rows, HEAD_SIZE), bf16, 2),
+                    ((rows, HEAD_SIZE), f32, 2),
                 )
-                for _ in range(2)
+                for _ in range(count)
             ],
         ),
         input_output_aliases=aliases,

time: 107 us -> 103 us (0.963)
  Pallas kernels: 39.9 us -> 36.4 us
    pallas_call x2, Pallas kernels: 39.9 us -> 36.4 us  [attention(): pl.pallas_call(attention_kernel, out_shape=[jax.ShapeDtypeStruct(queries....]
  transfers between devices with their start and end apart: 12 -> 12, of which waited for: 8 -> 8; matrix products, arithmetic and copies ran while one was open for 2% -> 2% of each run, Pallas kernels for 37% -> 35%
where the time goes in v6:
time: 103 us
  Pallas kernels  36.4 us (35%)
  waiting for transfers between devices  31.8 us (31%)
  starting transfers between devices  28.7 us (28%)
  other arithmetic  3.83 us (4%)
  local copies, waits for them, and re-layouts  1.38 us (1%)
    pallas_call x2, Pallas kernels, attention(): pl.pallas_call(attention_kernel, out_shape=[jax.ShapeDtypeStruct(queries....  36.4 us
    ppermute x8, waiting for transfers between devices, passed_along(): lax.ppermute(value, AXES, [(source, source + steps) for source in range(f...  27.8 us
    ppermute x8, starting transfers between devices, passed_along(): lax.ppermute(value, AXES, [(source, source + steps) for source in range(f...  27.6 us
    ppermute x4, waiting for transfers between devices, swapped(): lax.ppermute(value, AXES, [(source, source ^ 1) for source in range(devic...  4.01 us
  transfers between devices with their start and end apart: 12, of which 8 were waited for; matrix products, arithmetic and copies ran while one was open for 2% of the time, Pallas kernels for 35%

profile of v6, /device:TPU:29, one launch (start us, length us, event | category | flops | bytes accessed | tf_op | source)
XLA Modules:
  0.0 103.0 jit_solution(1437864732059744446)
XLA Ops:
  0.7 1.3 %fusion.12 = (bf16[256,128]{1,0:T(8,128)(2,1)S(1)}, bf16[256,128]{1,0:T(8,128)(2,1)S(1)}, bf16[256,128]{1,0:T(8,128)(2,1)S(1)}, bf16[256,128]{1,0:T(8,128)(2,1)S...) fusion(bf16[256,512]{1,0:T(8,128)(2,1)} %param.6, ...), kind=kLoop, calls=%fused_computation.24 | loop fusion | bytes 1048576 | tf_op jit(solution)/shard_map/slice | solution.py:260
  2.0 3.3 %collective-permute-start.3 = (bf16[256,512]{1,0:T(8,128)(2,1)S(1)}, bf16[256,512]{1,0:T(8,128)(2,1)S(1)}, u32[]{:S(2)}, u32[]{:S(2)}) collective-permute-start(bf16[256,512]{1,0:T(8,128)(2,1)S(1)} %pad_maximum_fusion.1.own_ref), channel_id=1, source_target_pairs={{0,2},{1,3},{2,4},{3,5},{4,6},{5,7},{6,8},{7,9},{8,10},{9,11},{10,... | collective-permute-start | bytes 786440 | tf_op jit(solution)/shard_map/ppermute | solution.py:36
  5.4 3.5 %collective-permute-start = (bf16[256,512]{1,0:T(8,128)(2,1)S(1)}, bf16[256,512]{1,0:T(8,128)(2,1)S(1)}, u32[]{:S(2)}, u32[]{:S(2)}) collective-permute-start(bf16[256,512]{1,0:T(8,128)(2,1)S(1)} %pad_maximum_fusion.own_ref), channel_id=1, source_target_pairs={{0,2},{1,3},{2,4},{3,5},{4,6},{5,7},{6,8},{7,9},{8,10},{9,11},{10,... | collective-permute-start | bytes 786440 | tf_op jit(solution)/shard_map/ppermute | solution.py:36
  8.9 2.5 %collective-permute-done.3.mid_ref = bf16[256,512]{1,0:T(8,128)(2,1)S(1)} collective-permute-done((bf16[256,512]{1,0:T(8,128)(2,1)S(1)}, bf16[256,512]{1,0:T(8,128)(2,1)S(1)}, u32[]{:S(2)}, u32[]{:S(2)}) %collective-permute-start.3) | collective-permute-done | bytes 262176 | tf_op jit(solution)/shard_map/ppermute | solution.py:36
  11.4 1.0 broadcast_select_fusion
  12.3 0.3 collective-permute-start.4
  12.6 4.1 %collective-permute-done.mid_ref = bf16[256,512]{1,0:T(8,128)(2,1)S(1)} collective-permute-done((bf16[256,512]{1,0:T(8,128)(2,1)S(1)}, bf16[256,512]{1,0:T(8,128)(2,1)S(1)}, u32[]{:S(2)}, u32[]{:S(2)}) %collective-permute-start) | collective-permute-done | bytes 262176 | tf_op jit(solution)/shard_map/ppermute | solution.py:36
  16.7 0.8 broadcast_select_fusion.1
  17.4 0.2 collective-permute-start.1
  17.7 0.2 collective-permute-done.4.near_ref
  17.8 10.4 %collective-permute-start.5 = (bf16[256,512]{1,0:T(8,128)(2,1)}, bf16[256,512]{1,0:T(8,128)(2,1)}, u32[]{:S(2)}, u32[]{:S(2)}) collective-permute-start(bf16[256,512]{1,0:T(8,128)(2,1)} %collective-permute-done.4.near_ref), channel_id=1, source_target_pairs={{0,2},{1,3},{2,4},{3,5},{4,6},{5,7},{6,8},{7,9},{8,10},{9,11},{10,... | collective-permute-start | bytes 786440 | tf_op jit(solution)/shard_map/ppermute | solution.py:36
  28.2 2.7 %collective-permute-start.2 = (bf16[256,512]{1,0:T(8,128)(2,1)S(1)}, bf16[256,512]{1,0:T(8,128)(2,1)S(1)}, u32[]{:S(2)}, u32[]{:S(2)}) collective-permute-start(bf16[256,512]{1,0:T(8,128)(2,1)S(1)} %collective-permute-done.1.near_ref), channel_id=1, source_target_pairs={{0,2},{1,3},{2,4},{3,5},{4,6},{5,7},{6,8},{7,9},{8,10},{9,11},{10,... | collective-permute-start | bytes 786440 | tf_op jit(solution)/shard_map/ppermute | solution.py:36
  30.9 2.6 %collective-permute-done.5.far_ref = bf16[256,512]{1,0:T(8,128)(2,1)} collective-permute-done((bf16[256,512]{1,0:T(8,128)(2,1)}, bf16[256,512]{1,0:T(8,128)(2,1)}, u32[]{:S(2)}, u32[]{:S(2)}) %collective-permute-start.5) | collective-permute-done | bytes 262176 | tf_op jit(solution)/shard_map/ppermute | solution.py:36
  33.5 18.2 %attention.2 = (bf16[256,4096]{1,0:T(8,128)(2,1)}, bf16[256,4096]{1,0:T(8,128)(2,1)}, bf16[256,512]{1,0:T(8,128)(2,1)S(1)}, f32[256,512]{1,0:T(8,128)S(1)}, f32[...) custom-call(s32[1]{0:T(128)} %bitcast.first_ref, s32[16]{0:T(128)S(1)} %copy-done.1, bf16[256,4096]{1,0:T(8,128)(2,1)S(1)} %copy-done, ...), custom_call_target="tpu_custom_call" | custom-call | flops 9663676416 | bytes 7077888 | tf_op jit(solution)/shard_map/attention/pallas_call | solution.py:204
  51.8 1.9 %collective-permute-start.6 = (bf16[256,512]{1,0:T(8,128)(2,1)S(1)}, bf16[256,512]{1,0:T(8,128)(2,1)S(1)}, u32[]{:S(2)}, u32[]{:S(2)}) collective-permute-start(bf16[256,512]{1,0:T(8,128)(2,1)S(1)} %get-tuple-element.22), channel_id=1, source_target_pairs={{2,0},{3,1},{4,2},{5,3},{6,4},{7,5},{8,6},{9,7},{10,8},{11,9},{12,... | collective-permute-start | bytes 786440 | tf_op jit(solution)/shard_map/ppermute | solution.py:36
  53.7 18.2 %attention.3 = (bf16[256,4096]{1,0:T(8,128)(2,1)}, bf16[256,4096]{1,0:T(8,128)(2,1)}, bf16[256,512]{1,0:T(8,128)(2,1)S(1)}, f32[256,512]{1,0:T(8,128)S(1)}, f32[...) custom-call(s32[1]{0:T(128)} %bitcast.first_ref, s32[16]{0:T(128)S(1)} %copy-done.1, ...), custom_call_target="tpu_custom_call", output_to_operand_aliasing={{0}: (8, {}), {1}: (9, {})} | custom-call | flops 9663676416 | bytes 7077888 | tf_op jit(solution)/shard_map/attention/pallas_call | solution.py:204
  71.9 1.9 %collective-permute-start.9 = (bf16[256,512]{1,0:T(8,128)(2,1)S(1)}, bf16[256,512]{1,0:T(8,128)(2,1)S(1)}, u32[]{:S(2)}, u32[]{:S(2)}) collective-permute-start(bf16[256,512]{1,0:T(8,128)(2,1)S(1)} %get-tuple-element.26), channel_id=1, source_target_pairs={{2,0},{3,1},{4,2},{5,3},{6,4},{7,5},{8,6},{9,7},{10,8},{11,9},{12,... | collective-permute-start | bytes 786440 | tf_op jit(solution)/shard_map/ppermute | solution.py:36
  73.9 0.3 collective-permute-start.7
  74.2 8.8 %collective-permute-done.9 = bf16[256,512]{1,0:T(8,128)(2,1)S(1)} collective-permute-done((bf16[256,512]{1,0:T(8,128)(2,1)S(1)}, bf16[256,512]{1,0:T(8,128)(2,1)S(1)}, u32[]{:S(2)}, u32[]{:S(2)}) %collective-permute-start.9) | collective-permute-done | bytes 262176 | tf_op jit(solution)/shard_map/ppermute | solution.py:36
  83.0 0.1 add_convert_fusion
  83.1 0.3 collective-permute-start.10
  83.4 0.1 fusion.4
  83.5 1.9 %collective-permute-start.8 = (bf16[256,512]{1,0:T(8,128)(2,1)S(1)}, bf16[256,512]{1,0:T(8,128)(2,1)S(1)}, u32[]{:S(2)}, u32[]{:S(2)}) collective-permute-start(bf16[256,512]{1,0:T(8,128)(2,1)S(1)} %fusion.4), channel_id=1, source_target_pairs={{2,0},{3,1},{4,2},{5,3},{6,4},{7,5},{8,6},{9,7},{10,8},{11,9},{12,... | collective-permute-start | bytes 786440 | tf_op jit(solution)/shard_map/ppermute | solution.py:36
  85.4 3.9 %collective-permute-done.10 = bf16[256,512]{1,0:T(8,128)(2,1)S(1)} collective-permute-done((bf16[256,512]{1,0:T(8,128)(2,1)S(1)}, bf16[256,512]{1,0:T(8,128)(2,1)S(1)}, u32[]{:S(2)}, u32[]{:S(2)}) %collective-permute-start.10) | collective-permute-done | bytes 262176 | tf_op jit(solution)/shard_map/ppermute | solution.py:40
  89.2 0.1 fusion.9
  89.3 1.9 %collective-permute-start.11 = (bf16[256,512]{1,0:T(8,128)(2,1)S(1)}, bf16[256,512]{1,0:T(8,128)(2,1)S(1)}, u32[]{:S(2)}, u32[]{:S(2)}) collective-permute-start(bf16[256,512]{1,0:T(8,128)(2,1)S(1)} %fusion.9), channel_id=1, source_target_pairs={{2,0},{3,1},{4,2},{5,3},{6,4},{7,5},{8,6},{9,7},{10,8},{11,9},{12,... | collective-permute-start | bytes 786440 | tf_op jit(solution)/shard_map/ppermute | solution.py:36
  91.3 5.0 %collective-permute-done.8 = bf16[256,512]{1,0:T(8,128)(2,1)S(1)} collective-permute-done((bf16[256,512]{1,0:T(8,128)(2,1)S(1)}, bf16[256,512]{1,0:T(8,128)(2,1)S(1)}, u32[]{:S(2)}, u32[]{:S(2)}) %collective-permute-start.8) | collective-permute-done | bytes 262176 | tf_op jit(solution)/shard_map/ppermute | solution.py:36
  96.2 0.1 fusion.2
  96.4 4.9 %collective-permute-done.11 = bf16[256,512]{1,0:T(8,128)(2,1)S(1)} collective-permute-done((bf16[256,512]{1,0:T(8,128)(2,1)S(1)}, bf16[256,512]{1,0:T(8,128)(2,1)S(1)}, u32[]{:S(2)}, u32[]{:S(2)}) %collective-permute-start.11) | collective-permute-done | bytes 262176 | tf_op jit(solution)/shard_map/ppermute | solution.py:36
  101.3 0.1 fusion.7
  101.5 0.7 pad_maximum_fusion.3
  102.2 0.7 pad_maximum_fusion.2
  (17 shorter events, 0.3 us)
Async XLA Ops:
  0.6 32.9 %copy-start.1 = (s32[16]{0:T(128)S(1)}, s32[16]{0:T(128)}, u32[]{:S(2)}) copy-start(s32[16]{0:T(128)} %lengths_ref.3) | copy-start | bytes 196
  0.6 32.9 %copy-start = (bf16[256,4096]{1,0:T(8,128)(2,1)S(1)}, bf16[256,4096]{1,0:T(8,128)(2,1)}, u32[]{:S(2)}) copy-start(bf16[256,4096]{1,0:T(8,128)(2,1)} %q_ref.3) | copy-start | bytes 6291460
  1.9 3.4 %copy-start.2 = (bf16[256,128]{1,0:T(8,128)(2,1)}, bf16[256,128]{1,0:T(8,128)(2,1)S(1)}, u32[]{:S(2)}) copy-start(bf16[256,128]{1,0:T(8,128)(2,1)S(1)} %get-tuple-element.44) | copy-start | bytes 196612
  1.9 3.4 %copy-start.3 = (bf16[256,128]{1,0:T(8,128)(2,1)}, bf16[256,128]{1,0:T(8,128)(2,1)S(1)}, u32[]{:S(2)}) copy-start(bf16[256,128]{1,0:T(8,128)(2,1)S(1)} %get-tuple-element.47) | copy-start | bytes 196612
  2.0 9.4 %collective-permute-start.3 = (bf16[256,512]{1,0:T(8,128)(2,1)S(1)}, bf16[256,512]{1,0:T(8,128)(2,1)S(1)}, u32[]{:S(2)}, u32[]{:S(2)}) collective-permute-start(bf16[256,512]{1,0:T(8,128)(2,1)S(1)} %pad_maximum_fusion.1.own_ref), channel_id=1, source_target_pairs={{0,2},{1,3},{2,4},{3,5},{4,6},{5,7},{6,8},{7,9},{8,10},{9,11},{10,... | collective-permute-start | bytes 786440 | tf_op jit(solution)/shard_map/ppermute | solution.py:36
  5.4 11.3 %collective-permute-start = (bf16[256,512]{1,0:T(8,128)(2,1)S(1)}, bf16[256,512]{1,0:T(8,128)(2,1)S(1)}, u32[]{:S(2)}, u32[]{:S(2)}) collective-permute-start(bf16[256,512]{1,0:T(8,128)(2,1)S(1)} %pad_maximum_fusion.own_ref), channel_id=1, source_target_pairs={{0,2},{1,3},{2,4},{3,5},{4,6},{5,7},{6,8},{7,9},{8,10},{9,11},{10,... | collective-permute-start | bytes 786440 | tf_op jit(solution)/shard_map/ppermute | solution.py:36
  12.3 5.5 %collective-permute-start.4 = (bf16[256,512]{1,0:T(8,128)(2,1)S(1)}, bf16[256,512]{1,0:T(8,128)(2,1)}, u32[]{:S(2)}, u32[]{:S(2)}) collective-permute-start(bf16[256,512]{1,0:T(8,128)(2,1)S(1)} %broadcast_select_fusion), channel_id=1, source_target_pairs={{0,1},{1,0},{2,3},{3,2},{4,5},{5,4},{6,7},{7,6},{8,9},{9,8},{10,11... | collective-permute-start | bytes 786440 | tf_op jit(solution)/shard_map/ppermute | solution.py:40
  17.4 10.8 %collective-permute-start.1 = (bf16[256,512]{1,0:T(8,128)(2,1)}, bf16[256,512]{1,0:T(8,128)(2,1)S(1)}, u32[]{:S(2)}, u32[]{:S(2)}) collective-permute-start(bf16[256,512]{1,0:T(8,128)(2,1)} %broadcast_select_fusion.1), channel_id=1, source_target_pairs={{0,1},{1,0},{2,3},{3,2},{4,5},{5,4},{6,7},{7,6},{8,9},{9,8},{10,11... | collective-permute-start | bytes 786440 | tf_op jit(solution)/shard_map/ppermute | solution.py:40
  17.8 15.7 %collective-permute-start.5 = (bf16[256,512]{1,0:T(8,128)(2,1)}, bf16[256,512]{1,0:T(8,128)(2,1)}, u32[]{:S(2)}, u32[]{:S(2)}) collective-permute-start(bf16[256,512]{1,0:T(8,128)(2,1)} %collective-permute-done.4.near_ref), channel_id=1, source_target_pairs={{0,2},{1,3},{2,4},{3,5},{4,6},{5,7},{6,8},{7,9},{8,10},{9,11},{10,... | collective-permute-start | bytes 786440 | tf_op jit(solution)/shard_map/ppermute | solution.py:36
  28.2 25.5 %collective-permute-start.2 = (bf16[256,512]{1,0:T(8,128)(2,1)S(1)}, bf16[256,512]{1,0:T(8,128)(2,1)S(1)}, u32[]{:S(2)}, u32[]{:S(2)}) collective-permute-start(bf16[256,512]{1,0:T(8,128)(2,1)S(1)} %collective-permute-done.1.near_ref), channel_id=1, source_target_pairs={{0,2},{1,3},{2,4},{3,5},{4,6},{5,7},{6,8},{7,9},{8,10},{9,11},{10,... | collective-permute-start | bytes 786440 | tf_op jit(solution)/shard_map/ppermute | solution.py:36
  51.8 22.0 %collective-permute-start.6 = (bf16[256,512]{1,0:T(8,128)(2,1)S(1)}, bf16[256,512]{1,0:T(8,128)(2,1)S(1)}, u32[]{:S(2)}, u32[]{:S(2)}) collective-permute-start(bf16[256,512]{1,0:T(8,128)(2,1)S(1)} %get-tuple-element.22), channel_id=1, source_target_pairs={{2,0},{3,1},{4,2},{5,3},{6,4},{7,5},{8,6},{9,7},{10,8},{11,9},{12,... | collective-permute-start | bytes 786440 | tf_op jit(solution)/shard_map/ppermute | solution.py:36
  71.9 11.1 %collective-permute-start.9 = (bf16[256,512]{1,0:T(8,128)(2,1)S(1)}, bf16[256,512]{1,0:T(8,128)(2,1)S(1)}, u32[]{:S(2)}, u32[]{:S(2)}) collective-permute-start(bf16[256,512]{1,0:T(8,128)(2,1)S(1)} %get-tuple-element.26), channel_id=1, source_target_pairs={{2,0},{3,1},{4,2},{5,3},{6,4},{7,5},{8,6},{9,7},{10,8},{11,9},{12,... | collective-permute-start | bytes 786440 | tf_op jit(solution)/shard_map/ppermute | solution.py:36
  73.9 9.5 %collective-permute-start.7 = (bf16[256,512]{1,0:T(8,128)(2,1)S(1)}, bf16[256,512]{1,0:T(8,128)(2,1)S(1)}, u32[]{:S(2)}, u32[]{:S(2)}) collective-permute-start(bf16[256,512]{1,0:T(8,128)(2,1)S(1)} %add_convert_fusion.1), channel_id=1, source_target_pairs={{0,1},{1,0},{2,3},{3,2},{4,5},{5,4},{6,7},{7,6},{8,9},{9,8},{10,11... | collective-permute-start | bytes 786440 | tf_op jit(solution)/shard_map/ppermute | solution.py:40
  83.1 6.1 %collective-permute-start.10 = (bf16[256,512]{1,0:T(8,128)(2,1)S(1)}, bf16[256,512]{1,0:T(8,128)(2,1)S(1)}, u32[]{:S(2)}, u32[]{:S(2)}) collective-permute-start(bf16[256,512]{1,0:T(8,128)(2,1)S(1)} %add_convert_fusion), channel_id=1, source_target_pairs={{0,1},{1,0},{2,3},{3,2},{4,5},{5,4},{6,7},{7,6},{8,9},{9,8},{10,11... | collective-permute-start | bytes 786440 | tf_op jit(solution)/shard_map/ppermute | solution.py:40
  83.5 12.7 %collective-permute-start.8 = (bf16[256,512]{1,0:T(8,128)(2,1)S(1)}, bf16[256,512]{1,0:T(8,128)(2,1)S(1)}, u32[]{:S(2)}, u32[]{:S(2)}) collective-permute-start(bf16[256,512]{1,0:T(8,128)(2,1)S(1)} %fusion.4), channel_id=1, source_target_pairs={{2,0},{3,1},{4,2},{5,3},{6,4},{7,5},{8,6},{9,7},{10,8},{11,9},{12,... | collective-permute-start | bytes 786440 | tf_op jit(solution)/shard_map/ppermute | solution.py:36
  89.3 12.0 %collective-permute-start.11 = (bf16[256,512]{1,0:T(8,128)(2,1)S(1)}, bf16[256,512]{1,0:T(8,128)(2,1)S(1)}, u32[]{:S(2)}, u32[]{:S(2)}) collective-permute-start(bf16[256,512]{1,0:T(8,128)(2,1)S(1)} %fusion.9), channel_id=1, source_target_pairs={{2,0},{3,1},{4,2},{5,3},{6,4},{7,5},{8,6},{9,7},{10,8},{11,9},{12,... | collective-permute-start | bytes 786440 | tf_op jit(solution)/shard_map/ppermute | solution.py:36

commit v7 on v6

--- a/solution.py
+++ b/solution.py
@@ -73,35 +73,39 @@
         out_ref, dq_ref, dfar_ref, dmid_ref, dnear_ref, down_ref,
         bias_ref, old_ref, cut_ref,
         key_ref, value_ref, key_t_ref, value_t_ref, key2_ref, value2_ref, key2_t_ref, value2_t_ref,
-        dk_ref, dv_ref, dk2_ref, dv2_ref, inv_ref, *slots,
-    ) = refs[-34:]
-    s_refs, p_refs, dp_refs, d_refs, g_refs, delta_refs = (slots[i : i + 2] for i in range(0, 12, 2))
+        dk_ref, dv_ref, dk2_ref, dv2_ref, *slots,
+    ) = refs[-37:]
+    p_refs, (s_refs, dp_refs, d_refs, g_refs, delta_refs, inv_refs) = (
+        slots[:4],
+        (slots[i : i + 2] for i in range(4, 16, 2)),
+    )
     rows = q_ref.shape[0]
     window = (SPAN - 1) * rows
+    heads = CHUNK * GROUP
     two = slice(0, rows)
     rest = slice(rows, window)
 
-    @pl.when(pl.program_id(0) == 0)
-    def _():
-        write_masks(bias_ref, old_ref, cut_ref, lengths_ref, first_ref, rows)
-
-    for j, block in enumerate((mid_ref, near_ref)):
-        span = slice(j * rows, (j + 1) * rows)
-        key_ref[span] = block[:, :HEAD_SIZE]
-        value_ref[span] = block[:, HEAD_SIZE:]
-        key_t_ref[:, span] = block[:, :HEAD_SIZE].T
-        value_t_ref[:, span] = block[:, HEAD_SIZE:].T
+    write_masks(bias_ref, old_ref, cut_ref, lengths_ref, first_ref, rows)
     from_far = lax.broadcasted_iota(jnp.int32, (rows, 2 * HEAD_SIZE), 0) >= cut_ref[0, 0]
-    mixed = jnp.where(from_far, far_ref[...].astype(jnp.float32), own_ref[...].astype(jnp.float32))
-    mixed = mixed.astype(jnp.bfloat16)
-    for j, block in enumerate((mixed, own_ref)):
-        span = slice(j * HEAD_SIZE, (j + 1) * HEAD_SIZE)
-        key2_ref[:, span] = block[:, :HEAD_SIZE]
-        value2_ref[:, span] = block[:, HEAD_SIZE:]
-        key2_t_ref[span] = block[:, :HEAD_SIZE].T
-        value2_t_ref[span] = block[:, HEAD_SIZE:].T
-    for ref in (dk_ref, dv_ref, dk2_ref, dv2_ref, p_refs[1], dp_refs[1], g_refs[1], delta_refs[1]):
+    for kv in range(CHUNK):
+        pair = slice(kv * 2 * HEAD_SIZE, (kv + 1) * 2 * HEAD_SIZE)
+        far, mid, near, own = (ref[:, pair] for ref in (far_ref, mid_ref, near_ref, own_ref))
+        for j, block in enumerate((mid, near)):
+            span = slice(j * rows, (j + 1) * rows)
+            key_ref[kv, span] = block[:, :HEAD_SIZE]
+            value_ref[kv, span] = block[:, HEAD_SIZE:]
+            key_t_ref[kv, :, span] = block[:, :HEAD_SIZE].T
+            value_t_ref[kv, :, span] = block[:, HEAD_SIZE:].T
+        mixed = jnp.where(from_far, far.astype(jnp.float32), own.astype(jnp.float32))
+        for j, block in enumerate((mixed.astype(jnp.bfloat16), own)):
+            span = slice(j * HEAD_SIZE, (j + 1) * HEAD_SIZE)
+            key2_ref[kv, :, span] = block[:, :HEAD_SIZE]
+            value2_ref[kv, :, span] = block[:, HEAD_SIZE:]
+            key2_t_ref[kv, span] = block[:, :HEAD_SIZE].T
+            value2_t_ref[kv, span] = block[:, HEAD_SIZE:].T
+    for ref in (dk_ref, dv_ref, dk2_ref, dv2_ref, p_refs[2], p_refs[3], dp_refs[0], delta_refs[0], g_refs[0]):
         ref[...] = jnp.zeros_like(ref)
+    inv_refs[1][...] = jnp.ones_like(inv_refs[1])
 
     def columns(head):
         return pl.ds(pl.multiple_of(head * HEAD_SIZE, HEAD_SIZE), HEAD_SIZE)
@@ -114,84 +118,93 @@
         return jnp.where(old_ref[...] > 0.5, x[:, :HEAD_SIZE], x[:, HEAD_SIZE:])
 
     def scores(head, slot):
+        kv = head // GROUP
         q = q_ref[:, columns(head)]
-        s_refs[slot][:, two] = dot(doubled(q), key2_t_ref[...])
-        s_refs[slot][:, rest] = dot(q, key_t_ref[...])
+        s_refs[slot % 2][:, two] = dot(doubled(q), key2_t_ref[kv])
+        s_refs[slot % 2][:, rest] = dot(q, key_t_ref[kv])
 
     def softmax(slot):
         for r in range(0, rows, ROWS):
             here = slice(r, r + ROWS)
-            s = s_refs[slot][here] * EXP2_SCALE + bias_ref[here]
+            s = s_refs[slot % 2][here] * EXP2_SCALE + bias_ref[here]
             e = jnp.exp2(s - jnp.max(s, axis=1, keepdims=True))
             inv = 1.0 / jnp.sum(e, axis=1, keepdims=True)
-            inv_ref[here] = jnp.broadcast_to(inv, (ROWS, HEAD_SIZE))
+            inv_refs[slot % 2][here] = jnp.broadcast_to(inv, (ROWS, HEAD_SIZE))
             p_refs[slot][here] = e.astype(jnp.bfloat16)
 
     def mix(head, slot):
-        cols = columns(head)
-        total = picked(dot(p_refs[slot][:, two], value2_ref[...])) + dot(p_refs[slot][:, rest], value_ref[...])
-        inv = inv_ref[...]
+        kv, cols = head // GROUP, columns(head)
+        p_ref, at = p_refs[slot], slot % 2
+        total = picked(dot(p_ref[:, two], value2_ref[kv])) + dot(p_ref[:, rest], value_ref[kv])
+        inv = inv_refs[at][...]
         out = (total * inv).astype(jnp.bfloat16)
         out_ref[:, cols] = out
         g = g_ref[:, cols].astype(jnp.float32) * inv
         delta = jnp.sum(g * out.astype(jnp.float32), axis=1, keepdims=True)
-        delta_refs[slot][...] = jnp.broadcast_to(delta, (rows, HEAD_SIZE))
+        delta_refs[at][...] = jnp.broadcast_to(delta, (rows, HEAD_SIZE))
         g = g.astype(jnp.bfloat16)
-        g_refs[slot][...] = g
-        dp_refs[slot][:, two] = dot(doubled(g), value2_t_ref[...])
-        dp_refs[slot][:, rest] = dot(g, value_t_ref[...])
+        g_refs[at][...] = g
+        dp_refs[at][:, two] = dot(doubled(g), value2_t_ref[kv])
+        dp_refs[at][:, rest] = dot(g, value_t_ref[kv])
 
     def score_grad(slot):
+        p_ref, at = p_refs[slot], slot % 2
         for r in range(0, rows, ROWS):
             here = slice(r, r + ROWS)
-            delta = jnp.concatenate([delta_refs[slot][here]] * (window // HEAD_SIZE), axis=1)
-            d_refs[slot][here] = p_refs[slot][here] * (dp_refs[slot][here] - delta).astype(jnp.bfloat16)
+            delta = jnp.concatenate([delta_refs[at][here]] * (window // HEAD_SIZE), axis=1)
+            d_refs[at][here] = p_ref[here] * (dp_refs[at][here] - delta).astype(jnp.bfloat16)
 
     def spread(head, slot):
-        cols = columns(head)
-        total = picked(dot(d_refs[slot][:, two], key2_ref[...])) + dot(d_refs[slot][:, rest], key_ref[...])
+        kv, cols = head // GROUP, columns(head)
+        p_ref, at = p_refs[slot], slot % 2
+        d_ref = d_refs[at]
+        total = picked(dot(d_ref[:, two], key2_ref[kv])) + dot(d_ref[:, rest], key_ref[kv])
         dq_ref[:, cols] = (total * SCALE).astype(jnp.bfloat16)
         q = q_ref[:, cols]
-        g = g_refs[slot][...]
-        dk2_ref[...] += dot(doubled(q).T, d_refs[slot][:, two])
-        dk_ref[...] += dot(q.T, d_refs[slot][:, rest])
-        dv2_ref[...] += dot(doubled(g).T, p_refs[slot][:, two])
-        dv_ref[...] += dot(g.T, p_refs[slot][:, rest])
+        g = g_refs[at][...]
+        dk2_ref[kv] += dot(doubled(q).T, d_ref[:, two])
+        dk_ref[kv] += dot(q.T, d_ref[:, rest])
+        dv2_ref[kv] += dot(doubled(g).T, p_ref[:, two])
+        dv_ref[kv] += dot(g.T, p_ref[:, rest])
 
     scores(0, 0)
 
     def step(index, carry):
-        for slot in range(2):
-            head = 2 * index + slot
-            before = jnp.maximum(head - 1, 0)
-            scores(jnp.minimum(head + 1, GROUP - 1), 1 - slot)
-            score_grad(1 - slot)
+        for slot in range(4):
+            head = 4 * index + slot
+            scores(jnp.minimum(head + 1, heads - 1), (slot + 1) % 4)
+            score_grad((slot + 2) % 4)
             softmax(slot)
-            spread(before, 1 - slot)
-            mix(head, slot)
+            spread(jnp.maximum(head - 2, 0), (slot + 2) % 4)
+            mix(jnp.maximum(head - 1, 0), (slot + 3) % 4)
         return carry
 
-    lax.fori_loop(0, GROUP // 2, step, 0)
-    score_grad(1)
-    spread(GROUP - 1, 1)
+    lax.fori_loop(0, heads // 4, step, 0)
+    score_grad(2)
+    mix(heads - 1, 3)
+    spread(heads - 2, 2)
+    score_grad(3)
+    spread(heads - 1, 3)
     from_far = from_far[:, :HEAD_SIZE]
-    for part, grad, grad2, scale in ((0, dk_ref, dk2_ref, SCALE), (1, dv_ref, dv2_ref, 1.0)):
-        span = slice(part * HEAD_SIZE, (part + 1) * HEAD_SIZE)
-        either = grad2[:HEAD_SIZE].T * scale
-        own = grad2[HEAD_SIZE:].T * scale
-        dfar_ref[:, span] = jnp.where(from_far, either, 0.0).astype(dfar_ref.dtype)
-        down_ref[:, span] = own + jnp.where(from_far, 0.0, either)
-        dmid_ref[:, span] = grad[:, :rows].T * scale
-        dnear_ref[:, span] = grad[:, rows:].T * scale
+    for kv in range(CHUNK):
+        for part, grad, grad2, scale in ((0, dk_ref, dk2_ref, SCALE), (1, dv_ref, dv2_ref, 1.0)):
+            start = (2 * kv + part) * HEAD_SIZE
+            span = slice(start, start + HEAD_SIZE)
+            either = grad2[kv, :HEAD_SIZE].T * scale
+            own = grad2[kv, HEAD_SIZE:].T * scale
+            dfar_ref[:, span] = jnp.where(from_far, either, 0.0).astype(dfar_ref.dtype)
+            down_ref[:, span] = own + jnp.where(from_far, 0.0, either)
+            dmid_ref[:, span] = grad[kv, :, :rows].T * scale
+            dnear_ref[:, span] = grad[kv, :, rows:].T * scale
 
 
 def attention(chunk, first, lengths, queries, out_grad, blocks, grads):
     rows = queries.shape[0]
-    wide = GROUP * HEAD_SIZE
+    wide = CHUNK * GROUP * HEAD_SIZE
     pair = 2 * HEAD_SIZE
     window = (SPAN - 1) * rows
-    query_spec = pl.BlockSpec((rows, wide), lambda i, *_: (0, chunk * CHUNK + i))
-    block_spec = pl.BlockSpec((rows, pair), lambda i, *_: (0, i))
+    query_spec = pl.BlockSpec((rows, wide), lambda i, *_: (0, chunk))
+    block_spec = pl.BlockSpec((rows, CHUNK * pair), lambda i, *_: (0, 0))
     operands = [first, lengths, queries, out_grad, *blocks]
     in_specs = [query_spec] * 2 + [block_spec] * 4
     aliases = {}
@@ -207,7 +220,7 @@
         + [jax.ShapeDtypeStruct((rows, CHUNK * pair), kind) for kind in (bf16, f32, f32, f32)],
         grid_spec=pltpu.PrefetchScalarGridSpec(
             num_scalar_prefetch=2,
-            grid=(CHUNK,),
+            grid=(1,),
             in_specs=in_specs,
             out_specs=[query_spec] * 2 + [block_spec] * 4,
             scratch_shapes=[
@@ -216,18 +229,18 @@
                     ((rows, window), f32, 1),
                     ((rows, HEAD_SIZE), f32, 1),
                     ((8, HEAD_SIZE), jnp.int32, 1),
-                    ((2 * rows, HEAD_SIZE), bf16, 2),
-                    ((HEAD_SIZE, 2 * rows), bf16, 2),
-                    ((rows, pair), bf16, 2),
-                    ((pair, rows), bf16, 2),
-                    ((HEAD_SIZE, 2 * rows), f32, 2),
-                    ((pair, rows), f32, 2),
-                    ((rows, HEAD_SIZE), f32, 1),
+                    ((CHUNK, 2 * rows, HEAD_SIZE), bf16, 2),
+                    ((CHUNK, HEAD_SIZE, 2 * rows), bf16, 2),
+                    ((CHUNK, rows, pair), bf16, 2),
+                    ((CHUNK, pair, rows), bf16, 2),
+                    ((CHUNK, HEAD_SIZE, 2 * rows), f32, 2),
+                    ((CHUNK, pair, rows), f32, 2),
+                    ((rows, window), bf16, 4),
                     ((rows, window), f32, 2),
-                    ((rows, window), bf16, 2),
                     ((rows, window), f32, 2),
                     ((rows, window), bf16, 2),
                     ((rows, HEAD_SIZE), bf16, 2),
+                    ((rows, HEAD_SIZE), f32, 2),
                     ((rows, HEAD_SIZE), f32, 2),
                 )
                 for _ in range(count)
@@ -237,7 +250,7 @@
         compiler_params=pltpu.CompilerParams(vmem_limit_bytes=48 * 1024 * 1024),
         cost_estimate=pl.CostEstimate(
             flops=12 * CHUNK * rows * GROUP * window * HEAD_SIZE * 2,
-            bytes_accessed=CHUNK * (4 * rows * wide * 2 + 22 * rows * pair),
+            bytes_accessed=4 * rows * wide * 2 + CHUNK * 22 * rows * pair,
             transcendentals=0,
         ),
         name="attention",

time: 103 us -> 106 us (1.029)
  Pallas kernels: 36.4 us -> 39 us
    pallas_call x2, Pallas kernels: 36.4 us -> 39 us  [attention(): pl.pallas_call(attention_kernel, out_shape=[jax.ShapeDtypeStruct(queries....]
  transfers between devices with their start and end apart: 12 -> 12, of which waited for: 8 -> 8; matrix products, arithmetic and copies ran while one was open for 2% -> 2% of each run, Pallas kernels for 35% -> 37%
where the time goes in v7:
time: 106 us
  Pallas kernels  39 us (37%)
  waiting for transfers between devices  31.8 us (30%)
  starting transfers between devices  28.9 us (27%)
  other arithmetic  3.83 us (4%)
  local copies, waits for them, and re-layouts  1.38 us (1%)
    pallas_call x2, Pallas kernels, attention(): pl.pallas_call(attention_kernel, out_shape=[jax.ShapeDtypeStruct(queries....  39 us
    ppermute x8, waiting for transfers between devices, passed_along(): lax.ppermute(value, AXES, [(source, source + steps) for source in range(f...  27.8 us
    ppermute x8, starting transfers between devices, passed_along(): lax.ppermute(value, AXES, [(source, source + steps) for source in range(f...  27.8 us
    ppermute x4, waiting for transfers between devices, swapped(): lax.ppermute(value, AXES, [(source, source ^ 1) for source in range(devic...  3.99 us
  transfers between devices with their start and end apart: 12, of which 8 were waited for; matrix products, arithmetic and copies ran while one was open for 2% of the time, Pallas kernels for 37%

profile of v7, /device:TPU:29, one launch (start us, length us, event | category | flops | bytes accessed | tf_op | source)
XLA Modules:
  0.0 105.7 jit_solution(3209493670989620129)
XLA Ops:
  0.7 1.3 %fusion.12 = (bf16[256,128]{1,0:T(8,128)(2,1)S(1)}, bf16[256,128]{1,0:T(8,128)(2,1)S(1)}, bf16[256,128]{1,0:T(8,128)(2,1)S(1)}, bf16[256,128]{1,0:T(8,128)(2,1)S...) fusion(bf16[256,512]{1,0:T(8,128)(2,1)} %param.6, ...), kind=kLoop, calls=%fused_computation.24 | loop fusion | bytes 1048576 | tf_op jit(solution)/shard_map/slice | solution.py:273
  2.0 3.3 %collective-permute-start.3 = (bf16[256,512]{1,0:T(8,128)(2,1)S(1)}, bf16[256,512]{1,0:T(8,128)(2,1)S(1)}, u32[]{:S(2)}, u32[]{:S(2)}) collective-permute-start(bf16[256,512]{1,0:T(8,128)(2,1)S(1)} %pad_maximum_fusion.1.own_ref), channel_id=1, source_target_pairs={{0,2},{1,3},{2,4},{3,5},{4,6},{5,7},{6,8},{7,9},{8,10},{9,11},{10,... | collective-permute-start | bytes 786440 | tf_op jit(solution)/shard_map/ppermute | solution.py:36
  5.4 3.5 %collective-permute-start = (bf16[256,512]{1,0:T(8,128)(2,1)S(1)}, bf16[256,512]{1,0:T(8,128)(2,1)S(1)}, u32[]{:S(2)}, u32[]{:S(2)}) collective-permute-start(bf16[256,512]{1,0:T(8,128)(2,1)S(1)} %pad_maximum_fusion.own_ref), channel_id=1, source_target_pairs={{0,2},{1,3},{2,4},{3,5},{4,6},{5,7},{6,8},{7,9},{8,10},{9,11},{10,... | collective-permute-start | bytes 786440 | tf_op jit(solution)/shard_map/ppermute | solution.py:36
  8.9 2.5 %collective-permute-done.3.mid_ref = bf16[256,512]{1,0:T(8,128)(2,1)S(1)} collective-permute-done((bf16[256,512]{1,0:T(8,128)(2,1)S(1)}, bf16[256,512]{1,0:T(8,128)(2,1)S(1)}, u32[]{:S(2)}, u32[]{:S(2)}) %collective-permute-start.3) | collective-permute-done | bytes 262176 | tf_op jit(solution)/shard_map/ppermute | solution.py:36
  11.4 1.0 broadcast_select_fusion
  12.3 0.3 collective-permute-start.4
  12.6 4.1 %collective-permute-done.mid_ref = bf16[256,512]{1,0:T(8,128)(2,1)S(1)} collective-permute-done((bf16[256,512]{1,0:T(8,128)(2,1)S(1)}, bf16[256,512]{1,0:T(8,128)(2,1)S(1)}, u32[]{:S(2)}, u32[]{:S(2)}) %collective-permute-start) | collective-permute-done | bytes 262176 | tf_op jit(solution)/shard_map/ppermute | solution.py:36
  16.7 0.8 broadcast_select_fusion.1
  17.4 0.2 collective-permute-start.1
  17.7 0.2 collective-permute-done.4.near_ref
  17.8 10.4 %collective-permute-start.5 = (bf16[256,512]{1,0:T(8,128)(2,1)}, bf16[256,512]{1,0:T(8,128)(2,1)}, u32[]{:S(2)}, u32[]{:S(2)}) collective-permute-start(bf16[256,512]{1,0:T(8,128)(2,1)} %collective-permute-done.4.near_ref), channel_id=1, source_target_pairs={{0,2},{1,3},{2,4},{3,5},{4,6},{5,7},{6,8},{7,9},{8,10},{9,11},{10,... | collective-permute-start | bytes 786440 | tf_op jit(solution)/shard_map/ppermute | solution.py:36
  28.2 2.7 %collective-permute-start.2 = (bf16[256,512]{1,0:T(8,128)(2,1)S(1)}, bf16[256,512]{1,0:T(8,128)(2,1)S(1)}, u32[]{:S(2)}, u32[]{:S(2)}) collective-permute-start(bf16[256,512]{1,0:T(8,128)(2,1)S(1)} %collective-permute-done.1.near_ref), channel_id=1, source_target_pairs={{0,2},{1,3},{2,4},{3,5},{4,6},{5,7},{6,8},{7,9},{8,10},{9,11},{10,... | collective-permute-start | bytes 786440 | tf_op jit(solution)/shard_map/ppermute | solution.py:36
  30.9 2.6 %collective-permute-done.5.far_ref = bf16[256,512]{1,0:T(8,128)(2,1)} collective-permute-done((bf16[256,512]{1,0:T(8,128)(2,1)}, bf16[256,512]{1,0:T(8,128)(2,1)}, u32[]{:S(2)}, u32[]{:S(2)}) %collective-permute-start.5) | collective-permute-done | bytes 262176 | tf_op jit(solution)/shard_map/ppermute | solution.py:36
  33.5 19.4 %attention.2 = (bf16[256,4096]{1,0:T(8,128)(2,1)}, bf16[256,4096]{1,0:T(8,128)(2,1)}, bf16[256,512]{1,0:T(8,128)(2,1)S(1)}, f32[256,512]{1,0:T(8,128)S(1)}, f32[...) custom-call(s32[1]{0:T(128)} %bitcast.first_ref, s32[16]{0:T(128)S(1)} %copy-done.1, bf16[256,4096]{1,0:T(8,128)(2,1)S(1)} %copy-done, ...), custom_call_target="tpu_custom_call" | custom-call | flops 9663676416 | bytes 7077888 | tf_op jit(solution)/shard_map/attention/pallas_call | solution.py:217
  52.9 2.1 %collective-permute-start.6 = (bf16[256,512]{1,0:T(8,128)(2,1)S(1)}, bf16[256,512]{1,0:T(8,128)(2,1)S(1)}, u32[]{:S(2)}, u32[]{:S(2)}) collective-permute-start(bf16[256,512]{1,0:T(8,128)(2,1)S(1)} %get-tuple-element.22), channel_id=1, source_target_pairs={{2,0},{3,1},{4,2},{5,3},{6,4},{7,5},{8,6},{9,7},{10,8},{11,9},{12,... | collective-permute-start | bytes 786440 | tf_op jit(solution)/shard_map/ppermute | solution.py:36
  55.0 19.6 %attention.3 = (bf16[256,4096]{1,0:T(8,128)(2,1)}, bf16[256,4096]{1,0:T(8,128)(2,1)}, bf16[256,512]{1,0:T(8,128)(2,1)S(1)}, f32[256,512]{1,0:T(8,128)S(1)}, f32[...) custom-call(s32[1]{0:T(128)} %bitcast.first_ref, s32[16]{0:T(128)S(1)} %copy-done.1, ...), custom_call_target="tpu_custom_call", output_to_operand_aliasing={{0}: (8, {}), {1}: (9, {})} | custom-call | flops 9663676416 | bytes 7077888 | tf_op jit(solution)/shard_map/attention/pallas_call | solution.py:217
  74.6 1.9 %collective-permute-start.9 = (bf16[256,512]{1,0:T(8,128)(2,1)S(1)}, bf16[256,512]{1,0:T(8,128)(2,1)S(1)}, u32[]{:S(2)}, u32[]{:S(2)}) collective-permute-start(bf16[256,512]{1,0:T(8,128)(2,1)S(1)} %get-tuple-element.26), channel_id=1, source_target_pairs={{2,0},{3,1},{4,2},{5,3},{6,4},{7,5},{8,6},{9,7},{10,8},{11,9},{12,... | collective-permute-start | bytes 786440 | tf_op jit(solution)/shard_map/ppermute | solution.py:36
  76.6 0.3 collective-permute-start.7
  76.9 8.8 %collective-permute-done.9 = bf16[256,512]{1,0:T(8,128)(2,1)S(1)} collective-permute-done((bf16[256,512]{1,0:T(8,128)(2,1)S(1)}, bf16[256,512]{1,0:T(8,128)(2,1)S(1)}, u32[]{:S(2)}, u32[]{:S(2)}) %collective-permute-start.9) | collective-permute-done | bytes 262176 | tf_op jit(solution)/shard_map/ppermute | solution.py:36
  85.7 0.1 add_convert_fusion
  85.8 0.3 collective-permute-start.10
  86.1 0.1 fusion.4
  86.2 1.9 %collective-permute-start.8 = (bf16[256,512]{1,0:T(8,128)(2,1)S(1)}, bf16[256,512]{1,0:T(8,128)(2,1)S(1)}, u32[]{:S(2)}, u32[]{:S(2)}) collective-permute-start(bf16[256,512]{1,0:T(8,128)(2,1)S(1)} %fusion.4), channel_id=1, source_target_pairs={{2,0},{3,1},{4,2},{5,3},{6,4},{7,5},{8,6},{9,7},{10,8},{11,9},{12,... | collective-permute-start | bytes 786440 | tf_op jit(solution)/shard_map/ppermute | solution.py:36
  88.1 3.8 %collective-permute-done.10 = bf16[256,512]{1,0:T(8,128)(2,1)S(1)} collective-permute-done((bf16[256,512]{1,0:T(8,128)(2,1)S(1)}, bf16[256,512]{1,0:T(8,128)(2,1)S(1)}, u32[]{:S(2)}, u32[]{:S(2)}) %collective-permute-start.10) | collective-permute-done | bytes 262176 | tf_op jit(solution)/shard_map/ppermute | solution.py:40
  91.9 0.1 fusion.9
  92.0 1.9 %collective-permute-start.11 = (bf16[256,512]{1,0:T(8,128)(2,1)S(1)}, bf16[256,512]{1,0:T(8,128)(2,1)S(1)}, u32[]{:S(2)}, u32[]{:S(2)}) collective-permute-start(bf16[256,512]{1,0:T(8,128)(2,1)S(1)} %fusion.9), channel_id=1, source_target_pairs={{2,0},{3,1},{4,2},{5,3},{6,4},{7,5},{8,6},{9,7},{10,8},{11,9},{12,... | collective-permute-start | bytes 786440 | tf_op jit(solution)/shard_map/ppermute | solution.py:36
  94.0 4.9 %collective-permute-done.8 = bf16[256,512]{1,0:T(8,128)(2,1)S(1)} collective-permute-done((bf16[256,512]{1,0:T(8,128)(2,1)S(1)}, bf16[256,512]{1,0:T(8,128)(2,1)S(1)}, u32[]{:S(2)}, u32[]{:S(2)}) %collective-permute-start.8) | collective-permute-done | bytes 262176 | tf_op jit(solution)/shard_map/ppermute | solution.py:36
  98.9 0.1 fusion.2
  99.1 4.9 %collective-permute-done.11 = bf16[256,512]{1,0:T(8,128)(2,1)S(1)} collective-permute-done((bf16[256,512]{1,0:T(8,128)(2,1)S(1)}, bf16[256,512]{1,0:T(8,128)(2,1)S(1)}, u32[]{:S(2)}, u32[]{:S(2)}) %collective-permute-start.11) | collective-permute-done | bytes 262176 | tf_op jit(solution)/shard_map/ppermute | solution.py:36
  104.0 0.1 fusion.7
  104.2 0.7 pad_maximum_fusion.3
  104.9 0.7 pad_maximum_fusion.2
  (17 shorter events, 0.3 us)
Async XLA Ops:
  0.6 32.9 %copy-start.1 = (s32[16]{0:T(128)S(1)}, s32[16]{0:T(128)}, u32[]{:S(2)}) copy-start(s32[16]{0:T(128)} %lengths_ref.3) | copy-start | bytes 196
  0.6 32.9 %copy-start = (bf16[256,4096]{1,0:T(8,128)(2,1)S(1)}, bf16[256,4096]{1,0:T(8,128)(2,1)}, u32[]{:S(2)}) copy-start(bf16[256,4096]{1,0:T(8,128)(2,1)} %q_ref.3) | copy-start | bytes 6291460
  1.9 3.4 %copy-start.2 = (bf16[256,128]{1,0:T(8,128)(2,1)}, bf16[256,128]{1,0:T(8,128)(2,1)S(1)}, u32[]{:S(2)}) copy-start(bf16[256,128]{1,0:T(8,128)(2,1)S(1)} %get-tuple-element.44) | copy-start | bytes 196612
  1.9 3.4 %copy-start.3 = (bf16[256,128]{1,0:T(8,128)(2,1)}, bf16[256,128]{1,0:T(8,128)(2,1)S(1)}, u32[]{:S(2)}) copy-start(bf16[256,128]{1,0:T(8,128)(2,1)S(1)} %get-tuple-element.47) | copy-start | bytes 196612
  2.0 9.4 %collective-permute-start.3 = (bf16[256,512]{1,0:T(8,128)(2,1)S(1)}, bf16[256,512]{1,0:T(8,128)(2,1)S(1)}, u32[]{:S(2)}, u32[]{:S(2)}) collective-permute-start(bf16[256,512]{1,0:T(8,128)(2,1)S(1)} %pad_maximum_fusion.1.own_ref), channel_id=1, source_target_pairs={{0,2},{1,3},{2,4},{3,5},{4,6},{5,7},{6,8},{7,9},{8,10},{9,11},{10,... | collective-permute-start | bytes 786440 | tf_op jit(solution)/shard_map/ppermute | solution.py:36
  5.4 11.3 %collective-permute-start = (bf16[256,512]{1,0:T(8,128)(2,1)S(1)}, bf16[256,512]{1,0:T(8,128)(2,1)S(1)}, u32[]{:S(2)}, u32[]{:S(2)}) collective-permute-start(bf16[256,512]{1,0:T(8,128)(2,1)S(1)} %pad_maximum_fusion.own_ref), channel_id=1, source_target_pairs={{0,2},{1,3},{2,4},{3,5},{4,6},{5,7},{6,8},{7,9},{8,10},{9,11},{10,... | collective-permute-start | bytes 786440 | tf_op jit(solution)/shard_map/ppermute | solution.py:36
  12.3 5.5 %collective-permute-start.4 = (bf16[256,512]{1,0:T(8,128)(2,1)S(1)}, bf16[256,512]{1,0:T(8,128)(2,1)}, u32[]{:S(2)}, u32[]{:S(2)}) collective-permute-start(bf16[256,512]{1,0:T(8,128)(2,1)S(1)} %broadcast_select_fusion), channel_id=1, source_target_pairs={{0,1},{1,0},{2,3},{3,2},{4,5},{5,4},{6,7},{7,6},{8,9},{9,8},{10,11... | collective-permute-start | bytes 786440 | tf_op jit(solution)/shard_map/ppermute | solution.py:40
  17.4 10.8 %collective-permute-start.1 = (bf16[256,512]{1,0:T(8,128)(2,1)}, bf16[256,512]{1,0:T(8,128)(2,1)S(1)}, u32[]{:S(2)}, u32[]{:S(2)}) collective-permute-start(bf16[256,512]{1,0:T(8,128)(2,1)} %broadcast_select_fusion.1), channel_id=1, source_target_pairs={{0,1},{1,0},{2,3},{3,2},{4,5},{5,4},{6,7},{7,6},{8,9},{9,8},{10,11... | collective-permute-start | bytes 786440 | tf_op jit(solution)/shard_map/ppermute | solution.py:40
  17.8 15.7 %collective-permute-start.5 = (bf16[256,512]{1,0:T(8,128)(2,1)}, bf16[256,512]{1,0:T(8,128)(2,1)}, u32[]{:S(2)}, u32[]{:S(2)}) collective-permute-start(bf16[256,512]{1,0:T(8,128)(2,1)} %collective-permute-done.4.near_ref), channel_id=1, source_target_pairs={{0,2},{1,3},{2,4},{3,5},{4,6},{5,7},{6,8},{7,9},{8,10},{9,11},{10,... | collective-permute-start | bytes 786440 | tf_op jit(solution)/shard_map/ppermute | solution.py:36
  28.2 26.8 %collective-permute-start.2 = (bf16[256,512]{1,0:T(8,128)(2,1)S(1)}, bf16[256,512]{1,0:T(8,128)(2,1)S(1)}, u32[]{:S(2)}, u32[]{:S(2)}) collective-permute-start(bf16[256,512]{1,0:T(8,128)(2,1)S(1)} %collective-permute-done.1.near_ref), channel_id=1, source_target_pairs={{0,2},{1,3},{2,4},{3,5},{4,6},{5,7},{6,8},{7,9},{8,10},{9,11},{10,... | collective-permute-start | bytes 786440 | tf_op jit(solution)/shard_map/ppermute | solution.py:36
  52.9 23.6 %collective-permute-start.6 = (bf16[256,512]{1,0:T(8,128)(2,1)S(1)}, bf16[256,512]{1,0:T(8,128)(2,1)S(1)}, u32[]{:S(2)}, u32[]{:S(2)}) collective-permute-start(bf16[256,512]{1,0:T(8,128)(2,1)S(1)} %get-tuple-element.22), channel_id=1, source_target_pairs={{2,0},{3,1},{4,2},{5,3},{6,4},{7,5},{8,6},{9,7},{10,8},{11,9},{12,... | collective-permute-start | bytes 786440 | tf_op jit(solution)/shard_map/ppermute | solution.py:36
  74.6 11.1 %collective-permute-start.9 = (bf16[256,512]{1,0:T(8,128)(2,1)S(1)}, bf16[256,512]{1,0:T(8,128)(2,1)S(1)}, u32[]{:S(2)}, u32[]{:S(2)}) collective-permute-start(bf16[256,512]{1,0:T(8,128)(2,1)S(1)} %get-tuple-element.26), channel_id=1, source_target_pairs={{2,0},{3,1},{4,2},{5,3},{6,4},{7,5},{8,6},{9,7},{10,8},{11,9},{12,... | collective-permute-start | bytes 786440 | tf_op jit(solution)/shard_map/ppermute | solution.py:36
  76.6 9.5 %collective-permute-start.7 = (bf16[256,512]{1,0:T(8,128)(2,1)S(1)}, bf16[256,512]{1,0:T(8,128)(2,1)S(1)}, u32[]{:S(2)}, u32[]{:S(2)}) collective-permute-start(bf16[256,512]{1,0:T(8,128)(2,1)S(1)} %add_convert_fusion.1), channel_id=1, source_target_pairs={{0,1},{1,0},{2,3},{3,2},{4,5},{5,4},{6,7},{7,6},{8,9},{9,8},{10,11... | collective-permute-start | bytes 786440 | tf_op jit(solution)/shard_map/ppermute | solution.py:40
  85.8 6.1 %collective-permute-start.10 = (bf16[256,512]{1,0:T(8,128)(2,1)S(1)}, bf16[256,512]{1,0:T(8,128)(2,1)S(1)}, u32[]{:S(2)}, u32[]{:S(2)}) collective-permute-start(bf16[256,512]{1,0:T(8,128)(2,1)S(1)} %add_convert_fusion), channel_id=1, source_target_pairs={{0,1},{1,0},{2,3},{3,2},{4,5},{5,4},{6,7},{7,6},{8,9},{9,8},{10,11... | collective-permute-start | bytes 786440 | tf_op jit(solution)/shard_map/ppermute | solution.py:40
  86.2 12.7 %collective-permute-start.8 = (bf16[256,512]{1,0:T(8,128)(2,1)S(1)}, bf16[256,512]{1,0:T(8,128)(2,1)S(1)}, u32[]{:S(2)}, u32[]{:S(2)}) collective-permute-start(bf16[256,512]{1,0:T(8,128)(2,1)S(1)} %fusion.4), channel_id=1, source_target_pairs={{2,0},{3,1},{4,2},{5,3},{6,4},{7,5},{8,6},{9,7},{10,8},{11,9},{12,... | collective-permute-start | bytes 786440 | tf_op jit(solution)/shard_map/ppermute | solution.py:36
  92.0 12.0 %collective-permute-start.11 = (bf16[256,512]{1,0:T(8,128)(2,1)S(1)}, bf16[256,512]{1,0:T(8,128)(2,1)S(1)}, u32[]{:S(2)}, u32[]{:S(2)}) collective-permute-start(bf16[256,512]{1,0:T(8,128)(2,1)S(1)} %fusion.9), channel_id=1, source_target_pairs={{2,0},{3,1},{4,2},{5,3},{6,4},{7,5},{8,6},{9,7},{10,8},{11,9},{12,... | collective-permute-start | bytes 786440 | tf_op jit(solution)/shard_map/ppermute | solution.py:36

commit v8 on v7

--- a/solution.py
+++ b/solution.py
@@ -15,6 +15,7 @@
 AXES = ("blk", "inner")
 CHUNK = 2
 ROWS = 32
+UNIT = 2
 MASKED = -1e30
 SCALE = 1.0 / math.sqrt(HEAD_SIZE)
 EXP2_SCALE = SCALE * math.log2(math.e)
@@ -74,14 +75,13 @@
         bias_ref, old_ref, cut_ref,
         key_ref, value_ref, key_t_ref, value_t_ref, key2_ref, value2_ref, key2_t_ref, value2_t_ref,
         dk_ref, dv_ref, dk2_ref, dv2_ref, *slots,
-    ) = refs[-37:]
-    p_refs, (s_refs, dp_refs, d_refs, g_refs, delta_refs, inv_refs) = (
-        slots[:4],
-        (slots[i : i + 2] for i in range(4, 16, 2)),
-    )
+    ) = refs[-34:]
+    s_refs, p_refs, dp_refs, d_refs, g_refs, delta_refs = (slots[i : i + 2] for i in range(0, 12, 2))
+    (inv_ref,) = slots[12:]
     rows = q_ref.shape[0]
     window = (SPAN - 1) * rows
-    heads = CHUNK * GROUP
+    units = CHUNK * GROUP // UNIT
+    stack = UNIT * rows
     two = slice(0, rows)
     rest = slice(rows, window)
 
@@ -103,65 +103,75 @@
             value2_ref[kv, :, span] = block[:, HEAD_SIZE:]
             key2_t_ref[kv, span] = block[:, :HEAD_SIZE].T
             value2_t_ref[kv, span] = block[:, HEAD_SIZE:].T
-    for ref in (dk_ref, dv_ref, dk2_ref, dv2_ref, p_refs[2], p_refs[3], dp_refs[0], delta_refs[0], g_refs[0]):
+    for ref in (dk_ref, dv_ref, dk2_ref, dv2_ref, p_refs[1], dp_refs[1], delta_refs[1], g_refs[1]):
         ref[...] = jnp.zeros_like(ref)
-    inv_refs[1][...] = jnp.ones_like(inv_refs[1])
-
-    def columns(head):
-        return pl.ds(pl.multiple_of(head * HEAD_SIZE, HEAD_SIZE), HEAD_SIZE)
+
+    def places(unit):
+        return [
+            (
+                slice(i * rows, (i + 1) * rows),
+                pl.ds(pl.multiple_of((unit * UNIT + i) * HEAD_SIZE, HEAD_SIZE), HEAD_SIZE),
+            )
+            for i in range(UNIT)
+        ]
+
+    def stacked(ref, unit):
+        return jnp.concatenate([ref[:, cols] for _, cols in places(unit)], axis=0)
 
     def doubled(x):
-        old = old_ref[...].astype(jnp.bfloat16)
+        old = jnp.concatenate([old_ref[...].astype(jnp.bfloat16)] * UNIT, axis=0)
         return jnp.concatenate([x * old, x * (1 - old)], axis=1)
 
     def picked(x):
-        return jnp.where(old_ref[...] > 0.5, x[:, :HEAD_SIZE], x[:, HEAD_SIZE:])
-
-    def scores(head, slot):
-        kv = head // GROUP
-        q = q_ref[:, columns(head)]
-        s_refs[slot % 2][:, two] = dot(doubled(q), key2_t_ref[kv])
-        s_refs[slot % 2][:, rest] = dot(q, key_t_ref[kv])
+        old = jnp.concatenate([old_ref[...]] * UNIT, axis=0)
+        return jnp.where(old > 0.5, x[:, :HEAD_SIZE], x[:, HEAD_SIZE:])
+
+    def scores(unit, slot):
+        kv = unit * UNIT // GROUP
+        q = stacked(q_ref, unit)
+        s_refs[slot][:, two] = dot(doubled(q), key2_t_ref[kv])
+        s_refs[slot][:, rest] = dot(q, key_t_ref[kv])
 
     def softmax(slot):
-        for r in range(0, rows, ROWS):
+        for r in range(0, stack, ROWS):
             here = slice(r, r + ROWS)
-            s = s_refs[slot % 2][here] * EXP2_SCALE + bias_ref[here]
+            row = slice(r % rows, r % rows + ROWS)
+            s = s_refs[slot][here] * EXP2_SCALE + bias_ref[row]
             e = jnp.exp2(s - jnp.max(s, axis=1, keepdims=True))
             inv = 1.0 / jnp.sum(e, axis=1, keepdims=True)
-            inv_refs[slot % 2][here] = jnp.broadcast_to(inv, (ROWS, HEAD_SIZE))
+            inv_ref[here] = jnp.broadcast_to(inv, (ROWS, HEAD_SIZE))
             p_refs[slot][here] = e.astype(jnp.bfloat16)
 
-    def mix(head, slot):
-        kv, cols = head // GROUP, columns(head)
-        p_ref, at = p_refs[slot], slot % 2
+    def mix(unit, slot):
+        kv = unit * UNIT // GROUP
+        p_ref, g_ref_here = p_refs[slot], g_refs[slot]
         total = picked(dot(p_ref[:, two], value2_ref[kv])) + dot(p_ref[:, rest], value_ref[kv])
-        inv = inv_refs[at][...]
-        out = (total * inv).astype(jnp.bfloat16)
-        out_ref[:, cols] = out
-        g = g_ref[:, cols].astype(jnp.float32) * inv
-        delta = jnp.sum(g * out.astype(jnp.float32), axis=1, keepdims=True)
-        delta_refs[at][...] = jnp.broadcast_to(delta, (rows, HEAD_SIZE))
-        g = g.astype(jnp.bfloat16)
-        g_refs[at][...] = g
-        dp_refs[at][:, two] = dot(doubled(g), value2_t_ref[kv])
-        dp_refs[at][:, rest] = dot(g, value_t_ref[kv])
+        for here, cols in places(unit):
+            inv = inv_ref[here]
+            out = (total[here] * inv).astype(jnp.bfloat16)
+            out_ref[:, cols] = out
+            g = g_ref[:, cols].astype(jnp.float32) * inv
+            delta = jnp.sum(g * out.astype(jnp.float32), axis=1, keepdims=True)
+            delta_refs[slot][here] = jnp.broadcast_to(delta, (rows, HEAD_SIZE))
+            g_ref_here[here] = g.astype(jnp.bfloat16)
+        g = g_ref_here[...]
+        dp_refs[slot][:, two] = dot(doubled(g), value2_t_ref[kv])
+        dp_refs[slot][:, rest] = dot(g, value_t_ref[kv])
 
     def score_grad(slot):
-        p_ref, at = p_refs[slot], slot % 2
-        for r in range(0, rows, ROWS):
+        for r in range(0, stack, ROWS):
             here = slice(r, r + ROWS)
-            delta = jnp.concatenate([delta_refs[at][here]] * (window // HEAD_SIZE), axis=1)
-            d_refs[at][here] = p_ref[here] * (dp_refs[at][here] - delta).astype(jnp.bfloat16)
-
-    def spread(head, slot):
-        kv, cols = head // GROUP, columns(head)
-        p_ref, at = p_refs[slot], slot % 2
-        d_ref = d_refs[at]
+            delta = jnp.concatenate([delta_refs[slot][here]] * (window // HEAD_SIZE), axis=1)
+            d_refs[slot][here] = p_refs[slot][here] * (dp_refs[slot][here] - delta).astype(jnp.bfloat16)
+
+    def spread(unit, slot):
+        kv = unit * UNIT // GROUP
+        p_ref, d_ref = p_refs[slot], d_refs[slot]
         total = picked(dot(d_ref[:, two], key2_ref[kv])) + dot(d_ref[:, rest], key_ref[kv])
-        dq_ref[:, cols] = (total * SCALE).astype(jnp.bfloat16)
-        q = q_ref[:, cols]
-        g = g_refs[at][...]
+        for here, cols in places(unit):
+            dq_ref[:, cols] = (total[here] * SCALE).astype(jnp.bfloat16)
+        q = stacked(q_ref, unit)
+        g = g_refs[slot][...]
         dk2_ref[kv] += dot(doubled(q).T, d_ref[:, two])
         dk_ref[kv] += dot(q.T, d_ref[:, rest])
         dv2_ref[kv] += dot(doubled(g).T, p_ref[:, two])
@@ -170,21 +180,18 @@
     scores(0, 0)
 
     def step(index, carry):
-        for slot in range(4):
-            head = 4 * index + slot
-            scores(jnp.minimum(head + 1, heads - 1), (slot + 1) % 4)
-            score_grad((slot + 2) % 4)
+        for slot in range(2):
+            unit = 2 * index + slot
+            scores(jnp.minimum(unit + 1, units - 1), 1 - slot)
+            score_grad(1 - slot)
             softmax(slot)
-            spread(jnp.maximum(head - 2, 0), (slot + 2) % 4)
-            mix(jnp.maximum(head - 1, 0), (slot + 3) % 4)
+            spread(jnp.maximum(unit - 1, 0), 1 - slot)
+            mix(unit, slot)
         return carry
 
-    lax.fori_loop(0, heads // 4, step, 0)
-    score_grad(2)
-    mix(heads - 1, 3)
-    spread(heads - 2, 2)
-    score_grad(3)
-    spread(heads - 1, 3)
+    lax.fori_loop(0, units // 2, step, 0)
+    score_grad(1)
+    spread(units - 1, 1)
     from_far = from_far[:, :HEAD_SIZE]
     for kv in range(CHUNK):
         for part, grad, grad2, scale in ((0, dk_ref, dk2_ref, SCALE), (1, dv_ref, dv2_ref, 1.0)):
@@ -235,19 +242,19 @@
                     ((CHUNK, pair, rows), bf16, 2),
                     ((CHUNK, HEAD_SIZE, 2 * rows), f32, 2),
                     ((CHUNK, pair, rows), f32, 2),
-                    ((rows, window), bf16, 4),
-                    ((rows, window), f32, 2),
-                    ((rows, window), f32, 2),
-                    ((rows, window), bf16, 2),
-                    ((rows, HEAD_SIZE), bf16, 2),
-                    ((rows, HEAD_SIZE), f32, 2),
-                    ((rows, HEAD_SIZE), f32, 2),
+                    ((UNIT * rows, window), f32, 2),
+                    ((UNIT * rows, window), bf16, 2),
+                    ((UNIT * rows, window), f32, 2),
+                    ((UNIT * rows, window), bf16, 2),
+                    ((UNIT * rows, HEAD_SIZE), bf16, 2),
+                    ((UNIT * rows, HEAD_SIZE), f32, 2),
+                    ((UNIT * rows, HEAD_SIZE), f32, 1),
                 )
                 for _ in range(count)
             ],
         ),
         input_output_aliases=aliases,
-        compiler_params=pltpu.CompilerParams(vmem_limit_bytes=48 * 1024 * 1024),
+        compiler_params=pltpu.CompilerParams(vmem_limit_bytes=32 * 1024 * 1024),
         cost_estimate=pl.CostEstimate(
             flops=12 * CHUNK * rows * GROUP * window * HEAD_SIZE * 2,
             bytes_accessed=4 * rows * wide * 2 + CHUNK * 22 * rows * pair,

time: 106 us -> 103 us (0.972)
  Pallas kernels: 39 us -> 34.3 us
  local copies, waits for them, and re-layouts: 1.38 us -> 2.97 us
    pallas_call x2, Pallas kernels: 39 us -> 34.3 us  [attention(): pl.pallas_call(attention_kernel, out_shape=[jax.ShapeDtypeStruct(queries....]
    unnamed x8 -> x10, local copies, waits for them, and re-layouts: 0.02 us -> 1.61 us
  transfers between devices with their start and end apart: 12 -> 12, of which waited for: 8 -> 8; matrix products, arithmetic and copies ran while one was open for 2% -> 2% of each run, Pallas kernels for 37% -> 34%
where the time goes in v8:
time: 103 us; the launch traced here: 102 us
  Pallas kernels  34.3 us (33%)
  waiting for transfers between devices  31.8 us (31%)
  starting transfers between devices  28.7 us (28%)
  other arithmetic  3.83 us (4%)
  local copies, waits for them, and re-layouts  2.97 us (3%)
    pallas_call x2, Pallas kernels, attention(): pl.pallas_call(attention_kernel, out_shape=[jax.ShapeDtypeStruct(queries....  34.3 us
    ppermute x8, waiting for transfers between devices, passed_along(): lax.ppermute(value, AXES, [(source, source + steps) for source in range(f...  27.8 us
    ppermute x8, starting transfers between devices, passed_along(): lax.ppermute(value, AXES, [(source, source + steps) for source in range(f...  27.6 us
    ppermute x4, waiting for transfers between devices, swapped(): lax.ppermute(value, AXES, [(source, source ^ 1) for source in range(devic...  4 us
  transfers between devices with their start and end apart: 12, of which 8 were waited for; matrix products, arithmetic and copies ran while one was open for 2% of the time, Pallas kernels for 34%

profile of v8, /device:TPU:29, one launch (start us, length us, event | category | flops | bytes accessed | tf_op | source)
XLA Modules:
  0.0 102.4 jit_solution(81056694721863820)
XLA Ops:
  0.7 1.3 %fusion.12 = (bf16[256,128]{1,0:T(8,128)(2,1)S(1)}, bf16[256,128]{1,0:T(8,128)(2,1)S(1)}, bf16[256,128]{1,0:T(8,128)(2,1)S(1)}, bf16[256,128]{1,0:T(8,128)(2,1)S...) fusion(bf16[256,512]{1,0:T(8,128)(2,1)} %param.6, ...), kind=kLoop, calls=%fused_computation.24 | loop fusion | bytes 1048576 | tf_op jit(solution)/shard_map/slice | solution.py:280
  2.0 3.3 %collective-permute-start.3 = (bf16[256,512]{1,0:T(8,128)(2,1)S(1)}, bf16[256,512]{1,0:T(8,128)(2,1)S(1)}, u32[]{:S(2)}, u32[]{:S(2)}) collective-permute-start(bf16[256,512]{1,0:T(8,128)(2,1)S(1)} %pad_maximum_fusion.1.own_ref), channel_id=1, source_target_pairs={{0,2},{1,3},{2,4},{3,5},{4,6},{5,7},{6,8},{7,9},{8,10},{9,11},{10,... | collective-permute-start | bytes 786440 | tf_op jit(solution)/shard_map/ppermute | solution.py:37
  5.4 3.5 %collective-permute-start = (bf16[256,512]{1,0:T(8,128)(2,1)S(1)}, bf16[256,512]{1,0:T(8,128)(2,1)S(1)}, u32[]{:S(2)}, u32[]{:S(2)}) collective-permute-start(bf16[256,512]{1,0:T(8,128)(2,1)S(1)} %pad_maximum_fusion.own_ref), channel_id=1, source_target_pairs={{0,2},{1,3},{2,4},{3,5},{4,6},{5,7},{6,8},{7,9},{8,10},{9,11},{10,... | collective-permute-start | bytes 786440 | tf_op jit(solution)/shard_map/ppermute | solution.py:37
  8.9 2.5 %collective-permute-done.3.mid_ref = bf16[256,512]{1,0:T(8,128)(2,1)S(1)} collective-permute-done((bf16[256,512]{1,0:T(8,128)(2,1)S(1)}, bf16[256,512]{1,0:T(8,128)(2,1)S(1)}, u32[]{:S(2)}, u32[]{:S(2)}) %collective-permute-start.3) | collective-permute-done | bytes 262176 | tf_op jit(solution)/shard_map/ppermute | solution.py:37
  11.4 1.0 broadcast_select_fusion
  12.3 0.3 collective-permute-start.4
  12.6 4.1 %collective-permute-done.mid_ref = bf16[256,512]{1,0:T(8,128)(2,1)S(1)} collective-permute-done((bf16[256,512]{1,0:T(8,128)(2,1)S(1)}, bf16[256,512]{1,0:T(8,128)(2,1)S(1)}, u32[]{:S(2)}, u32[]{:S(2)}) %collective-permute-start) | collective-permute-done | bytes 262176 | tf_op jit(solution)/shard_map/ppermute | solution.py:37
  16.7 0.8 broadcast_select_fusion.1
  17.4 0.2 collective-permute-start.1
  17.7 0.2 collective-permute-done.4.near_ref
  17.8 10.4 %collective-permute-start.5 = (bf16[256,512]{1,0:T(8,128)(2,1)}, bf16[256,512]{1,0:T(8,128)(2,1)}, u32[]{:S(2)}, u32[]{:S(2)}) collective-permute-start(bf16[256,512]{1,0:T(8,128)(2,1)} %collective-permute-done.4.near_ref), channel_id=1, source_target_pairs={{0,2},{1,3},{2,4},{3,5},{4,6},{5,7},{6,8},{7,9},{8,10},{9,11},{10,... | collective-permute-start | bytes 786440 | tf_op jit(solution)/shard_map/ppermute | solution.py:37
  28.2 2.7 %collective-permute-start.2 = (bf16[256,512]{1,0:T(8,128)(2,1)S(1)}, bf16[256,512]{1,0:T(8,128)(2,1)S(1)}, u32[]{:S(2)}, u32[]{:S(2)}) collective-permute-start(bf16[256,512]{1,0:T(8,128)(2,1)S(1)} %collective-permute-done.1.near_ref), channel_id=1, source_target_pairs={{0,2},{1,3},{2,4},{3,5},{4,6},{5,7},{6,8},{7,9},{8,10},{9,11},{10,... | collective-permute-start | bytes 786440 | tf_op jit(solution)/shard_map/ppermute | solution.py:37
  30.9 2.6 %collective-permute-done.5.far_ref = bf16[256,512]{1,0:T(8,128)(2,1)} collective-permute-done((bf16[256,512]{1,0:T(8,128)(2,1)}, bf16[256,512]{1,0:T(8,128)(2,1)}, u32[]{:S(2)}, u32[]{:S(2)}) %collective-permute-start.5) | collective-permute-done | bytes 262176 | tf_op jit(solution)/shard_map/ppermute | solution.py:37
  33.5 1.6 %copy-done.1 = bf16[256,4096]{1,0:T(8,128)(2,1)S(1)} copy-done((bf16[256,4096]{1,0:T(8,128)(2,1)S(1)}, bf16[256,4096]{1,0:T(8,128)(2,1)}, u32[]{:S(2)}) %copy-start.1) | copy-done | bytes 2097176
  35.1 17.7 %attention.2 = (bf16[256,4096]{1,0:T(8,128)(2,1)}, bf16[256,4096]{1,0:T(8,128)(2,1)}, bf16[256,512]{1,0:T(8,128)(2,1)S(1)}, f32[256,512]{1,0:T(8,128)S(1)}, f32[...) custom-call(s32[1]{0:T(128)} %bitcast.first_ref, s32[16]{0:T(128)S(1)} %copy-done.2, bf16[256,4096]{1,0:T(8,128)(2,1)S(1)} %copy-done, ...), custom_call_target="tpu_custom_call" | custom-call | flops 9663676416 | bytes 7077888 | tf_op jit(solution)/shard_map/attention/pallas_call | solution.py:224
  52.8 1.9 %collective-permute-start.6 = (bf16[256,512]{1,0:T(8,128)(2,1)S(1)}, bf16[256,512]{1,0:T(8,128)(2,1)S(1)}, u32[]{:S(2)}, u32[]{:S(2)}) collective-permute-start(bf16[256,512]{1,0:T(8,128)(2,1)S(1)} %get-tuple-element.22), channel_id=1, source_target_pairs={{2,0},{3,1},{4,2},{5,3},{6,4},{7,5},{8,6},{9,7},{10,8},{11,9},{12,... | collective-permute-start | bytes 786440 | tf_op jit(solution)/shard_map/ppermute | solution.py:37
  54.7 16.7 %attention.3 = (bf16[256,4096]{1,0:T(8,128)(2,1)}, bf16[256,4096]{1,0:T(8,128)(2,1)}, bf16[256,512]{1,0:T(8,128)(2,1)S(1)}, f32[256,512]{1,0:T(8,128)S(1)}, f32[...) custom-call(s32[1]{0:T(128)} %bitcast.first_ref, s32[16]{0:T(128)S(1)} %copy-done.2, ...), custom_call_target="tpu_custom_call", output_to_operand_aliasing={{0}: (8, {}), {1}: (9, {})} | custom-call | flops 9663676416 | bytes 7077888 | tf_op jit(solution)/shard_map/attention/pallas_call | solution.py:224
  71.4 1.9 %collective-permute-start.9 = (bf16[256,512]{1,0:T(8,128)(2,1)S(1)}, bf16[256,512]{1,0:T(8,128)(2,1)S(1)}, u32[]{:S(2)}, u32[]{:S(2)}) collective-permute-start(bf16[256,512]{1,0:T(8,128)(2,1)S(1)} %get-tuple-element.26), channel_id=1, source_target_pairs={{2,0},{3,1},{4,2},{5,3},{6,4},{7,5},{8,6},{9,7},{10,8},{11,9},{12,... | collective-permute-start | bytes 786440 | tf_op jit(solution)/shard_map/ppermute | solution.py:37
  73.4 0.3 collective-permute-start.7
  73.7 8.8 %collective-permute-done.9 = bf16[256,512]{1,0:T(8,128)(2,1)S(1)} collective-permute-done((bf16[256,512]{1,0:T(8,128)(2,1)S(1)}, bf16[256,512]{1,0:T(8,128)(2,1)S(1)}, u32[]{:S(2)}, u32[]{:S(2)}) %collective-permute-start.9) | collective-permute-done | bytes 262176 | tf_op jit(solution)/shard_map/ppermute | solution.py:37
  82.5 0.1 add_convert_fusion
  82.6 0.3 collective-permute-start.10
  83.0 1.9 %collective-permute-start.8 = (bf16[256,512]{1,0:T(8,128)(2,1)S(1)}, bf16[256,512]{1,0:T(8,128)(2,1)S(1)}, u32[]{:S(2)}, u32[]{:S(2)}) collective-permute-start(bf16[256,512]{1,0:T(8,128)(2,1)S(1)} %fusion.4), channel_id=1, source_target_pairs={{2,0},{3,1},{4,2},{5,3},{6,4},{7,5},{8,6},{9,7},{10,8},{11,9},{12,... | collective-permute-start | bytes 786440 | tf_op jit(solution)/shard_map/ppermute | solution.py:37
  84.9 3.8 %collective-permute-done.10 = bf16[256,512]{1,0:T(8,128)(2,1)S(1)} collective-permute-done((bf16[256,512]{1,0:T(8,128)(2,1)S(1)}, bf16[256,512]{1,0:T(8,128)(2,1)S(1)}, u32[]{:S(2)}, u32[]{:S(2)}) %collective-permute-start.10) | collective-permute-done | bytes 262176 | tf_op jit(solution)/shard_map/ppermute | solution.py:41
  88.7 0.1 fusion.9
  88.8 1.9 %collective-permute-start.11 = (bf16[256,512]{1,0:T(8,128)(2,1)S(1)}, bf16[256,512]{1,0:T(8,128)(2,1)S(1)}, u32[]{:S(2)}, u32[]{:S(2)}) collective-permute-start(bf16[256,512]{1,0:T(8,128)(2,1)S(1)} %fusion.9), channel_id=1, source_target_pairs={{2,0},{3,1},{4,2},{5,3},{6,4},{7,5},{8,6},{9,7},{10,8},{11,9},{12,... | collective-permute-start | bytes 786440 | tf_op jit(solution)/shard_map/ppermute | solution.py:37
  90.8 4.9 %collective-permute-done.8 = bf16[256,512]{1,0:T(8,128)(2,1)S(1)} collective-permute-done((bf16[256,512]{1,0:T(8,128)(2,1)S(1)}, bf16[256,512]{1,0:T(8,128)(2,1)S(1)}, u32[]{:S(2)}, u32[]{:S(2)}) %collective-permute-start.8) | collective-permute-done | bytes 262176 | tf_op jit(solution)/shard_map/ppermute | solution.py:37
  95.7 0.1 fusion.2
  95.9 4.9 %collective-permute-done.11 = bf16[256,512]{1,0:T(8,128)(2,1)S(1)} collective-permute-done((bf16[256,512]{1,0:T(8,128)(2,1)S(1)}, bf16[256,512]{1,0:T(8,128)(2,1)S(1)}, u32[]{:S(2)}, u32[]{:S(2)}) %collective-permute-start.11) | collective-permute-done | bytes 262176 | tf_op jit(solution)/shard_map/ppermute | solution.py:37
  100.8 0.1 fusion.7
  101.0 0.7 pad_maximum_fusion.3
  101.7 0.7 pad_maximum_fusion.2
  (19 shorter events, 0.3 us)
Async XLA Ops:
  0.6 32.9 %copy-start.2 = (s32[16]{0:T(128)S(1)}, s32[16]{0:T(128)}, u32[]{:S(2)}) copy-start(s32[16]{0:T(128)} %lengths_ref.3) | copy-start | bytes 196
  0.6 32.9 %copy-start = (bf16[256,4096]{1,0:T(8,128)(2,1)S(1)}, bf16[256,4096]{1,0:T(8,128)(2,1)}, u32[]{:S(2)}) copy-start(bf16[256,4096]{1,0:T(8,128)(2,1)} %q_ref.3) | copy-start | bytes 6291460
  1.9 3.4 %copy-start.3 = (bf16[256,128]{1,0:T(8,128)(2,1)}, bf16[256,128]{1,0:T(8,128)(2,1)S(1)}, u32[]{:S(2)}) copy-start(bf16[256,128]{1,0:T(8,128)(2,1)S(1)} %get-tuple-element.44) | copy-start | bytes 196612
  1.9 3.4 %copy-start.4 = (bf16[256,128]{1,0:T(8,128)(2,1)}, bf16[256,128]{1,0:T(8,128)(2,1)S(1)}, u32[]{:S(2)}) copy-start(bf16[256,128]{1,0:T(8,128)(2,1)S(1)} %get-tuple-element.47) | copy-start | bytes 196612
  2.0 9.4 %collective-permute-start.3 = (bf16[256,512]{1,0:T(8,128)(2,1)S(1)}, bf16[256,512]{1,0:T(8,128)(2,1)S(1)}, u32[]{:S(2)}, u32[]{:S(2)}) collective-permute-start(bf16[256,512]{1,0:T(8,128)(2,1)S(1)} %pad_maximum_fusion.1.own_ref), channel_id=1, source_target_pairs={{0,2},{1,3},{2,4},{3,5},{4,6},{5,7},{6,8},{7,9},{8,10},{9,11},{10,... | collective-permute-start | bytes 786440 | tf_op jit(solution)/shard_map/ppermute | solution.py:37
  5.4 11.3 %collective-permute-start = (bf16[256,512]{1,0:T(8,128)(2,1)S(1)}, bf16[256,512]{1,0:T(8,128)(2,1)S(1)}, u32[]{:S(2)}, u32[]{:S(2)}) collective-permute-start(bf16[256,512]{1,0:T(8,128)(2,1)S(1)} %pad_maximum_fusion.own_ref), channel_id=1, source_target_pairs={{0,2},{1,3},{2,4},{3,5},{4,6},{5,7},{6,8},{7,9},{8,10},{9,11},{10,... | collective-permute-start | bytes 786440 | tf_op jit(solution)/shard_map/ppermute | solution.py:37
  12.3 5.5 %collective-permute-start.4 = (bf16[256,512]{1,0:T(8,128)(2,1)S(1)}, bf16[256,512]{1,0:T(8,128)(2,1)}, u32[]{:S(2)}, u32[]{:S(2)}) collective-permute-start(bf16[256,512]{1,0:T(8,128)(2,1)S(1)} %broadcast_select_fusion), channel_id=1, source_target_pairs={{0,1},{1,0},{2,3},{3,2},{4,5},{5,4},{6,7},{7,6},{8,9},{9,8},{10,11... | collective-permute-start | bytes 786440 | tf_op jit(solution)/shard_map/ppermute | solution.py:41
  17.4 10.8 %collective-permute-start.1 = (bf16[256,512]{1,0:T(8,128)(2,1)}, bf16[256,512]{1,0:T(8,128)(2,1)S(1)}, u32[]{:S(2)}, u32[]{:S(2)}) collective-permute-start(bf16[256,512]{1,0:T(8,128)(2,1)} %broadcast_select_fusion.1), channel_id=1, source_target_pairs={{0,1},{1,0},{2,3},{3,2},{4,5},{5,4},{6,7},{7,6},{8,9},{9,8},{10,11... | collective-permute-start | bytes 786440 | tf_op jit(solution)/shard_map/ppermute | solution.py:41
  17.8 15.7 %collective-permute-start.5 = (bf16[256,512]{1,0:T(8,128)(2,1)}, bf16[256,512]{1,0:T(8,128)(2,1)}, u32[]{:S(2)}, u32[]{:S(2)}) collective-permute-start(bf16[256,512]{1,0:T(8,128)(2,1)} %collective-permute-done.4.near_ref), channel_id=1, source_target_pairs={{0,2},{1,3},{2,4},{3,5},{4,6},{5,7},{6,8},{7,9},{8,10},{9,11},{10,... | collective-permute-start | bytes 786440 | tf_op jit(solution)/shard_map/ppermute | solution.py:37
  28.2 26.5 %collective-permute-start.2 = (bf16[256,512]{1,0:T(8,128)(2,1)S(1)}, bf16[256,512]{1,0:T(8,128)(2,1)S(1)}, u32[]{:S(2)}, u32[]{:S(2)}) collective-permute-start(bf16[256,512]{1,0:T(8,128)(2,1)S(1)} %collective-permute-done.1.near_ref), channel_id=1, source_target_pairs={{0,2},{1,3},{2,4},{3,5},{4,6},{5,7},{6,8},{7,9},{8,10},{9,11},{10,... | collective-permute-start | bytes 786440 | tf_op jit(solution)/shard_map/ppermute | solution.py:37
  33.5 1.6 %copy-start.1 = (bf16[256,4096]{1,0:T(8,128)(2,1)S(1)}, bf16[256,4096]{1,0:T(8,128)(2,1)}, u32[]{:S(2)}) copy-start(bf16[256,4096]{1,0:T(8,128)(2,1)} %g_ref.3) | copy-start | bytes 6291460
  52.8 20.5 %collective-permute-start.6 = (bf16[256,512]{1,0:T(8,128)(2,1)S(1)}, bf16[256,512]{1,0:T(8,128)(2,1)S(1)}, u32[]{:S(2)}, u32[]{:S(2)}) collective-permute-start(bf16[256,512]{1,0:T(8,128)(2,1)S(1)} %get-tuple-element.22), channel_id=1, source_target_pairs={{2,0},{3,1},{4,2},{5,3},{6,4},{7,5},{8,6},{9,7},{10,8},{11,9},{12,... | collective-permute-start | bytes 786440 | tf_op jit(solution)/shard_map/ppermute | solution.py:37
  71.4 11.1 %collective-permute-start.9 = (bf16[256,512]{1,0:T(8,128)(2,1)S(1)}, bf16[256,512]{1,0:T(8,128)(2,1)S(1)}, u32[]{:S(2)}, u32[]{:S(2)}) collective-permute-start(bf16[256,512]{1,0:T(8,128)(2,1)S(1)} %get-tuple-element.26), channel_id=1, source_target_pairs={{2,0},{3,1},{4,2},{5,3},{6,4},{7,5},{8,6},{9,7},{10,8},{11,9},{12,... | collective-permute-start | bytes 786440 | tf_op jit(solution)/shard_map/ppermute | solution.py:37
  73.4 9.5 %collective-permute-start.7 = (bf16[256,512]{1,0:T(8,128)(2,1)S(1)}, bf16[256,512]{1,0:T(8,128)(2,1)S(1)}, u32[]{:S(2)}, u32[]{:S(2)}) collective-permute-start(bf16[256,512]{1,0:T(8,128)(2,1)S(1)} %add_convert_fusion.1), channel_id=1, source_target_pairs={{0,1},{1,0},{2,3},{3,2},{4,5},{5,4},{6,7},{7,6},{8,9},{9,8},{10,11... | collective-permute-start | bytes 786440 | tf_op jit(solution)/shard_map/ppermute | solution.py:41
  82.6 6.1 %collective-permute-start.10 = (bf16[256,512]{1,0:T(8,128)(2,1)S(1)}, bf16[256,512]{1,0:T(8,128)(2,1)S(1)}, u32[]{:S(2)}, u32[]{:S(2)}) collective-permute-start(bf16[256,512]{1,0:T(8,128)(2,1)S(1)} %add_convert_fusion), channel_id=1, source_target_pairs={{0,1},{1,0},{2,3},{3,2},{4,5},{5,4},{6,7},{7,6},{8,9},{9,8},{10,11... | collective-permute-start | bytes 786440 | tf_op jit(solution)/shard_map/ppermute | solution.py:41
  83.0 12.7 %collective-permute-start.8 = (bf16[256,512]{1,0:T(8,128)(2,1)S(1)}, bf16[256,512]{1,0:T(8,128)(2,1)S(1)}, u32[]{:S(2)}, u32[]{:S(2)}) collective-permute-start(bf16[256,512]{1,0:T(8,128)(2,1)S(1)} %fusion.4), channel_id=1, source_target_pairs={{2,0},{3,1},{4,2},{5,3},{6,4},{7,5},{8,6},{9,7},{10,8},{11,9},{12,... | collective-permute-start | bytes 786440 | tf_op jit(solution)/shard_map/ppermute | solution.py:37
  88.8 12.0 %collective-permute-start.11 = (bf16[256,512]{1,0:T(8,128)(2,1)S(1)}, bf16[256,512]{1,0:T(8,128)(2,1)S(1)}, u32[]{:S(2)}, u32[]{:S(2)}) collective-permute-start(bf16[256,512]{1,0:T(8,128)(2,1)S(1)} %fusion.9), channel_id=1, source_target_pairs={{2,0},{3,1},{4,2},{5,3},{6,4},{7,5},{8,6},{9,7},{10,8},{11,9},{12,... | collective-permute-start | bytes 786440 | tf_op jit(solution)/shard_map/ppermute | solution.py:37

commit v9 on v8

--- a/solution.py
+++ b/solution.py
@@ -13,9 +13,11 @@
 GROUP = QUERY_HEADS // KEY_VALUE_HEADS
 SPAN = 4
 AXES = ("blk", "inner")
-CHUNK = 2
+CHUNK = 1
 ROWS = 32
 UNIT = 2
+FORWARD = ((0,), (1,), (2, 3))
+BACKWARD = ((0, 1), (2,), (3,))
 MASKED = -1e30
 SCALE = 1.0 / math.sqrt(HEAD_SIZE)
 EXP2_SCALE = SCALE * math.log2(math.e)
@@ -35,10 +37,6 @@
     count = device_count()
     first, last = (max(0, -steps), min(count, count - steps))
     return lax.ppermute(value, AXES, [(source, source + steps) for source in range(first, last)])
-
-
-def swapped(value):
-    return lax.ppermute(value, AXES, [(source, source ^ 1) for source in range(device_count())])
 
 
 def write_masks(bias_ref, old_ref, cut_ref, lengths_ref, first_ref, rows):
@@ -69,13 +67,13 @@
         bias_ref[:, part * 128 : (part + 1) * 128] = jnp.where(allowed, 0.0, MASKED)
 
 
-def attention_kernel(first_ref, lengths_ref, q_ref, g_ref, far_ref, mid_ref, near_ref, own_ref, *refs):
+def attention_kernel(first_ref, lengths_ref, q_ref, g_ref, behind_ref, near_ref, own_ref, *refs):
     (
-        out_ref, dq_ref, dfar_ref, dmid_ref, dnear_ref, down_ref,
+        out_ref, dq_ref, dbehind_ref, dnear_ref, down_ref,
         bias_ref, old_ref, cut_ref,
         key_ref, value_ref, key_t_ref, value_t_ref, key2_ref, value2_ref, key2_t_ref, value2_t_ref,
         dk_ref, dv_ref, dk2_ref, dv2_ref, *slots,
-    ) = refs[-34:]
+    ) = refs[-33:]
     s_refs, p_refs, dp_refs, d_refs, g_refs, delta_refs = (slots[i : i + 2] for i in range(0, 12, 2))
     (inv_ref,) = slots[12:]
     rows = q_ref.shape[0]
@@ -88,8 +86,7 @@
     write_masks(bias_ref, old_ref, cut_ref, lengths_ref, first_ref, rows)
     from_far = lax.broadcasted_iota(jnp.int32, (rows, 2 * HEAD_SIZE), 0) >= cut_ref[0, 0]
     for kv in range(CHUNK):
-        pair = slice(kv * 2 * HEAD_SIZE, (kv + 1) * 2 * HEAD_SIZE)
-        far, mid, near, own = (ref[:, pair] for ref in (far_ref, mid_ref, near_ref, own_ref))
+        mid, far, near, own = behind_ref[0], behind_ref[1], near_ref[...], own_ref[...]
         for j, block in enumerate((mid, near)):
             span = slice(j * rows, (j + 1) * rows)
             key_ref[kv, span] = block[:, :HEAD_SIZE]
@@ -199,23 +196,27 @@
             span = slice(start, start + HEAD_SIZE)
             either = grad2[kv, :HEAD_SIZE].T * scale
             own = grad2[kv, HEAD_SIZE:].T * scale
-            dfar_ref[:, span] = jnp.where(from_far, either, 0.0).astype(dfar_ref.dtype)
+            dbehind_ref[1, :, span] = jnp.where(from_far, either, 0.0).astype(jnp.bfloat16)
             down_ref[:, span] = own + jnp.where(from_far, 0.0, either)
-            dmid_ref[:, span] = grad[kv, :, :rows].T * scale
+            dbehind_ref[0, :, span] = (grad[kv, :, :rows].T * scale).astype(jnp.bfloat16)
             dnear_ref[:, span] = grad[kv, :, rows:].T * scale
 
 
-def attention(chunk, first, lengths, queries, out_grad, blocks, grads):
+def attention(head, first, lengths, queries, out_grad, blocks, place, grads, parts, back, back_place):
     rows = queries.shape[0]
-    wide = CHUNK * GROUP * HEAD_SIZE
+    wide = GROUP * HEAD_SIZE
     pair = 2 * HEAD_SIZE
     window = (SPAN - 1) * rows
-    query_spec = pl.BlockSpec((rows, wide), lambda i, *_: (0, chunk))
-    block_spec = pl.BlockSpec((rows, CHUNK * pair), lambda i, *_: (0, 0))
+    query_spec = pl.BlockSpec((rows, wide), lambda i, *_: (0, head))
+
+    def pair_specs(at):
+        one = pl.BlockSpec((rows, pair), lambda i, *_: (0, at))
+        return [pl.BlockSpec((2, rows, pair), lambda i, *_: (0, 0, at)), one, one]
+
     operands = [first, lengths, queries, out_grad, *blocks]
-    in_specs = [query_spec] * 2 + [block_spec] * 4
+    in_specs = [query_spec] * 2 + pair_specs(place)
     aliases = {}
-    for at, array in enumerate(grads):
+    for at, array in enumerate((*grads, *parts)):
         if array is not None:
             aliases[len(operands)] = at
             operands.append(array)
@@ -223,13 +224,18 @@
     bf16, f32 = jnp.bfloat16, jnp.float32
     results = pl.pallas_call(
         attention_kernel,
-        out_shape=[jax.ShapeDtypeStruct(queries.shape, bf16)] * 2
-        + [jax.ShapeDtypeStruct((rows, CHUNK * pair), kind) for kind in (bf16, f32, f32, f32)],
+        out_shape=[
+            jax.ShapeDtypeStruct(queries.shape, bf16),
+            jax.ShapeDtypeStruct(queries.shape, bf16),
+            jax.ShapeDtypeStruct((2, rows, back * pair), bf16),
+            jax.ShapeDtypeStruct((rows, back * pair), f32),
+            jax.ShapeDtypeStruct((rows, back * pair), f32),
+        ],
         grid_spec=pltpu.PrefetchScalarGridSpec(
             num_scalar_prefetch=2,
             grid=(1,),
             in_specs=in_specs,
-            out_specs=[query_spec] * 2 + [block_spec] * 4,
+            out_specs=[query_spec] * 2 + pair_specs(back_place),
             scratch_shapes=[
                 pltpu.VMEM(shape, kind)
                 for shape, kind, count in (
@@ -268,42 +274,40 @@
 def local(queries, keys, values, out_grad, doc_lengths):
     rows = queries.shape[0]
     index = lax.axis_index(AXES)
-    odd = index % 2 == 1
     first = (index * rows).astype(jnp.int32).reshape(1)
     bf16, f32 = jnp.bfloat16, jnp.float32
-    chunks = range(KEY_VALUE_HEADS // CHUNK)
-    owns, mids, nears, fars = [], [], [], []
-    for chunk in chunks:
+    blocks = {}
+    owns, nears = [], []
+    for heads in FORWARD:
         parts = []
-        for head in range(chunk * CHUNK, (chunk + 1) * CHUNK):
+        for head in heads:
             span = slice(head * HEAD_SIZE, (head + 1) * HEAD_SIZE)
             parts += [keys[:, span], values[:, span]]
         owns.append(jnp.concatenate(parts, axis=1))
-        mids.append(passed_along(owns[chunk], 2))
-        nears.append(swapped(jnp.where(odd, mids[chunk], owns[chunk])))
-        fars.append(passed_along(nears[chunk], 2))
+    for own in owns:
+        nears.append(passed_along(own, 1))
+    for heads, own, near in zip(FORWARD, owns, nears):
+        behind = passed_along(jnp.stack([own, near]), 2)
+        for place, head in enumerate(heads):
+            blocks[head] = ((behind, near, own), place)
     grads = (None, None)
     totals = []
-    for chunk in chunks:
-        blocks = (fars[chunk], mids[chunk], nears[chunk], owns[chunk])
-        grads, parts = attention(chunk, first, doc_lengths, queries, out_grad, blocks, grads)
-        far, mid, near, own = parts
-        near = (near + passed_along(far, -2).astype(f32)).astype(bf16)
-        got = swapped(near).astype(f32)
-        mid = (mid + jnp.where(odd, got, 0.0)).astype(bf16)
-        own = own + jnp.where(odd, 0.0, got)
-        totals.append((own + passed_along(mid, -2).astype(f32)).astype(bf16))
-    key_parts, value_parts = [], []
-    for total in totals:
-        for head in range(CHUNK):
-            start = head * 2 * HEAD_SIZE
-            key_parts.append(total[:, start : start + HEAD_SIZE])
-            value_parts.append(total[:, start + HEAD_SIZE : start + 2 * HEAD_SIZE])
+    for heads in BACKWARD:
+        parts = (None,) * 3
+        for at, head in enumerate(heads):
+            grads, parts = attention(
+                head, first, doc_lengths, queries, out_grad, *blocks[head], grads, parts, len(heads), at
+            )
+        behind, near, own = parts
+        got = passed_along(behind, -2).astype(f32)
+        last = passed_along((near + got[1]).astype(bf16), -1).astype(f32)
+        total = (own + got[0] + last).astype(bf16)
+        totals += [total[:, i * HEAD_SIZE : (i + 1) * HEAD_SIZE] for i in range(2 * len(heads))]
     return (
         grads[0],
         grads[1],
-        jnp.concatenate(key_parts, axis=1),
-        jnp.concatenate(value_parts, axis=1),
+        jnp.concatenate(totals[0::2], axis=1),
+        jnp.concatenate(totals[1::2], axis=1),
     )
 
 

time: 103 us -> 101 us (0.981)
  waiting for transfers between devices: 31.8 us -> 12.6 us
  starting transfers between devices: 28.7 us -> 40.7 us
  Pallas kernels: 34.3 us -> 38.5 us
    ppermute x8 -> x12, waiting for transfers between devices: 27.8 us -> 12.6 us  [passed_along(): lax.ppermute(value, AXES, [(source, source + steps) for source in range(f...]
    ppermute x8 -> x12, starting transfers between devices: 27.6 us -> 40.7 us  [passed_along(): lax.ppermute(value, AXES, [(source, source + steps) for source in range(f...]
    pallas_call x2 -> x4, Pallas kernels: 34.3 us -> 38.5 us  [attention(): pl.pallas_call(attention_kernel, out_shape=[jax.ShapeDtypeStruct(queries....]
    ppermute x4 -> x0, waiting for transfers between devices: 4 us -> none  [swapped(): lax.ppermute(value, AXES, [(source, source ^ 1) for source in range(devic...]
    another operation x0 -> x6, other arithmetic: none -> 2.54 us  [local(): behind = passed_along(jnp.stack([own, near]), 2)]
    select_n x2 -> x0, other arithmetic: 1.72 us -> none  [local(): nears.append(swapped(jnp.where(odd, mids[chunk], owns[chunk])))]
    ppermute x4 -> x0, starting transfers between devices: 1.1 us -> none  [swapped(): lax.ppermute(value, AXES, [(source, source ^ 1) for source in range(devic...]
  transfers between devices with their start and end apart: 12 -> 12, of which waited for: 8 -> 4; matrix products, arithmetic and copies ran while one was open for 2% -> 3% of each run, Pallas kernels for 34% -> 38%
where the time goes in v9:
time: 101 us; the launch traced here: 100 us
  starting transfers between devices  40.7 us (40%)
  Pallas kernels  38.5 us (38%)
  waiting for transfers between devices  12.6 us (12%)
  other arithmetic  4.59 us (5%)
  local copies, waits for them, and re-layouts  2.79 us (3%)
    ppermute x12, starting transfers between devices, passed_along(): lax.ppermute(value, AXES, [(source, source + steps) for source in range(f...  40.7 us
    pallas_call x4, Pallas kernels, attention(): pl.pallas_call(attention_kernel, out_shape=[jax.ShapeDtypeStruct(queries....  38.5 us
    ppermute x12, waiting for transfers between devices, passed_along(): lax.ppermute(value, AXES, [(source, source + steps) for source in range(f...  12.6 us
    another operation x6, other arithmetic, local(): behind = passed_along(jnp.stack([own, near]), 2)  2.54 us
  transfers between devices with their start and end apart: 12, of which 4 were waited for; matrix products, arithmetic and copies ran while one was open for 3% of the time, Pallas kernels for 38%

profile of v9, /device:TPU:29, one launch (start us, length us, event | category | flops | bytes accessed | tf_op | source)
XLA Modules:
  0.0 100.1 jit_solution(12690504031702589260)
XLA Ops:
  0.6 1.1 %fusion.19 = (bf16[256,128]{1,0:T(8,128)(2,1)S(1)}, bf16[256,128]{1,0:T(8,128)(2,1)S(1)}, bf16[256,128]{1,0:T(8,128)(2,1)S(1)}, bf16[256,128]{1,0:T(8,128)(2,1)S...) fusion(bf16[256,512]{1,0:T(8,128)(2,1)} %param.6, ...), kind=kLoop, calls=%fused_computation.33 | loop fusion | bytes 1048576 | tf_op jit(solution)/shard_map/slice | solution.py:285
  1.8 0.0 copy-start
  1.8 0.0 copy-start.2
  1.8 3.4 %collective-permute-start.4 = (bf16[256,256]{1,0:T(8,128)(2,1)S(1)}, bf16[256,256]{1,0:T(8,128)(2,1)S(1)}, u32[]{:S(2)}, u32[]{:S(2)}) collective-permute-start(bf16[256,256]{1,0:T(8,128)(2,1)S(1)} %get-tuple-element.63.own_ref), channel_id=1, source_target_pairs={{0,1},{1,2},{2,3},{3,4},{4,5},{5,6},{6,7},{7,8},{8,9},{9,10},{10,1... | collective-permute-start | bytes 393224 | tf_op jit(solution)/shard_map/ppermute | solution.py:39
  5.2 0.7 fusion.17
  6.0 3.4 %collective-permute-start = (bf16[256,512]{1,0:T(8,128)(2,1)S(1)}, bf16[256,512]{1,0:T(8,128)(2,1)S(1)}, u32[]{:S(2)}, u32[]{:S(2)}) collective-permute-start(bf16[256,512]{1,0:T(8,128)(2,1)S(1)} %get-tuple-element.57.own_ref), channel_id=1, source_target_pairs={{0,1},{1,2},{2,3},{3,4},{4,5},{5,6},{6,7},{7,8},{8,9},{9,10},{10,1... | collective-permute-start | bytes 786440 | tf_op jit(solution)/shard_map/ppermute | solution.py:39
  9.4 3.4 %collective-permute-start.2 = (bf16[256,256]{1,0:T(8,128)(2,1)S(1)}, bf16[256,256]{1,0:T(8,128)(2,1)S(1)}, u32[]{:S(2)}, u32[]{:S(2)}) collective-permute-start(bf16[256,256]{1,0:T(8,128)(2,1)S(1)} %get-tuple-element.65.own_ref), channel_id=1, source_target_pairs={{0,1},{1,2},{2,3},{3,4},{4,5},{5,6},{6,7},{7,8},{8,9},{9,10},{10,1... | collective-permute-start | bytes 393224 | tf_op jit(solution)/shard_map/ppermute | solution.py:39
  12.9 0.7 pad_maximum_fusion.3
  13.6 3.5 %collective-permute-start.5 = (bf16[2,256,256]{2,1,0:T(8,128)(2,1)}, bf16[2,256,256]{2,1,0:T(8,128)(2,1)S(1)}, u32[]{:S(2)}, u32[]{:S(2)}) collective-permute-start(bf16[2,256,256]{2,1,0:T(8,128)(2,1)} %pad_maximum_fusion.3), channel_id=1, source_target_pairs={{0,2},{1,3},{2,4},{3,5},{4,6},{5,7},{6,8},{7,9},{8,10},{9,11},{10,... | collective-permute-start | bytes 786440 | tf_op jit(solution)/shard_map/ppermute | solution.py:39
  17.1 1.4 %collective-permute-done.2.near_ref = bf16[256,256]{1,0:T(8,128)(2,1)S(1)} collective-permute-done((bf16[256,256]{1,0:T(8,128)(2,1)S(1)}, bf16[256,256]{1,0:T(8,128)(2,1)S(1)}, u32[]{:S(2)}, u32[]{:S(2)}) %collective-permute-start.2) | collective-permute-done | bytes 131104 | tf_op jit(solution)/shard_map/ppermute | solution.py:39
  18.6 3.4 %collective-permute-start.3 = (bf16[2,256,256]{2,1,0:T(8,128)(2,1)S(1)}, bf16[2,256,256]{2,1,0:T(8,128)(2,1)S(1)}, u32[]{:S(2)}, u32[]{:S(2)}) collective-permute-start(bf16[2,256,256]{2,1,0:T(8,128)(2,1)S(1)} %pad_maximum_fusion.2), channel_id=1, source_target_pairs={{0,2},{1,3},{2,4},{3,5},{4,6},{5,7},{6,8},{7,9},{8,10},{9,11},{10,... | collective-permute-start | bytes 786440 | tf_op jit(solution)/shard_map/ppermute | solution.py:39
  22.0 1.0 %pad_maximum_fusion = bf16[2,256,512]{2,1,0:T(8,128)(2,1)S(1)} fusion(bf16[1,256,512]{2,1,0:T(8,128)(2,1)S(1)} %bitcast.52, bf16[1,256,512]{2,1,0:T(8,128)(2,1)} %get-tuple-element.56), kind=kLoop, calls=%fused_computation.7 | loop fusion | flops 262144 | bytes 1048576 | tf_op jit(solution)/shard_map/stack | solution.py:290
  23.0 3.9 %collective-permute-start.1 = (bf16[2,256,512]{2,1,0:T(8,128)(2,1)S(1)}, bf16[2,256,512]{2,1,0:T(8,128)(2,1)S(1)}, u32[]{:S(2)}, u32[]{:S(2)}) collective-permute-start(bf16[2,256,512]{2,1,0:T(8,128)(2,1)S(1)} %pad_maximum_fusion), channel_id=1, source_target_pairs={{0,2},{1,3},{2,4},{3,5},{4,6},{5,7},{6,8},{7,9},{8,10},{9,11},{10,... | collective-permute-start | bytes 1572872 | tf_op jit(solution)/shard_map/ppermute | solution.py:39
  27.0 1.6 %copy-done.1 = bf16[256,4096]{1,0:T(8,128)(2,1)S(1)} copy-done((bf16[256,4096]{1,0:T(8,128)(2,1)S(1)}, bf16[256,4096]{1,0:T(8,128)(2,1)}, u32[]{:S(2)}) %copy-start.1) | copy-done | bytes 2097176
  28.6 9.6 %attention.4 = (bf16[256,4096]{1,0:T(8,128)(2,1)}, bf16[256,4096]{1,0:T(8,128)(2,1)}, bf16[2,256,512]{2,1,0:T(8,128)(2,1)S(1)}, f32[256,512]{1,0:T(8,128)S(1)}, f32[256,512]{1,0:T(8,128)S(1)}) custom-call(s32[1]{0:T(128)} %bitcast.first_ref, s32[16]{0:T(128)S(1)} %copy-done.2, bf16[256,4096]{1,0:T(8,128)(2,1)S(1)} %copy-done, ...), custom_call_target="tpu_custom_call" | custom-call | flops 4831838208 | bytes 3538944 | tf_op jit(solution)/shard_map/attention/pallas_call | solution.py:225
  38.2 9.6 %attention.5 = (bf16[256,4096]{1,0:T(8,128)(2,1)}, bf16[256,4096]{1,0:T(8,128)(2,1)}, bf16[2,256,512]{2,1,0:T(8,128)(2,1)S(1)}, f32[256,512]{1,0:T(8,128)S(1)}, f32[256,512]{1,0:T(8,128)S(1)}) custom-call(s32[1]{0:T(128)} %bitcast.first_ref, s32[16]{0:T(128)S(1)} %copy-done.2, ...), custom_call_target="tpu_custom_call", output_to_operand_aliasing={{0}: (7, {}), {1}: (8, {}), {2}: (9, {}), {3}: (10, {}), {4... | custom-call | flops 4831838208 | bytes 3538944 | tf_op jit(solution)/shard_map/attention/pallas_call | solution.py:225
  47.8 2.1 %collective-permute-start.6 = (bf16[2,256,512]{2,1,0:T(8,128)(2,1)S(1)}, bf16[2,256,512]{2,1,0:T(8,128)(2,1)S(1)}, u32[]{:S(2)}, u32[]{:S(2)}) collective-permute-start(bf16[2,256,512]{2,1,0:T(8,128)(2,1)S(1)} %get-tuple-element.36), channel_id=1, source_target_pairs={{2,0},{3,1},{4,2},{5,3},{6,4},{7,5},{8,6},{9,7},{10,8},{11,9},{12,... | collective-permute-start | bytes 1572872 | tf_op jit(solution)/shard_map/ppermute | solution.py:39
  49.9 9.6 %attention.6 = (bf16[256,4096]{1,0:T(8,128)(2,1)}, bf16[256,4096]{1,0:T(8,128)(2,1)}, bf16[2,256,256]{2,1,0:T(8,128)(2,1)S(1)}, f32[256,256]{1,0:T(8,128)S(1)}, f32[256,256]{1,0:T(8,128)S(1)}) custom-call(s32[1]{0:T(128)} %bitcast.first_ref, s32[16]{0:T(128)S(1)} %copy-done.2, ...), custom_call_target="tpu_custom_call", output_to_operand_aliasing={{0}: (7, {}), {1}: (8, {})} | custom-call | flops 4831838208 | bytes 3538944 | tf_op jit(solution)/shard_map/attention/pallas_call | solution.py:225
  59.5 1.9 %collective-permute-start.8 = (bf16[2,256,256]{2,1,0:T(8,128)(2,1)S(1)}, bf16[2,256,256]{2,1,0:T(8,128)(2,1)S(1)}, u32[]{:S(2)}, u32[]{:S(2)}) collective-permute-start(bf16[2,256,256]{2,1,0:T(8,128)(2,1)S(1)} %get-tuple-element.39), channel_id=1, source_target_pairs={{2,0},{3,1},{4,2},{5,3},{6,4},{7,5},{8,6},{9,7},{10,8},{11,9},{12,... | collective-permute-start | bytes 786440 | tf_op jit(solution)/shard_map/ppermute | solution.py:39
  61.4 9.6 %attention.7 = (bf16[256,4096]{1,0:T(8,128)(2,1)}, bf16[256,4096]{1,0:T(8,128)(2,1)}, bf16[2,256,256]{2,1,0:T(8,128)(2,1)S(1)}, f32[256,256]{1,0:T(8,128)S(1)}, f32[256,256]{1,0:T(8,128)S(1)}) custom-call(s32[1]{0:T(128)} %bitcast.first_ref, s32[16]{0:T(128)S(1)} %copy-done.2, ...), custom_call_target="tpu_custom_call", output_to_operand_aliasing={{0}: (7, {}), {1}: (8, {})} | custom-call | flops 4831838208 | bytes 3538944 | tf_op jit(solution)/shard_map/attention/pallas_call | solution.py:225
  71.1 1.9 %collective-permute-start.10 = (bf16[2,256,256]{2,1,0:T(8,128)(2,1)S(1)}, bf16[2,256,256]{2,1,0:T(8,128)(2,1)S(1)}, u32[]{:S(2)}, u32[]{:S(2)}) collective-permute-start(bf16[2,256,256]{2,1,0:T(8,128)(2,1)S(1)} %get-tuple-element.42), channel_id=1, source_target_pairs={{2,0},{3,1},{4,2},{5,3},{6,4},{7,5},{8,6},{9,7},{10,8},{11,9},{12,... | collective-permute-start | bytes 786440 | tf_op jit(solution)/shard_map/ppermute | solution.py:39
  73.0 0.1 convert_element_type.36
  73.1 0.1 fusion.1
  73.2 5.8 %collective-permute-start.7 = (bf16[256,512]{1,0:T(8,128)(2,1)S(1)}, bf16[256,512]{1,0:T(8,128)(2,1)S(1)}, u32[]{:S(2)}, u32[]{:S(2)}) collective-permute-start(bf16[256,512]{1,0:T(8,128)(2,1)S(1)} %fusion.1), channel_id=1, source_target_pairs={{1,0},{2,1},{3,2},{4,3},{5,4},{6,5},{7,6},{8,7},{9,8},{10,9},{11,1... | collective-permute-start | bytes 786440 | tf_op jit(solution)/shard_map/ppermute | solution.py:39
  79.1 1.9 %collective-permute-start.9 = (bf16[256,256]{1,0:T(8,128)(2,1)S(1)}, bf16[256,256]{1,0:T(8,128)(2,1)S(1)}, u32[]{:S(2)}, u32[]{:S(2)}) collective-permute-start(bf16[256,256]{1,0:T(8,128)(2,1)S(1)} %fusion.11), channel_id=1, source_target_pairs={{1,0},{2,1},{3,2},{4,3},{5,4},{6,5},{7,6},{8,7},{9,8},{10,9},{11,1... | collective-permute-start | bytes 393224 | tf_op jit(solution)/shard_map/ppermute | solution.py:39
  81.0 3.0 %collective-permute-done.10 = bf16[2,256,256]{2,1,0:T(8,128)(2,1)S(1)} collective-permute-done((bf16[2,256,256]{2,1,0:T(8,128)(2,1)S(1)}, bf16[2,256,256]{2,1,0:T(8,128)(2,1)S(1)}, u32[]{:S(2)}, u32[]{:S(2)}) %collective-permute-start.10) | collective-permute-done | bytes 262176 | tf_op jit(solution)/shard_map/ppermute | solution.py:39
  84.1 6.0 %collective-permute-start.11 = (bf16[256,256]{1,0:T(8,128)(2,1)S(1)}, bf16[256,256]{1,0:T(8,128)(2,1)S(1)}, u32[]{:S(2)}, u32[]{:S(2)}) collective-permute-start(bf16[256,256]{1,0:T(8,128)(2,1)S(1)} %fusion.6), channel_id=1, source_target_pairs={{1,0},{2,1},{3,2},{4,3},{5,4},{6,5},{7,6},{8,7},{9,8},{10,9},{11,1... | collective-permute-start | bytes 393224 | tf_op jit(solution)/shard_map/ppermute | solution.py:39
  90.1 6.1 %collective-permute-done.9 = bf16[256,256]{1,0:T(8,128)(2,1)S(1)} collective-permute-done((bf16[256,256]{1,0:T(8,128)(2,1)S(1)}, bf16[256,256]{1,0:T(8,128)(2,1)S(1)}, u32[]{:S(2)}, u32[]{:S(2)}) %collective-permute-start.9) | collective-permute-done | bytes 131104 | tf_op jit(solution)/shard_map/ppermute | solution.py:39
  96.3 2.1 %collective-permute-done.11 = bf16[256,256]{1,0:T(8,128)(2,1)S(1)} collective-permute-done((bf16[256,256]{1,0:T(8,128)(2,1)S(1)}, bf16[256,256]{1,0:T(8,128)(2,1)S(1)}, u32[]{:S(2)}, u32[]{:S(2)}) %collective-permute-start.11) | collective-permute-done | bytes 131104 | tf_op jit(solution)/shard_map/ppermute | solution.py:39
  98.4 0.1 fusion.4
  98.6 0.7 pad_maximum_fusion.5
  99.4 0.7 pad_maximum_fusion.4
  (23 shorter events, 0.4 us)
Async XLA Ops:
  1.8 25.2 %copy-start = (bf16[256,4096]{1,0:T(8,128)(2,1)S(1)}, bf16[256,4096]{1,0:T(8,128)(2,1)}, u32[]{:S(2)}) copy-start(bf16[256,4096]{1,0:T(8,128)(2,1)} %q_ref.7) | copy-start | bytes 6291460
  1.8 25.2 %copy-start.2 = (s32[16]{0:T(128)S(1)}, s32[16]{0:T(128)}, u32[]{:S(2)}) copy-start(s32[16]{0:T(128)} %lengths_ref.7) | copy-start | bytes 196
  1.8 11.1 %collective-permute-start.4 = (bf16[256,256]{1,0:T(8,128)(2,1)S(1)}, bf16[256,256]{1,0:T(8,128)(2,1)S(1)}, u32[]{:S(2)}, u32[]{:S(2)}) collective-permute-start(bf16[256,256]{1,0:T(8,128)(2,1)S(1)} %get-tuple-element.63.own_ref), channel_id=1, source_target_pairs={{0,1},{1,2},{2,3},{3,4},{4,5},{5,6},{6,7},{7,8},{8,9},{9,10},{10,1... | collective-permute-start | bytes 393224 | tf_op jit(solution)/shard_map/ppermute | solution.py:39
  6.0 16.0 %collective-permute-start = (bf16[256,512]{1,0:T(8,128)(2,1)S(1)}, bf16[256,512]{1,0:T(8,128)(2,1)S(1)}, u32[]{:S(2)}, u32[]{:S(2)}) collective-permute-start(bf16[256,512]{1,0:T(8,128)(2,1)S(1)} %get-tuple-element.57.own_ref), channel_id=1, source_target_pairs={{0,1},{1,2},{2,3},{3,4},{4,5},{5,6},{6,7},{7,8},{8,9},{9,10},{10,1... | collective-permute-start | bytes 786440 | tf_op jit(solution)/shard_map/ppermute | solution.py:39
  9.4 9.1 %collective-permute-start.2 = (bf16[256,256]{1,0:T(8,128)(2,1)S(1)}, bf16[256,256]{1,0:T(8,128)(2,1)S(1)}, u32[]{:S(2)}, u32[]{:S(2)}) collective-permute-start(bf16[256,256]{1,0:T(8,128)(2,1)S(1)} %get-tuple-element.65.own_ref), channel_id=1, source_target_pairs={{0,1},{1,2},{2,3},{3,4},{4,5},{5,6},{6,7},{7,8},{8,9},{9,10},{10,1... | collective-permute-start | bytes 393224 | tf_op jit(solution)/shard_map/ppermute | solution.py:39
  13.6 13.4 %collective-permute-start.5 = (bf16[2,256,256]{2,1,0:T(8,128)(2,1)}, bf16[2,256,256]{2,1,0:T(8,128)(2,1)S(1)}, u32[]{:S(2)}, u32[]{:S(2)}) collective-permute-start(bf16[2,256,256]{2,1,0:T(8,128)(2,1)} %pad_maximum_fusion.3), channel_id=1, source_target_pairs={{0,2},{1,3},{2,4},{3,5},{4,6},{5,7},{6,8},{7,9},{8,10},{9,11},{10,... | collective-permute-start | bytes 786440 | tf_op jit(solution)/shard_map/ppermute | solution.py:39
  18.6 19.6 %collective-permute-start.3 = (bf16[2,256,256]{2,1,0:T(8,128)(2,1)S(1)}, bf16[2,256,256]{2,1,0:T(8,128)(2,1)S(1)}, u32[]{:S(2)}, u32[]{:S(2)}) collective-permute-start(bf16[2,256,256]{2,1,0:T(8,128)(2,1)S(1)} %pad_maximum_fusion.2), channel_id=1, source_target_pairs={{0,2},{1,3},{2,4},{3,5},{4,6},{5,7},{6,8},{7,9},{8,10},{9,11},{10,... | collective-permute-start | bytes 786440 | tf_op jit(solution)/shard_map/ppermute | solution.py:39
  23.0 26.9 %collective-permute-start.1 = (bf16[2,256,512]{2,1,0:T(8,128)(2,1)S(1)}, bf16[2,256,512]{2,1,0:T(8,128)(2,1)S(1)}, u32[]{:S(2)}, u32[]{:S(2)}) collective-permute-start(bf16[2,256,512]{2,1,0:T(8,128)(2,1)S(1)} %pad_maximum_fusion), channel_id=1, source_target_pairs={{0,2},{1,3},{2,4},{3,5},{4,6},{5,7},{6,8},{7,9},{8,10},{9,11},{10,... | collective-permute-start | bytes 1572872 | tf_op jit(solution)/shard_map/ppermute | solution.py:39
  27.0 1.6 %copy-start.1 = (bf16[256,4096]{1,0:T(8,128)(2,1)S(1)}, bf16[256,4096]{1,0:T(8,128)(2,1)}, u32[]{:S(2)}) copy-start(bf16[256,4096]{1,0:T(8,128)(2,1)} %g_ref.7) | copy-start | bytes 6291460
  47.8 25.2 %collective-permute-start.6 = (bf16[2,256,512]{2,1,0:T(8,128)(2,1)S(1)}, bf16[2,256,512]{2,1,0:T(8,128)(2,1)S(1)}, u32[]{:S(2)}, u32[]{:S(2)}) collective-permute-start(bf16[2,256,512]{2,1,0:T(8,128)(2,1)S(1)} %get-tuple-element.36), channel_id=1, source_target_pairs={{2,0},{3,1},{4,2},{5,3},{6,4},{7,5},{8,6},{9,7},{10,8},{11,9},{12,... | collective-permute-start | bytes 1572872 | tf_op jit(solution)/shard_map/ppermute | solution.py:39
  59.5 19.5 %collective-permute-start.8 = (bf16[2,256,256]{2,1,0:T(8,128)(2,1)S(1)}, bf16[2,256,256]{2,1,0:T(8,128)(2,1)S(1)}, u32[]{:S(2)}, u32[]{:S(2)}) collective-permute-start(bf16[2,256,256]{2,1,0:T(8,128)(2,1)S(1)} %get-tuple-element.39), channel_id=1, source_target_pairs={{2,0},{3,1},{4,2},{5,3},{6,4},{7,5},{8,6},{9,7},{10,8},{11,9},{12,... | collective-permute-start | bytes 786440 | tf_op jit(solution)/shard_map/ppermute | solution.py:39
  71.1 13.0 %collective-permute-start.10 = (bf16[2,256,256]{2,1,0:T(8,128)(2,1)S(1)}, bf16[2,256,256]{2,1,0:T(8,128)(2,1)S(1)}, u32[]{:S(2)}, u32[]{:S(2)}) collective-permute-start(bf16[2,256,256]{2,1,0:T(8,128)(2,1)S(1)} %get-tuple-element.42), channel_id=1, source_target_pairs={{2,0},{3,1},{4,2},{5,3},{6,4},{7,5},{8,6},{9,7},{10,8},{11,9},{12,... | collective-permute-start | bytes 786440 | tf_op jit(solution)/shard_map/ppermute | solution.py:39
  73.2 25.2 %collective-permute-start.7 = (bf16[256,512]{1,0:T(8,128)(2,1)S(1)}, bf16[256,512]{1,0:T(8,128)(2,1)S(1)}, u32[]{:S(2)}, u32[]{:S(2)}) collective-permute-start(bf16[256,512]{1,0:T(8,128)(2,1)S(1)} %fusion.1), channel_id=1, source_target_pairs={{1,0},{2,1},{3,2},{4,3},{5,4},{6,5},{7,6},{8,7},{9,8},{10,9},{11,1... | collective-permute-start | bytes 786440 | tf_op jit(solution)/shard_map/ppermute | solution.py:39
  79.1 17.1 %collective-permute-start.9 = (bf16[256,256]{1,0:T(8,128)(2,1)S(1)}, bf16[256,256]{1,0:T(8,128)(2,1)S(1)}, u32[]{:S(2)}, u32[]{:S(2)}) collective-permute-start(bf16[256,256]{1,0:T(8,128)(2,1)S(1)} %fusion.11), channel_id=1, source_target_pairs={{1,0},{2,1},{3,2},{4,3},{5,4},{6,5},{7,6},{8,7},{9,8},{10,9},{11,1... | collective-permute-start | bytes 393224 | tf_op jit(solution)/shard_map/ppermute | solution.py:39
  84.1 14.2 %collective-permute-start.11 = (bf16[256,256]{1,0:T(8,128)(2,1)S(1)}, bf16[256,256]{1,0:T(8,128)(2,1)S(1)}, u32[]{:S(2)}, u32[]{:S(2)}) collective-permute-start(bf16[256,256]{1,0:T(8,128)(2,1)S(1)} %fusion.6), channel_id=1, source_target_pairs={{1,0},{2,1},{3,2},{4,3},{5,4},{6,5},{7,6},{8,7},{9,8},{10,9},{11,1... | collective-permute-start | bytes 393224 | tf_op jit(solution)/shard_map/ppermute | solution.py:39

commit v10 on v9

v10 whole, which is shorter than its diff:
```python
import functools
import math

import jax
import jax.numpy as jnp
from jax import lax
from jax.experimental import pallas as pl
from jax.experimental.pallas import tpu as pltpu
from jax.sharding import PartitionSpec as P

HEAD_SIZE = 128
QUERY_HEADS = 32
KEY_VALUE_HEADS = 4
GROUP = QUERY_HEADS // KEY_VALUE_HEADS
SPAN = 4
AXES = ("blk", "inner")
ROWS = 32
UNIT = 4
FORWARD = ((0,), (1,), (2, 3))
BACKWARD = ((0, 1), (2,), (3,))
MASKED = -1e30
SCALE = 1.0 / math.sqrt(HEAD_SIZE)
EXP2_SCALE = SCALE * math.log2(math.e)

NN = (((1,), (0,)), ((), ()))


def dot(a, b, dims=NN):
    return lax.dot_general(a, b, dims, preferred_element_type=jnp.float32)


def device_count():
    return lax.axis_size("blk") * lax.axis_size("inner")


def passed_along(value, steps):
    count = device_count()
    first, last = (max(0, -steps), min(count, count - steps))
    return lax.ppermute(value, AXES, [(source, source + steps) for source in range(first, last)])


def write_masks(bias_ref, old_ref, cut_ref, lengths_ref, first_ref, rows):
    docs = lengths_ref.shape[0]
    first = first_ref[0]
    row = lax.broadcasted_iota(jnp.int32, (rows, 128), 0)
    query_pos = first + row

    def step(doc, carry):
        end, start = carry
        end = end + lengths_ref[doc]
        return end, jnp.where(query_pos >= end, end, start)

    _, start = lax.fori_loop(0, docs, step, (jnp.int32(0), jnp.zeros((rows, 128), jnp.int32)))
    lane = lax.broadcasted_iota(jnp.int32, (rows, 128), 1)
    old = start < first - (SPAN - 2) * rows
    old_ref[...] = jnp.where(old, 1.0, 0.0)
    cut = jnp.min(jnp.where(old, start - (first - (SPAN - 1) * rows), rows), axis=0, keepdims=True)
    cut_ref[...] = jnp.broadcast_to(cut, cut_ref.shape)
    cut = jnp.broadcast_to(cut, (rows, 128))
    for part in range((SPAN - 1) * rows // 128):
        offset = part * 128 + lane
        if part < rows // 128:
            own = (offset <= row) & ((first + offset >= start) | (old & (offset < cut)))
            allowed = own | (old & (offset >= cut))
        else:
            allowed = first - (SPAN - 1) * rows + offset >= start
        bias_ref[:, part * 128 : (part + 1) * 128] = jnp.where(allowed, 0.0, MASKED)


def attention_kernel(places, first_ref, lengths_ref, q_ref, g_ref, behind_ref, near_ref, own_ref, *refs):
    (
        out_ref, dq_ref, dbehind_ref, dnear_ref, down_ref,
        bias_ref, old_ref, cut_ref,
        key_ref, value_ref, key_t_ref, value_t_ref, key2_ref, value2_ref, key2_t_ref, value2_t_ref,
        dk_ref, dv_ref, dk2_ref, dv2_ref, *slots,
    ) = refs[-33:]
    s_refs, p_refs, dp_refs, d_refs, g_refs, delta_refs = (slots[i : i + 2] for i in range(0, 12, 2))
    (inv_ref,) = slots[12:]
    rows = q_ref.shape[0]
    window = (SPAN - 1) * rows
    units = GROUP // UNIT
    key_in, value_in, key_out, value_out = (slice(at, at + HEAD_SIZE) for at in places)
    stack = UNIT * rows
    two = slice(0, rows)
    rest = slice(rows, window)

    write_masks(bias_ref, old_ref, cut_ref, lengths_ref, first_ref, rows)
    from_far = lax.broadcasted_iota(jnp.int32, (rows, HEAD_SIZE), 0) >= cut_ref[0, 0]
    mid, far, near, own = behind_ref.at[0], behind_ref.at[1], near_ref, own_ref
    for j, block in enumerate((mid, near)):
        span = slice(j * rows, (j + 1) * rows)
        key_ref[span] = block[:, key_in]
        value_ref[span] = block[:, value_in]
        key_t_ref[:, span] = block[:, key_in].T
        value_t_ref[:, span] = block[:, value_in].T
    for which, plain_ref, turned_ref in ((key_in, key2_ref, key2_t_ref), (value_in, value2_ref, value2_t_ref)):
        mine = own[:, which]
        either = jnp.where(from_far, far[:, which].astype(jnp.float32), mine.astype(jnp.float32))
        for j, block in enumerate((either.astype(jnp.bfloat16), mine)):
            span = slice(j * HEAD_SIZE, (j + 1) * HEAD_SIZE)
            plain_ref[:, span] = block
            turned_ref[span] = block.T
    for ref in (dk_ref, dv_ref, dk2_ref, dv2_ref):
        ref[...] = jnp.zeros_like(ref)

    def places(unit):
        return [
            (
                slice(i * rows, (i + 1) * rows),
                slice((unit * UNIT + i) * HEAD_SIZE, (unit * UNIT + i + 1) * HEAD_SIZE),
            )
            for i in range(UNIT)
        ]

    def stacked(ref, unit):
        return jnp.concatenate([ref[:, cols] for _, cols in places(unit)], axis=0)

    def doubled(x):
        old = jnp.concatenate([old_ref[...].astype(jnp.bfloat16)] * UNIT, axis=0)
        return jnp.concatenate([x * old, x * (1 - old)], axis=1)

    def picked(x):
        old = jnp.concatenate([old_ref[...]] * UNIT, axis=0)
        return jnp.where(old > 0.5, x[:, :HEAD_SIZE], x[:, HEAD_SIZE:])

    def scores(unit, slot):
        q = stacked(q_ref, unit)
        s_refs[slot][:, two] = dot(doubled(q), key2_t_ref[...])
        s_refs[slot][:, rest] = dot(q, key_t_ref[...])

    def softmax(slot):
        for r in range(0, stack, ROWS):
            here = slice(r, r + ROWS)
            row = slice(r % rows, r % rows + ROWS)
            s = s_refs[slot][here] * EXP2_SCALE + bias_ref[row]
            e = jnp.exp2(s - jnp.max(s, axis=1, keepdims=True))
            inv = 1.0 / jnp.sum(e, axis=1, keepdims=True)
            inv_ref[here] = jnp.broadcast_to(inv, (ROWS, HEAD_SIZE))
            p_refs[slot][here] = e.astype(jnp.bfloat16)

    def mix(unit, slot):
        p_ref, g_ref_here = p_refs[slot], g_refs[slot]
        total = picked(dot(p_ref[:, two], value2_ref[...])) + dot(p_ref[:, rest], value_ref[...])
        for here, cols in places(unit):
            inv = inv_ref[here]
            out = (total[here] * inv).astype(jnp.bfloat16)
            out_ref[:, cols] = out
            g = g_ref[:, cols].astype(jnp.float32) * inv
            delta = jnp.sum(g * out.astype(jnp.float32), axis=1, keepdims=True)
            delta_refs[slot][here] = jnp.broadcast_to(delta, (rows, HEAD_SIZE))
            g_ref_here[here] = g.astype(jnp.bfloat16)
        g = g_ref_here[...]
        dp_refs[slot][:, two] = dot(doubled(g), value2_t_ref[...])
        dp_refs[slot][:, rest] = dot(g, value_t_ref[...])

    def score_grad(slot):
        for r in range(0, stack, ROWS):
            here = slice(r, r + ROWS)
            delta = jnp.concatenate([delta_refs[slot][here]] * (window // HEAD_SIZE), axis=1)
            d_refs[slot][here] = p_refs[slot][here] * (dp_refs[slot][here] - delta).astype(jnp.bfloat16)

    def spread(unit, slot):
        p_ref, d_ref = p_refs[slot], d_refs[slot]
        total = picked(dot(d_ref[:, two], key2_ref[...])) + dot(d_ref[:, rest], key_ref[...])
        for here, cols in places(unit):
            dq_ref[:, cols] = (total[here] * SCALE).astype(jnp.bfloat16)
        q = stacked(q_ref, unit)
        g = g_refs[slot][...]
        dk2_ref[...] += dot(doubled(q).T, d_ref[:, two])
        dk_ref[...] += dot(q.T, d_ref[:, rest])
        dv2_ref[...] += dot(doubled(g).T, p_ref[:, two])
        dv_ref[...] += dot(g.T, p_ref[:, rest])

    scores(0, 0)
    for unit in range(units):
        slot = unit % 2
        if unit + 1 < units:
            scores(unit + 1, 1 - slot)
        if unit > 0:
            score_grad(1 - slot)
        softmax(slot)
        if unit > 0:
            spread(unit - 1, 1 - slot)
        mix(unit, slot)
    score_grad((units - 1) % 2)
    spread(units - 1, (units - 1) % 2)
    for span, grad, grad2, scale in ((key_out, dk_ref, dk2_ref, SCALE), (value_out, dv_ref, dv2_ref, 1.0)):
        either = grad2[:HEAD_SIZE].T * scale
        own = grad2[HEAD_SIZE:].T * scale
        dbehind_ref[0, :, span] = (grad[:, :rows].T * scale).astype(jnp.bfloat16)
        dbehind_ref[1, :, span] = jnp.where(from_far, either, 0.0).astype(jnp.bfloat16)
        dnear_ref[:, span] = grad[:, rows:].T * scale
        down_ref[:, span] = own + jnp.where(from_far, 0.0, either)


def attention(head, first, lengths, queries, out_grad, blocks, place, grads, parts, back, back_place):
    rows = queries.shape[0]
    wide = GROUP * HEAD_SIZE
    pair = 2 * HEAD_SIZE
    window = (SPAN - 1) * rows
    query_spec = pl.BlockSpec((rows, wide), lambda i, *_: (0, head))

    def pair_specs(heads, at):
        one = pl.BlockSpec((rows, heads * pair), lambda i, *_: (0, at))
        return [pl.BlockSpec((2, rows, heads * pair), lambda i, *_: (0, 0, at)), one, one]

    fore = blocks[-1].shape[1] // pair
    places = [at * HEAD_SIZE for at in (place, fore + place, 0, 1)]
    operands = [first, lengths, queries, out_grad, *blocks]
    in_specs = [query_spec] * 2 + pair_specs(fore, 0)
    aliases = {}
    for at, array in enumerate((*grads, *parts)):
        if array is not None:
            aliases[len(operands)] = at
            operands.append(array)
            in_specs.append(pl.BlockSpec(memory_space=pl.ANY))
    bf16, f32 = jnp.bfloat16, jnp.float32
    results = pl.pallas_call(
        functools.partial(attention_kernel, places),
        out_shape=[
            jax.ShapeDtypeStruct(queries.shape, bf16),
            jax.ShapeDtypeStruct(queries.shape, bf16),
            jax.ShapeDtypeStruct((2, rows, back * pair), bf16),
            jax.ShapeDtypeStruct((rows, back * pair), f32),
            jax.ShapeDtypeStruct((rows, back * pair), f32),
        ],
        grid_spec=pltpu.PrefetchScalarGridSpec(
            num_scalar_prefetch=2,
            grid=(1,),
            in_specs=in_specs,
            out_specs=[query_spec] * 2 + pair_specs(1, back_place),
            scratch_shapes=[
                pltpu.VMEM(shape, kind)
                for shape, kind, count in (
                    ((rows, window), f32, 1),
                    ((rows, HEAD_SIZE), f32, 1),
                    ((8, HEAD_SIZE), jnp.int32, 1),
                    ((2 * rows, HEAD_SIZE), bf16, 2),
                    ((HEAD_SIZE, 2 * rows), bf16, 2),
                    ((rows, pair), bf16, 2),
                    ((pair, rows), bf16, 2),
                    ((HEAD_SIZE, 2 * rows), f32, 2),
                    ((pair, rows), f32, 2),
                    ((UNIT * rows, window), f32, 2),
                    ((UNIT * rows, window), bf16, 2),
                    ((UNIT * rows, window), f32, 2),
                    ((UNIT * rows, window), bf16, 2),
                    ((UNIT * rows, HEAD_SIZE), bf16, 2),
                    ((UNIT * rows, HEAD_SIZE), f32, 2),
                    ((UNIT * rows, HEAD_SIZE), f32, 1),
                )
                for _ in range(count)
            ],
        ),
        input_output_aliases=aliases,
        compiler_params=pltpu.CompilerParams(vmem_limit_bytes=48 * 1024 * 1024),
        cost_estimate=pl.CostEstimate(
            flops=12 * rows * GROUP * window * HEAD_SIZE * 2,
            bytes_accessed=4 * rows * wide * 2 + 22 * rows * pair,
            transcendentals=0,
        ),
        name="attention",
    )(*operands)
    return results[:2], results[2:]


def local(queries, keys, values, out_grad, doc_lengths):
    rows = queries.shape[0]
    index = lax.axis_index(AXES)
    first = (index * rows).astype(jnp.int32).reshape(1)
    bf16, f32 = jnp.bfloat16, jnp.float32
    blocks = {}
    owns, nears = [], []
    for heads in FORWARD:
        span = slice(heads[0] * HEAD_SIZE, (heads[-1] + 1) * HEAD_SIZE)
        owns.append(jnp.concatenate([keys[:, span], values[:, span]], axis=1))
    for own in owns:
        nears.append(passed_along(own, 1))
    for heads, own, near in zip(FORWARD, owns, nears):
        behind = passed_along(jnp.stack([own, near]), 2)
        for place, head in enumerate(heads):
            blocks[head] = ((behind, near, own), place)
    grads = (None, None)
    sent = []

    def second(own, near, got):
        got = got.astype(f32)
        return [own + got[0], (near + got[1]).astype(bf16)]

    for heads in BACKWARD:
        parts = (None,) * 3
        for at, head in enumerate(heads):
            (behind, near, own), place = blocks[head]
            if head == KEY_VALUE_HEADS - 1:
                own, *sent[0] = lax.optimization_barrier((own, *sent[0]))
                last = passed_along(sent[0][1], -1)
            grads, parts = attention(
                head, first, doc_lengths, queries, out_grad, (behind, near, own), place, grads, parts, len(heads), at
            )
        behind, near, own = parts
        if heads == BACKWARD[-1]:
            behind, near, last, middle = lax.optimization_barrier((behind, near, last, sent[1][2]))
            sent[1] = [*sent[1][:2], middle]
        sent.append([own, near, passed_along(behind, -2)])
        if len(sent) == 1:
            sent[0] = second(*sent[0])
    rest = [second(*sent[1]), second(*sent[2])]
    own = [sent[0][0], *(piece[0] for piece in rest)]
    near = passed_along(jnp.concatenate([piece[1] for piece in rest], axis=1), -1)
    total = (jnp.concatenate(own, axis=1) + jnp.concatenate([last, near], axis=1).astype(f32)).astype(bf16)
    parts = [total[:, at : at + HEAD_SIZE] for at in range(0, total.shape[1], HEAD_SIZE)]
    key_grads, value_grads = parts[0::2], parts[1::2]
    return (
        grads[0],
        grads[1],
        jnp.concatenate(key_grads, axis=1),
        jnp.concatenate(value_grads, axis=1),
    )


def solution(mesh):
    spec = P(AXES, None)
    return jax.shard_map(
        local,
        mesh=mesh,
        in_specs=(spec, spec, spec, spec, P()),
        out_specs=(spec, spec, spec, spec),
        check_vma=False,
    )
```

time: 101 us -> 100 us (0.990)
  waiting for transfers between devices: 12.6 us -> 27.7 us
  starting transfers between devices: 40.7 us -> 30.7 us
  Pallas kernels: 38.5 us -> 32.8 us
    ppermute x12 -> x11, waiting for transfers between devices: 12.6 us -> 27.7 us  [passed_along(): lax.ppermute(value, AXES, [(source, source + steps) for source in range(f...]
    ppermute x12 -> x11, starting transfers between devices: 40.7 us -> 30.7 us  [passed_along(): lax.ppermute(value, AXES, [(source, source + steps) for source in range(f...]
    pallas_call x4, Pallas kernels: 38.5 us -> 32.8 us  [attention(): pl.pallas_call(functools.partial(attention_kernel, places), out_shape=[ja...]
    slice x4, local copies, waits for them, and re-layouts: 1.19 us -> 2.9 us  [the longest x3 2.8 us: local(): owns.append(jnp.concatenate([keys[:, span], values[:, span]], axis=1))]
    unnamed x6, local copies, waits for them, and re-layouts: 1.6 us -> 0.02 us
  transfers between devices with their start and end apart: 12 -> 11, of which waited for: 4 -> 5; matrix products, arithmetic and copies ran while one was open for 3% -> 5% of each run, Pallas kernels for 38% -> 33%
where the time goes in v10:
time: 100 us; the launch traced here: 99.6 us
  Pallas kernels  32.8 us (33%)
  starting transfers between devices  30.7 us (31%)
  waiting for transfers between devices  27.7 us (28%)
  other arithmetic  4.71 us (5%)
  local copies, waits for them, and re-layouts  2.91 us (3%)
    pallas_call x4, Pallas kernels, attention(): pl.pallas_call(functools.partial(attention_kernel, places), out_shape=[ja...  32.8 us
    ppermute x11, starting transfers between devices, passed_along(): lax.ppermute(value, AXES, [(source, source + steps) for source in range(f...  30.7 us
    ppermute x11, waiting for transfers between devices, passed_along(): lax.ppermute(value, AXES, [(source, source + steps) for source in range(f...  27.7 us
    slice x3, local copies, waits for them, and re-layouts, local(): owns.append(jnp.concatenate([keys[:, span], values[:, span]], axis=1))  2.8 us
    another operation x6, other arithmetic, local(): behind = passed_along(jnp.stack([own, near]), 2)  2.54 us
  transfers between devices with their start and end apart: 11, of which 5 were waited for; matrix products, arithmetic and copies ran while one was open for 5% of the time, Pallas kernels for 33%

profile of v10, /device:TPU:29, one launch (start us, length us, event | category | flops | bytes accessed | tf_op | source)
XLA Modules:
  0.0 99.6 jit_solution(11711779904435973565)
XLA Ops:
  0.6 1.0 fusion.14
  1.7 3.4 %collective-permute-start.4 = (bf16[256,256]{1,0:T(8,128)(2,1)S(1)}, bf16[256,256]{1,0:T(8,128)(2,1)S(1)}, u32[]{:S(2)}, u32[]{:S(2)}) collective-permute-start(bf16[256,256]{1,0:T(8,128)(2,1)S(1)} %get-tuple-element.79.own_ref), channel_id=1, source_target_pairs={{0,1},{1,2},{2,3},{3,4},{4,5},{5,6},{6,7},{7,8},{8,9},{9,10},{10,1... | collective-permute-start | bytes 393224 | tf_op jit(solution)/shard_map/ppermute | solution.py:39
  5.1 0.9 slice.60
  6.0 0.9 slice.61
  6.9 0.7 fusion.12
  7.7 3.4 %collective-permute-start = (bf16[256,512]{1,0:T(8,128)(2,1)S(1)}, bf16[256,512]{1,0:T(8,128)(2,1)S(1)}, u32[]{:S(2)}, u32[]{:S(2)}) collective-permute-start(bf16[256,512]{1,0:T(8,128)(2,1)S(1)} %get-tuple-element.39.own_ref), channel_id=1, source_target_pairs={{0,1},{1,2},{2,3},{3,4},{4,5},{5,6},{6,7},{7,8},{8,9},{9,10},{10,1... | collective-permute-start | bytes 786440 | tf_op jit(solution)/shard_map/ppermute | solution.py:39
  11.1 3.4 %collective-permute-start.2 = (bf16[256,256]{1,0:T(8,128)(2,1)S(1)}, bf16[256,256]{1,0:T(8,128)(2,1)S(1)}, u32[]{:S(2)}, u32[]{:S(2)}) collective-permute-start(bf16[256,256]{1,0:T(8,128)(2,1)S(1)} %get-tuple-element.81.own_ref), channel_id=1, source_target_pairs={{0,1},{1,2},{2,3},{3,4},{4,5},{5,6},{6,7},{7,8},{8,9},{9,10},{10,1... | collective-permute-start | bytes 393224 | tf_op jit(solution)/shard_map/ppermute | solution.py:39
  14.5 0.7 pad_maximum_fusion.3
  15.3 3.5 %collective-permute-start.5 = (bf16[2,256,256]{2,1,0:T(8,128)(2,1)}, bf16[2,256,256]{2,1,0:T(8,128)(2,1)S(1)}, u32[]{:S(2)}, u32[]{:S(2)}) collective-permute-start(bf16[2,256,256]{2,1,0:T(8,128)(2,1)} %pad_maximum_fusion.3), channel_id=1, source_target_pairs={{0,2},{1,3},{2,4},{3,5},{4,6},{5,7},{6,8},{7,9},{8,10},{9,11},{10,... | collective-permute-start | bytes 786440 | tf_op jit(solution)/shard_map/ppermute | solution.py:39
  18.8 1.4 %collective-permute-done.2.near_ref = bf16[256,256]{1,0:T(8,128)(2,1)S(1)} collective-permute-done((bf16[256,256]{1,0:T(8,128)(2,1)S(1)}, bf16[256,256]{1,0:T(8,128)(2,1)S(1)}, u32[]{:S(2)}, u32[]{:S(2)}) %collective-permute-start.2) | collective-permute-done | bytes 131104 | tf_op jit(solution)/shard_map/ppermute | solution.py:39
  20.2 3.4 %collective-permute-start.3 = (bf16[2,256,256]{2,1,0:T(8,128)(2,1)S(1)}, bf16[2,256,256]{2,1,0:T(8,128)(2,1)S(1)}, u32[]{:S(2)}, u32[]{:S(2)}) collective-permute-start(bf16[2,256,256]{2,1,0:T(8,128)(2,1)S(1)} %pad_maximum_fusion.2), channel_id=1, source_target_pairs={{0,2},{1,3},{2,4},{3,5},{4,6},{5,7},{6,8},{7,9},{8,10},{9,11},{10,... | collective-permute-start | bytes 786440 | tf_op jit(solution)/shard_map/ppermute | solution.py:39
  23.7 1.0 %pad_maximum_fusion = bf16[2,256,512]{2,1,0:T(8,128)(2,1)S(1)} fusion(bf16[1,256,512]{2,1,0:T(8,128)(2,1)S(1)} %bitcast.40, bf16[1,256,512]{2,1,0:T(8,128)(2,1)} %get-tuple-element.76), kind=kLoop, calls=%fused_computation.7 | loop fusion | flops 262144 | bytes 1048576 | tf_op jit(solution)/shard_map/stack | solution.py:280
  24.7 3.9 %collective-permute-start.1 = (bf16[2,256,512]{2,1,0:T(8,128)(2,1)S(1)}, bf16[2,256,512]{2,1,0:T(8,128)(2,1)S(1)}, u32[]{:S(2)}, u32[]{:S(2)}) collective-permute-start(bf16[2,256,512]{2,1,0:T(8,128)(2,1)S(1)} %pad_maximum_fusion), channel_id=1, source_target_pairs={{0,2},{1,3},{2,4},{3,5},{4,6},{5,7},{6,8},{7,9},{8,10},{9,11},{10,... | collective-permute-start | bytes 1572872 | tf_op jit(solution)/shard_map/ppermute | solution.py:39
  28.7 8.5 %attention.4 = (bf16[256,4096]{1,0:T(8,128)(2,1)}, bf16[256,4096]{1,0:T(8,128)(2,1)}, bf16[2,256,512]{2,1,0:T(8,128)(2,1)S(1)}, f32[256,512]{1,0:T(8,128)S(1)}, f32[256,512]{1,0:T(8,128)S(1)}) custom-call(s32[1]{0:T(128)} %bitcast.first_ref, s32[16]{0:T(128)S(1)} %copy-done.2, bf16[256,4096]{1,0:T(8,128)(2,1)S(1)} %copy-done, bf16[256,4096]{1,0:T(8,128)(2,1)} %g_ref.7, ...), custom_call_target="tpu_custom_call" | custom-call | flops 4831838208 | bytes 3538944 | tf_op jit(solution)/shard_map/attention/pallas_call | solution.py:218
  37.2 8.7 %attention.5 = (bf16[256,4096]{1,0:T(8,128)(2,1)}, bf16[256,4096]{1,0:T(8,128)(2,1)}, bf16[2,256,512]{2,1,0:T(8,128)(2,1)S(1)}, f32[256,512]{1,0:T(8,128)S(1)}, f32[256,512]{1,0:T(8,128)S(1)}) custom-call(s32[1]{0:T(128)} %bitcast.first_ref, s32[16]{0:T(128)S(1)} %copy-done.2, ...), custom_call_target="tpu_custom_call", output_to_operand_aliasing={{0}: (7, {}), {1}: (8, {}), {2}: (9, {}), {3}: (10, {}), {4... | custom-call | flops 4831838208 | bytes 3538944 | tf_op jit(solution)/shard_map/attention/pallas_call | solution.py:218
  46.0 1.9 %collective-permute-start.6 = (bf16[2,256,512]{2,1,0:T(8,128)(2,1)S(1)}, bf16[2,256,512]{2,1,0:T(8,128)(2,1)S(1)}, u32[]{:S(2)}, u32[]{:S(2)}) collective-permute-start(bf16[2,256,512]{2,1,0:T(8,128)(2,1)S(1)} %get-tuple-element.37), channel_id=1, source_target_pairs={{2,0},{3,1},{4,2},{5,3},{6,4},{7,5},{8,6},{9,7},{10,8},{11,9},{12,... | collective-permute-start | bytes 1572872 | tf_op jit(solution)/shard_map/ppermute | solution.py:39
  47.9 7.7 %attention.6 = (bf16[256,4096]{1,0:T(8,128)(2,1)}, bf16[256,4096]{1,0:T(8,128)(2,1)}, bf16[2,256,256]{2,1,0:T(8,128)(2,1)S(1)}, f32[256,256]{1,0:T(8,128)S(1)}, f32[256,256]{1,0:T(8,128)S(1)}) custom-call(s32[1]{0:T(128)} %bitcast.first_ref, s32[16]{0:T(128)S(1)} %copy-done.2, ...), custom_call_target="tpu_custom_call", output_to_operand_aliasing={{0}: (7, {}), {1}: (8, {})} | custom-call | flops 4831838208 | bytes 3538944 | tf_op jit(solution)/shard_map/attention/pallas_call | solution.py:218
  55.6 1.9 %collective-permute-start.8 = (bf16[2,256,256]{2,1,0:T(8,128)(2,1)S(1)}, bf16[2,256,256]{2,1,0:T(8,128)(2,1)S(1)}, u32[]{:S(2)}, u32[]{:S(2)}) collective-permute-start(bf16[2,256,256]{2,1,0:T(8,128)(2,1)S(1)} %get-tuple-element.51), channel_id=1, source_target_pairs={{2,0},{3,1},{4,2},{5,3},{6,4},{7,5},{8,6},{9,7},{10,8},{11,9},{12,... | collective-permute-start | bytes 786440 | tf_op jit(solution)/shard_map/ppermute | solution.py:39
  57.5 6.9 %collective-permute-done.6 = bf16[2,256,512]{2,1,0:T(8,128)(2,1)S(1)} collective-permute-done((bf16[2,256,512]{2,1,0:T(8,128)(2,1)S(1)}, bf16[2,256,512]{2,1,0:T(8,128)(2,1)S(1)}, u32[]{:S(2)}, u32[]{:S(2)}) %collective-permute-start.6) | collective-permute-done | bytes 524320 | tf_op jit(solution)/shard_map/ppermute | solution.py:39
  64.4 0.1 convert_element_type.24
  64.6 0.2 fusion.2
  64.8 1.9 %collective-permute-start.7 = (bf16[256,512]{1,0:T(8,128)(2,1)S(1)}, bf16[256,512]{1,0:T(8,128)(2,1)S(1)}, u32[]{:S(2)}, u32[]{:S(2)}) collective-permute-start(bf16[256,512]{1,0:T(8,128)(2,1)S(1)} %get-tuple-element.50), channel_id=1, source_target_pairs={{1,0},{2,1},{3,2},{4,3},{5,4},{6,5},{7,6},{8,7},{9,8},{10,9},{11,1... | collective-permute-start | bytes 786440 | tf_op jit(solution)/shard_map/ppermute | solution.py:39
  66.7 7.8 %attention.7 = (bf16[256,4096]{1,0:T(8,128)(2,1)}, bf16[256,4096]{1,0:T(8,128)(2,1)}, bf16[2,256,256]{2,1,0:T(8,128)(2,1)S(1)}, f32[256,256]{1,0:T(8,128)S(1)}, f32[256,256]{1,0:T(8,128)S(1)}) custom-call(s32[1]{0:T(128)} %bitcast.first_ref, s32[16]{0:T(128)S(1)} %copy-done.2, ...), custom_call_target="tpu_custom_call", output_to_operand_aliasing={{0}: (7, {}), {1}: (8, {})} | custom-call | flops 4831838208 | bytes 3538944 | tf_op jit(solution)/shard_map/attention/pallas_call | solution.py:218
  74.5 1.6 %collective-permute-done.7 = bf16[256,512]{1,0:T(8,128)(2,1)S(1)} collective-permute-done((bf16[256,512]{1,0:T(8,128)(2,1)S(1)}, bf16[256,512]{1,0:T(8,128)(2,1)S(1)}, u32[]{:S(2)}, u32[]{:S(2)}) %collective-permute-start.7) | collective-permute-done | bytes 262176 | tf_op jit(solution)/shard_map/ppermute | solution.py:39
  76.1 1.9 %collective-permute-start.9 = (bf16[2,256,256]{2,1,0:T(8,128)(2,1)S(1)}, bf16[2,256,256]{2,1,0:T(8,128)(2,1)S(1)}, u32[]{:S(2)}, u32[]{:S(2)}) collective-permute-start(bf16[2,256,256]{2,1,0:T(8,128)(2,1)S(1)} %get-tuple-element.54), channel_id=1, source_target_pairs={{2,0},{3,1},{4,2},{5,3},{6,4},{7,5},{8,6},{9,7},{10,8},{11,9},{12,... | collective-permute-start | bytes 786440 | tf_op jit(solution)/shard_map/ppermute | solution.py:39
  78.1 8.3 %collective-permute-done.9 = bf16[2,256,256]{2,1,0:T(8,128)(2,1)S(1)} collective-permute-done((bf16[2,256,256]{2,1,0:T(8,128)(2,1)S(1)}, bf16[2,256,256]{2,1,0:T(8,128)(2,1)S(1)}, u32[]{:S(2)}, u32[]{:S(2)}) %collective-permute-start.9) | collective-permute-done | bytes 262176 | tf_op jit(solution)/shard_map/ppermute | solution.py:39
  86.6 1.9 %collective-permute-start.10 = (bf16[256,512]{1,0:T(8,128)(2,1)S(1)}, bf16[256,512]{1,0:T(8,128)(2,1)S(1)}, u32[]{:S(2)}, u32[]{:S(2)}) collective-permute-start(bf16[256,512]{1,0:T(8,128)(2,1)S(1)} %pad_maximum_fusion.4), channel_id=1, source_target_pairs={{1,0},{2,1},{3,2},{4,3},{5,4},{6,5},{7,6},{8,7},{9,8},{10,9},{11,1... | collective-permute-start | bytes 786440 | tf_op jit(solution)/shard_map/ppermute | solution.py:39
  88.5 9.4 %collective-permute-done.10 = bf16[256,512]{1,0:T(8,128)(2,1)S(1)} collective-permute-done((bf16[256,512]{1,0:T(8,128)(2,1)S(1)}, bf16[256,512]{1,0:T(8,128)(2,1)S(1)}, u32[]{:S(2)}, u32[]{:S(2)}) %collective-permute-start.10) | collective-permute-done | bytes 262176 | tf_op jit(solution)/shard_map/ppermute | solution.py:39
  97.9 0.1 fusion
  98.0 0.1 fusion.13
  98.1 0.7 pad_maximum_fusion.6
  98.9 0.7 pad_maximum_fusion.5
  (20 shorter events, 0.3 us)
Async XLA Ops:
  1.6 27.1 %copy-start = (bf16[256,4096]{1,0:T(8,128)(2,1)S(1)}, bf16[256,4096]{1,0:T(8,128)(2,1)}, u32[]{:S(2)}) copy-start(bf16[256,4096]{1,0:T(8,128)(2,1)} %q_ref.7) | copy-start | bytes 6291460
  1.6 27.1 %copy-start.2 = (s32[16]{0:T(128)S(1)}, s32[16]{0:T(128)}, u32[]{:S(2)}) copy-start(s32[16]{0:T(128)} %lengths_ref.7) | copy-start | bytes 196
  1.7 12.9 %collective-permute-start.4 = (bf16[256,256]{1,0:T(8,128)(2,1)S(1)}, bf16[256,256]{1,0:T(8,128)(2,1)S(1)}, u32[]{:S(2)}, u32[]{:S(2)}) collective-permute-start(bf16[256,256]{1,0:T(8,128)(2,1)S(1)} %get-tuple-element.79.own_ref), channel_id=1, source_target_pairs={{0,1},{1,2},{2,3},{3,4},{4,5},{5,6},{6,7},{7,8},{8,9},{9,10},{10,1... | collective-permute-start | bytes 393224 | tf_op jit(solution)/shard_map/ppermute | solution.py:39
  7.7 16.0 %collective-permute-start = (bf16[256,512]{1,0:T(8,128)(2,1)S(1)}, bf16[256,512]{1,0:T(8,128)(2,1)S(1)}, u32[]{:S(2)}, u32[]{:S(2)}) collective-permute-start(bf16[256,512]{1,0:T(8,128)(2,1)S(1)} %get-tuple-element.39.own_ref), channel_id=1, source_target_pairs={{0,1},{1,2},{2,3},{3,4},{4,5},{5,6},{6,7},{7,8},{8,9},{9,10},{10,1... | collective-permute-start | bytes 786440 | tf_op jit(solution)/shard_map/ppermute | solution.py:39
  11.1 9.1 %collective-permute-start.2 = (bf16[256,256]{1,0:T(8,128)(2,1)S(1)}, bf16[256,256]{1,0:T(8,128)(2,1)S(1)}, u32[]{:S(2)}, u32[]{:S(2)}) collective-permute-start(bf16[256,256]{1,0:T(8,128)(2,1)S(1)} %get-tuple-element.81.own_ref), channel_id=1, source_target_pairs={{0,1},{1,2},{2,3},{3,4},{4,5},{5,6},{6,7},{7,8},{8,9},{9,10},{10,1... | collective-permute-start | bytes 393224 | tf_op jit(solution)/shard_map/ppermute | solution.py:39
  15.3 13.4 %collective-permute-start.5 = (bf16[2,256,256]{2,1,0:T(8,128)(2,1)}, bf16[2,256,256]{2,1,0:T(8,128)(2,1)S(1)}, u32[]{:S(2)}, u32[]{:S(2)}) collective-permute-start(bf16[2,256,256]{2,1,0:T(8,128)(2,1)} %pad_maximum_fusion.3), channel_id=1, source_target_pairs={{0,2},{1,3},{2,4},{3,5},{4,6},{5,7},{6,8},{7,9},{8,10},{9,11},{10,... | collective-permute-start | bytes 786440 | tf_op jit(solution)/shard_map/ppermute | solution.py:39
  20.2 17.0 %collective-permute-start.3 = (bf16[2,256,256]{2,1,0:T(8,128)(2,1)S(1)}, bf16[2,256,256]{2,1,0:T(8,128)(2,1)S(1)}, u32[]{:S(2)}, u32[]{:S(2)}) collective-permute-start(bf16[2,256,256]{2,1,0:T(8,128)(2,1)S(1)} %pad_maximum_fusion.2), channel_id=1, source_target_pairs={{0,2},{1,3},{2,4},{3,5},{4,6},{5,7},{6,8},{7,9},{8,10},{9,11},{10,... | collective-permute-start | bytes 786440 | tf_op jit(solution)/shard_map/ppermute | solution.py:39
  24.7 23.2 %collective-permute-start.1 = (bf16[2,256,512]{2,1,0:T(8,128)(2,1)S(1)}, bf16[2,256,512]{2,1,0:T(8,128)(2,1)S(1)}, u32[]{:S(2)}, u32[]{:S(2)}) collective-permute-start(bf16[2,256,512]{2,1,0:T(8,128)(2,1)S(1)} %pad_maximum_fusion), channel_id=1, source_target_pairs={{0,2},{1,3},{2,4},{3,5},{4,6},{5,7},{6,8},{7,9},{8,10},{9,11},{10,... | collective-permute-start | bytes 1572872 | tf_op jit(solution)/shard_map/ppermute | solution.py:39
  37.2 10.7 %copy-start.1 = (bf16[256,4096]{1,0:T(8,128)(2,1)S(1)}, bf16[256,4096]{1,0:T(8,128)(2,1)}, u32[]{:S(2)}) copy-start(bf16[256,4096]{1,0:T(8,128)(2,1)} %g_ref.7) | copy-start | bytes 6291460
  46.0 18.5 %collective-permute-start.6 = (bf16[2,256,512]{2,1,0:T(8,128)(2,1)S(1)}, bf16[2,256,512]{2,1,0:T(8,128)(2,1)S(1)}, u32[]{:S(2)}, u32[]{:S(2)}) collective-permute-start(bf16[2,256,512]{2,1,0:T(8,128)(2,1)S(1)} %get-tuple-element.37), channel_id=1, source_target_pairs={{2,0},{3,1},{4,2},{5,3},{6,4},{7,5},{8,6},{9,7},{10,8},{11,9},{12,... | collective-permute-start | bytes 1572872 | tf_op jit(solution)/shard_map/ppermute | solution.py:39
  55.6 18.9 %collective-permute-start.8 = (bf16[2,256,256]{2,1,0:T(8,128)(2,1)S(1)}, bf16[2,256,256]{2,1,0:T(8,128)(2,1)S(1)}, u32[]{:S(2)}, u32[]{:S(2)}) collective-permute-start(bf16[2,256,256]{2,1,0:T(8,128)(2,1)S(1)} %get-tuple-element.51), channel_id=1, source_target_pairs={{2,0},{3,1},{4,2},{5,3},{6,4},{7,5},{8,6},{9,7},{10,8},{11,9},{12,... | collective-permute-start | bytes 786440 | tf_op jit(solution)/shard_map/ppermute | solution.py:39
  64.8 11.3 %collective-permute-start.7 = (bf16[256,512]{1,0:T(8,128)(2,1)S(1)}, bf16[256,512]{1,0:T(8,128)(2,1)S(1)}, u32[]{:S(2)}, u32[]{:S(2)}) collective-permute-start(bf16[256,512]{1,0:T(8,128)(2,1)S(1)} %get-tuple-element.50), channel_id=1, source_target_pairs={{1,0},{2,1},{3,2},{4,3},{5,4},{6,5},{7,6},{8,7},{9,8},{10,9},{11,1... | collective-permute-start | bytes 786440 | tf_op jit(solution)/shard_map/ppermute | solution.py:39
  76.1 10.4 %collective-permute-start.9 = (bf16[2,256,256]{2,1,0:T(8,128)(2,1)S(1)}, bf16[2,256,256]{2,1,0:T(8,128)(2,1)S(1)}, u32[]{:S(2)}, u32[]{:S(2)}) collective-permute-start(bf16[2,256,256]{2,1,0:T(8,128)(2,1)S(1)} %get-tuple-element.54), channel_id=1, source_target_pairs={{2,0},{3,1},{4,2},{5,3},{6,4},{7,5},{8,6},{9,7},{10,8},{11,9},{12,... | collective-permute-start | bytes 786440 | tf_op jit(solution)/shard_map/ppermute | solution.py:39
  86.6 11.3 %collective-permute-start.10 = (bf16[256,512]{1,0:T(8,128)(2,1)S(1)}, bf16[256,512]{1,0:T(8,128)(2,1)S(1)}, u32[]{:S(2)}, u32[]{:S(2)}) collective-permute-start(bf16[256,512]{1,0:T(8,128)(2,1)S(1)} %pad_maximum_fusion.4), channel_id=1, source_target_pairs={{1,0},{2,1},{3,2},{4,3},{5,4},{6,5},{7,6},{8,7},{9,8},{10,9},{11,1... | collective-permute-start | bytes 786440 | tf_op jit(solution)/shard_map/ppermute | solution.py:39

commit v11 on v10

--- a/solution.py
+++ b/solution.py
@@ -17,7 +17,8 @@
 ROWS = 32
 UNIT = 4
 FORWARD = ((0,), (1,), (2, 3))
-BACKWARD = ((0, 1), (2,), (3,))
+OUTS = 5
+SCRATCH = 30
 MASKED = -1e30
 SCALE = 1.0 / math.sqrt(HEAD_SIZE)
 EXP2_SCALE = SCALE * math.log2(math.e)
@@ -67,24 +68,38 @@
         bias_ref[:, part * 128 : (part + 1) * 128] = jnp.where(allowed, 0.0, MASKED)
 
 
-def attention_kernel(places, first_ref, lengths_ref, q_ref, g_ref, behind_ref, near_ref, own_ref, *refs):
+def attention_kernel(where, leads, first_ref, lengths_ref, q_ref, g_ref, behind_ref, near_ref, own_ref, *refs):
+    if not leads:
+        bias_ref, old_ref, cut_ref, *refs = refs
+    made = 3 if leads else 0
+    out_ref, dq_ref, dbehind_ref, dnear_ref, down_ref, *masks = refs[-(OUTS + SCRATCH + made) : -SCRATCH]
+    if leads:
+        bias_ref, old_ref, cut_ref = masks
     (
-        out_ref, dq_ref, dbehind_ref, dnear_ref, down_ref,
-        bias_ref, old_ref, cut_ref,
         key_ref, value_ref, key_t_ref, value_t_ref, key2_ref, value2_ref, key2_t_ref, value2_t_ref,
         dk_ref, dv_ref, dk2_ref, dv2_ref, *slots,
-    ) = refs[-33:]
+    ) = refs[-SCRATCH:]
+    slots, copies = slots[:13], slots[13:]
     s_refs, p_refs, dp_refs, d_refs, g_refs, delta_refs = (slots[i : i + 2] for i in range(0, 12, 2))
     (inv_ref,) = slots[12:]
-    rows = q_ref.shape[0]
+    head, *offsets = where
+    key_in, value_in, key_out, value_out = (slice(at, at + HEAD_SIZE) for at in offsets)
+    q_full_ref, g_full_ref, out_full_ref, dq_full_ref = q_ref, g_ref, out_ref, dq_ref
+    q_ref, g_ref, out_ref, dq_ref, sem = copies
+    rows, wide = q_ref.shape
+    mine = slice(head * wide, (head + 1) * wide)
+    q_copy = pltpu.make_async_copy(q_full_ref.at[:, mine], q_ref, sem.at[0])
+    g_copy = pltpu.make_async_copy(g_full_ref.at[:, mine], g_ref, sem.at[1])
+    q_copy.start()
+    g_copy.start()
     window = (SPAN - 1) * rows
     units = GROUP // UNIT
-    key_in, value_in, key_out, value_out = (slice(at, at + HEAD_SIZE) for at in places)
     stack = UNIT * rows
     two = slice(0, rows)
     rest = slice(rows, window)
 
-    write_masks(bias_ref, old_ref, cut_ref, lengths_ref, first_ref, rows)
+    if leads:
+        write_masks(bias_ref, old_ref, cut_ref, lengths_ref, first_ref, rows)
     from_far = lax.broadcasted_iota(jnp.int32, (rows, HEAD_SIZE), 0) >= cut_ref[0, 0]
     mid, far, near, own = behind_ref.at[0], behind_ref.at[1], near_ref, own_ref
     for j, block in enumerate((mid, near)):
@@ -100,8 +115,6 @@
             span = slice(j * HEAD_SIZE, (j + 1) * HEAD_SIZE)
             plain_ref[:, span] = block
             turned_ref[span] = block.T
-    for ref in (dk_ref, dv_ref, dk2_ref, dv2_ref):
-        ref[...] = jnp.zeros_like(ref)
 
     def places(unit):
         return [
@@ -166,12 +179,25 @@
             dq_ref[:, cols] = (total[here] * SCALE).astype(jnp.bfloat16)
         q = stacked(q_ref, unit)
         g = g_refs[slot][...]
-        dk2_ref[...] += dot(doubled(q).T, d_ref[:, two])
-        dk_ref[...] += dot(q.T, d_ref[:, rest])
-        dv2_ref[...] += dot(doubled(g).T, p_ref[:, two])
-        dv_ref[...] += dot(g.T, p_ref[:, rest])
-
+        for total_ref, left, right in (
+            (dk2_ref, doubled(q), d_ref[:, two]),
+            (dk_ref, q, d_ref[:, rest]),
+            (dv2_ref, doubled(g), p_ref[:, two]),
+            (dv_ref, g, p_ref[:, rest]),
+        ):
+            term = dot(left.T, right)
+            total_ref[...] = term if unit == 0 else total_ref[...] + term
+
+    def send(unit, scratch_ref, full_ref, at):
+        part = slice(unit * UNIT * HEAD_SIZE, (unit + 1) * UNIT * HEAD_SIZE)
+        place = slice(head * wide + part.start, head * wide + part.stop)
+        copy = pltpu.make_async_copy(scratch_ref.at[:, part], full_ref.at[:, place], sem.at[at])
+        copy.start()
+        return copy
+
+    q_copy.wait()
     scores(0, 0)
+    sent = []
     for unit in range(units):
         slot = unit % 2
         if unit + 1 < units:
@@ -181,9 +207,14 @@
         softmax(slot)
         if unit > 0:
             spread(unit - 1, 1 - slot)
+            sent.append(send(unit - 1, dq_ref, dq_full_ref, 2 + 2 * (unit - 1)))
+        if unit == 0:
+            g_copy.wait()
         mix(unit, slot)
+        sent.append(send(unit, out_ref, out_full_ref, 3 + 2 * unit))
     score_grad((units - 1) % 2)
     spread(units - 1, (units - 1) % 2)
+    sent.append(send(units - 1, dq_ref, dq_full_ref, 2 * units))
     for span, grad, grad2, scale in ((key_out, dk_ref, dk2_ref, SCALE), (value_out, dv_ref, dv2_ref, 1.0)):
         either = grad2[:HEAD_SIZE].T * scale
         own = grad2[HEAD_SIZE:].T * scale
@@ -191,50 +222,57 @@
         dbehind_ref[1, :, span] = jnp.where(from_far, either, 0.0).astype(jnp.bfloat16)
         dnear_ref[:, span] = grad[:, rows:].T * scale
         down_ref[:, span] = own + jnp.where(from_far, 0.0, either)
-
-
-def attention(head, first, lengths, queries, out_grad, blocks, place, grads, parts, back, back_place):
+    for copy in sent:
+        copy.wait()
+
+
+def attention(head, first, lengths, queries, out_grad, blocks, place, grads, masks):
     rows = queries.shape[0]
     wide = GROUP * HEAD_SIZE
     pair = 2 * HEAD_SIZE
     window = (SPAN - 1) * rows
-    query_spec = pl.BlockSpec((rows, wide), lambda i, *_: (0, head))
-
-    def pair_specs(heads, at):
-        one = pl.BlockSpec((rows, heads * pair), lambda i, *_: (0, at))
-        return [pl.BlockSpec((2, rows, heads * pair), lambda i, *_: (0, 0, at)), one, one]
-
+    leads = masks is None
+    query_spec = pl.BlockSpec(memory_space=pl.ANY)
+
+    def whole(shape):
+        return pl.BlockSpec(shape, lambda i, *_: (0,) * len(shape))
+
+    mask_shapes = ((rows, window), (rows, HEAD_SIZE), (8, HEAD_SIZE))
+    mask_specs = [whole(shape) for shape in mask_shapes]
     fore = blocks[-1].shape[1] // pair
-    places = [at * HEAD_SIZE for at in (place, fore + place, 0, 1)]
+    where = [head, *(at * HEAD_SIZE for at in (place, fore + place, 0, 1))]
     operands = [first, lengths, queries, out_grad, *blocks]
-    in_specs = [query_spec] * 2 + pair_specs(fore, 0)
+    in_specs = [query_spec] * 2 + [whole(block.shape) for block in blocks]
     aliases = {}
-    for at, array in enumerate((*grads, *parts)):
+    if not leads:
+        operands += masks
+        in_specs += mask_specs
+    for at, array in enumerate(grads):
         if array is not None:
             aliases[len(operands)] = at
             operands.append(array)
             in_specs.append(pl.BlockSpec(memory_space=pl.ANY))
     bf16, f32 = jnp.bfloat16, jnp.float32
     results = pl.pallas_call(
-        functools.partial(attention_kernel, places),
+        functools.partial(attention_kernel, where, leads),
         out_shape=[
             jax.ShapeDtypeStruct(queries.shape, bf16),
             jax.ShapeDtypeStruct(queries.shape, bf16),
-            jax.ShapeDtypeStruct((2, rows, back * pair), bf16),
-            jax.ShapeDtypeStruct((rows, back * pair), f32),
-            jax.ShapeDtypeStruct((rows, back * pair), f32),
-        ],
+            jax.ShapeDtypeStruct((2, rows, pair), bf16),
+            jax.ShapeDtypeStruct((rows, pair), f32),
+            jax.ShapeDtypeStruct((rows, pair), f32),
+        ]
+        + [jax.ShapeDtypeStruct(*mask) for mask in zip(mask_shapes, (f32, f32, jnp.int32)) if leads],
         grid_spec=pltpu.PrefetchScalarGridSpec(
             num_scalar_prefetch=2,
             grid=(1,),
             in_specs=in_specs,
-            out_specs=[query_spec] * 2 + pair_specs(1, back_place),
+            out_specs=[query_spec] * 2
+            + [whole((2, rows, pair)), whole((rows, pair)), whole((rows, pair))]
+            + (mask_specs if leads else []),
             scratch_shapes=[
                 pltpu.VMEM(shape, kind)
                 for shape, kind, count in (
-                    ((rows, window), f32, 1),
-                    ((rows, HEAD_SIZE), f32, 1),
-                    ((8, HEAD_SIZE), jnp.int32, 1),
                     ((2 * rows, HEAD_SIZE), bf16, 2),
                     ((HEAD_SIZE, 2 * rows), bf16, 2),
                     ((rows, pair), bf16, 2),
@@ -250,7 +288,9 @@
                     ((UNIT * rows, HEAD_SIZE), f32, 1),
                 )
                 for _ in range(count)
-            ],
+            ]
+            + [pltpu.VMEM((rows, wide), bf16)] * 4
+            + [pltpu.SemaphoreType.DMA((2 + 2 * GROUP // UNIT,))],
         ),
         input_output_aliases=aliases,
         compiler_params=pltpu.CompilerParams(vmem_limit_bytes=48 * 1024 * 1024),
@@ -261,7 +301,26 @@
         ),
         name="attention",
     )(*operands)
-    return results[:2], results[2:]
+    return results[:2], results[2:OUTS], results[OUTS:] if leads else masks
+
+
+def pack_kernel(keys_ref, values_ref, *out_refs):
+    for heads, out_ref in zip(FORWARD, out_refs):
+        span = slice(heads[0] * HEAD_SIZE, (heads[-1] + 1) * HEAD_SIZE)
+        width = span.stop - span.start
+        out_ref[:, :width] = keys_ref[:, span]
+        out_ref[:, width:] = values_ref[:, span]
+
+
+def pack(keys, values):
+    rows = keys.shape[0]
+    return pl.pallas_call(
+        pack_kernel,
+        out_shape=[
+            jax.ShapeDtypeStruct((rows, 2 * HEAD_SIZE * len(heads)), keys.dtype) for heads in FORWARD
+        ],
+        name="pack",
+    )(keys, values)
 
 
 def local(queries, keys, values, out_grad, doc_lengths):
@@ -269,52 +328,62 @@
     index = lax.axis_index(AXES)
     first = (index * rows).astype(jnp.int32).reshape(1)
     bf16, f32 = jnp.bfloat16, jnp.float32
-    blocks = {}
-    owns, nears = [], []
-    for heads in FORWARD:
-        span = slice(heads[0] * HEAD_SIZE, (heads[-1] + 1) * HEAD_SIZE)
-        owns.append(jnp.concatenate([keys[:, span], values[:, span]], axis=1))
+    blocks, nears = {}, []
+    owns = pack(keys, values)
     for own in owns:
         nears.append(passed_along(own, 1))
-    for heads, own, near in zip(FORWARD, owns, nears):
-        behind = passed_along(jnp.stack([own, near]), 2)
+    pairs = [jnp.stack([own, near]) for own, near in zip(owns, nears)]
+    for heads, own, near, pair in zip(FORWARD, owns, nears, pairs):
+        behind = passed_along(pair, 2)
         for place, head in enumerate(heads):
             blocks[head] = ((behind, near, own), place)
-    grads = (None, None)
-    sent = []
-
-    def second(own, near, got):
+    grads, masks = (None, None), None
+    parts = []
+
+    def attend(head, after=()):
+        nonlocal grads, masks
+        (behind, near, own), place = blocks[head]
+        own, *after = lax.optimization_barrier((own, *after))
+        grads, part, masks = attention(
+            head, first, doc_lengths, queries, out_grad, (behind, near, own), place, grads, masks
+        )
+        parts.append(part)
+        return after
+
+    def first_hop(head):
+        behind, near, own = parts[head]
+        return near, own, passed_along(behind, -2)
+
+    def second_hop(near, own, got):
         got = got.astype(f32)
-        return [own + got[0], (near + got[1]).astype(bf16)]
-
-    for heads in BACKWARD:
-        parts = (None,) * 3
-        for at, head in enumerate(heads):
-            (behind, near, own), place = blocks[head]
-            if head == KEY_VALUE_HEADS - 1:
-                own, *sent[0] = lax.optimization_barrier((own, *sent[0]))
-                last = passed_along(sent[0][1], -1)
-            grads, parts = attention(
-                head, first, doc_lengths, queries, out_grad, (behind, near, own), place, grads, parts, len(heads), at
-            )
-        behind, near, own = parts
-        if heads == BACKWARD[-1]:
-            behind, near, last, middle = lax.optimization_barrier((behind, near, last, sent[1][2]))
-            sent[1] = [*sent[1][:2], middle]
-        sent.append([own, near, passed_along(behind, -2)])
-        if len(sent) == 1:
-            sent[0] = second(*sent[0])
-    rest = [second(*sent[1]), second(*sent[2])]
-    own = [sent[0][0], *(piece[0] for piece in rest)]
-    near = passed_along(jnp.concatenate([piece[1] for piece in rest], axis=1), -1)
-    total = (jnp.concatenate(own, axis=1) + jnp.concatenate([last, near], axis=1).astype(f32)).astype(bf16)
-    parts = [total[:, at : at + HEAD_SIZE] for at in range(0, total.shape[1], HEAD_SIZE)]
-    key_grads, value_grads = parts[0::2], parts[1::2]
+        return (near + got[1]).astype(bf16), own + got[0]
+
+    attend(0, pairs)
+    zero = first_hop(0)
+    attend(1)
+    one = first_hop(1)
+    attend(2)
+    two = first_hop(2)
+    got, _ = lax.optimization_barrier((one[2], parts[2][0]))
+    nears, owns = zip(second_hop(*zero), second_hop(*one[:2], got))
+    nears = jnp.concatenate(nears, axis=1)
+    (nears,) = attend(3, (nears,))
+    early = passed_along(nears, -1)
+    behind, near, own = parts[3]
+    behind, near, own, early, got = lax.optimization_barrier((behind, near, own, early, two[2]))
+    far = passed_along(behind[1], -3)
+    mid = passed_along(behind[0], -2)
+    near_two, own_two = second_hop(two[0], two[1], got)
+    late = passed_along(jnp.concatenate([near_two, near.astype(bf16)], axis=1), -1)
+    own = own + mid.astype(f32) + far.astype(f32)
+    total = jnp.concatenate([*owns, own_two, own], axis=1)
+    total = (total + jnp.concatenate([early, late], axis=1).astype(f32)).astype(bf16)
+    columns = [total[:, at : at + HEAD_SIZE] for at in range(0, total.shape[1], HEAD_SIZE)]
     return (
         grads[0],
         grads[1],
-        jnp.concatenate(key_grads, axis=1),
-        jnp.concatenate(value_grads, axis=1),
+        jnp.concatenate(columns[0::2], axis=1),
+        jnp.concatenate(columns[1::2], axis=1),
     )
 
 

time: 100 us -> 97.4 us (0.974)
  starting transfers between devices: 30.7 us -> 39.3 us
  waiting for transfers between devices: 27.7 us -> 20.2 us
  local copies, waits for them, and re-layouts: 2.91 us -> 0.14 us
  Pallas kernels: 32.8 us -> 31.4 us
    ppermute x11 -> x13, starting transfers between devices: 30.7 us -> 39.3 us  [passed_along(): lax.ppermute(value, AXES, [(source, source + steps) for source in range(f...]
    ppermute x11 -> x13, waiting for transfers between devices: 27.7 us -> 20.2 us  [passed_along(): lax.ppermute(value, AXES, [(source, source + steps) for source in range(f...]
    slice x3 -> x0, local copies, waits for them, and re-layouts: 2.8 us -> none  [local(): owns.append(jnp.concatenate([keys[:, span], values[:, span]], axis=1))]
    pallas_call x4 -> x5, Pallas kernels: 32.8 us -> 31.4 us  [the longest x4 29.3 us: attention(): pl.pallas_call(functools.partial(attention_kernel, where, leads), out_sha...]
    another operation x6 -> x3, other arithmetic: 2.54 us -> 2.86 us  [local(): pairs = [jnp.stack([own, near]) for own, near in zip(owns, nears)]]
  transfers between devices with their start and end apart: 11 -> 13, of which waited for: 5 -> 5; matrix products, arithmetic and copies ran while one was open for 5% -> 3% of each run, Pallas kernels for 33% -> 30%
where the time goes in v11:
time: 97.4 us; the launch traced here: 96.3 us
  starting transfers between devices  39.3 us (40%)
  Pallas kernels  31.4 us (32%)
  waiting for transfers between devices  20.2 us (21%)
  other arithmetic  4.28 us (4%)
  between operations  0.99 us (1%)
    ppermute x13, starting transfers between devices, passed_along(): lax.ppermute(value, AXES, [(source, source + steps) for source in range(f...  39.3 us
    pallas_call x4, Pallas kernels, attention(): pl.pallas_call(functools.partial(attention_kernel, where, leads), out_sha...  29.3 us
    ppermute x13, waiting for transfers between devices, passed_along(): lax.ppermute(value, AXES, [(source, source + steps) for source in range(f...  20.2 us
    another operation x3, other arithmetic, local(): pairs = [jnp.stack([own, near]) for own, near in zip(owns, nears)]  2.86 us
    pallas_call x1, Pallas kernels, pack(): pl.pallas_call(pack_kernel, out_shape=[jax.ShapeDtypeStruct((rows, 2 * HE...  2.01 us
  transfers between devices with their start and end apart: 13, of which 5 were waited for; matrix products, arithmetic and copies ran while one was open for 3% of the time, Pallas kernels for 30%

profile of v11, /device:TPU:29, one launch (start us, length us, event | category | flops | bytes accessed | tf_op | source)
XLA Modules:
  0.0 96.3 jit_solution(10855713530637970834)
XLA Ops:
  0.7 2.0 %pack.1 = (bf16[256,256]{1,0:T(8,128)(2,1)}, bf16[256,256]{1,0:T(8,128)(2,1)}, bf16[256,512]{1,0:T(8,128)(2,1)}) custom-call(bf16[256,512]{1,0:T(8,128)(2,1)} %keys_ref.1, bf16[256,512]{1,0:T(8,128)(2,1)} %values_ref.1), custom_call_target="tpu_custom_call" | custom-call | tf_op jit(solution)/shard_map/pack/pallas_call | solution.py:317
  2.7 3.4 %collective-permute-start.2 = (bf16[256,256]{1,0:T(8,128)(2,1)}, bf16[256,256]{1,0:T(8,128)(2,1)S(1)}, u32[]{:S(2)}, u32[]{:S(2)}) collective-permute-start(bf16[256,256]{1,0:T(8,128)(2,1)} %get-tuple-element.42.own_ref), channel_id=1, source_target_pairs={{0,1},{1,2},{2,3},{3,4},{4,5},{5,6},{6,7},{7,8},{8,9},{9,10},{10,1... | collective-permute-start | bytes 393224 | tf_op jit(solution)/shard_map/ppermute | solution.py:40
  6.1 3.4 %collective-permute-start = (bf16[256,512]{1,0:T(8,128)(2,1)}, bf16[256,512]{1,0:T(8,128)(2,1)S(1)}, u32[]{:S(2)}, u32[]{:S(2)}) collective-permute-start(bf16[256,512]{1,0:T(8,128)(2,1)} %get-tuple-element.56.own_ref), channel_id=1, source_target_pairs={{0,1},{1,2},{2,3},{3,4},{4,5},{5,6},{6,7},{7,8},{8,9},{9,10},{10,1... | collective-permute-start | bytes 786440 | tf_op jit(solution)/shard_map/ppermute | solution.py:40
  9.5 3.4 %collective-permute-start.4 = (bf16[256,256]{1,0:T(8,128)(2,1)}, bf16[256,256]{1,0:T(8,128)(2,1)S(1)}, u32[]{:S(2)}, u32[]{:S(2)}) collective-permute-start(bf16[256,256]{1,0:T(8,128)(2,1)} %get-tuple-element.41.own_ref), channel_id=1, source_target_pairs={{0,1},{1,2},{2,3},{3,4},{4,5},{5,6},{6,7},{7,8},{8,9},{9,10},{10,1... | collective-permute-start | bytes 393224 | tf_op jit(solution)/shard_map/ppermute | solution.py:40
  13.0 0.9 pad_maximum_fusion.1
  13.9 3.5 %collective-permute-start.3 = (bf16[2,256,256]{2,1,0:T(8,128)(2,1)S(1)}, bf16[2,256,256]{2,1,0:T(8,128)(2,1)S(1)}, u32[]{:S(2)}, u32[]{:S(2)}) collective-permute-start(bf16[2,256,256]{2,1,0:T(8,128)(2,1)S(1)} %pad_maximum_fusion.1), channel_id=1, source_target_pairs={{0,2},{1,3},{2,4},{3,5},{4,6},{5,7},{6,8},{7,9},{8,10},{9,11},{10,... | collective-permute-start | bytes 786440 | tf_op jit(solution)/shard_map/ppermute | solution.py:40
  17.4 1.5 %collective-permute-done.4.near_ref = bf16[256,256]{1,0:T(8,128)(2,1)S(1)} collective-permute-done((bf16[256,256]{1,0:T(8,128)(2,1)}, bf16[256,256]{1,0:T(8,128)(2,1)S(1)}, u32[]{:S(2)}, u32[]{:S(2)}) %collective-permute-start.4) | collective-permute-done | bytes 131104 | tf_op jit(solution)/shard_map/ppermute | solution.py:40
  18.9 0.9 pad_maximum_fusion.2
  19.8 3.8 %collective-permute-start.6 = (bf16[2,256,256]{2,1,0:T(8,128)(2,1)S(1)}, bf16[2,256,256]{2,1,0:T(8,128)(2,1)S(1)}, u32[]{:S(2)}, u32[]{:S(2)}) collective-permute-start(bf16[2,256,256]{2,1,0:T(8,128)(2,1)S(1)} %pad_maximum_fusion.2), channel_id=1, source_target_pairs={{0,2},{1,3},{2,4},{3,5},{4,6},{5,7},{6,8},{7,9},{8,10},{9,11},{10,... | collective-permute-start | bytes 786440 | tf_op jit(solution)/shard_map/ppermute | solution.py:40
  23.6 1.0 %pad_maximum_fusion = bf16[2,256,512]{2,1,0:T(8,128)(2,1)S(1)} fusion(bf16[1,256,512]{2,1,0:T(8,128)(2,1)S(1)} %bitcast.42, bf16[1,256,512]{2,1,0:T(8,128)(2,1)} %bitcast.41), kind=kLoop, calls=%fused_computation.2 | loop fusion | flops 262144 | bytes 1048576 | tf_op jit(solution)/shard_map/stack | solution.py:335
  24.6 3.7 %collective-permute-start.1 = (bf16[2,256,512]{2,1,0:T(8,128)(2,1)S(1)}, bf16[2,256,512]{2,1,0:T(8,128)(2,1)S(1)}, u32[]{:S(2)}, u32[]{:S(2)}) collective-permute-start(bf16[2,256,512]{2,1,0:T(8,128)(2,1)S(1)} %pad_maximum_fusion), channel_id=1, source_target_pairs={{0,2},{1,3},{2,4},{3,5},{4,6},{5,7},{6,8},{7,9},{8,10},{9,11},{10,... | collective-permute-start | bytes 1572872 | tf_op jit(solution)/shard_map/ppermute | solution.py:40
  28.3 7.7 %attention.4 = (bf16[256,4096]{1,0:T(8,128)(2,1)}, bf16[256,4096]{1,0:T(8,128)(2,1)}, bf16[2,256,256]{2,1,0:T(8,128)(2,1)S(1)}, f32[256,256]{1,0:T(8,128)S(1)}, ...) custom-call(s32[1]{0:T(128)} %bitcast.first_ref, ...), custom_call_target="tpu_custom_call" | custom-call | flops 4831838208 | bytes 3538944 | tf_op jit(solution)/shard_map/attention/pallas_call | solution.py:256
  36.1 2.1 %collective-permute-start.5 = (bf16[2,256,256]{2,1,0:T(8,128)(2,1)S(1)}, bf16[2,256,256]{2,1,0:T(8,128)(2,1)S(1)}, u32[]{:S(2)}, u32[]{:S(2)}) collective-permute-start(bf16[2,256,256]{2,1,0:T(8,128)(2,1)S(1)} %get-tuple-element.44), channel_id=1, source_target_pairs={{2,0},{3,1},{4,2},{5,3},{6,4},{7,5},{8,6},{9,7},{10,8},{11,9},{12,... | collective-permute-start | bytes 786440 | tf_op jit(solution)/shard_map/ppermute | solution.py:40
  38.2 7.2 %attention.5 = (bf16[256,4096]{1,0:T(8,128)(2,1)}, bf16[256,4096]{1,0:T(8,128)(2,1)}, bf16[2,256,256]{2,1,0:T(8,128)(2,1)S(1)}, f32[256,256]{1,0:T(8,128)S(1)}, f32[256,256]{1,0:T(8,128)S(1)}) custom-call(s32[1]{0:T(128)} %bitcast.first_ref, s32[16]{0:T(128)S(1)} %copy-done.4, ...), custom_call_target="tpu_custom_call", output_to_operand_aliasing={{0}: (10, {}), {1}: (11, {})} | custom-call | flops 4831838208 | bytes 3538944 | tf_op jit(solution)/shard_map/attention/pallas_call | solution.py:256
  45.4 2.3 %collective-permute-start.7 = (bf16[2,256,256]{2,1,0:T(8,128)(2,1)S(1)}, bf16[2,256,256]{2,1,0:T(8,128)(2,1)S(1)}, u32[]{:S(2)}, u32[]{:S(2)}) collective-permute-start(bf16[2,256,256]{2,1,0:T(8,128)(2,1)S(1)} %get-tuple-element.51), channel_id=1, source_target_pairs={{2,0},{3,1},{4,2},{5,3},{6,4},{7,5},{8,6},{9,7},{10,8},{11,9},{12,... | collective-permute-start | bytes 786440 | tf_op jit(solution)/shard_map/ppermute | solution.py:40
  47.7 0.1 collective-permute-done.5
  47.8 0.1 fusion.5
  47.9 7.2 %attention.6 = (bf16[256,4096]{1,0:T(8,128)(2,1)}, bf16[256,4096]{1,0:T(8,128)(2,1)}, bf16[2,256,256]{2,1,0:T(8,128)(2,1)S(1)}, f32[256,256]{1,0:T(8,128)S(1)}, f32[256,256]{1,0:T(8,128)S(1)}) custom-call(s32[1]{0:T(128)} %bitcast.first_ref, s32[16]{0:T(128)S(1)} %copy-done.4, ...), custom_call_target="tpu_custom_call", output_to_operand_aliasing={{0}: (10, {}), {1}: (11, {})} | custom-call | flops 4831838208 | bytes 3538944 | tf_op jit(solution)/shard_map/attention/pallas_call | solution.py:256
  55.1 1.9 %collective-permute-start.9 = (bf16[2,256,256]{2,1,0:T(8,128)(2,1)S(1)}, bf16[2,256,256]{2,1,0:T(8,128)(2,1)S(1)}, u32[]{:S(2)}, u32[]{:S(2)}) collective-permute-start(bf16[2,256,256]{2,1,0:T(8,128)(2,1)S(1)} %get-tuple-element.54), channel_id=1, source_target_pairs={{2,0},{3,1},{4,2},{5,3},{6,4},{7,5},{8,6},{9,7},{10,8},{11,9},{12,... | collective-permute-start | bytes 786440 | tf_op jit(solution)/shard_map/ppermute | solution.py:40
  57.1 0.1 fusion.4
  57.2 6.1 %collective-permute-start.8 = (bf16[256,512]{1,0:T(8,128)(2,1)S(1)}, bf16[256,512]{1,0:T(8,128)(2,1)S(1)}, u32[]{:S(2)}, u32[]{:S(2)}) collective-permute-start(bf16[256,512]{1,0:T(8,128)(2,1)S(1)} %pad_maximum_fusion.3), channel_id=1, source_target_pairs={{1,0},{2,1},{3,2},{4,3},{5,4},{6,5},{7,6},{8,7},{9,8},{10,9},{11,1... | collective-permute-start | bytes 786440 | tf_op jit(solution)/shard_map/ppermute | solution.py:40
  63.3 7.2 %attention.7 = (bf16[256,4096]{1,0:T(8,128)(2,1)}, bf16[256,4096]{1,0:T(8,128)(2,1)}, bf16[2,256,256]{2,1,0:T(8,128)(2,1)S(1)}, f32[256,256]{1,0:T(8,128)S(1)}, f32[256,256]{1,0:T(8,128)S(1)}) custom-call(s32[1]{0:T(128)} %bitcast.first_ref, s32[16]{0:T(128)S(1)} %copy-done.4, ...), custom_call_target="tpu_custom_call", output_to_operand_aliasing={{0}: (10, {}), {1}: (11, {})} | custom-call | flops 4831838208 | bytes 3538944 | tf_op jit(solution)/shard_map/attention/pallas_call | solution.py:256
  70.5 6.1 %collective-permute-done.8 = bf16[256,512]{1,0:T(8,128)(2,1)S(1)} collective-permute-done((bf16[256,512]{1,0:T(8,128)(2,1)S(1)}, bf16[256,512]{1,0:T(8,128)(2,1)S(1)}, u32[]{:S(2)}, u32[]{:S(2)}) %collective-permute-start.8) | collective-permute-done | bytes 262176 | tf_op jit(solution)/shard_map/ppermute | solution.py:40
  76.7 1.9 %collective-permute-start.10 = (bf16[256,256]{1,0:T(8,128)(2,1)S(1)}, bf16[256,256]{1,0:T(8,128)(2,1)S(1)}, u32[]{:S(2)}, u32[]{:S(2)}) collective-permute-start(bf16[256,256]{1,0:T(8,128)(2,1)S(1)} %get-tuple-element.88), channel_id=1, source_target_pairs={{2,0},{3,1},{4,2},{5,3},{6,4},{7,5},{8,6},{9,7},{10,8},{11,9},{12,... | collective-permute-start | bytes 393224 | tf_op jit(solution)/shard_map/ppermute | solution.py:40
  78.7 1.9 %collective-permute-start.11 = (bf16[256,256]{1,0:T(8,128)(2,1)S(1)}, bf16[256,256]{1,0:T(8,128)(2,1)S(1)}, u32[]{:S(2)}, u32[]{:S(2)}) collective-permute-start(bf16[256,256]{1,0:T(8,128)(2,1)S(1)} %get-tuple-element.89), channel_id=1, source_target_pairs={{3,0},{4,1},{5,2},{6,3},{7,4},{8,5},{9,6},{10,7},{11,8},{12,9},{13... | collective-permute-start | bytes 393224 | tf_op jit(solution)/shard_map/ppermute | solution.py:40
  80.6 0.1 fusion.2
  80.7 1.9 %collective-permute-start.12 = (bf16[256,512]{1,0:T(8,128)(2,1)S(1)}, bf16[256,512]{1,0:T(8,128)(2,1)S(1)}, u32[]{:S(2)}, u32[]{:S(2)}) collective-permute-start(bf16[256,512]{1,0:T(8,128)(2,1)S(1)} %pad_maximum_fusion.4), channel_id=1, source_target_pairs={{1,0},{2,1},{3,2},{4,3},{5,4},{6,5},{7,6},{8,7},{9,8},{10,9},{11,1... | collective-permute-start | bytes 786440 | tf_op jit(solution)/shard_map/ppermute | solution.py:40
  82.6 4.7 %collective-permute-done.10 = bf16[256,256]{1,0:T(8,128)(2,1)S(1)} collective-permute-done((bf16[256,256]{1,0:T(8,128)(2,1)S(1)}, bf16[256,256]{1,0:T(8,128)(2,1)S(1)}, u32[]{:S(2)}, u32[]{:S(2)}) %collective-permute-start.10) | collective-permute-done | bytes 131104 | tf_op jit(solution)/shard_map/ppermute | solution.py:40
  87.3 7.8 %collective-permute-done.11 = bf16[256,256]{1,0:T(8,128)(2,1)S(1)} collective-permute-done((bf16[256,256]{1,0:T(8,128)(2,1)S(1)}, bf16[256,256]{1,0:T(8,128)(2,1)S(1)}, u32[]{:S(2)}, u32[]{:S(2)}) %collective-permute-start.11) | collective-permute-done | bytes 131104 | tf_op jit(solution)/shard_map/ppermute | solution.py:40
  95.2 0.1 fusion
  95.4 0.1 fusion.10
  95.5 0.9 pad_maximum_fusion.5
  (26 shorter events, 0.3 us)
Async XLA Ops:
  0.6 27.7 %copy-start.4 = (s32[16]{0:T(128)S(1)}, s32[16]{0:T(128)}, u32[]{:S(2)}) copy-start(s32[16]{0:T(128)} %lengths_ref.7) | copy-start | bytes 196
  0.6 27.7 %copy-start.3 = (bf16[256,4096]{1,0:T(8,128)(2,1)S(1)}, bf16[256,4096]{1,0:T(8,128)(2,1)}, u32[]{:S(2)}) copy-start(bf16[256,4096]{1,0:T(8,128)(2,1)} %q_ref.7) | copy-start | bytes 6291460
  2.7 25.7 %copy-start.2 = (bf16[256,256]{1,0:T(8,128)(2,1)S(1)}, bf16[256,256]{1,0:T(8,128)(2,1)}, u32[]{:S(2)}) copy-start(bf16[256,256]{1,0:T(8,128)(2,1)} %get-tuple-element.42.own_ref) | copy-start | bytes 393220
  2.7 10.3 %collective-permute-start.2 = (bf16[256,256]{1,0:T(8,128)(2,1)}, bf16[256,256]{1,0:T(8,128)(2,1)S(1)}, u32[]{:S(2)}, u32[]{:S(2)}) collective-permute-start(bf16[256,256]{1,0:T(8,128)(2,1)} %get-tuple-element.42.own_ref), channel_id=1, source_target_pairs={{0,1},{1,2},{2,3},{3,4},{4,5},{5,6},{6,7},{7,8},{8,9},{9,10},{10,1... | collective-permute-start | bytes 393224 | tf_op jit(solution)/shard_map/ppermute | solution.py:40
  6.1 17.5 %collective-permute-start = (bf16[256,512]{1,0:T(8,128)(2,1)}, bf16[256,512]{1,0:T(8,128)(2,1)S(1)}, u32[]{:S(2)}, u32[]{:S(2)}) collective-permute-start(bf16[256,512]{1,0:T(8,128)(2,1)} %get-tuple-element.56.own_ref), channel_id=1, source_target_pairs={{0,1},{1,2},{2,3},{3,4},{4,5},{5,6},{6,7},{7,8},{8,9},{9,10},{10,1... | collective-permute-start | bytes 786440 | tf_op jit(solution)/shard_map/ppermute | solution.py:40
  9.5 9.3 %collective-permute-start.4 = (bf16[256,256]{1,0:T(8,128)(2,1)}, bf16[256,256]{1,0:T(8,128)(2,1)S(1)}, u32[]{:S(2)}, u32[]{:S(2)}) collective-permute-start(bf16[256,256]{1,0:T(8,128)(2,1)} %get-tuple-element.41.own_ref), channel_id=1, source_target_pairs={{0,1},{1,2},{2,3},{3,4},{4,5},{5,6},{6,7},{7,8},{8,9},{9,10},{10,1... | collective-permute-start | bytes 393224 | tf_op jit(solution)/shard_map/ppermute | solution.py:40
  13.9 14.4 %collective-permute-start.3 = (bf16[2,256,256]{2,1,0:T(8,128)(2,1)S(1)}, bf16[2,256,256]{2,1,0:T(8,128)(2,1)S(1)}, u32[]{:S(2)}, u32[]{:S(2)}) collective-permute-start(bf16[2,256,256]{2,1,0:T(8,128)(2,1)S(1)} %pad_maximum_fusion.1), channel_id=1, source_target_pairs={{0,2},{1,3},{2,4},{3,5},{4,6},{5,7},{6,8},{7,9},{8,10},{9,11},{10,... | collective-permute-start | bytes 786440 | tf_op jit(solution)/shard_map/ppermute | solution.py:40
  19.8 18.4 %collective-permute-start.6 = (bf16[2,256,256]{2,1,0:T(8,128)(2,1)S(1)}, bf16[2,256,256]{2,1,0:T(8,128)(2,1)S(1)}, u32[]{:S(2)}, u32[]{:S(2)}) collective-permute-start(bf16[2,256,256]{2,1,0:T(8,128)(2,1)S(1)} %pad_maximum_fusion.2), channel_id=1, source_target_pairs={{0,2},{1,3},{2,4},{3,5},{4,6},{5,7},{6,8},{7,9},{8,10},{9,11},{10,... | collective-permute-start | bytes 786440 | tf_op jit(solution)/shard_map/ppermute | solution.py:40
  24.6 23.3 %collective-permute-start.1 = (bf16[2,256,512]{2,1,0:T(8,128)(2,1)S(1)}, bf16[2,256,512]{2,1,0:T(8,128)(2,1)S(1)}, u32[]{:S(2)}, u32[]{:S(2)}) collective-permute-start(bf16[2,256,512]{2,1,0:T(8,128)(2,1)S(1)} %pad_maximum_fusion), channel_id=1, source_target_pairs={{0,2},{1,3},{2,4},{3,5},{4,6},{5,7},{6,8},{7,9},{8,10},{9,11},{10,... | collective-permute-start | bytes 1572872 | tf_op jit(solution)/shard_map/ppermute | solution.py:40
  28.3 9.8 %copy-start.1 = (bf16[256,256]{1,0:T(8,128)(2,1)S(1)}, bf16[256,256]{1,0:T(8,128)(2,1)}, u32[]{:S(2)}) copy-start(bf16[256,256]{1,0:T(8,128)(2,1)} %get-tuple-element.41.own_ref) | copy-start | bytes 393220
  36.1 11.7 %collective-permute-start.5 = (bf16[2,256,256]{2,1,0:T(8,128)(2,1)S(1)}, bf16[2,256,256]{2,1,0:T(8,128)(2,1)S(1)}, u32[]{:S(2)}, u32[]{:S(2)}) collective-permute-start(bf16[2,256,256]{2,1,0:T(8,128)(2,1)S(1)} %get-tuple-element.44), channel_id=1, source_target_pairs={{2,0},{3,1},{4,2},{5,3},{6,4},{7,5},{8,6},{9,7},{10,8},{11,9},{12,... | collective-permute-start | bytes 786440 | tf_op jit(solution)/shard_map/ppermute | solution.py:40
  45.4 2.5 %copy-start = (bf16[256,512]{1,0:T(8,128)(2,1)S(1)}, bf16[256,512]{1,0:T(8,128)(2,1)}, u32[]{:S(2)}) copy-start(bf16[256,512]{1,0:T(8,128)(2,1)} %get-tuple-element.56.own_ref) | copy-start | bytes 786436
  45.4 11.6 %collective-permute-start.7 = (bf16[2,256,256]{2,1,0:T(8,128)(2,1)S(1)}, bf16[2,256,256]{2,1,0:T(8,128)(2,1)S(1)}, u32[]{:S(2)}, u32[]{:S(2)}) collective-permute-start(bf16[2,256,256]{2,1,0:T(8,128)(2,1)S(1)} %get-tuple-element.51), channel_id=1, source_target_pairs={{2,0},{3,1},{4,2},{5,3},{6,4},{7,5},{8,6},{9,7},{10,8},{11,9},{12,... | collective-permute-start | bytes 786440 | tf_op jit(solution)/shard_map/ppermute | solution.py:40
  55.1 21.5 %collective-permute-start.9 = (bf16[2,256,256]{2,1,0:T(8,128)(2,1)S(1)}, bf16[2,256,256]{2,1,0:T(8,128)(2,1)S(1)}, u32[]{:S(2)}, u32[]{:S(2)}) collective-permute-start(bf16[2,256,256]{2,1,0:T(8,128)(2,1)S(1)} %get-tuple-element.54), channel_id=1, source_target_pairs={{2,0},{3,1},{4,2},{5,3},{6,4},{7,5},{8,6},{9,7},{10,8},{11,9},{12,... | collective-permute-start | bytes 786440 | tf_op jit(solution)/shard_map/ppermute | solution.py:40
  57.2 19.4 %collective-permute-start.8 = (bf16[256,512]{1,0:T(8,128)(2,1)S(1)}, bf16[256,512]{1,0:T(8,128)(2,1)S(1)}, u32[]{:S(2)}, u32[]{:S(2)}) collective-permute-start(bf16[256,512]{1,0:T(8,128)(2,1)S(1)} %pad_maximum_fusion.3), channel_id=1, source_target_pairs={{1,0},{2,1},{3,2},{4,3},{5,4},{6,5},{7,6},{8,7},{9,8},{10,9},{11,1... | collective-permute-start | bytes 786440 | tf_op jit(solution)/shard_map/ppermute | solution.py:40
  76.7 10.6 %collective-permute-start.10 = (bf16[256,256]{1,0:T(8,128)(2,1)S(1)}, bf16[256,256]{1,0:T(8,128)(2,1)S(1)}, u32[]{:S(2)}, u32[]{:S(2)}) collective-permute-start(bf16[256,256]{1,0:T(8,128)(2,1)S(1)} %get-tuple-element.88), channel_id=1, source_target_pairs={{2,0},{3,1},{4,2},{5,3},{6,4},{7,5},{8,6},{9,7},{10,8},{11,9},{12,... | collective-permute-start | bytes 393224 | tf_op jit(solution)/shard_map/ppermute | solution.py:40
  78.7 16.5 %collective-permute-start.11 = (bf16[256,256]{1,0:T(8,128)(2,1)S(1)}, bf16[256,256]{1,0:T(8,128)(2,1)S(1)}, u32[]{:S(2)}, u32[]{:S(2)}) collective-permute-start(bf16[256,256]{1,0:T(8,128)(2,1)S(1)} %get-tuple-element.89), channel_id=1, source_target_pairs={{3,0},{4,1},{5,2},{6,3},{7,4},{8,5},{9,6},{10,7},{11,8},{12,9},{13... | collective-permute-start | bytes 393224 | tf_op jit(solution)/shard_map/ppermute | solution.py:40
  80.7 14.5 %collective-permute-start.12 = (bf16[256,512]{1,0:T(8,128)(2,1)S(1)}, bf16[256,512]{1,0:T(8,128)(2,1)S(1)}, u32[]{:S(2)}, u32[]{:S(2)}) collective-permute-start(bf16[256,512]{1,0:T(8,128)(2,1)S(1)} %pad_maximum_fusion.4), channel_id=1, source_target_pairs={{1,0},{2,1},{3,2},{4,3},{5,4},{6,5},{7,6},{8,7},{9,8},{10,9},{11,1... | collective-permute-start | bytes 786440 | tf_op jit(solution)/shard_map/ppermute | solution.py:40

commit v12 on v11

--- a/solution.py
+++ b/solution.py
@@ -18,7 +18,7 @@
 UNIT = 4
 FORWARD = ((0,), (1,), (2, 3))
 OUTS = 5
-SCRATCH = 30
+SCRATCH = 32
 MASKED = -1e30
 SCALE = 1.0 / math.sqrt(HEAD_SIZE)
 EXP2_SCALE = SCALE * math.log2(math.e)
@@ -38,6 +38,16 @@
     count = device_count()
     first, last = (max(0, -steps), min(count, count - steps))
     return lax.ppermute(value, AXES, [(source, source + steps) for source in range(first, last)])
+
+
+def next_group(value):
+    groups, inner = lax.axis_size("blk"), lax.axis_size("inner")
+    pairs = [
+        (group * inner + place, (group + 1) * inner + place)
+        for group in range(groups - 1)
+        for place in range(SPAN - 1)
+    ]
+    return lax.ppermute(value, AXES, pairs)
 
 
 def write_masks(bias_ref, old_ref, cut_ref, lengths_ref, first_ref, rows):
@@ -68,7 +78,7 @@
         bias_ref[:, part * 128 : (part + 1) * 128] = jnp.where(allowed, 0.0, MASKED)
 
 
-def attention_kernel(where, leads, first_ref, lengths_ref, q_ref, g_ref, behind_ref, near_ref, own_ref, *refs):
+def attention_kernel(where, leads, first_ref, inner_ref, lengths_ref, q_ref, g_ref, halo_ref, wrap_ref, own_ref, *refs):
     if not leads:
         bias_ref, old_ref, cut_ref, *refs = refs
     made = 3 if leads else 0
@@ -85,11 +95,24 @@
     head, *offsets = where
     key_in, value_in, key_out, value_out = (slice(at, at + HEAD_SIZE) for at in offsets)
     q_full_ref, g_full_ref, out_full_ref, dq_full_ref = q_ref, g_ref, out_ref, dq_ref
-    q_ref, g_ref, out_ref, dq_ref, sem = copies
+    q_ref, g_ref, out_ref, dq_ref, before_ref, sem, before_sem = copies
     rows, wide = q_ref.shape
     mine = slice(head * wide, (head + 1) * wide)
     q_copy = pltpu.make_async_copy(q_full_ref.at[:, mine], q_ref, sem.at[0])
     g_copy = pltpu.make_async_copy(g_full_ref.at[:, mine], g_ref, sem.at[1])
+    inner = inner_ref[0]
+    before_copies = []
+    for back in range(1, SPAN):
+        for part, cols in enumerate((key_in, value_in)):
+            target = before_ref.at[back - 1, :, part * HEAD_SIZE : (part + 1) * HEAD_SIZE]
+            signal = before_sem.at[2 * (back - 1) + part]
+            here = pltpu.make_async_copy(halo_ref.at[jnp.maximum(inner - back, 0), :, cols], target, signal)
+            there = pltpu.make_async_copy(
+                wrap_ref.at[jnp.minimum(inner - back + SPAN - 1, SPAN - 2), :, cols], target, signal
+            )
+            pl.when(inner >= back)(here.start)
+            pl.when(inner < back)(there.start)
+            before_copies.append(here)
     q_copy.start()
     g_copy.start()
     window = (SPAN - 1) * rows
@@ -101,16 +124,21 @@
     if leads:
         write_masks(bias_ref, old_ref, cut_ref, lengths_ref, first_ref, rows)
     from_far = lax.broadcasted_iota(jnp.int32, (rows, HEAD_SIZE), 0) >= cut_ref[0, 0]
-    mid, far, near, own = behind_ref.at[0], behind_ref.at[1], near_ref, own_ref
+    for copy in before_copies:
+        copy.wait()
+    near, mid, far = (before_ref.at[back] for back in range(SPAN - 1))
     for j, block in enumerate((mid, near)):
         span = slice(j * rows, (j + 1) * rows)
-        key_ref[span] = block[:, key_in]
-        value_ref[span] = block[:, value_in]
-        key_t_ref[:, span] = block[:, key_in].T
-        value_t_ref[:, span] = block[:, value_in].T
-    for which, plain_ref, turned_ref in ((key_in, key2_ref, key2_t_ref), (value_in, value2_ref, value2_t_ref)):
-        mine = own[:, which]
-        either = jnp.where(from_far, far[:, which].astype(jnp.float32), mine.astype(jnp.float32))
+        key_ref[span] = block[:, :HEAD_SIZE]
+        value_ref[span] = block[:, HEAD_SIZE:]
+        key_t_ref[:, span] = block[:, :HEAD_SIZE].T
+        value_t_ref[:, span] = block[:, HEAD_SIZE:].T
+    for part, which, plain_ref, turned_ref in (
+        (slice(0, HEAD_SIZE), key_in, key2_ref, key2_t_ref),
+        (slice(HEAD_SIZE, 2 * HEAD_SIZE), value_in, value2_ref, value2_t_ref),
+    ):
+        mine = own_ref[:, which]
+        either = jnp.where(from_far, far[:, part].astype(jnp.float32), mine.astype(jnp.float32))
         for j, block in enumerate((either.astype(jnp.bfloat16), mine)):
             span = slice(j * HEAD_SIZE, (j + 1) * HEAD_SIZE)
             plain_ref[:, span] = block
@@ -226,7 +254,7 @@
         copy.wait()
 
 
-def attention(head, first, lengths, queries, out_grad, blocks, place, grads, masks):
+def attention(head, first, inner, lengths, queries, out_grad, blocks, place, grads, masks):
     rows = queries.shape[0]
     wide = GROUP * HEAD_SIZE
     pair = 2 * HEAD_SIZE
@@ -241,8 +269,8 @@
     mask_specs = [whole(shape) for shape in mask_shapes]
     fore = blocks[-1].shape[1] // pair
     where = [head, *(at * HEAD_SIZE for at in (place, fore + place, 0, 1))]
-    operands = [first, lengths, queries, out_grad, *blocks]
-    in_specs = [query_spec] * 2 + [whole(block.shape) for block in blocks]
+    operands = [first, inner, lengths, queries, out_grad, *blocks]
+    in_specs = [query_spec] * 4 + [whole(blocks[-1].shape)]
     aliases = {}
     if not leads:
         operands += masks
@@ -264,7 +292,7 @@
         ]
         + [jax.ShapeDtypeStruct(*mask) for mask in zip(mask_shapes, (f32, f32, jnp.int32)) if leads],
         grid_spec=pltpu.PrefetchScalarGridSpec(
-            num_scalar_prefetch=2,
+            num_scalar_prefetch=3,
             grid=(1,),
             in_specs=in_specs,
             out_specs=[query_spec] * 2
@@ -290,7 +318,11 @@
                 for _ in range(count)
             ]
             + [pltpu.VMEM((rows, wide), bf16)] * 4
-            + [pltpu.SemaphoreType.DMA((2 + 2 * GROUP // UNIT,))],
+            + [
+                pltpu.VMEM((SPAN - 1, rows, pair), bf16),
+                pltpu.SemaphoreType.DMA((2 + 2 * GROUP // UNIT,)),
+                pltpu.SemaphoreType.DMA((2 * (SPAN - 1),)),
+            ],
         ),
         input_output_aliases=aliases,
         compiler_params=pltpu.CompilerParams(vmem_limit_bytes=48 * 1024 * 1024),
@@ -328,24 +360,23 @@
     index = lax.axis_index(AXES)
     first = (index * rows).astype(jnp.int32).reshape(1)
     bf16, f32 = jnp.bfloat16, jnp.float32
-    blocks, nears = {}, []
+    inner = lax.axis_index("inner").astype(jnp.int32).reshape(1)
+    blocks = {}
     owns = pack(keys, values)
-    for own in owns:
-        nears.append(passed_along(own, 1))
-    pairs = [jnp.stack([own, near]) for own, near in zip(owns, nears)]
-    for heads, own, near, pair in zip(FORWARD, owns, nears, pairs):
-        behind = passed_along(pair, 2)
+    for heads, own in zip(FORWARD, owns):
+        halo = lax.all_gather(own, "inner")
+        wrap = next_group(halo[1 - SPAN :])
         for place, head in enumerate(heads):
-            blocks[head] = ((behind, near, own), place)
+            blocks[head] = ((halo, wrap, own), place)
     grads, masks = (None, None), None
     parts = []
 
     def attend(head, after=()):
         nonlocal grads, masks
-        (behind, near, own), place = blocks[head]
+        (halo, wrap, own), place = blocks[head]
         own, *after = lax.optimization_barrier((own, *after))
         grads, part, masks = attention(
-            head, first, doc_lengths, queries, out_grad, (behind, near, own), place, grads, masks
+            head, first, inner, doc_lengths, queries, out_grad, (halo, wrap, own), place, grads, masks
         )
         parts.append(part)
         return after
@@ -358,7 +389,7 @@
         got = got.astype(f32)
         return (near + got[1]).astype(bf16), own + got[0]
 
-    attend(0, pairs)
+    attend(0)
     zero = first_hop(0)
     attend(1)
     one = first_hop(1)
@@ -370,7 +401,7 @@
     (nears,) = attend(3, (nears,))
     early = passed_along(nears, -1)
     behind, near, own = parts[3]
-    behind, near, own, early, got = lax.optimization_barrier((behind, near, own, early, two[2]))
+    behind, near, own, got = lax.optimization_barrier((behind, near, own, two[2]))
     far = passed_along(behind[1], -3)
     mid = passed_along(behind[0], -2)
     near_two, own_two = second_hop(two[0], two[1], got)

time: 97.4 us -> 219 us (2.25)
  waiting for transfers between devices: 20.2 us -> 138 us
  between operations: 0.99 us -> 14.1 us
  starting transfers between devices: 39.3 us -> 26.4 us
  local copies, waits for them, and re-layouts: 0.14 us -> 4.99 us
  other arithmetic: 4.28 us -> 1.4 us
    all_gather x0 -> x3, waiting for transfers between devices: none -> 124 us  [local(): halo = lax.all_gather(own, 'inner')]
    ppermute x13 -> x7, starting transfers between devices: 39.3 us -> 22.7 us  [passed_along(): lax.ppermute(value, AXES, [(source, source + steps) for source in range(f...]
    ppermute x13 -> x7, waiting for transfers between devices: 20.2 us -> 12.9 us  [passed_along(): lax.ppermute(value, AXES, [(source, source + steps) for source in range(f...]
    slice x0 -> x3, local copies, waits for them, and re-layouts: none -> 4.84 us  [local(): wrap = next_group(halo[1 - SPAN:])]
    ppermute x0 -> x3, starting transfers between devices: none -> 3.55 us  [next_group(): return lax.ppermute(value, AXES, pairs)]
    another operation x3 -> x0, other arithmetic: 2.86 us -> none  [local(): pairs = [jnp.stack([own, near]) for own, near in zip(owns, nears)]]
  transfers between devices with their start and end apart: 13 -> 13, of which waited for: 5 -> 6; matrix products, arithmetic and copies ran while one was open for 3% -> 2% of each run, Pallas kernels for 30% -> 14%
where the time goes in v12:
time: 219 us; the launch traced here: 218 us
  waiting for transfers between devices  138 us (63%)
  Pallas kernels  32.9 us (15%)
  starting transfers between devices  26.4 us (12%)
  between operations  14.1 us (6%)
  local copies, waits for them, and re-layouts  4.99 us (2%)
    all_gather x3, waiting for transfers between devices, local(): halo = lax.all_gather(own, 'inner')  124 us
    pallas_call x4, Pallas kernels, attention(): pl.pallas_call(functools.partial(attention_kernel, where, leads), out_sha...  30.9 us
    ppermute x7, starting transfers between devices, passed_along(): lax.ppermute(value, AXES, [(source, source + steps) for source in range(f...  22.7 us
    ppermute x7, waiting for transfers between devices, passed_along(): lax.ppermute(value, AXES, [(source, source + steps) for source in range(f...  12.9 us
    slice x3, local copies, waits for them, and re-layouts, local(): wrap = next_group(halo[1 - SPAN:])  4.84 us
  transfers between devices with their start and end apart: 13, of which 6 were waited for; matrix products, arithmetic and copies ran while one was open for 2% of the time, Pallas kernels for 14%

profile of v12, /device:TPU:29, one launch (start us, length us, event | category | flops | bytes accessed | tf_op | source)
XLA Modules:
  0.0 218.0 jit_solution(17274578220625237326)
XLA Ops:
  7.2 2.0 pack.1
  9.3 0.7 all-gather.11.cloned.1.call-update
  10.1 0.7 all-gather.7.cloned.1.call-update
  10.7 37.1 %all-gather.9.cloned.1.call-done = bf16[2048,256]{1,0:T(8,128)(2,1)} async-done(((bf16[256,256]{1,0:T(8,128)(2,1)}), bf16[2048,256]{1,0:T(8,128)(2,1)}) %all-gather.9.cloned.1.call-update) | async-done | bytes 1048592 | tf_op jit(solution)/shard_map/all_gather | solution.py:367
  47.9 1.9 slice.80
  49.7 1.4 collective-permute-start.1
  51.1 37.8 %all-gather.11.cloned.1.call-done = bf16[2048,256]{1,0:T(8,128)(2,1)} async-done(((bf16[256,256]{1,0:T(8,128)(2,1)}), bf16[2048,256]{1,0:T(8,128)(2,1)}) %all-gather.11.cloned.1.call-update) | async-done | bytes 1048592 | tf_op jit(solution)/shard_map/all_gather | solution.py:367
  88.9 1.8 slice.82
  90.7 1.4 collective-permute-start.3
  92.1 49.0 %all-gather.7.cloned.1.call-done = bf16[2048,512]{1,0:T(8,128)(2,1)} async-done(((bf16[256,512]{1,0:T(8,128)(2,1)}), bf16[2048,512]{1,0:T(8,128)(2,1)}) %all-gather.7.cloned.1.call-update) | async-done | bytes 2097168 | tf_op jit(solution)/shard_map/all_gather | solution.py:367
  141.1 1.2 slice.79
  142.3 0.7 collective-permute-start
  143.1 7.7 %attention.4 = (bf16[256,4096]{1,0:T(8,128)(2,1)}, bf16[256,4096]{1,0:T(8,128)(2,1)}, bf16[2,256,256]{2,1,0:T(8,128)(2,1)S(1)}, f32[256,256]{1,0:T(8,128)S(1)}, ...) custom-call(s32[1]{0:T(128)} %bitcast.first_ref, ...), custom_call_target="tpu_custom_call" | custom-call | flops 4831838208 | bytes 3538944 | tf_op jit(solution)/shard_map/attention/pallas_call | solution.py:284
  150.8 2.7 %collective-permute-start.2 = (bf16[2,256,256]{2,1,0:T(8,128)(2,1)S(1)}, bf16[2,256,256]{2,1,0:T(8,128)(2,1)S(1)}, u32[]{:S(2)}, u32[]{:S(2)}) collective-permute-start(bf16[2,256,256]{2,1,0:T(8,128)(2,1)S(1)} %get-tuple-element.40), channel_id=1, source_target_pairs={{2,0},{3,1},{4,2},{5,3},{6,4},{7,5},{8,6},{9,7},{10,8},{11,9},{12,... | collective-permute-start | bytes 786440 | tf_op jit(solution)/shard_map/ppermute | solution.py:40
  153.5 7.3 %attention.5 = (bf16[256,4096]{1,0:T(8,128)(2,1)}, bf16[256,4096]{1,0:T(8,128)(2,1)}, bf16[2,256,256]{2,1,0:T(8,128)(2,1)S(1)}, f32[256,256]{1,0:T(8,128)S(1)}, f32[256,256]{1,0:T(8,128)S(1)}) custom-call(s32[1]{0:T(128)} %bitcast.first_ref, s32[1]{0:T(128)} %bitcast.1.inner_ref, s32[16]{0:T(128)S(1)} %copy-done.6, ...), custom_call_target="tpu_custom_call", output_to_operand_aliasing={{0}: (11, {}), {1}: (12, {})} | custom-call | flops 4831838208 | bytes 3538944 | tf_op jit(solution)/shard_map/attention/pallas_call | solution.py:284
  160.9 2.5 %collective-permute-start.4 = (bf16[2,256,256]{2,1,0:T(8,128)(2,1)S(1)}, bf16[2,256,256]{2,1,0:T(8,128)(2,1)S(1)}, u32[]{:S(2)}, u32[]{:S(2)}) collective-permute-start(bf16[2,256,256]{2,1,0:T(8,128)(2,1)S(1)} %get-tuple-element.48), channel_id=1, source_target_pairs={{2,0},{3,1},{4,2},{5,3},{6,4},{7,5},{8,6},{9,7},{10,8},{11,9},{12,... | collective-permute-start | bytes 786440 | tf_op jit(solution)/shard_map/ppermute | solution.py:40
  163.4 0.7 collective-permute-done.2
  164.1 0.1 fusion.5
  164.2 8.0 %attention.6 = (bf16[256,4096]{1,0:T(8,128)(2,1)}, bf16[256,4096]{1,0:T(8,128)(2,1)}, bf16[2,256,256]{2,1,0:T(8,128)(2,1)S(1)}, f32[256,256]{1,0:T(8,128)S(1)}, f32[256,256]{1,0:T(8,128)S(1)}) custom-call(s32[1]{0:T(128)} %bitcast.first_ref, s32[1]{0:T(128)} %bitcast.1.inner_ref, s32[16]{0:T(128)S(1)} %copy-done.6, ...), custom_call_target="tpu_custom_call", output_to_operand_aliasing={{0}: (11, {}), {1}: (12, {})} | custom-call | flops 4831838208 | bytes 3538944 | tf_op jit(solution)/shard_map/attention/pallas_call | solution.py:284
  172.2 5.5 %collective-permute-start.5 = (bf16[2,256,256]{2,1,0:T(8,128)(2,1)S(1)}, bf16[2,256,256]{2,1,0:T(8,128)(2,1)S(1)}, u32[]{:S(2)}, u32[]{:S(2)}) collective-permute-start(bf16[2,256,256]{2,1,0:T(8,128)(2,1)S(1)} %get-tuple-element.51), channel_id=1, source_target_pairs={{2,0},{3,1},{4,2},{5,3},{6,4},{7,5},{8,6},{9,7},{10,8},{11,9},{12,... | collective-permute-start | bytes 786440 | tf_op jit(solution)/shard_map/ppermute | solution.py:40
  177.8 0.1 fusion.4
  177.9 3.9 %collective-permute-start.8 = (bf16[256,512]{1,0:T(8,128)(2,1)S(1)}, bf16[256,512]{1,0:T(8,128)(2,1)S(1)}, u32[]{:S(2)}, u32[]{:S(2)}) collective-permute-start(bf16[256,512]{1,0:T(8,128)(2,1)S(1)} %pad_maximum_fusion), channel_id=1, source_target_pairs={{1,0},{2,1},{3,2},{4,3},{5,4},{6,5},{7,6},{8,7},{9,8},{10,9},{11,1... | collective-permute-start | bytes 786440 | tf_op jit(solution)/shard_map/ppermute | solution.py:40
  181.8 8.0 %attention.7 = (bf16[256,4096]{1,0:T(8,128)(2,1)}, bf16[256,4096]{1,0:T(8,128)(2,1)}, bf16[2,256,256]{2,1,0:T(8,128)(2,1)S(1)}, f32[256,256]{1,0:T(8,128)S(1)}, f32[256,256]{1,0:T(8,128)S(1)}) custom-call(s32[1]{0:T(128)} %bitcast.first_ref, s32[1]{0:T(128)} %bitcast.1.inner_ref, s32[16]{0:T(128)S(1)} %copy-done.6, ...), custom_call_target="tpu_custom_call", output_to_operand_aliasing={{0}: (11, {}), {1}: (12, {})} | custom-call | flops 4831838208 | bytes 3538944 | tf_op jit(solution)/shard_map/attention/pallas_call | solution.py:284
  189.9 1.9 collective-permute-start.6
  191.8 2.3 %collective-permute-start.7 = (bf16[256,256]{1,0:T(8,128)(2,1)S(1)}, bf16[256,256]{1,0:T(8,128)(2,1)S(1)}, u32[]{:S(2)}, u32[]{:S(2)}) collective-permute-start(bf16[256,256]{1,0:T(8,128)(2,1)S(1)} %get-tuple-element.85), channel_id=1, source_target_pairs={{3,0},{4,1},{5,2},{6,3},{7,4},{8,5},{9,6},{10,7},{11,8},{12,9},{13... | collective-permute-start | bytes 393224 | tf_op jit(solution)/shard_map/ppermute | solution.py:40
  194.1 0.1 fusion.2
  194.2 3.9 %collective-permute-start.9 = (bf16[256,512]{1,0:T(8,128)(2,1)S(1)}, bf16[256,512]{1,0:T(8,128)(2,1)S(1)}, u32[]{:S(2)}, u32[]{:S(2)}) collective-permute-start(bf16[256,512]{1,0:T(8,128)(2,1)S(1)} %pad_maximum_fusion.1), channel_id=1, source_target_pairs={{1,0},{2,1},{3,2},{4,3},{5,4},{6,5},{7,6},{8,7},{9,8},{10,9},{11,1... | collective-permute-start | bytes 786440 | tf_op jit(solution)/shard_map/ppermute | solution.py:40
  198.1 2.4 %collective-permute-done.6 = bf16[256,256]{1,0:T(8,128)(2,1)S(1)} collective-permute-done((bf16[256,256]{1,0:T(8,128)(2,1)S(1)}, bf16[256,256]{1,0:T(8,128)(2,1)S(1)}, u32[]{:S(2)}, u32[]{:S(2)}) %collective-permute-start.6) | collective-permute-done | bytes 131104 | tf_op jit(solution)/shard_map/ppermute | solution.py:40
  200.5 9.8 %collective-permute-done.7 = bf16[256,256]{1,0:T(8,128)(2,1)S(1)} collective-permute-done((bf16[256,256]{1,0:T(8,128)(2,1)S(1)}, bf16[256,256]{1,0:T(8,128)(2,1)S(1)}, u32[]{:S(2)}, u32[]{:S(2)}) %collective-permute-start.7) | collective-permute-done | bytes 131104 | tf_op jit(solution)/shard_map/ppermute | solution.py:40
  210.4 0.1 fusion
  210.5 0.1 fusion.10
  210.6 0.9 pad_maximum_fusion.2
  (33 shorter events, 0.4 us)
Async XLA Ops:
  7.2 135.9 %copy-start.5 = (bf16[256,4096]{1,0:T(8,128)(2,1)S(1)}, bf16[256,4096]{1,0:T(8,128)(2,1)}, u32[]{:S(2)}) copy-start(bf16[256,4096]{1,0:T(8,128)(2,1)} %q_ref.7) | copy-start | bytes 6291460
  7.2 135.9 %copy-start.6 = (s32[16]{0:T(128)S(1)}, s32[16]{0:T(128)}, u32[]{:S(2)}) copy-start(s32[16]{0:T(128)} %lengths_ref.7) | copy-start | bytes 196
  7.2 40.7 %all-gather.9.cloned.1.call-start = ((), (), s32[]{:S(2)}) async-start(), calls=%async_computation.1 | async-start | bytes 1179648 | tf_op jit(solution)/shard_map/all_gather | solution.py:367
  9.2 133.8 %copy-start.4 = (bf16[256,256]{1,0:T(8,128)(2,1)S(1)}, bf16[256,256]{1,0:T(8,128)(2,1)}, u32[]{:S(2)}) copy-start(bf16[256,256]{1,0:T(8,128)(2,1)} %get-tuple-element.38.own_ref) | copy-start | bytes 393220
  9.3 79.7 %all-gather.11.cloned.1.call-start = ((), (), s32[]{:S(2)}) async-start(), calls=%async_computation.2 | async-start | bytes 1179648 | tf_op jit(solution)/shard_map/all_gather | solution.py:367
  10.0 131.1 %all-gather.7.cloned.1.call-start = ((), (), s32[]{:S(2)}) async-start(), calls=%async_computation | async-start | bytes 2359296 | tf_op jit(solution)/shard_map/all_gather | solution.py:367
  47.9 95.2 %copy-start.2 = (bf16[2048,256]{1,0:T(8,128)(2,1)S(1)}, bf16[2048,256]{1,0:T(8,128)(2,1)}, u32[]{:S(2)}) copy-start(bf16[2048,256]{1,0:T(8,128)(2,1)} %all-gather.9.cloned.1.call-done) | copy-start | bytes 3145732
  49.7 93.3 %collective-permute-start.1 = (bf16[3,256,256]{2,1,0:T(8,128)(2,1)}, bf16[3,256,256]{2,1,0:T(8,128)(2,1)}, u32[]{:S(2)}, u32[]{:S(2)}) collective-permute-start(bf16[3,256,256]{2,1,0:T(8,128)(2,1)} %bitcast.5), channel_id=1, source_target_pairs={{0,8},{1,9},{2,10},{8,16},{9,17},{10,18},{16,24},{17,25},{18,26}} | collective-permute-start | bytes 1179656 | tf_op jit(solution)/shard_map/ppermute | solution.py:50
  90.7 62.8 %collective-permute-start.3 = (bf16[3,256,256]{2,1,0:T(8,128)(2,1)}, bf16[3,256,256]{2,1,0:T(8,128)(2,1)}, u32[]{:S(2)}, u32[]{:S(2)}) collective-permute-start(bf16[3,256,256]{2,1,0:T(8,128)(2,1)} %bitcast.8), channel_id=1, source_target_pairs={{0,8},{1,9},{2,10},{8,16},{9,17},{10,18},{16,24},{17,25},{18,26}} | collective-permute-start | bytes 1179656 | tf_op jit(solution)/shard_map/ppermute | solution.py:50
  142.3 21.9 %collective-permute-start = (bf16[3,256,512]{2,1,0:T(8,128)(2,1)S(1)}, bf16[3,256,512]{2,1,0:T(8,128)(2,1)S(1)}, u32[]{:S(2)}, u32[]{:S(2)}) collective-permute-start(bf16[3,256,512]{2,1,0:T(8,128)(2,1)S(1)} %bitcast.44), channel_id=1, source_target_pairs={{0,8},{1,9},{2,10},{8,16},{9,17},{10,18},{16,24},{17,25},{18,26}} | collective-permute-start | bytes 2359304 | tf_op jit(solution)/shard_map/ppermute | solution.py:50
  143.1 10.4 %copy-start.1 = (bf16[2048,256]{1,0:T(8,128)(2,1)S(1)}, bf16[2048,256]{1,0:T(8,128)(2,1)}, u32[]{:S(2)}) copy-start(bf16[2048,256]{1,0:T(8,128)(2,1)} %all-gather.11.cloned.1.call-done) | copy-start | bytes 3145732
  143.1 10.4 %copy-start.3 = (bf16[256,256]{1,0:T(8,128)(2,1)S(1)}, bf16[256,256]{1,0:T(8,128)(2,1)}, u32[]{:S(2)}) copy-start(bf16[256,256]{1,0:T(8,128)(2,1)} %get-tuple-element.41.own_ref) | copy-start | bytes 393220
  150.8 13.3 %collective-permute-start.2 = (bf16[2,256,256]{2,1,0:T(8,128)(2,1)S(1)}, bf16[2,256,256]{2,1,0:T(8,128)(2,1)S(1)}, u32[]{:S(2)}, u32[]{:S(2)}) collective-permute-start(bf16[2,256,256]{2,1,0:T(8,128)(2,1)S(1)} %get-tuple-element.40), channel_id=1, source_target_pairs={{2,0},{3,1},{4,2},{5,3},{6,4},{7,5},{8,6},{9,7},{10,8},{11,9},{12,... | collective-permute-start | bytes 786440 | tf_op jit(solution)/shard_map/ppermute | solution.py:40
  160.9 3.4 %copy-start = (bf16[256,512]{1,0:T(8,128)(2,1)S(1)}, bf16[256,512]{1,0:T(8,128)(2,1)}, u32[]{:S(2)}) copy-start(bf16[256,512]{1,0:T(8,128)(2,1)} %get-tuple-element.53.own_ref) | copy-start | bytes 786436
  160.9 16.9 %collective-permute-start.4 = (bf16[2,256,256]{2,1,0:T(8,128)(2,1)S(1)}, bf16[2,256,256]{2,1,0:T(8,128)(2,1)S(1)}, u32[]{:S(2)}, u32[]{:S(2)}) collective-permute-start(bf16[2,256,256]{2,1,0:T(8,128)(2,1)S(1)} %get-tuple-element.48), channel_id=1, source_target_pairs={{2,0},{3,1},{4,2},{5,3},{6,4},{7,5},{8,6},{9,7},{10,8},{11,9},{12,... | collective-permute-start | bytes 786440 | tf_op jit(solution)/shard_map/ppermute | solution.py:40
  172.2 17.6 %collective-permute-start.5 = (bf16[2,256,256]{2,1,0:T(8,128)(2,1)S(1)}, bf16[2,256,256]{2,1,0:T(8,128)(2,1)S(1)}, u32[]{:S(2)}, u32[]{:S(2)}) collective-permute-start(bf16[2,256,256]{2,1,0:T(8,128)(2,1)S(1)} %get-tuple-element.51), channel_id=1, source_target_pairs={{2,0},{3,1},{4,2},{5,3},{6,4},{7,5},{8,6},{9,7},{10,8},{11,9},{12,... | collective-permute-start | bytes 786440 | tf_op jit(solution)/shard_map/ppermute | solution.py:40
  177.9 32.4 %collective-permute-start.8 = (bf16[256,512]{1,0:T(8,128)(2,1)S(1)}, bf16[256,512]{1,0:T(8,128)(2,1)S(1)}, u32[]{:S(2)}, u32[]{:S(2)}) collective-permute-start(bf16[256,512]{1,0:T(8,128)(2,1)S(1)} %pad_maximum_fusion), channel_id=1, source_target_pairs={{1,0},{2,1},{3,2},{4,3},{5,4},{6,5},{7,6},{8,7},{9,8},{10,9},{11,1... | collective-permute-start | bytes 786440 | tf_op jit(solution)/shard_map/ppermute | solution.py:40
  189.9 10.6 %collective-permute-start.6 = (bf16[256,256]{1,0:T(8,128)(2,1)S(1)}, bf16[256,256]{1,0:T(8,128)(2,1)S(1)}, u32[]{:S(2)}, u32[]{:S(2)}) collective-permute-start(bf16[256,256]{1,0:T(8,128)(2,1)S(1)} %get-tuple-element.84), channel_id=1, source_target_pairs={{2,0},{3,1},{4,2},{5,3},{6,4},{7,5},{8,6},{9,7},{10,8},{11,9},{12,... | collective-permute-start | bytes 393224 | tf_op jit(solution)/shard_map/ppermute | solution.py:40
  191.8 18.5 %collective-permute-start.7 = (bf16[256,256]{1,0:T(8,128)(2,1)S(1)}, bf16[256,256]{1,0:T(8,128)(2,1)S(1)}, u32[]{:S(2)}, u32[]{:S(2)}) collective-permute-start(bf16[256,256]{1,0:T(8,128)(2,1)S(1)} %get-tuple-element.85), channel_id=1, source_target_pairs={{3,0},{4,1},{5,2},{6,3},{7,4},{8,5},{9,6},{10,7},{11,8},{12,9},{13... | collective-permute-start | bytes 393224 | tf_op jit(solution)/shard_map/ppermute | solution.py:40
  194.2 16.2 %collective-permute-start.9 = (bf16[256,512]{1,0:T(8,128)(2,1)S(1)}, bf16[256,512]{1,0:T(8,128)(2,1)S(1)}, u32[]{:S(2)}, u32[]{:S(2)}) collective-permute-start(bf16[256,512]{1,0:T(8,128)(2,1)S(1)} %pad_maximum_fusion.1), channel_id=1, source_target_pairs={{1,0},{2,1},{3,2},{4,3},{5,4},{6,5},{7,6},{8,7},{9,8},{10,9},{11,1... | collective-permute-start | bytes 786440 | tf_op jit(solution)/shard_map/ppermute | solution.py:40
Sparse Core Ops, SparseCore 0:
  10.7 37.0 all-gather.8
  50.0 38.8 all-gather.10
  91.6 49.4 all-gather.6

commit v13 on v11

--- a/solution.py
+++ b/solution.py
@@ -304,23 +304,37 @@
     return results[:2], results[2:OUTS], results[OUTS:] if leads else masks
 
 
-def pack_kernel(keys_ref, values_ref, *out_refs):
-    for heads, out_ref in zip(FORWARD, out_refs):
+def pack_kernel(keys_ref, values_ref, *refs):
+    sem = refs[-1]
+    copies = []
+    for at, heads in enumerate(FORWARD):
         span = slice(heads[0] * HEAD_SIZE, (heads[-1] + 1) * HEAD_SIZE)
         width = span.stop - span.start
-        out_ref[:, :width] = keys_ref[:, span]
-        out_ref[:, width:] = values_ref[:, span]
+        own_ref, pair_ref = refs[2 * at : 2 * at + 2]
+        for target_ref in (own_ref, pair_ref.at[0]):
+            for source_ref, cols in ((keys_ref, slice(0, width)), (values_ref, slice(width, 2 * width))):
+                signal = sem.at[len(copies)]
+                copies.append(pltpu.make_async_copy(source_ref.at[:, span], target_ref.at[:, cols], signal))
+                copies[-1].start()
+    for copy in copies:
+        copy.wait()
 
 
 def pack(keys, values):
     rows = keys.shape[0]
-    return pl.pallas_call(
+    shapes = []
+    for heads in FORWARD:
+        own = (rows, 2 * HEAD_SIZE * len(heads))
+        shapes += [jax.ShapeDtypeStruct(own, keys.dtype), jax.ShapeDtypeStruct((2, *own), keys.dtype)]
+    results = pl.pallas_call(
         pack_kernel,
-        out_shape=[
-            jax.ShapeDtypeStruct((rows, 2 * HEAD_SIZE * len(heads)), keys.dtype) for heads in FORWARD
-        ],
+        out_shape=shapes,
+        in_specs=[pl.BlockSpec(memory_space=pl.ANY)] * 2,
+        out_specs=[pl.BlockSpec(memory_space=pl.ANY)] * len(shapes),
+        scratch_shapes=[pltpu.SemaphoreType.DMA((2 * len(shapes),))],
         name="pack",
     )(keys, values)
+    return results[0::2], results[1::2]
 
 
 def local(queries, keys, values, out_grad, doc_lengths):
@@ -329,10 +343,10 @@
     first = (index * rows).astype(jnp.int32).reshape(1)
     bf16, f32 = jnp.bfloat16, jnp.float32
     blocks, nears = {}, []
-    owns = pack(keys, values)
+    owns, pairs = pack(keys, values)
     for own in owns:
         nears.append(passed_along(own, 1))
-    pairs = [jnp.stack([own, near]) for own, near in zip(owns, nears)]
+    pairs = [pair.at[1].set(near) for pair, near in zip(pairs, nears)]
     for heads, own, near, pair in zip(FORWARD, owns, nears, pairs):
         behind = passed_along(pair, 2)
         for place, head in enumerate(heads):
@@ -350,34 +364,30 @@
         parts.append(part)
         return after
 
-    def first_hop(head):
-        behind, near, own = parts[head]
-        return near, own, passed_along(behind, -2)
-
     def second_hop(near, own, got):
         got = got.astype(f32)
         return (near + got[1]).astype(bf16), own + got[0]
 
     attend(0, pairs)
-    zero = first_hop(0)
     attend(1)
-    one = first_hop(1)
+    got_early = passed_along(jnp.concatenate([parts[0][0], parts[1][0]], axis=2), -2)
     attend(2)
-    two = first_hop(2)
-    got, _ = lax.optimization_barrier((one[2], parts[2][0]))
-    nears, owns = zip(second_hop(*zero), second_hop(*one[:2], got))
-    nears = jnp.concatenate(nears, axis=1)
-    (nears,) = attend(3, (nears,))
-    early = passed_along(nears, -1)
+    got_two = passed_along(parts[2][0], -2)
+    attend(3)
     behind, near, own = parts[3]
-    behind, near, own, early, got = lax.optimization_barrier((behind, near, own, early, two[2]))
+    behind, near, own, got_early, got_two = lax.optimization_barrier((behind, near, own, got_early, got_two))
     far = passed_along(behind[1], -3)
     mid = passed_along(behind[0], -2)
-    near_two, own_two = second_hop(two[0], two[1], got)
-    late = passed_along(jnp.concatenate([near_two, near.astype(bf16)], axis=1), -1)
-    own = own + mid.astype(f32) + far.astype(f32)
-    total = jnp.concatenate([*owns, own_two, own], axis=1)
-    total = (total + jnp.concatenate([early, late], axis=1).astype(f32)).astype(bf16)
+    pair = 2 * HEAD_SIZE
+    ready = [
+        second_hop(*parts[0][1:], got_early[:, :, :pair]),
+        second_hop(*parts[1][1:], got_early[:, :, pair:]),
+        second_hop(*parts[2][1:], got_two),
+        (near.astype(bf16), own + mid.astype(f32) + far.astype(f32)),
+    ]
+    nears, owns = ([piece[at] for piece in ready] for at in range(2))
+    last = passed_along(jnp.concatenate(nears, axis=1), -1)
+    total = (jnp.concatenate(owns, axis=1) + last.astype(f32)).astype(bf16)
     columns = [total[:, at : at + HEAD_SIZE] for at in range(0, total.shape[1], HEAD_SIZE)]
     return (
         grads[0],

time: 97.4 us -> 128 us (1.31)
  Pallas kernels: 31.4 us -> 61.8 us
  starting transfers between devices: 39.3 us -> 29.4 us
  waiting for transfers between devices: 20.2 us -> 28.1 us
  local copies, waits for them, and re-layouts: 0.14 us -> 5.34 us
  other arithmetic: 4.28 us -> 2.11 us
    pallas_call x1, Pallas kernels: 2.01 us -> 33 us  [pack(): pl.pallas_call(pack_kernel, out_shape=shapes, in_specs=[pl.BlockSpec(memo...]
    ppermute x13 -> x11, starting transfers between devices: 39.3 us -> 29.4 us  [passed_along(): lax.ppermute(value, AXES, [(source, source + steps) for source in range(f...]
    ppermute x13 -> x11, waiting for transfers between devices: 20.2 us -> 28.1 us  [passed_along(): lax.ppermute(value, AXES, [(source, source + steps) for source in range(f...]
    unnamed x10 -> x14, local copies, waits for them, and re-layouts: 0.02 us -> 3.17 us
    another operation x3 -> x0, other arithmetic: 2.86 us -> none  [local(): pairs = [jnp.stack([own, near]) for own, near in zip(owns, nears)]]
    scatter x0 -> x3, local copies, waits for them, and re-layouts: none -> 2.06 us  [local(): pairs = [pair.at[1].set(near) for pair, near in zip(pairs, nears)]]
  transfers between devices with their start and end apart: 13 -> 11, of which waited for: 5 -> 5; matrix products, arithmetic and copies ran while one was open for 3% -> 2% of each run, Pallas kernels for 30% -> 23%
where the time goes in v13:
time: 128 us
  Pallas kernels  61.8 us (48%)
  starting transfers between devices  29.4 us (23%)
  waiting for transfers between devices  28.1 us (22%)
  local copies, waits for them, and re-layouts  5.34 us (4%)
  other arithmetic  2.11 us (2%)
    pallas_call x1, Pallas kernels, pack(): pl.pallas_call(pack_kernel, out_shape=shapes, in_specs=[pl.BlockSpec(memo...  33 us
    ppermute x11, starting transfers between devices, passed_along(): lax.ppermute(value, AXES, [(source, source + steps) for source in range(f...  29.4 us
    pallas_call x4, Pallas kernels, attention(): pl.pallas_call(functools.partial(attention_kernel, where, leads), out_sha...  28.8 us
    ppermute x11, waiting for transfers between devices, passed_along(): lax.ppermute(value, AXES, [(source, source + steps) for source in range(f...  28.1 us
    unnamed x14, local copies, waits for them, and re-layouts  3.17 us
  transfers between devices with their start and end apart: 11, of which 5 were waited for; matrix products, arithmetic and copies ran while one was open for 2% of the time, Pallas kernels for 23%

profile of v13, /device:TPU:29, one launch (start us, length us, event | category | flops | bytes accessed | tf_op | source)
XLA Modules:
  0.0 127.7 jit_solution(13193993445180551404)
XLA Ops:
  0.6 33.0 %pack.1 = (bf16[256,256]{1,0:T(8,128)(2,1)}, bf16[2,256,256]{2,1,0:T(8,128)(2,1)}, bf16[256,256]{1,0:T(8,128)(2,1)}, bf16[2,256,256]{2,1,0:T(8,128)(2,1)}, bf16[...) custom-call(bf16[256,512]{1,0:T(8,128)(2,1)} %keys_ref.1, bf16[256,512]{1,0:T(8,128)(2,1)} %values_ref.1), custom_call_target="tpu_custom_call" | custom-call | tf_op jit(solution)/shard_map/pack/pallas_call | solution.py:329
  33.6 3.3 %collective-permute-start.2 = (bf16[256,256]{1,0:T(8,128)(2,1)}, bf16[256,256]{1,0:T(8,128)(2,1)S(1)}, u32[]{:S(2)}, u32[]{:S(2)}) collective-permute-start(bf16[256,256]{1,0:T(8,128)(2,1)} %get-tuple-element.81.own_ref), channel_id=1, source_target_pairs={{0,1},{1,2},{2,3},{3,4},{4,5},{5,6},{6,7},{7,8},{8,9},{9,10},{10,1... | collective-permute-start | bytes 393224 | tf_op jit(solution)/shard_map/ppermute | solution.py:40
  36.9 3.4 %collective-permute-start.4 = (bf16[256,256]{1,0:T(8,128)(2,1)}, bf16[256,256]{1,0:T(8,128)(2,1)S(1)}, u32[]{:S(2)}, u32[]{:S(2)}) collective-permute-start(bf16[256,256]{1,0:T(8,128)(2,1)} %get-tuple-element.80.own_ref), channel_id=1, source_target_pairs={{0,1},{1,2},{2,3},{3,4},{4,5},{5,6},{6,7},{7,8},{8,9},{9,10},{10,1... | collective-permute-start | bytes 393224 | tf_op jit(solution)/shard_map/ppermute | solution.py:40
  40.3 3.4 %collective-permute-start = (bf16[256,512]{1,0:T(8,128)(2,1)}, bf16[256,512]{1,0:T(8,128)(2,1)S(1)}, u32[]{:S(2)}, u32[]{:S(2)}) collective-permute-start(bf16[256,512]{1,0:T(8,128)(2,1)} %get-tuple-element.76.own_ref), channel_id=1, source_target_pairs={{0,1},{1,2},{2,3},{3,4},{4,5},{5,6},{6,7},{7,8},{8,9},{9,10},{10,1... | collective-permute-start | bytes 786440 | tf_op jit(solution)/shard_map/ppermute | solution.py:40
  43.8 0.7 bitcast_dynamic-update-slice_fusion.2
  44.5 3.5 %collective-permute-start.3 = (bf16[2,256,256]{2,1,0:T(8,128)(2,1)}, bf16[2,256,256]{2,1,0:T(8,128)(2,1)S(1)}, u32[]{:S(2)}, u32[]{:S(2)}) collective-permute-start(bf16[2,256,256]{2,1,0:T(8,128)(2,1)} %bitcast_dynamic-update-slice_fusion.2), channel_id=1, source_target_pairs={{0,2},{1,3},{2,4},{3,5},{4,6},{5,7},{6,8},{7,9},{8,10},{9,11},{10,... | collective-permute-start | bytes 786440 | tf_op jit(solution)/shard_map/ppermute | solution.py:40
  47.9 0.7 bitcast_dynamic-update-slice_fusion.1
  48.6 3.5 %collective-permute-start.5 = (bf16[2,256,256]{2,1,0:T(8,128)(2,1)}, bf16[2,256,256]{2,1,0:T(8,128)(2,1)S(1)}, u32[]{:S(2)}, u32[]{:S(2)}) collective-permute-start(bf16[2,256,256]{2,1,0:T(8,128)(2,1)} %bitcast_dynamic-update-slice_fusion.1), channel_id=1, source_target_pairs={{0,2},{1,3},{2,4},{3,5},{4,6},{5,7},{6,8},{7,9},{8,10},{9,11},{10,... | collective-permute-start | bytes 786440 | tf_op jit(solution)/shard_map/ppermute | solution.py:40
  52.1 0.7 bitcast_dynamic-update-slice_fusion
  52.8 2.1 %collective-permute-start.1 = (bf16[2,256,512]{2,1,0:T(8,128)(2,1)}, bf16[2,256,512]{2,1,0:T(8,128)(2,1)S(1)}, u32[]{:S(2)}, u32[]{:S(2)}) collective-permute-start(bf16[2,256,512]{2,1,0:T(8,128)(2,1)} %bitcast_dynamic-update-slice_fusion), channel_id=1, source_target_pairs={{0,2},{1,3},{2,4},{3,5},{4,6},{5,7},{6,8},{7,9},{8,10},{9,11},{10,... | collective-permute-start | bytes 1572872 | tf_op jit(solution)/shard_map/ppermute | solution.py:40
  54.9 1.1 collective-permute-done.3.behind_ref
  56.0 1.6 %copy-done = bf16[256,4096]{1,0:T(8,128)(2,1)S(1)} copy-done((bf16[256,4096]{1,0:T(8,128)(2,1)S(1)}, bf16[256,4096]{1,0:T(8,128)(2,1)}, u32[]{:S(2)}) %copy-start) | copy-done | bytes 2097176
  57.6 0.9 copy-done.4
  58.5 0.7 copy-done.5
  59.1 7.4 %attention.4 = (bf16[256,4096]{1,0:T(8,128)(2,1)}, bf16[256,4096]{1,0:T(8,128)(2,1)}, bf16[2,256,256]{2,1,0:T(8,128)(2,1)S(1)}, f32[256,256]{1,0:T(8,128)S(1)}, ...) custom-call(s32[1]{0:T(128)} %bitcast.first_ref, ...), custom_call_target="tpu_custom_call" | custom-call | flops 4831838208 | bytes 3538944 | tf_op jit(solution)/shard_map/attention/pallas_call | solution.py:256
  66.6 7.1 %attention.5 = (bf16[256,4096]{1,0:T(8,128)(2,1)}, bf16[256,4096]{1,0:T(8,128)(2,1)}, bf16[2,256,256]{2,1,0:T(8,128)(2,1)S(1)}, f32[256,256]{1,0:T(8,128)S(1)}, f32[256,256]{1,0:T(8,128)S(1)}) custom-call(s32[1]{0:T(128)} %bitcast.first_ref, s32[16]{0:T(128)S(1)} %copy-done.5, ...), custom_call_target="tpu_custom_call", output_to_operand_aliasing={{0}: (10, {}), {1}: (11, {})} | custom-call | flops 4831838208 | bytes 3538944 | tf_op jit(solution)/shard_map/attention/pallas_call | solution.py:256
  73.8 2.1 %collective-permute-start.6 = (bf16[2,256,512]{2,1,0:T(8,128)(2,1)S(1)}, bf16[2,256,512]{2,1,0:T(8,128)(2,1)S(1)}, u32[]{:S(2)}, u32[]{:S(2)}) collective-permute-start(bf16[2,256,512]{2,1,0:T(8,128)(2,1)S(1)} %pad_maximum_fusion), channel_id=1, source_target_pairs={{2,0},{3,1},{4,2},{5,3},{6,4},{7,5},{8,6},{9,7},{10,8},{11,9},{12,... | collective-permute-start | bytes 1572872 | tf_op jit(solution)/shard_map/ppermute | solution.py:40
  75.9 7.1 %attention.6 = (bf16[256,4096]{1,0:T(8,128)(2,1)}, bf16[256,4096]{1,0:T(8,128)(2,1)}, bf16[2,256,256]{2,1,0:T(8,128)(2,1)S(1)}, f32[256,256]{1,0:T(8,128)S(1)}, f32[256,256]{1,0:T(8,128)S(1)}) custom-call(s32[1]{0:T(128)} %bitcast.first_ref, s32[16]{0:T(128)S(1)} %copy-done.6, ...), custom_call_target="tpu_custom_call", output_to_operand_aliasing={{0}: (10, {}), {1}: (11, {})} | custom-call | flops 4831838208 | bytes 3538944 | tf_op jit(solution)/shard_map/attention/pallas_call | solution.py:256
  83.1 1.9 %collective-permute-start.7 = (bf16[2,256,256]{2,1,0:T(8,128)(2,1)S(1)}, bf16[2,256,256]{2,1,0:T(8,128)(2,1)S(1)}, u32[]{:S(2)}, u32[]{:S(2)}) collective-permute-start(bf16[2,256,256]{2,1,0:T(8,128)(2,1)S(1)} %get-tuple-element.99), channel_id=1, source_target_pairs={{2,0},{3,1},{4,2},{5,3},{6,4},{7,5},{8,6},{9,7},{10,8},{11,9},{12,... | collective-permute-start | bytes 786440 | tf_op jit(solution)/shard_map/ppermute | solution.py:40
  85.0 7.2 %attention.7 = (bf16[256,4096]{1,0:T(8,128)(2,1)}, bf16[256,4096]{1,0:T(8,128)(2,1)}, bf16[2,256,256]{2,1,0:T(8,128)(2,1)S(1)}, f32[256,256]{1,0:T(8,128)S(1)}, f32[256,256]{1,0:T(8,128)S(1)}) custom-call(s32[1]{0:T(128)} %bitcast.first_ref, s32[16]{0:T(128)S(1)} %copy-done.6, ...), custom_call_target="tpu_custom_call", output_to_operand_aliasing={{0}: (10, {}), {1}: (11, {})} | custom-call | flops 4831838208 | bytes 3538944 | tf_op jit(solution)/shard_map/attention/pallas_call | solution.py:256
  92.2 0.9 collective-permute-done.6
  93.1 5.4 %collective-permute-done.7 = bf16[2,256,256]{2,1,0:T(8,128)(2,1)S(1)} collective-permute-done((bf16[2,256,256]{2,1,0:T(8,128)(2,1)S(1)}, bf16[2,256,256]{2,1,0:T(8,128)(2,1)S(1)}, u32[]{:S(2)}, u32[]{:S(2)}) %collective-permute-start.7) | collective-permute-done | bytes 262176 | tf_op jit(solution)/shard_map/ppermute | solution.py:40
  98.7 0.1 fusion.4
  98.9 1.9 %collective-permute-start.10 = (bf16[256,1024]{1,0:T(8,128)(2,1)S(1)}, bf16[256,1024]{1,0:T(8,128)(2,1)S(1)}, u32[]{:S(2)}, u32[]{:S(2)}) collective-permute-start(bf16[256,1024]{1,0:T(8,128)(2,1)S(1)} %pad_maximum_fusion.1), channel_id=1, source_target_pairs={{1,0},{2,1},{3,2},{4,3},{5,4},{6,5},{7,6},{8,7},{9,8},{10,9},{11,1... | collective-permute-start | bytes 1572872 | tf_op jit(solution)/shard_map/ppermute | solution.py:40
  100.9 1.9 %collective-permute-start.8 = (bf16[256,256]{1,0:T(8,128)(2,1)S(1)}, bf16[256,256]{1,0:T(8,128)(2,1)S(1)}, u32[]{:S(2)}, u32[]{:S(2)}) collective-permute-start(bf16[256,256]{1,0:T(8,128)(2,1)S(1)} %get-tuple-element.126), channel_id=1, source_target_pairs={{2,0},{3,1},{4,2},{5,3},{6,4},{7,5},{8,6},{9,7},{10,8},{11,9},{12,... | collective-permute-start | bytes 393224 | tf_op jit(solution)/shard_map/ppermute | solution.py:40
  102.8 2.3 %collective-permute-start.9 = (bf16[256,256]{1,0:T(8,128)(2,1)S(1)}, bf16[256,256]{1,0:T(8,128)(2,1)S(1)}, u32[]{:S(2)}, u32[]{:S(2)}) collective-permute-start(bf16[256,256]{1,0:T(8,128)(2,1)S(1)} %get-tuple-element.127), channel_id=1, source_target_pairs={{3,0},{4,1},{5,2},{6,3},{7,4},{8,5},{9,6},{10,7},{11,8},{12,9},{13... | collective-permute-start | bytes 393224 | tf_op jit(solution)/shard_map/ppermute | solution.py:40
  105.1 5.4 %collective-permute-done.8 = bf16[256,256]{1,0:T(8,128)(2,1)S(1)} collective-permute-done((bf16[256,256]{1,0:T(8,128)(2,1)S(1)}, bf16[256,256]{1,0:T(8,128)(2,1)S(1)}, u32[]{:S(2)}, u32[]{:S(2)}) %collective-permute-start.8) | collective-permute-done | bytes 131104 | tf_op jit(solution)/shard_map/ppermute | solution.py:40
  110.5 15.4 %collective-permute-done.9 = bf16[256,256]{1,0:T(8,128)(2,1)S(1)} collective-permute-done((bf16[256,256]{1,0:T(8,128)(2,1)S(1)}, bf16[256,256]{1,0:T(8,128)(2,1)S(1)}, u32[]{:S(2)}, u32[]{:S(2)}) %collective-permute-start.9) | collective-permute-done | bytes 131104 | tf_op jit(solution)/shard_map/ppermute | solution.py:40
  126.0 0.2 fusion
  126.1 0.1 fusion.10
  126.2 0.7 pad_maximum_fusion.3
  127.0 0.7 pad_maximum_fusion.2
  (25 shorter events, 0.4 us)
Async XLA Ops:
  33.6 10.2 %collective-permute-start.2 = (bf16[256,256]{1,0:T(8,128)(2,1)}, bf16[256,256]{1,0:T(8,128)(2,1)S(1)}, u32[]{:S(2)}, u32[]{:S(2)}) collective-permute-start(bf16[256,256]{1,0:T(8,128)(2,1)} %get-tuple-element.81.own_ref), channel_id=1, source_target_pairs={{0,1},{1,2},{2,3},{3,4},{4,5},{5,6},{6,7},{7,8},{8,9},{9,10},{10,1... | collective-permute-start | bytes 393224 | tf_op jit(solution)/shard_map/ppermute | solution.py:40
  36.9 11.0 %collective-permute-start.4 = (bf16[256,256]{1,0:T(8,128)(2,1)}, bf16[256,256]{1,0:T(8,128)(2,1)S(1)}, u32[]{:S(2)}, u32[]{:S(2)}) collective-permute-start(bf16[256,256]{1,0:T(8,128)(2,1)} %get-tuple-element.80.own_ref), channel_id=1, source_target_pairs={{0,1},{1,2},{2,3},{3,4},{4,5},{5,6},{6,7},{7,8},{8,9},{9,10},{10,1... | collective-permute-start | bytes 393224 | tf_op jit(solution)/shard_map/ppermute | solution.py:40
  40.3 11.8 %collective-permute-start = (bf16[256,512]{1,0:T(8,128)(2,1)}, bf16[256,512]{1,0:T(8,128)(2,1)S(1)}, u32[]{:S(2)}, u32[]{:S(2)}) collective-permute-start(bf16[256,512]{1,0:T(8,128)(2,1)} %get-tuple-element.76.own_ref), channel_id=1, source_target_pairs={{0,1},{1,2},{2,3},{3,4},{4,5},{5,6},{6,7},{7,8},{8,9},{9,10},{10,1... | collective-permute-start | bytes 786440 | tf_op jit(solution)/shard_map/ppermute | solution.py:40
  44.5 11.5 %collective-permute-start.3 = (bf16[2,256,256]{2,1,0:T(8,128)(2,1)}, bf16[2,256,256]{2,1,0:T(8,128)(2,1)S(1)}, u32[]{:S(2)}, u32[]{:S(2)}) collective-permute-start(bf16[2,256,256]{2,1,0:T(8,128)(2,1)} %bitcast_dynamic-update-slice_fusion.2), channel_id=1, source_target_pairs={{0,2},{1,3},{2,4},{3,5},{4,6},{5,7},{6,8},{7,9},{8,10},{9,11},{10,... | collective-permute-start | bytes 786440 | tf_op jit(solution)/shard_map/ppermute | solution.py:40
  48.6 17.9 %collective-permute-start.5 = (bf16[2,256,256]{2,1,0:T(8,128)(2,1)}, bf16[2,256,256]{2,1,0:T(8,128)(2,1)S(1)}, u32[]{:S(2)}, u32[]{:S(2)}) collective-permute-start(bf16[2,256,256]{2,1,0:T(8,128)(2,1)} %bitcast_dynamic-update-slice_fusion.1), channel_id=1, source_target_pairs={{0,2},{1,3},{2,4},{3,5},{4,6},{5,7},{6,8},{7,9},{8,10},{9,11},{10,... | collective-permute-start | bytes 786440 | tf_op jit(solution)/shard_map/ppermute | solution.py:40
  52.8 23.1 %collective-permute-start.1 = (bf16[2,256,512]{2,1,0:T(8,128)(2,1)}, bf16[2,256,512]{2,1,0:T(8,128)(2,1)S(1)}, u32[]{:S(2)}, u32[]{:S(2)}) collective-permute-start(bf16[2,256,512]{2,1,0:T(8,128)(2,1)} %bitcast_dynamic-update-slice_fusion), channel_id=1, source_target_pairs={{0,2},{1,3},{2,4},{3,5},{4,6},{5,7},{6,8},{7,9},{8,10},{9,11},{10,... | collective-permute-start | bytes 1572872 | tf_op jit(solution)/shard_map/ppermute | solution.py:40
  56.0 1.6 %copy-start = (bf16[256,4096]{1,0:T(8,128)(2,1)S(1)}, bf16[256,4096]{1,0:T(8,128)(2,1)}, u32[]{:S(2)}) copy-start(bf16[256,4096]{1,0:T(8,128)(2,1)} %q_ref.7) | copy-start | bytes 6291460
  57.6 0.9 copy-start.4
  58.5 0.7 copy-start.5
  59.1 7.4 %copy-start.3 = (bf16[256,256]{1,0:T(8,128)(2,1)S(1)}, bf16[256,256]{1,0:T(8,128)(2,1)}, u32[]{:S(2)}) copy-start(bf16[256,256]{1,0:T(8,128)(2,1)} %get-tuple-element.80.own_ref) | copy-start | bytes 393220
  66.6 9.3 %copy-start.1 = (bf16[256,4096]{1,0:T(8,128)(2,1)S(1)}, bf16[256,4096]{1,0:T(8,128)(2,1)}, u32[]{:S(2)}) copy-start(bf16[256,4096]{1,0:T(8,128)(2,1)} %q_ref.7) | copy-start | bytes 6291460
  66.6 9.3 %copy-start.2 = (bf16[256,512]{1,0:T(8,128)(2,1)S(1)}, bf16[256,512]{1,0:T(8,128)(2,1)}, u32[]{:S(2)}) copy-start(bf16[256,512]{1,0:T(8,128)(2,1)} %get-tuple-element.76.own_ref) | copy-start | bytes 786436
  66.6 9.3 %copy-start.6 = (s32[16]{0:T(128)S(1)}, s32[16]{0:T(128)}, u32[]{:S(2)}) copy-start(s32[16]{0:T(128)} %lengths_ref.7) | copy-start | bytes 196
  73.8 19.3 %collective-permute-start.6 = (bf16[2,256,512]{2,1,0:T(8,128)(2,1)S(1)}, bf16[2,256,512]{2,1,0:T(8,128)(2,1)S(1)}, u32[]{:S(2)}, u32[]{:S(2)}) collective-permute-start(bf16[2,256,512]{2,1,0:T(8,128)(2,1)S(1)} %pad_maximum_fusion), channel_id=1, source_target_pairs={{2,0},{3,1},{4,2},{5,3},{6,4},{7,5},{8,6},{9,7},{10,8},{11,9},{12,... | collective-permute-start | bytes 1572872 | tf_op jit(solution)/shard_map/ppermute | solution.py:40
  83.1 15.4 %collective-permute-start.7 = (bf16[2,256,256]{2,1,0:T(8,128)(2,1)S(1)}, bf16[2,256,256]{2,1,0:T(8,128)(2,1)S(1)}, u32[]{:S(2)}, u32[]{:S(2)}) collective-permute-start(bf16[2,256,256]{2,1,0:T(8,128)(2,1)S(1)} %get-tuple-element.99), channel_id=1, source_target_pairs={{2,0},{3,1},{4,2},{5,3},{6,4},{7,5},{8,6},{9,7},{10,8},{11,9},{12,... | collective-permute-start | bytes 786440 | tf_op jit(solution)/shard_map/ppermute | solution.py:40
  98.9 27.1 %collective-permute-start.10 = (bf16[256,1024]{1,0:T(8,128)(2,1)S(1)}, bf16[256,1024]{1,0:T(8,128)(2,1)S(1)}, u32[]{:S(2)}, u32[]{:S(2)}) collective-permute-start(bf16[256,1024]{1,0:T(8,128)(2,1)S(1)} %pad_maximum_fusion.1), channel_id=1, source_target_pairs={{1,0},{2,1},{3,2},{4,3},{5,4},{6,5},{7,6},{8,7},{9,8},{10,9},{11,1... | collective-permute-start | bytes 1572872 | tf_op jit(solution)/shard_map/ppermute | solution.py:40
  100.9 9.7 %collective-permute-start.8 = (bf16[256,256]{1,0:T(8,128)(2,1)S(1)}, bf16[256,256]{1,0:T(8,128)(2,1)S(1)}, u32[]{:S(2)}, u32[]{:S(2)}) collective-permute-start(bf16[256,256]{1,0:T(8,128)(2,1)S(1)} %get-tuple-element.126), channel_id=1, source_target_pairs={{2,0},{3,1},{4,2},{5,3},{6,4},{7,5},{8,6},{9,7},{10,8},{11,9},{12,... | collective-permute-start | bytes 393224 | tf_op jit(solution)/shard_map/ppermute | solution.py:40
  102.8 23.1 %collective-permute-start.9 = (bf16[256,256]{1,0:T(8,128)(2,1)S(1)}, bf16[256,256]{1,0:T(8,128)(2,1)S(1)}, u32[]{:S(2)}, u32[]{:S(2)}) collective-permute-start(bf16[256,256]{1,0:T(8,128)(2,1)S(1)} %get-tuple-element.127), channel_id=1, source_target_pairs={{3,0},{4,1},{5,2},{6,3},{7,4},{8,5},{9,6},{10,7},{11,8},{12,9},{13... | collective-permute-start | bytes 393224 | tf_op jit(solution)/shard_map/ppermute | solution.py:40

commit v14 on v13

--- a/solution.py
+++ b/solution.py
@@ -305,33 +305,28 @@
 
 
 def pack_kernel(keys_ref, values_ref, *refs):
-    sem = refs[-1]
-    copies = []
     for at, heads in enumerate(FORWARD):
         span = slice(heads[0] * HEAD_SIZE, (heads[-1] + 1) * HEAD_SIZE)
         width = span.stop - span.start
         own_ref, pair_ref = refs[2 * at : 2 * at + 2]
         for target_ref in (own_ref, pair_ref.at[0]):
-            for source_ref, cols in ((keys_ref, slice(0, width)), (values_ref, slice(width, 2 * width))):
-                signal = sem.at[len(copies)]
-                copies.append(pltpu.make_async_copy(source_ref.at[:, span], target_ref.at[:, cols], signal))
-                copies[-1].start()
-    for copy in copies:
-        copy.wait()
+            target_ref[:, :width] = keys_ref[:, span]
+            target_ref[:, width:] = values_ref[:, span]
 
 
 def pack(keys, values):
     rows = keys.shape[0]
-    shapes = []
+    shapes, specs = [], []
     for heads in FORWARD:
         own = (rows, 2 * HEAD_SIZE * len(heads))
         shapes += [jax.ShapeDtypeStruct(own, keys.dtype), jax.ShapeDtypeStruct((2, *own), keys.dtype)]
+        specs += [pl.BlockSpec(own, lambda i: (0, 0)), pl.BlockSpec((1, *own), lambda i: (0, 0, 0))]
     results = pl.pallas_call(
         pack_kernel,
+        grid=(1,),
         out_shape=shapes,
-        in_specs=[pl.BlockSpec(memory_space=pl.ANY)] * 2,
-        out_specs=[pl.BlockSpec(memory_space=pl.ANY)] * len(shapes),
-        scratch_shapes=[pltpu.SemaphoreType.DMA((2 * len(shapes),))],
+        in_specs=[pl.BlockSpec(keys.shape, lambda i: (0, 0))] * 2,
+        out_specs=specs,
         name="pack",
     )(keys, values)
     return results[0::2], results[1::2]
@@ -361,7 +356,7 @@
         grads, part, masks = attention(
             head, first, doc_lengths, queries, out_grad, (behind, near, own), place, grads, masks
         )
-        parts.append(part)
+        parts.append(list(part))
         return after
 
     def second_hop(near, own, got):
@@ -369,25 +364,23 @@
         return (near + got[1]).astype(bf16), own + got[0]
 
     attend(0, pairs)
+    gots = [passed_along(parts[0][0], -2)]
     attend(1)
-    got_early = passed_along(jnp.concatenate([parts[0][0], parts[1][0]], axis=2), -2)
-    attend(2)
-    got_two = passed_along(parts[2][0], -2)
-    attend(3)
-    behind, near, own = parts[3]
-    behind, near, own, got_early, got_two = lax.optimization_barrier((behind, near, own, got_early, got_two))
-    far = passed_along(behind[1], -3)
-    mid = passed_along(behind[0], -2)
-    pair = 2 * HEAD_SIZE
-    ready = [
-        second_hop(*parts[0][1:], got_early[:, :, :pair]),
-        second_hop(*parts[1][1:], got_early[:, :, pair:]),
-        second_hop(*parts[2][1:], got_two),
-        (near.astype(bf16), own + mid.astype(f32) + far.astype(f32)),
-    ]
-    nears, owns = ([piece[at] for piece in ready] for at in range(2))
-    last = passed_along(jnp.concatenate(nears, axis=1), -1)
-    total = (jnp.concatenate(owns, axis=1) + last.astype(f32)).astype(bf16)
+    gots.append(passed_along(parts[1][0], -2))
+    gots[0], _ = lax.optimization_barrier((gots[0], parts[1][0]))
+    nears, owns = zip(second_hop(*parts[0][1:], gots[0]))
+    (nears,) = attend(2, nears)
+    gots.append(passed_along(parts[2][0], -2))
+    gots[1], _ = lax.optimization_barrier((gots[1], parts[2][0]))
+    more = second_hop(*parts[1][1:], gots[1])
+    (nears, *more) = attend(3, (nears, *more))
+    gots[2], near = lax.optimization_barrier((gots[2], parts[3][1]))
+    gots.append(passed_along(parts[3][0], -2))
+    parts[3][1] = near
+    rest = [second_hop(*part[1:], got) for part, got in zip(parts[2:], gots[2:])]
+    nears, owns = zip((nears, *owns), more, *rest)
+    last = [passed_along(jnp.concatenate(nears[at : at + 2], axis=1), -1) for at in (0, 2)]
+    total = (jnp.concatenate(owns, axis=1) + jnp.concatenate(last, axis=1).astype(f32)).astype(bf16)
     columns = [total[:, at : at + HEAD_SIZE] for at in range(0, total.shape[1], HEAD_SIZE)]
     return (
         grads[0],

time: 128 us -> 92.1 us (0.72); the launches traced: 128 us -> 90.3 us
  Pallas kernels: 61.8 us -> 30.2 us
  waiting for transfers between devices: 28.1 us -> 16.2 us
  starting transfers between devices: 29.4 us -> 36.1 us
    pallas_call x1, Pallas kernels: 33 us -> 2.06 us  [pack(): pl.pallas_call(pack_kernel, grid=(1,), out_shape=shapes, in_specs=[pl.Blo...]
    ppermute x11 -> x12, waiting for transfers between devices: 28.1 us -> 16.2 us  [passed_along(): lax.ppermute(value, AXES, [(source, source + steps) for source in range(f...]
    ppermute x11 -> x12, starting transfers between devices: 29.4 us -> 36.1 us  [passed_along(): lax.ppermute(value, AXES, [(source, source + steps) for source in range(f...]
  transfers between devices with their start and end apart: 11 -> 12, of which waited for: 5 -> 5; matrix products, arithmetic and copies ran while one was open for 2% -> 3% of each run, Pallas kernels for 23% -> 31%
where the time goes in v14:
time: 92.1 us; the launch traced here: 90.3 us
  starting transfers between devices  36.1 us (39%)
  Pallas kernels  30.2 us (33%)
  waiting for transfers between devices  16.2 us (18%)
  local copies, waits for them, and re-layouts  5.33 us (6%)
  other arithmetic  1.45 us (2%)
  between operations  0.96 us (1%)
    ppermute x12, starting transfers between devices, passed_along(): lax.ppermute(value, AXES, [(source, source + steps) for source in range(f...  36.1 us
    pallas_call x4, Pallas kernels, attention(): pl.pallas_call(functools.partial(attention_kernel, where, leads), out_sha...  28.2 us
    ppermute x12, waiting for transfers between devices, passed_along(): lax.ppermute(value, AXES, [(source, source + steps) for source in range(f...  16.2 us
    unnamed x14, local copies, waits for them, and re-layouts  3.17 us
    pallas_call x1, Pallas kernels, pack(): pl.pallas_call(pack_kernel, grid=(1,), out_shape=shapes, in_specs=[pl.Blo...  2.06 us
    scatter x3, local copies, waits for them, and re-layouts, local(): pairs = [pair.at[1].set(near) for pair, near in zip(pairs, nears)]  2.06 us
  transfers between devices with their start and end apart: 12, of which 5 were waited for; matrix products, arithmetic and copies ran while one was open for 3% of the time, Pallas kernels for 31%

profile of v14, /device:TPU:29, one launch (start us, length us, event | category | flops | bytes accessed | tf_op | source)
XLA Modules:
  0.0 90.3 jit_solution(3844681693616878922)
XLA Ops:
  0.6 2.1 %pack.1 = (bf16[256,256]{1,0:T(8,128)(2,1)}, bf16[2,256,256]{2,1,0:T(8,128)(2,1)}, bf16[256,256]{1,0:T(8,128)(2,1)}, bf16[2,256,256]{2,1,0:T(8,128)(2,1)}, bf16[...) custom-call(bf16[256,512]{1,0:T(8,128)(2,1)} %keys_ref.1, bf16[256,512]{1,0:T(8,128)(2,1)} %values_ref.1), custom_call_target="tpu_custom_call" | custom-call | tf_op jit(solution)/shard_map/pack/pallas_call | solution.py:324
  2.7 3.3 %collective-permute-start.2 = (bf16[256,256]{1,0:T(8,128)(2,1)}, bf16[256,256]{1,0:T(8,128)(2,1)S(1)}, u32[]{:S(2)}, u32[]{:S(2)}) collective-permute-start(bf16[256,256]{1,0:T(8,128)(2,1)} %get-tuple-element.86.own_ref), channel_id=1, source_target_pairs={{0,1},{1,2},{2,3},{3,4},{4,5},{5,6},{6,7},{7,8},{8,9},{9,10},{10,1... | collective-permute-start | bytes 393224 | tf_op jit(solution)/shard_map/ppermute | solution.py:40
  6.0 3.4 %collective-permute-start.4 = (bf16[256,256]{1,0:T(8,128)(2,1)}, bf16[256,256]{1,0:T(8,128)(2,1)S(1)}, u32[]{:S(2)}, u32[]{:S(2)}) collective-permute-start(bf16[256,256]{1,0:T(8,128)(2,1)} %get-tuple-element.85.own_ref), channel_id=1, source_target_pairs={{0,1},{1,2},{2,3},{3,4},{4,5},{5,6},{6,7},{7,8},{8,9},{9,10},{10,1... | collective-permute-start | bytes 393224 | tf_op jit(solution)/shard_map/ppermute | solution.py:40
  9.4 3.4 %collective-permute-start = (bf16[256,512]{1,0:T(8,128)(2,1)}, bf16[256,512]{1,0:T(8,128)(2,1)S(1)}, u32[]{:S(2)}, u32[]{:S(2)}) collective-permute-start(bf16[256,512]{1,0:T(8,128)(2,1)} %get-tuple-element.104.own_ref), channel_id=1, source_target_pairs={{0,1},{1,2},{2,3},{3,4},{4,5},{5,6},{6,7},{7,8},{8,9},{9,10},{10,1... | collective-permute-start | bytes 786440 | tf_op jit(solution)/shard_map/ppermute | solution.py:40
  12.9 0.7 bitcast_dynamic-update-slice_fusion.2
  13.5 3.5 %collective-permute-start.3 = (bf16[2,256,256]{2,1,0:T(8,128)(2,1)}, bf16[2,256,256]{2,1,0:T(8,128)(2,1)S(1)}, u32[]{:S(2)}, u32[]{:S(2)}) collective-permute-start(bf16[2,256,256]{2,1,0:T(8,128)(2,1)} %bitcast_dynamic-update-slice_fusion.2), channel_id=1, source_target_pairs={{0,2},{1,3},{2,4},{3,5},{4,6},{5,7},{6,8},{7,9},{8,10},{9,11},{10,... | collective-permute-start | bytes 786440 | tf_op jit(solution)/shard_map/ppermute | solution.py:40
  17.0 0.7 bitcast_dynamic-update-slice_fusion.1
  17.7 3.5 %collective-permute-start.6 = (bf16[2,256,256]{2,1,0:T(8,128)(2,1)}, bf16[2,256,256]{2,1,0:T(8,128)(2,1)S(1)}, u32[]{:S(2)}, u32[]{:S(2)}) collective-permute-start(bf16[2,256,256]{2,1,0:T(8,128)(2,1)} %bitcast_dynamic-update-slice_fusion.1), channel_id=1, source_target_pairs={{0,2},{1,3},{2,4},{3,5},{4,6},{5,7},{6,8},{7,9},{8,10},{9,11},{10,... | collective-permute-start | bytes 786440 | tf_op jit(solution)/shard_map/ppermute | solution.py:40
  21.2 0.7 bitcast_dynamic-update-slice_fusion
  21.9 2.1 %collective-permute-start.1 = (bf16[2,256,512]{2,1,0:T(8,128)(2,1)}, bf16[2,256,512]{2,1,0:T(8,128)(2,1)S(1)}, u32[]{:S(2)}, u32[]{:S(2)}) collective-permute-start(bf16[2,256,512]{2,1,0:T(8,128)(2,1)} %bitcast_dynamic-update-slice_fusion), channel_id=1, source_target_pairs={{0,2},{1,3},{2,4},{3,5},{4,6},{5,7},{6,8},{7,9},{8,10},{9,11},{10,... | collective-permute-start | bytes 1572872 | tf_op jit(solution)/shard_map/ppermute | solution.py:40
  24.0 1.1 %collective-permute-done.3.behind_ref = bf16[2,256,256]{2,1,0:T(8,128)(2,1)S(1)} collective-permute-done((bf16[2,256,256]{2,1,0:T(8,128)(2,1)}, bf16[2,256,256]{2,1,0:T(8,128)(2,1)S(1)}, u32[]{:S(2)}, u32[]{:S(2)}) %collective-permute-start.3) | collective-permute-done | bytes 262176 | tf_op jit(solution)/shard_map/ppermute | solution.py:40
  25.1 1.6 %copy-done = bf16[256,4096]{1,0:T(8,128)(2,1)S(1)} copy-done((bf16[256,4096]{1,0:T(8,128)(2,1)S(1)}, bf16[256,4096]{1,0:T(8,128)(2,1)}, u32[]{:S(2)}) %copy-start) | copy-done | bytes 2097176
  26.7 0.9 copy-done.4
  27.6 0.7 copy-done.5
  28.2 7.4 %attention.4 = (bf16[256,4096]{1,0:T(8,128)(2,1)}, bf16[256,4096]{1,0:T(8,128)(2,1)}, bf16[2,256,256]{2,1,0:T(8,128)(2,1)S(1)}, f32[256,256]{1,0:T(8,128)S(1)}, ...) custom-call(s32[1]{0:T(128)} %bitcast.first_ref, ...), custom_call_target="tpu_custom_call" | custom-call | flops 4831838208 | bytes 3538944 | tf_op jit(solution)/shard_map/attention/pallas_call | solution.py:256
  35.6 2.3 %collective-permute-start.5 = (bf16[2,256,256]{2,1,0:T(8,128)(2,1)S(1)}, bf16[2,256,256]{2,1,0:T(8,128)(2,1)S(1)}, u32[]{:S(2)}, u32[]{:S(2)}) collective-permute-start(bf16[2,256,256]{2,1,0:T(8,128)(2,1)S(1)} %get-tuple-element.88), channel_id=1, source_target_pairs={{2,0},{3,1},{4,2},{5,3},{6,4},{7,5},{8,6},{9,7},{10,8},{11,9},{12,... | collective-permute-start | bytes 786440 | tf_op jit(solution)/shard_map/ppermute | solution.py:40
  38.0 6.9 %attention.5 = (bf16[256,4096]{1,0:T(8,128)(2,1)}, bf16[256,4096]{1,0:T(8,128)(2,1)}, bf16[2,256,256]{2,1,0:T(8,128)(2,1)S(1)}, f32[256,256]{1,0:T(8,128)S(1)}, f32[256,256]{1,0:T(8,128)S(1)}) custom-call(s32[1]{0:T(128)} %bitcast.first_ref, s32[16]{0:T(128)S(1)} %copy-done.5, ...), custom_call_target="tpu_custom_call", output_to_operand_aliasing={{0}: (10, {}), {1}: (11, {})} | custom-call | flops 4831838208 | bytes 3538944 | tf_op jit(solution)/shard_map/attention/pallas_call | solution.py:256
  44.9 2.3 %collective-permute-start.7 = (bf16[2,256,256]{2,1,0:T(8,128)(2,1)S(1)}, bf16[2,256,256]{2,1,0:T(8,128)(2,1)S(1)}, u32[]{:S(2)}, u32[]{:S(2)}) collective-permute-start(bf16[2,256,256]{2,1,0:T(8,128)(2,1)S(1)} %get-tuple-element.94), channel_id=1, source_target_pairs={{2,0},{3,1},{4,2},{5,3},{6,4},{7,5},{8,6},{9,7},{10,8},{11,9},{12,... | collective-permute-start | bytes 786440 | tf_op jit(solution)/shard_map/ppermute | solution.py:40
  47.2 1.9 %collective-permute-done.5 = bf16[2,256,256]{2,1,0:T(8,128)(2,1)S(1)} collective-permute-done((bf16[2,256,256]{2,1,0:T(8,128)(2,1)S(1)}, bf16[2,256,256]{2,1,0:T(8,128)(2,1)S(1)}, u32[]{:S(2)}, u32[]{:S(2)}) %collective-permute-start.5) | collective-permute-done | bytes 262176 | tf_op jit(solution)/shard_map/ppermute | solution.py:40
  49.2 0.1 fusion.7
  49.3 6.9 %attention.6 = (bf16[256,4096]{1,0:T(8,128)(2,1)}, bf16[256,4096]{1,0:T(8,128)(2,1)}, bf16[2,256,256]{2,1,0:T(8,128)(2,1)S(1)}, f32[256,256]{1,0:T(8,128)S(1)}, f32[256,256]{1,0:T(8,128)S(1)}) custom-call(s32[1]{0:T(128)} %bitcast.first_ref, s32[16]{0:T(128)S(1)} %copy-done.6, ...), custom_call_target="tpu_custom_call", output_to_operand_aliasing={{0}: (10, {}), {1}: (11, {})} | custom-call | flops 4831838208 | bytes 3538944 | tf_op jit(solution)/shard_map/attention/pallas_call | solution.py:256
  56.2 2.2 %collective-permute-start.8 = (bf16[2,256,256]{2,1,0:T(8,128)(2,1)S(1)}, bf16[2,256,256]{2,1,0:T(8,128)(2,1)S(1)}, u32[]{:S(2)}, u32[]{:S(2)}) collective-permute-start(bf16[2,256,256]{2,1,0:T(8,128)(2,1)S(1)} %get-tuple-element.101), channel_id=1, source_target_pairs={{2,0},{3,1},{4,2},{5,3},{6,4},{7,5},{8,6},{9,7},{10,8},{11,9},{12,... | collective-permute-start | bytes 786440 | tf_op jit(solution)/shard_map/ppermute | solution.py:40
  58.5 6.9 %attention.7 = (bf16[256,4096]{1,0:T(8,128)(2,1)}, bf16[256,4096]{1,0:T(8,128)(2,1)}, bf16[2,256,256]{2,1,0:T(8,128)(2,1)S(1)}, f32[256,256]{1,0:T(8,128)S(1)}, f32[256,256]{1,0:T(8,128)S(1)}) custom-call(s32[1]{0:T(128)} %bitcast.first_ref, s32[16]{0:T(128)S(1)} %copy-done.6, ...), custom_call_target="tpu_custom_call", output_to_operand_aliasing={{0}: (10, {}), {1}: (11, {})} | custom-call | flops 4831838208 | bytes 3538944 | tf_op jit(solution)/shard_map/attention/pallas_call | solution.py:256
  65.5 4.0 %collective-permute-start.9 = (bf16[2,256,256]{2,1,0:T(8,128)(2,1)S(1)}, bf16[2,256,256]{2,1,0:T(8,128)(2,1)S(1)}, u32[]{:S(2)}, u32[]{:S(2)}) collective-permute-start(bf16[2,256,256]{2,1,0:T(8,128)(2,1)S(1)} %get-tuple-element.115), channel_id=1, source_target_pairs={{2,0},{3,1},{4,2},{5,3},{6,4},{7,5},{8,6},{9,7},{10,8},{11,9},{12,... | collective-permute-start | bytes 786440 | tf_op jit(solution)/shard_map/ppermute | solution.py:40
  69.5 1.9 %collective-permute-start.10 = (bf16[256,512]{1,0:T(8,128)(2,1)S(1)}, bf16[256,512]{1,0:T(8,128)(2,1)S(1)}, u32[]{:S(2)}, u32[]{:S(2)}) collective-permute-start(bf16[256,512]{1,0:T(8,128)(2,1)S(1)} %pad_maximum_fusion), channel_id=1, source_target_pairs={{1,0},{2,1},{3,2},{4,3},{5,4},{6,5},{7,6},{8,7},{9,8},{10,9},{11,1... | collective-permute-start | bytes 786440 | tf_op jit(solution)/shard_map/ppermute | solution.py:40
  71.5 4.7 %collective-permute-done.9 = bf16[2,256,256]{2,1,0:T(8,128)(2,1)S(1)} collective-permute-done((bf16[2,256,256]{2,1,0:T(8,128)(2,1)S(1)}, bf16[2,256,256]{2,1,0:T(8,128)(2,1)S(1)}, u32[]{:S(2)}, u32[]{:S(2)}) %collective-permute-start.9) | collective-permute-done | bytes 262176 | tf_op jit(solution)/shard_map/ppermute | solution.py:40
  76.4 4.3 %collective-permute-start.11 = (bf16[256,512]{1,0:T(8,128)(2,1)S(1)}, bf16[256,512]{1,0:T(8,128)(2,1)S(1)}, u32[]{:S(2)}, u32[]{:S(2)}) collective-permute-start(bf16[256,512]{1,0:T(8,128)(2,1)S(1)} %pad_maximum_fusion.1), channel_id=1, source_target_pairs={{1,0},{2,1},{3,2},{4,3},{5,4},{6,5},{7,6},{8,7},{9,8},{10,9},{11,1... | collective-permute-start | bytes 786440 | tf_op jit(solution)/shard_map/ppermute | solution.py:40
  80.7 3.7 %collective-permute-done.10 = bf16[256,512]{1,0:T(8,128)(2,1)S(1)} collective-permute-done((bf16[256,512]{1,0:T(8,128)(2,1)S(1)}, bf16[256,512]{1,0:T(8,128)(2,1)S(1)}, u32[]{:S(2)}, u32[]{:S(2)}) %collective-permute-start.10) | collective-permute-done | bytes 262176 | tf_op jit(solution)/shard_map/ppermute | solution.py:40
  84.4 4.8 %collective-permute-done.11 = bf16[256,512]{1,0:T(8,128)(2,1)S(1)} collective-permute-done((bf16[256,512]{1,0:T(8,128)(2,1)S(1)}, bf16[256,512]{1,0:T(8,128)(2,1)S(1)}, u32[]{:S(2)}, u32[]{:S(2)}) %collective-permute-start.11) | collective-permute-done | bytes 262176 | tf_op jit(solution)/shard_map/ppermute | solution.py:40
  89.2 0.1 fusion
  89.3 0.1 fusion.13
  89.4 0.9 pad_maximum_fusion.2
  (27 shorter events, 0.4 us)
Async XLA Ops:
  2.7 10.2 %collective-permute-start.2 = (bf16[256,256]{1,0:T(8,128)(2,1)}, bf16[256,256]{1,0:T(8,128)(2,1)S(1)}, u32[]{:S(2)}, u32[]{:S(2)}) collective-permute-start(bf16[256,256]{1,0:T(8,128)(2,1)} %get-tuple-element.86.own_ref), channel_id=1, source_target_pairs={{0,1},{1,2},{2,3},{3,4},{4,5},{5,6},{6,7},{7,8},{8,9},{9,10},{10,1... | collective-permute-start | bytes 393224 | tf_op jit(solution)/shard_map/ppermute | solution.py:40
  6.0 11.0 %collective-permute-start.4 = (bf16[256,256]{1,0:T(8,128)(2,1)}, bf16[256,256]{1,0:T(8,128)(2,1)S(1)}, u32[]{:S(2)}, u32[]{:S(2)}) collective-permute-start(bf16[256,256]{1,0:T(8,128)(2,1)} %get-tuple-element.85.own_ref), channel_id=1, source_target_pairs={{0,1},{1,2},{2,3},{3,4},{4,5},{5,6},{6,7},{7,8},{8,9},{9,10},{10,1... | collective-permute-start | bytes 393224 | tf_op jit(solution)/shard_map/ppermute | solution.py:40
  9.4 11.8 %collective-permute-start = (bf16[256,512]{1,0:T(8,128)(2,1)}, bf16[256,512]{1,0:T(8,128)(2,1)S(1)}, u32[]{:S(2)}, u32[]{:S(2)}) collective-permute-start(bf16[256,512]{1,0:T(8,128)(2,1)} %get-tuple-element.104.own_ref), channel_id=1, source_target_pairs={{0,1},{1,2},{2,3},{3,4},{4,5},{5,6},{6,7},{7,8},{8,9},{9,10},{10,1... | collective-permute-start | bytes 786440 | tf_op jit(solution)/shard_map/ppermute | solution.py:40
  13.5 11.5 %collective-permute-start.3 = (bf16[2,256,256]{2,1,0:T(8,128)(2,1)}, bf16[2,256,256]{2,1,0:T(8,128)(2,1)S(1)}, u32[]{:S(2)}, u32[]{:S(2)}) collective-permute-start(bf16[2,256,256]{2,1,0:T(8,128)(2,1)} %bitcast_dynamic-update-slice_fusion.2), channel_id=1, source_target_pairs={{0,2},{1,3},{2,4},{3,5},{4,6},{5,7},{6,8},{7,9},{8,10},{9,11},{10,... | collective-permute-start | bytes 786440 | tf_op jit(solution)/shard_map/ppermute | solution.py:40
  17.7 20.3 %collective-permute-start.6 = (bf16[2,256,256]{2,1,0:T(8,128)(2,1)}, bf16[2,256,256]{2,1,0:T(8,128)(2,1)S(1)}, u32[]{:S(2)}, u32[]{:S(2)}) collective-permute-start(bf16[2,256,256]{2,1,0:T(8,128)(2,1)} %bitcast_dynamic-update-slice_fusion.1), channel_id=1, source_target_pairs={{0,2},{1,3},{2,4},{3,5},{4,6},{5,7},{6,8},{7,9},{8,10},{9,11},{10,... | collective-permute-start | bytes 786440 | tf_op jit(solution)/shard_map/ppermute | solution.py:40
  21.9 27.3 %collective-permute-start.1 = (bf16[2,256,512]{2,1,0:T(8,128)(2,1)}, bf16[2,256,512]{2,1,0:T(8,128)(2,1)S(1)}, u32[]{:S(2)}, u32[]{:S(2)}) collective-permute-start(bf16[2,256,512]{2,1,0:T(8,128)(2,1)} %bitcast_dynamic-update-slice_fusion), channel_id=1, source_target_pairs={{0,2},{1,3},{2,4},{3,5},{4,6},{5,7},{6,8},{7,9},{8,10},{9,11},{10,... | collective-permute-start | bytes 1572872 | tf_op jit(solution)/shard_map/ppermute | solution.py:40
  25.1 1.6 %copy-start = (bf16[256,4096]{1,0:T(8,128)(2,1)S(1)}, bf16[256,4096]{1,0:T(8,128)(2,1)}, u32[]{:S(2)}) copy-start(bf16[256,4096]{1,0:T(8,128)(2,1)} %q_ref.7) | copy-start | bytes 6291460
  26.6 0.9 %copy-start.4 = (bf16[256,256]{1,0:T(8,128)(2,1)S(1)}, bf16[256,256]{1,0:T(8,128)(2,1)}, u32[]{:S(2)}) copy-start(bf16[256,256]{1,0:T(8,128)(2,1)} %get-tuple-element.86.own_ref) | copy-start | bytes 393220
  27.6 0.7 copy-start.5
  28.2 9.8 %copy-start.3 = (bf16[256,256]{1,0:T(8,128)(2,1)S(1)}, bf16[256,256]{1,0:T(8,128)(2,1)}, u32[]{:S(2)}) copy-start(bf16[256,256]{1,0:T(8,128)(2,1)} %get-tuple-element.85.own_ref) | copy-start | bytes 393220
  35.6 13.5 %collective-permute-start.5 = (bf16[2,256,256]{2,1,0:T(8,128)(2,1)S(1)}, bf16[2,256,256]{2,1,0:T(8,128)(2,1)S(1)}, u32[]{:S(2)}, u32[]{:S(2)}) collective-permute-start(bf16[2,256,256]{2,1,0:T(8,128)(2,1)S(1)} %get-tuple-element.88), channel_id=1, source_target_pairs={{2,0},{3,1},{4,2},{5,3},{6,4},{7,5},{8,6},{9,7},{10,8},{11,9},{12,... | collective-permute-start | bytes 786440 | tf_op jit(solution)/shard_map/ppermute | solution.py:40
  38.0 11.3 %copy-start.2 = (bf16[256,512]{1,0:T(8,128)(2,1)S(1)}, bf16[256,512]{1,0:T(8,128)(2,1)}, u32[]{:S(2)}) copy-start(bf16[256,512]{1,0:T(8,128)(2,1)} %get-tuple-element.104.own_ref) | copy-start | bytes 786436
  44.9 4.3 %copy-start.1 = (bf16[256,4096]{1,0:T(8,128)(2,1)S(1)}, bf16[256,4096]{1,0:T(8,128)(2,1)}, u32[]{:S(2)}) copy-start(bf16[256,4096]{1,0:T(8,128)(2,1)} %q_ref.7) | copy-start | bytes 6291460
  44.9 4.3 %copy-start.6 = (s32[16]{0:T(128)S(1)}, s32[16]{0:T(128)}, u32[]{:S(2)}) copy-start(s32[16]{0:T(128)} %lengths_ref.7) | copy-start | bytes 196
  44.9 13.5 %collective-permute-start.7 = (bf16[2,256,256]{2,1,0:T(8,128)(2,1)S(1)}, bf16[2,256,256]{2,1,0:T(8,128)(2,1)S(1)}, u32[]{:S(2)}, u32[]{:S(2)}) collective-permute-start(bf16[2,256,256]{2,1,0:T(8,128)(2,1)S(1)} %get-tuple-element.94), channel_id=1, source_target_pairs={{2,0},{3,1},{4,2},{5,3},{6,4},{7,5},{8,6},{9,7},{10,8},{11,9},{12,... | collective-permute-start | bytes 786440 | tf_op jit(solution)/shard_map/ppermute | solution.py:40
  56.2 15.2 %collective-permute-start.8 = (bf16[2,256,256]{2,1,0:T(8,128)(2,1)S(1)}, bf16[2,256,256]{2,1,0:T(8,128)(2,1)S(1)}, u32[]{:S(2)}, u32[]{:S(2)}) collective-permute-start(bf16[2,256,256]{2,1,0:T(8,128)(2,1)S(1)} %get-tuple-element.101), channel_id=1, source_target_pairs={{2,0},{3,1},{4,2},{5,3},{6,4},{7,5},{8,6},{9,7},{10,8},{11,9},{12,... | collective-permute-start | bytes 786440 | tf_op jit(solution)/shard_map/ppermute | solution.py:40
  65.5 10.7 %collective-permute-start.9 = (bf16[2,256,256]{2,1,0:T(8,128)(2,1)S(1)}, bf16[2,256,256]{2,1,0:T(8,128)(2,1)S(1)}, u32[]{:S(2)}, u32[]{:S(2)}) collective-permute-start(bf16[2,256,256]{2,1,0:T(8,128)(2,1)S(1)} %get-tuple-element.115), channel_id=1, source_target_pairs={{2,0},{3,1},{4,2},{5,3},{6,4},{7,5},{8,6},{9,7},{10,8},{11,9},{12,... | collective-permute-start | bytes 786440 | tf_op jit(solution)/shard_map/ppermute | solution.py:40
  69.5 14.9 %collective-permute-start.10 = (bf16[256,512]{1,0:T(8,128)(2,1)S(1)}, bf16[256,512]{1,0:T(8,128)(2,1)S(1)}, u32[]{:S(2)}, u32[]{:S(2)}) collective-permute-start(bf16[256,512]{1,0:T(8,128)(2,1)S(1)} %pad_maximum_fusion), channel_id=1, source_target_pairs={{1,0},{2,1},{3,2},{4,3},{5,4},{6,5},{7,6},{8,7},{9,8},{10,9},{11,1... | collective-permute-start | bytes 786440 | tf_op jit(solution)/shard_map/ppermute | solution.py:40
  76.4 12.8 %collective-permute-start.11 = (bf16[256,512]{1,0:T(8,128)(2,1)S(1)}, bf16[256,512]{1,0:T(8,128)(2,1)S(1)}, u32[]{:S(2)}, u32[]{:S(2)}) collective-permute-start(bf16[256,512]{1,0:T(8,128)(2,1)S(1)} %pad_maximum_fusion.1), channel_id=1, source_target_pairs={{1,0},{2,1},{3,2},{4,3},{5,4},{6,5},{7,6},{8,7},{9,8},{10,9},{11,1... | collective-permute-start | bytes 786440 | tf_op jit(solution)/shard_map/ppermute | solution.py:40

commit v15 on v14

--- a/solution.py
+++ b/solution.py
@@ -18,7 +18,7 @@
 UNIT = 4
 FORWARD = ((0,), (1,), (2, 3))
 OUTS = 5
-SCRATCH = 30
+SCRATCH = 31
 MASKED = -1e30
 SCALE = 1.0 / math.sqrt(HEAD_SIZE)
 EXP2_SCALE = SCALE * math.log2(math.e)
@@ -68,13 +68,8 @@
         bias_ref[:, part * 128 : (part + 1) * 128] = jnp.where(allowed, 0.0, MASKED)
 
 
-def attention_kernel(where, leads, first_ref, lengths_ref, q_ref, g_ref, behind_ref, near_ref, own_ref, *refs):
-    if not leads:
-        bias_ref, old_ref, cut_ref, *refs = refs
-    made = 3 if leads else 0
-    out_ref, dq_ref, dbehind_ref, dnear_ref, down_ref, *masks = refs[-(OUTS + SCRATCH + made) : -SCRATCH]
-    if leads:
-        bias_ref, old_ref, cut_ref = masks
+def attention_kernel(where, q_ref, g_ref, behind_ref, near_ref, own_full_ref, bias_ref, old_ref, cut_ref, *refs):
+    out_ref, dq_ref, dbehind_ref, dnear_ref, down_ref = refs[-(OUTS + SCRATCH) : -SCRATCH]
     (
         key_ref, value_ref, key_t_ref, value_t_ref, key2_ref, value2_ref, key2_t_ref, value2_t_ref,
         dk_ref, dv_ref, dk2_ref, dv2_ref, *slots,
@@ -85,11 +80,13 @@
     head, *offsets = where
     key_in, value_in, key_out, value_out = (slice(at, at + HEAD_SIZE) for at in offsets)
     q_full_ref, g_full_ref, out_full_ref, dq_full_ref = q_ref, g_ref, out_ref, dq_ref
-    q_ref, g_ref, out_ref, dq_ref, sem = copies
+    q_ref, g_ref, out_ref, dq_ref, own_ref, sem = copies
     rows, wide = q_ref.shape
     mine = slice(head * wide, (head + 1) * wide)
     q_copy = pltpu.make_async_copy(q_full_ref.at[:, mine], q_ref, sem.at[0])
     g_copy = pltpu.make_async_copy(g_full_ref.at[:, mine], g_ref, sem.at[1])
+    own_copy = pltpu.make_async_copy(own_full_ref, own_ref, sem.at[2 + 2 * GROUP // UNIT])
+    own_copy.start()
     q_copy.start()
     g_copy.start()
     window = (SPAN - 1) * rows
@@ -98,8 +95,7 @@
     two = slice(0, rows)
     rest = slice(rows, window)
 
-    if leads:
-        write_masks(bias_ref, old_ref, cut_ref, lengths_ref, first_ref, rows)
+    own_copy.wait()
     from_far = lax.broadcasted_iota(jnp.int32, (rows, HEAD_SIZE), 0) >= cut_ref[0, 0]
     mid, far, near, own = behind_ref.at[0], behind_ref.at[1], near_ref, own_ref
     for j, block in enumerate((mid, near)):
@@ -226,50 +222,43 @@
         copy.wait()
 
 
-def attention(head, first, lengths, queries, out_grad, blocks, place, grads, masks):
+def attention(head, queries, out_grad, blocks, place, grads, masks):
     rows = queries.shape[0]
     wide = GROUP * HEAD_SIZE
     pair = 2 * HEAD_SIZE
     window = (SPAN - 1) * rows
-    leads = masks is None
-    query_spec = pl.BlockSpec(memory_space=pl.ANY)
+    query_spec = pl.BlockSpec(memory_space=pltpu.HBM)
 
     def whole(shape):
         return pl.BlockSpec(shape, lambda i, *_: (0,) * len(shape))
 
-    mask_shapes = ((rows, window), (rows, HEAD_SIZE), (8, HEAD_SIZE))
-    mask_specs = [whole(shape) for shape in mask_shapes]
     fore = blocks[-1].shape[1] // pair
     where = [head, *(at * HEAD_SIZE for at in (place, fore + place, 0, 1))]
-    operands = [first, lengths, queries, out_grad, *blocks]
-    in_specs = [query_spec] * 2 + [whole(block.shape) for block in blocks]
+    operands = [queries, out_grad, *blocks, *masks]
+    in_specs = [query_spec] * 2 + [whole(block.shape) for block in blocks[:-1]]
+    in_specs += [pl.BlockSpec(memory_space=pl.ANY)] + [whole(mask.shape) for mask in masks]
     aliases = {}
-    if not leads:
-        operands += masks
-        in_specs += mask_specs
     for at, array in enumerate(grads):
         if array is not None:
             aliases[len(operands)] = at
             operands.append(array)
-            in_specs.append(pl.BlockSpec(memory_space=pl.ANY))
+            in_specs.append(query_spec)
     bf16, f32 = jnp.bfloat16, jnp.float32
     results = pl.pallas_call(
-        functools.partial(attention_kernel, where, leads),
+        functools.partial(attention_kernel, where),
         out_shape=[
             jax.ShapeDtypeStruct(queries.shape, bf16),
             jax.ShapeDtypeStruct(queries.shape, bf16),
             jax.ShapeDtypeStruct((2, rows, pair), bf16),
             jax.ShapeDtypeStruct((rows, pair), f32),
             jax.ShapeDtypeStruct((rows, pair), f32),
-        ]
-        + [jax.ShapeDtypeStruct(*mask) for mask in zip(mask_shapes, (f32, f32, jnp.int32)) if leads],
+        ],
         grid_spec=pltpu.PrefetchScalarGridSpec(
-            num_scalar_prefetch=2,
+            num_scalar_prefetch=0,
             grid=(1,),
             in_specs=in_specs,
             out_specs=[query_spec] * 2
-            + [whole((2, rows, pair)), whole((rows, pair)), whole((rows, pair))]
-            + (mask_specs if leads else []),
+            + [whole((2, rows, pair)), whole((rows, pair)), whole((rows, pair))],
             scratch_shapes=[
                 pltpu.VMEM(shape, kind)
                 for shape, kind, count in (
@@ -290,10 +279,10 @@
                 for _ in range(count)
             ]
             + [pltpu.VMEM((rows, wide), bf16)] * 4
-            + [pltpu.SemaphoreType.DMA((2 + 2 * GROUP // UNIT,))],
+            + [pltpu.VMEM(blocks[-1].shape, bf16), pltpu.SemaphoreType.DMA((3 + 2 * GROUP // UNIT,))],
         ),
         input_output_aliases=aliases,
-        compiler_params=pltpu.CompilerParams(vmem_limit_bytes=48 * 1024 * 1024),
+        compiler_params=pltpu.CompilerParams(vmem_limit_bytes=51 * 1024 * 1024),
         cost_estimate=pl.CostEstimate(
             flops=12 * rows * GROUP * window * HEAD_SIZE * 2,
             bytes_accessed=4 * rows * wide * 2 + 22 * rows * pair,
@@ -301,10 +290,15 @@
         ),
         name="attention",
     )(*operands)
-    return results[:2], results[2:OUTS], results[OUTS:] if leads else masks
-
-
-def pack_kernel(keys_ref, values_ref, *refs):
+    return results[:2], results[2:]
+
+
+def origin(rank, *_):
+    return (0,) * rank
+
+
+def pack_kernel(first_ref, lengths_ref, keys_ref, values_ref, *refs):
+    write_masks(*refs[-3:], lengths_ref, first_ref, keys_ref.shape[0])
     for at, heads in enumerate(FORWARD):
         span = slice(heads[0] * HEAD_SIZE, (heads[-1] + 1) * HEAD_SIZE)
         width = span.stop - span.start
@@ -314,22 +308,35 @@
             target_ref[:, width:] = values_ref[:, span]
 
 
-def pack(keys, values):
+def pack(first, lengths, keys, values):
     rows = keys.shape[0]
-    shapes, specs = [], []
+    shapes = []
     for heads in FORWARD:
         own = (rows, 2 * HEAD_SIZE * len(heads))
         shapes += [jax.ShapeDtypeStruct(own, keys.dtype), jax.ShapeDtypeStruct((2, *own), keys.dtype)]
-        specs += [pl.BlockSpec(own, lambda i: (0, 0)), pl.BlockSpec((1, *own), lambda i: (0, 0, 0))]
+    specs = [
+        pl.BlockSpec((1,) * (len(packed.shape) - 2) + packed.shape[-2:], functools.partial(origin, len(packed.shape)))
+        for packed in shapes
+    ]
+    masks = [
+        jax.ShapeDtypeStruct((rows, (SPAN - 1) * rows), jnp.float32),
+        jax.ShapeDtypeStruct((rows, HEAD_SIZE), jnp.float32),
+        jax.ShapeDtypeStruct((8, HEAD_SIZE), jnp.int32),
+    ]
+    two = functools.partial(origin, 2)
     results = pl.pallas_call(
         pack_kernel,
-        grid=(1,),
-        out_shape=shapes,
-        in_specs=[pl.BlockSpec(keys.shape, lambda i: (0, 0))] * 2,
-        out_specs=specs,
+        out_shape=shapes + masks,
+        grid_spec=pltpu.PrefetchScalarGridSpec(
+            num_scalar_prefetch=2,
+            grid=(1,),
+            in_specs=[pl.BlockSpec(keys.shape, two)] * 2,
+            out_specs=specs + [pl.BlockSpec(mask.shape, two) for mask in masks],
+        ),
         name="pack",
-    )(keys, values)
-    return results[0::2], results[1::2]
+    )(first, lengths, keys, values)
+    packed = results[: len(shapes)]
+    return packed[0::2], packed[1::2], results[len(shapes) :]
 
 
 def local(queries, keys, values, out_grad, doc_lengths):
@@ -338,7 +345,7 @@
     first = (index * rows).astype(jnp.int32).reshape(1)
     bf16, f32 = jnp.bfloat16, jnp.float32
     blocks, nears = {}, []
-    owns, pairs = pack(keys, values)
+    owns, pairs, masks = pack(first, doc_lengths, keys, values)
     for own in owns:
         nears.append(passed_along(own, 1))
     pairs = [pair.at[1].set(near) for pair, near in zip(pairs, nears)]
@@ -346,16 +353,14 @@
         behind = passed_along(pair, 2)
         for place, head in enumerate(heads):
             blocks[head] = ((behind, near, own), place)
-    grads, masks = (None, None), None
+    grads = (None, None)
     parts = []
 
     def attend(head, after=()):
-        nonlocal grads, masks
+        nonlocal grads
         (behind, near, own), place = blocks[head]
         own, *after = lax.optimization_barrier((own, *after))
-        grads, part, masks = attention(
-            head, first, doc_lengths, queries, out_grad, (behind, near, own), place, grads, masks
-        )
+        grads, part = attention(head, queries, out_grad, (behind, near, own), place, grads, masks)
         parts.append(list(part))
         return after
 

time: 92.1 us -> 95.4 us (1.036)
  Pallas kernels: 30.2 us -> 33.3 us
  starting transfers between devices: 36.1 us -> 37.4 us
  waiting for transfers between devices: 16.2 us -> 15 us
    pallas_call x5, Pallas kernels: 30.2 us -> 33.3 us  [the longest x4 29.9 us: attention(): pl.pallas_call(functools.partial(attention_kernel, where), out_shape=[jax...]
    ppermute x12, starting transfers between devices: 36.1 us -> 37.4 us  [passed_along(): lax.ppermute(value, AXES, [(source, source + steps) for source in range(f...]
    ppermute x12, waiting for transfers between devices: 16.2 us -> 15 us  [passed_along(): lax.ppermute(value, AXES, [(source, source + steps) for source in range(f...]
  transfers between devices with their start and end apart: 12 -> 12, of which waited for: 5 -> 5; matrix products, arithmetic and copies ran while one was open for 3% -> 3% of each run, Pallas kernels for 31% -> 32%
where the time goes in v15:
time: 95.4 us; the launch traced here: 93.9 us
  starting transfers between devices  37.4 us (39%)
  Pallas kernels  33.3 us (35%)
  waiting for transfers between devices  15 us (16%)
  local copies, waits for them, and re-layouts  5.79 us (6%)
  other arithmetic  1.45 us (2%)
    ppermute x12, starting transfers between devices, passed_along(): lax.ppermute(value, AXES, [(source, source + steps) for source in range(f...  37.4 us
    pallas_call x4, Pallas kernels, attention(): pl.pallas_call(functools.partial(attention_kernel, where), out_shape=[jax...  29.9 us
    ppermute x12, waiting for transfers between devices, passed_along(): lax.ppermute(value, AXES, [(source, source + steps) for source in range(f...  15 us
    unnamed x14, local copies, waits for them, and re-layouts  3.64 us
    pallas_call x1, Pallas kernels, pack(): pl.pallas_call(pack_kernel, out_shape=shapes + masks, grid_spec=pltpu.Pre...  3.41 us
    scatter x3, local copies, waits for them, and re-layouts, local(): pairs = [pair.at[1].set(near) for pair, near in zip(pairs, nears)]  2.05 us
  transfers between devices with their start and end apart: 12, of which 5 were waited for; matrix products, arithmetic and copies ran while one was open for 3% of the time, Pallas kernels for 32%

profile of v15, /device:TPU:29, one launch (start us, length us, event | category | flops | bytes accessed | tf_op | source)
XLA Modules:
  0.0 93.9 jit_solution(4218795236472135887)
XLA Ops:
  0.6 3.4 %pack.1 = (bf16[256,256]{1,0:T(8,128)(2,1)}, bf16[2,256,256]{2,1,0:T(8,128)(2,1)}, bf16[256,256]{1,0:T(8,128)(2,1)}, bf16[2,256,256]{2,1,0:T(8,128)(2,1)}, bf16[...) custom-call(s32[1]{0:T(128)} %bitcast.first_ref, ...), custom_call_target="tpu_custom_call" | custom-call | tf_op jit(solution)/shard_map/pack/pallas_call | solution.py:327
  4.0 3.3 %collective-permute-start.2 = (bf16[256,256]{1,0:T(8,128)(2,1)}, bf16[256,256]{1,0:T(8,128)(2,1)S(1)}, u32[]{:S(2)}, u32[]{:S(2)}) collective-permute-start(bf16[256,256]{1,0:T(8,128)(2,1)} %get-tuple-element.86.own_full_ref), channel_id=1, source_target_pairs={{0,1},{1,2},{2,3},{3,4},{4,5},{5,6},{6,7},{7,8},{8,9},{9,10},{10,1... | collective-permute-start | bytes 393224 | tf_op jit(solution)/shard_map/ppermute | solution.py:40
  7.3 3.4 %collective-permute-start.4 = (bf16[256,256]{1,0:T(8,128)(2,1)}, bf16[256,256]{1,0:T(8,128)(2,1)S(1)}, u32[]{:S(2)}, u32[]{:S(2)}) collective-permute-start(bf16[256,256]{1,0:T(8,128)(2,1)} %get-tuple-element.85.own_full_ref), channel_id=1, source_target_pairs={{0,1},{1,2},{2,3},{3,4},{4,5},{5,6},{6,7},{7,8},{8,9},{9,10},{10,1... | collective-permute-start | bytes 393224 | tf_op jit(solution)/shard_map/ppermute | solution.py:40
  10.8 3.4 %collective-permute-start = (bf16[256,512]{1,0:T(8,128)(2,1)}, bf16[256,512]{1,0:T(8,128)(2,1)S(1)}, u32[]{:S(2)}, u32[]{:S(2)}) collective-permute-start(bf16[256,512]{1,0:T(8,128)(2,1)} %get-tuple-element.104.own_full_ref), channel_id=1, source_target_pairs={{0,1},{1,2},{2,3},{3,4},{4,5},{5,6},{6,7},{7,8},{8,9},{9,10},{10,1... | collective-permute-start | bytes 786440 | tf_op jit(solution)/shard_map/ppermute | solution.py:40
  14.2 0.7 bitcast_dynamic-update-slice_fusion.2
  14.9 3.5 %collective-permute-start.3 = (bf16[2,256,256]{2,1,0:T(8,128)(2,1)}, bf16[2,256,256]{2,1,0:T(8,128)(2,1)S(1)}, u32[]{:S(2)}, u32[]{:S(2)}) collective-permute-start(bf16[2,256,256]{2,1,0:T(8,128)(2,1)} %bitcast_dynamic-update-slice_fusion.2), channel_id=1, source_target_pairs={{0,2},{1,3},{2,4},{3,5},{4,6},{5,7},{6,8},{7,9},{8,10},{9,11},{10,... | collective-permute-start | bytes 786440 | tf_op jit(solution)/shard_map/ppermute | solution.py:40
  18.4 0.7 bitcast_dynamic-update-slice_fusion.1
  19.0 3.5 %collective-permute-start.6 = (bf16[2,256,256]{2,1,0:T(8,128)(2,1)}, bf16[2,256,256]{2,1,0:T(8,128)(2,1)S(1)}, u32[]{:S(2)}, u32[]{:S(2)}) collective-permute-start(bf16[2,256,256]{2,1,0:T(8,128)(2,1)} %bitcast_dynamic-update-slice_fusion.1), channel_id=1, source_target_pairs={{0,2},{1,3},{2,4},{3,5},{4,6},{5,7},{6,8},{7,9},{8,10},{9,11},{10,... | collective-permute-start | bytes 786440 | tf_op jit(solution)/shard_map/ppermute | solution.py:40
  22.5 0.7 bitcast_dynamic-update-slice_fusion
  23.2 2.1 %collective-permute-start.1 = (bf16[2,256,512]{2,1,0:T(8,128)(2,1)}, bf16[2,256,512]{2,1,0:T(8,128)(2,1)S(1)}, u32[]{:S(2)}, u32[]{:S(2)}) collective-permute-start(bf16[2,256,512]{2,1,0:T(8,128)(2,1)} %bitcast_dynamic-update-slice_fusion), channel_id=1, source_target_pairs={{0,2},{1,3},{2,4},{3,5},{4,6},{5,7},{6,8},{7,9},{8,10},{9,11},{10,... | collective-permute-start | bytes 1572872 | tf_op jit(solution)/shard_map/ppermute | solution.py:40
  25.4 1.1 %collective-permute-done.3.behind_ref = bf16[2,256,256]{2,1,0:T(8,128)(2,1)S(1)} collective-permute-done((bf16[2,256,256]{2,1,0:T(8,128)(2,1)}, bf16[2,256,256]{2,1,0:T(8,128)(2,1)S(1)}, u32[]{:S(2)}, u32[]{:S(2)}) %collective-permute-start.3) | collective-permute-done | bytes 262176 | tf_op jit(solution)/shard_map/ppermute | solution.py:40
  26.4 1.1 %copy-done = f32[256,768]{1,0:T(8,128)S(1)} copy-done((f32[256,768]{1,0:T(8,128)S(1)}, f32[256,768]{1,0:T(8,128)}, u32[]{:S(2)}) %copy-start) | copy-done | bytes 786456
  27.6 0.9 copy-done.3
  28.5 0.9 copy-done.5
  29.4 0.7 copy-done.6
  30.0 7.5 %attention.4 = (bf16[256,4096]{1,0:T(8,128)(2,1)}, bf16[256,4096]{1,0:T(8,128)(2,1)}, bf16[2,256,256]{2,1,0:T(8,128)(2,1)S(1)}, f32[256,256]{1,0:T(8,128)S(1)}, f32[256,256]{1,0:T(8,128)S(1)}) custom-call(bf16[256,4096]{1,0:T(8,128)(2,1)} %q_ref.7, bf16[256,4096]{1,0:T(8,128)(2,1)} %g_ref.7, bf16[2,256,256]{2,1,0:T(8,128)(2,1)S(1)} %collective-permute-done.3.behind_ref, ...), custom_call_target="tpu_custom_call" | custom-call | flops 4831838208 | bytes 3538944 | tf_op jit(solution)/shard_map/attention/pallas_call | solution.py:247
  37.6 2.3 %collective-permute-start.5 = (bf16[2,256,256]{2,1,0:T(8,128)(2,1)S(1)}, bf16[2,256,256]{2,1,0:T(8,128)(2,1)S(1)}, u32[]{:S(2)}, u32[]{:S(2)}) collective-permute-start(bf16[2,256,256]{2,1,0:T(8,128)(2,1)S(1)} %get-tuple-element.91), channel_id=1, source_target_pairs={{2,0},{3,1},{4,2},{5,3},{6,4},{7,5},{8,6},{9,7},{10,8},{11,9},{12,... | collective-permute-start | bytes 786440 | tf_op jit(solution)/shard_map/ppermute | solution.py:40
  39.9 7.6 %attention.5 = (bf16[256,4096]{1,0:T(8,128)(2,1)}, bf16[256,4096]{1,0:T(8,128)(2,1)}, bf16[2,256,256]{2,1,0:T(8,128)(2,1)S(1)}, f32[256,256]{1,0:T(8,128)S(1)}, f32[256,256]{1,0:T(8,128)S(1)}) custom-call(bf16[256,4096]{1,0:T(8,128)(2,1)} %q_ref.7, bf16[256,4096]{1,0:T(8,128)(2,1)} %g_ref.7, ...), custom_call_target="tpu_custom_call", output_to_operand_aliasing={{0}: (8, {}), {1}: (9, {})} | custom-call | flops 4831838208 | bytes 3538944 | tf_op jit(solution)/shard_map/attention/pallas_call | solution.py:247
  47.5 2.3 %collective-permute-start.7 = (bf16[2,256,256]{2,1,0:T(8,128)(2,1)S(1)}, bf16[2,256,256]{2,1,0:T(8,128)(2,1)S(1)}, u32[]{:S(2)}, u32[]{:S(2)}) collective-permute-start(bf16[2,256,256]{2,1,0:T(8,128)(2,1)S(1)} %get-tuple-element.94), channel_id=1, source_target_pairs={{2,0},{3,1},{4,2},{5,3},{6,4},{7,5},{8,6},{9,7},{10,8},{11,9},{12,... | collective-permute-start | bytes 786440 | tf_op jit(solution)/shard_map/ppermute | solution.py:40
  49.8 1.3 %collective-permute-done.5 = bf16[2,256,256]{2,1,0:T(8,128)(2,1)S(1)} collective-permute-done((bf16[2,256,256]{2,1,0:T(8,128)(2,1)S(1)}, bf16[2,256,256]{2,1,0:T(8,128)(2,1)S(1)}, u32[]{:S(2)}, u32[]{:S(2)}) %collective-permute-start.5) | collective-permute-done | bytes 262176 | tf_op jit(solution)/shard_map/ppermute | solution.py:40
  51.2 7.4 %attention.6 = (bf16[256,4096]{1,0:T(8,128)(2,1)}, bf16[256,4096]{1,0:T(8,128)(2,1)}, bf16[2,256,256]{2,1,0:T(8,128)(2,1)S(1)}, f32[256,256]{1,0:T(8,128)S(1)}, f32[256,256]{1,0:T(8,128)S(1)}) custom-call(bf16[256,4096]{1,0:T(8,128)(2,1)} %q_ref.7, bf16[256,4096]{1,0:T(8,128)(2,1)} %g_ref.7, ...), custom_call_target="tpu_custom_call", output_to_operand_aliasing={{0}: (8, {}), {1}: (9, {})} | custom-call | flops 4831838208 | bytes 3538944 | tf_op jit(solution)/shard_map/attention/pallas_call | solution.py:247
  58.6 2.2 %collective-permute-start.8 = (bf16[2,256,256]{2,1,0:T(8,128)(2,1)S(1)}, bf16[2,256,256]{2,1,0:T(8,128)(2,1)S(1)}, u32[]{:S(2)}, u32[]{:S(2)}) collective-permute-start(bf16[2,256,256]{2,1,0:T(8,128)(2,1)S(1)} %get-tuple-element.101), channel_id=1, source_target_pairs={{2,0},{3,1},{4,2},{5,3},{6,4},{7,5},{8,6},{9,7},{10,8},{11,9},{12,... | collective-permute-start | bytes 786440 | tf_op jit(solution)/shard_map/ppermute | solution.py:40
  60.9 7.4 %attention.7 = (bf16[256,4096]{1,0:T(8,128)(2,1)}, bf16[256,4096]{1,0:T(8,128)(2,1)}, bf16[2,256,256]{2,1,0:T(8,128)(2,1)S(1)}, f32[256,256]{1,0:T(8,128)S(1)}, f32[256,256]{1,0:T(8,128)S(1)}) custom-call(bf16[256,4096]{1,0:T(8,128)(2,1)} %q_ref.7, bf16[256,4096]{1,0:T(8,128)(2,1)} %g_ref.7, ...), custom_call_target="tpu_custom_call", output_to_operand_aliasing={{0}: (8, {}), {1}: (9, {})} | custom-call | flops 4831838208 | bytes 3538944 | tf_op jit(solution)/shard_map/attention/pallas_call | solution.py:247
  68.4 4.6 %collective-permute-start.9 = (bf16[2,256,256]{2,1,0:T(8,128)(2,1)S(1)}, bf16[2,256,256]{2,1,0:T(8,128)(2,1)S(1)}, u32[]{:S(2)}, u32[]{:S(2)}) collective-permute-start(bf16[2,256,256]{2,1,0:T(8,128)(2,1)S(1)} %get-tuple-element.115), channel_id=1, source_target_pairs={{2,0},{3,1},{4,2},{5,3},{6,4},{7,5},{8,6},{9,7},{10,8},{11,9},{12,... | collective-permute-start | bytes 786440 | tf_op jit(solution)/shard_map/ppermute | solution.py:40
  73.0 1.9 %collective-permute-start.10 = (bf16[256,512]{1,0:T(8,128)(2,1)S(1)}, bf16[256,512]{1,0:T(8,128)(2,1)S(1)}, u32[]{:S(2)}, u32[]{:S(2)}) collective-permute-start(bf16[256,512]{1,0:T(8,128)(2,1)S(1)} %pad_maximum_fusion), channel_id=1, source_target_pairs={{1,0},{2,1},{3,2},{4,3},{5,4},{6,5},{7,6},{8,7},{9,8},{10,9},{11,1... | collective-permute-start | bytes 786440 | tf_op jit(solution)/shard_map/ppermute | solution.py:40
  75.0 4.0 %collective-permute-done.9 = bf16[2,256,256]{2,1,0:T(8,128)(2,1)S(1)} collective-permute-done((bf16[2,256,256]{2,1,0:T(8,128)(2,1)S(1)}, bf16[2,256,256]{2,1,0:T(8,128)(2,1)S(1)}, u32[]{:S(2)}, u32[]{:S(2)}) %collective-permute-start.9) | collective-permute-done | bytes 262176 | tf_op jit(solution)/shard_map/ppermute | solution.py:40
  79.3 4.9 %collective-permute-start.11 = (bf16[256,512]{1,0:T(8,128)(2,1)S(1)}, bf16[256,512]{1,0:T(8,128)(2,1)S(1)}, u32[]{:S(2)}, u32[]{:S(2)}) collective-permute-start(bf16[256,512]{1,0:T(8,128)(2,1)S(1)} %pad_maximum_fusion.1), channel_id=1, source_target_pairs={{1,0},{2,1},{3,2},{4,3},{5,4},{6,5},{7,6},{8,7},{9,8},{10,9},{11,1... | collective-permute-start | bytes 786440 | tf_op jit(solution)/shard_map/ppermute | solution.py:40
  84.2 3.7 %collective-permute-done.10 = bf16[256,512]{1,0:T(8,128)(2,1)S(1)} collective-permute-done((bf16[256,512]{1,0:T(8,128)(2,1)S(1)}, bf16[256,512]{1,0:T(8,128)(2,1)S(1)}, u32[]{:S(2)}, u32[]{:S(2)}) %collective-permute-start.10) | collective-permute-done | bytes 262176 | tf_op jit(solution)/shard_map/ppermute | solution.py:40
  87.9 4.9 %collective-permute-done.11 = bf16[256,512]{1,0:T(8,128)(2,1)S(1)} collective-permute-done((bf16[256,512]{1,0:T(8,128)(2,1)S(1)}, bf16[256,512]{1,0:T(8,128)(2,1)S(1)}, u32[]{:S(2)}, u32[]{:S(2)}) %collective-permute-start.11) | collective-permute-done | bytes 262176 | tf_op jit(solution)/shard_map/ppermute | solution.py:40
  92.8 0.1 fusion
  92.9 0.1 fusion.13
  93.0 0.9 pad_maximum_fusion.2
  (27 shorter events, 0.5 us)
Async XLA Ops:
  4.0 10.2 %collective-permute-start.2 = (bf16[256,256]{1,0:T(8,128)(2,1)}, bf16[256,256]{1,0:T(8,128)(2,1)S(1)}, u32[]{:S(2)}, u32[]{:S(2)}) collective-permute-start(bf16[256,256]{1,0:T(8,128)(2,1)} %get-tuple-element.86.own_full_ref), channel_id=1, source_target_pairs={{0,1},{1,2},{2,3},{3,4},{4,5},{5,6},{6,7},{7,8},{8,9},{9,10},{10,1... | collective-permute-start | bytes 393224 | tf_op jit(solution)/shard_map/ppermute | solution.py:40
  7.3 11.0 %collective-permute-start.4 = (bf16[256,256]{1,0:T(8,128)(2,1)}, bf16[256,256]{1,0:T(8,128)(2,1)S(1)}, u32[]{:S(2)}, u32[]{:S(2)}) collective-permute-start(bf16[256,256]{1,0:T(8,128)(2,1)} %get-tuple-element.85.own_full_ref), channel_id=1, source_target_pairs={{0,1},{1,2},{2,3},{3,4},{4,5},{5,6},{6,7},{7,8},{8,9},{9,10},{10,1... | collective-permute-start | bytes 393224 | tf_op jit(solution)/shard_map/ppermute | solution.py:40
  10.8 11.8 %collective-permute-start = (bf16[256,512]{1,0:T(8,128)(2,1)}, bf16[256,512]{1,0:T(8,128)(2,1)S(1)}, u32[]{:S(2)}, u32[]{:S(2)}) collective-permute-start(bf16[256,512]{1,0:T(8,128)(2,1)} %get-tuple-element.104.own_full_ref), channel_id=1, source_target_pairs={{0,1},{1,2},{2,3},{3,4},{4,5},{5,6},{6,7},{7,8},{8,9},{9,10},{10,1... | collective-permute-start | bytes 786440 | tf_op jit(solution)/shard_map/ppermute | solution.py:40
  14.9 11.5 %collective-permute-start.3 = (bf16[2,256,256]{2,1,0:T(8,128)(2,1)}, bf16[2,256,256]{2,1,0:T(8,128)(2,1)S(1)}, u32[]{:S(2)}, u32[]{:S(2)}) collective-permute-start(bf16[2,256,256]{2,1,0:T(8,128)(2,1)} %bitcast_dynamic-update-slice_fusion.2), channel_id=1, source_target_pairs={{0,2},{1,3},{2,4},{3,5},{4,6},{5,7},{6,8},{7,9},{8,10},{9,11},{10,... | collective-permute-start | bytes 786440 | tf_op jit(solution)/shard_map/ppermute | solution.py:40
  19.0 20.9 %collective-permute-start.6 = (bf16[2,256,256]{2,1,0:T(8,128)(2,1)}, bf16[2,256,256]{2,1,0:T(8,128)(2,1)S(1)}, u32[]{:S(2)}, u32[]{:S(2)}) collective-permute-start(bf16[2,256,256]{2,1,0:T(8,128)(2,1)} %bitcast_dynamic-update-slice_fusion.1), channel_id=1, source_target_pairs={{0,2},{1,3},{2,4},{3,5},{4,6},{5,7},{6,8},{7,9},{8,10},{9,11},{10,... | collective-permute-start | bytes 786440 | tf_op jit(solution)/shard_map/ppermute | solution.py:40
  23.2 27.9 %collective-permute-start.1 = (bf16[2,256,512]{2,1,0:T(8,128)(2,1)}, bf16[2,256,512]{2,1,0:T(8,128)(2,1)S(1)}, u32[]{:S(2)}, u32[]{:S(2)}) collective-permute-start(bf16[2,256,512]{2,1,0:T(8,128)(2,1)} %bitcast_dynamic-update-slice_fusion), channel_id=1, source_target_pairs={{0,2},{1,3},{2,4},{3,5},{4,6},{5,7},{6,8},{7,9},{8,10},{9,11},{10,... | collective-permute-start | bytes 1572872 | tf_op jit(solution)/shard_map/ppermute | solution.py:40
  26.4 1.1 %copy-start = (f32[256,768]{1,0:T(8,128)S(1)}, f32[256,768]{1,0:T(8,128)}, u32[]{:S(2)}) copy-start(f32[256,768]{1,0:T(8,128)} %get-tuple-element.87.bias_ref) | copy-start | bytes 2359300
  27.5 0.9 copy-start.3
  28.5 0.9 copy-start.5
  29.4 0.7 copy-start.6
  30.0 9.9 %copy-start.4 = (bf16[256,256]{1,0:T(8,128)(2,1)S(1)}, bf16[256,256]{1,0:T(8,128)(2,1)}, u32[]{:S(2)}) copy-start(bf16[256,256]{1,0:T(8,128)(2,1)} %get-tuple-element.85.own_full_ref) | copy-start | bytes 393220
  37.6 13.5 %collective-permute-start.5 = (bf16[2,256,256]{2,1,0:T(8,128)(2,1)S(1)}, bf16[2,256,256]{2,1,0:T(8,128)(2,1)S(1)}, u32[]{:S(2)}, u32[]{:S(2)}) collective-permute-start(bf16[2,256,256]{2,1,0:T(8,128)(2,1)S(1)} %get-tuple-element.91), channel_id=1, source_target_pairs={{2,0},{3,1},{4,2},{5,3},{6,4},{7,5},{8,6},{9,7},{10,8},{11,9},{12,... | collective-permute-start | bytes 786440 | tf_op jit(solution)/shard_map/ppermute | solution.py:40
  47.5 3.7 %copy-start.1 = (f32[256,768]{1,0:T(8,128)S(1)}, f32[256,768]{1,0:T(8,128)}, u32[]{:S(2)}) copy-start(f32[256,768]{1,0:T(8,128)} %get-tuple-element.87.bias_ref) | copy-start | bytes 2359300
  47.5 3.7 %copy-start.2 = (bf16[256,512]{1,0:T(8,128)(2,1)S(1)}, bf16[256,512]{1,0:T(8,128)(2,1)}, u32[]{:S(2)}) copy-start(bf16[256,512]{1,0:T(8,128)(2,1)} %get-tuple-element.104.own_full_ref) | copy-start | bytes 786436
  47.5 13.3 %collective-permute-start.7 = (bf16[2,256,256]{2,1,0:T(8,128)(2,1)S(1)}, bf16[2,256,256]{2,1,0:T(8,128)(2,1)S(1)}, u32[]{:S(2)}, u32[]{:S(2)}) collective-permute-start(bf16[2,256,256]{2,1,0:T(8,128)(2,1)S(1)} %get-tuple-element.94), channel_id=1, source_target_pairs={{2,0},{3,1},{4,2},{5,3},{6,4},{7,5},{8,6},{9,7},{10,8},{11,9},{12,... | collective-permute-start | bytes 786440 | tf_op jit(solution)/shard_map/ppermute | solution.py:40
  58.6 16.3 %collective-permute-start.8 = (bf16[2,256,256]{2,1,0:T(8,128)(2,1)S(1)}, bf16[2,256,256]{2,1,0:T(8,128)(2,1)S(1)}, u32[]{:S(2)}, u32[]{:S(2)}) collective-permute-start(bf16[2,256,256]{2,1,0:T(8,128)(2,1)S(1)} %get-tuple-element.101), channel_id=1, source_target_pairs={{2,0},{3,1},{4,2},{5,3},{6,4},{7,5},{8,6},{9,7},{10,8},{11,9},{12,... | collective-permute-start | bytes 786440 | tf_op jit(solution)/shard_map/ppermute | solution.py:40
  68.4 10.7 %collective-permute-start.9 = (bf16[2,256,256]{2,1,0:T(8,128)(2,1)S(1)}, bf16[2,256,256]{2,1,0:T(8,128)(2,1)S(1)}, u32[]{:S(2)}, u32[]{:S(2)}) collective-permute-start(bf16[2,256,256]{2,1,0:T(8,128)(2,1)S(1)} %get-tuple-element.115), channel_id=1, source_target_pairs={{2,0},{3,1},{4,2},{5,3},{6,4},{7,5},{8,6},{9,7},{10,8},{11,9},{12,... | collective-permute-start | bytes 786440 | tf_op jit(solution)/shard_map/ppermute | solution.py:40
  73.0 14.9 %collective-permute-start.10 = (bf16[256,512]{1,0:T(8,128)(2,1)S(1)}, bf16[256,512]{1,0:T(8,128)(2,1)S(1)}, u32[]{:S(2)}, u32[]{:S(2)}) collective-permute-start(bf16[256,512]{1,0:T(8,128)(2,1)S(1)} %pad_maximum_fusion), channel_id=1, source_target_pairs={{1,0},{2,1},{3,2},{4,3},{5,4},{6,5},{7,6},{8,7},{9,8},{10,9},{11,1... | collective-permute-start | bytes 786440 | tf_op jit(solution)/shard_map/ppermute | solution.py:40
  79.3 13.5 %collective-permute-start.11 = (bf16[256,512]{1,0:T(8,128)(2,1)S(1)}, bf16[256,512]{1,0:T(8,128)(2,1)S(1)}, u32[]{:S(2)}, u32[]{:S(2)}) collective-permute-start(bf16[256,512]{1,0:T(8,128)(2,1)S(1)} %pad_maximum_fusion.1), channel_id=1, source_target_pairs={{1,0},{2,1},{3,2},{4,3},{5,4},{6,5},{7,6},{8,7},{9,8},{10,9},{11,1... | collective-permute-start | bytes 786440 | tf_op jit(solution)/shard_map/ppermute | solution.py:40

commit v16 on v15

--- a/solution.py
+++ b/solution.py
@@ -333,6 +333,7 @@
             in_specs=[pl.BlockSpec(keys.shape, two)] * 2,
             out_specs=specs + [pl.BlockSpec(mask.shape, two) for mask in masks],
         ),
+        compiler_params=pltpu.CompilerParams(vmem_limit_bytes=12 * 1024 * 1024),
         name="pack",
     )(first, lengths, keys, values)
     packed = results[: len(shapes)]
@@ -369,22 +370,23 @@
         return (near + got[1]).astype(bf16), own + got[0]
 
     attend(0, pairs)
-    gots = [passed_along(parts[0][0], -2)]
     attend(1)
-    gots.append(passed_along(parts[1][0], -2))
-    gots[0], _ = lax.optimization_barrier((gots[0], parts[1][0]))
-    nears, owns = zip(second_hop(*parts[0][1:], gots[0]))
-    (nears,) = attend(2, nears)
-    gots.append(passed_along(parts[2][0], -2))
-    gots[1], _ = lax.optimization_barrier((gots[1], parts[2][0]))
-    more = second_hop(*parts[1][1:], gots[1])
-    (nears, *more) = attend(3, (nears, *more))
-    gots[2], near = lax.optimization_barrier((gots[2], parts[3][1]))
-    gots.append(passed_along(parts[3][0], -2))
-    parts[3][1] = near
-    rest = [second_hop(*part[1:], got) for part, got in zip(parts[2:], gots[2:])]
-    nears, owns = zip((nears, *owns), more, *rest)
-    last = [passed_along(jnp.concatenate(nears[at : at + 2], axis=1), -1) for at in (0, 2)]
+    got_early = passed_along(jnp.concatenate([parts[0][0], parts[1][0]], axis=2), -2)
+    attend(2)
+    got = passed_along(parts[2][0], -2)
+    attend(3)
+    got_early, got, parts[3][1] = lax.optimization_barrier((got_early, got, parts[3][1]))
+    pair = 2 * HEAD_SIZE
+    early = [second_hop(*parts[at][1:], got_early[:, :, at * pair : (at + 1) * pair]) for at in range(2)]
+    nears, owns = zip(*early)
+    near = jnp.concatenate(nears, axis=1)
+    near, parts[3][0] = lax.optimization_barrier((near, parts[3][0]))
+    got_last = passed_along(parts[3][0], -2)
+    last = [passed_along(near, -1)]
+    late = [second_hop(*parts[2][1:], got), second_hop(*parts[3][1:], got_last)]
+    nears, late = zip(*late)
+    last.append(passed_along(jnp.concatenate(nears, axis=1), -1))
+    owns += late
     total = (jnp.concatenate(owns, axis=1) + jnp.concatenate(last, axis=1).astype(f32)).astype(bf16)
     columns = [total[:, at : at + HEAD_SIZE] for at in range(0, total.shape[1], HEAD_SIZE)]
     return (

time: 95.4 us -> 93.9 us (0.984); the launches traced: 93.9 us -> 93.4 us
  waiting for transfers between devices: 15 us -> 25.9 us
  starting transfers between devices: 37.4 us -> 29.9 us
  local copies, waits for them, and re-layouts: 5.79 us -> 2.69 us
  Pallas kernels: 33.3 us -> 31.9 us
    ppermute x12 -> x11, waiting for transfers between devices: 15 us -> 25.9 us  [passed_along(): lax.ppermute(value, AXES, [(source, source + steps) for source in range(f...]
    ppermute x12 -> x11, starting transfers between devices: 37.4 us -> 29.9 us  [passed_along(): lax.ppermute(value, AXES, [(source, source + steps) for source in range(f...]
    pallas_call x1, Pallas kernels: 3.41 us -> 1.17 us  [pack(): pl.pallas_call(pack_kernel, out_shape=shapes + masks, grid_spec=pltpu.Pre...]
    scatter x3, local copies, waits for them, and re-layouts: 2.05 us -> 0.04 us  [local(): pairs = [pair.at[1].set(near) for pair, near in zip(pairs, nears)]]
    unnamed x14 -> x6, local copies, waits for them, and re-layouts: 3.64 us -> 2.55 us
  transfers between devices with their start and end apart: 12 -> 11, of which waited for: 5 -> 5; matrix products, arithmetic and copies ran while one was open for 3% -> 0% of each run, Pallas kernels for 32% -> 33%
where the time goes in v16:
time: 93.9 us; the launch traced here: 93.4 us
  Pallas kernels  31.9 us (34%)
  starting transfers between devices  29.9 us (32%)
  waiting for transfers between devices  25.9 us (28%)
  local copies, waits for them, and re-layouts  2.69 us (3%)
  other arithmetic  2.1 us (2%)
    pallas_call x4, Pallas kernels, attention(): pl.pallas_call(functools.partial(attention_kernel, where), out_shape=[jax...  30.7 us
    ppermute x11, starting transfers between devices, passed_along(): lax.ppermute(value, AXES, [(source, source + steps) for source in range(f...  29.9 us
    ppermute x11, waiting for transfers between devices, passed_along(): lax.ppermute(value, AXES, [(source, source + steps) for source in range(f...  25.9 us
    unnamed x6, local copies, waits for them, and re-layouts  2.55 us
  transfers between devices with their start and end apart: 11, of which 5 were waited for; matrix products, arithmetic and copies ran while one was open for 0% of the time, Pallas kernels for 33%

profile of v16, /device:TPU:29, one launch (start us, length us, event | category | flops | bytes accessed | tf_op | source)
XLA Modules:
  0.0 93.4 jit_solution(17046263860986479954)
XLA Ops:
  0.6 0.9 %copy-done = bf16[256,512]{1,0:T(8,128)(2,1)S(1)} copy-done((bf16[256,512]{1,0:T(8,128)(2,1)S(1)}, bf16[256,512]{1,0:T(8,128)(2,1)}, u32[]{:S(2)}) %copy-start) | copy-done | bytes 262168
  1.6 0.9 %copy-done.1 = bf16[256,512]{1,0:T(8,128)(2,1)S(1)} copy-done((bf16[256,512]{1,0:T(8,128)(2,1)S(1)}, bf16[256,512]{1,0:T(8,128)(2,1)}, u32[]{:S(2)}) %copy-start.1) | copy-done | bytes 262168
  2.5 0.7 copy-done.2
  3.2 1.2 %pack.1 = (bf16[256,256]{1,0:T(8,128)(2,1)S(1)}, bf16[2,256,256]{2,1,0:T(8,128)(2,1)S(1)}, bf16[256,256]{1,0:T(8,128)(2,1)S(1)}, bf16[2,256,256]{2,1,0:T(8,128)(...) custom-call(s32[1]{0:T(128)} %bitcast.first_ref, ...), custom_call_target="tpu_custom_call" | custom-call | tf_op jit(solution)/shard_map/pack/pallas_call | solution.py:327
  4.4 3.3 %collective-permute-start.4 = (bf16[256,256]{1,0:T(8,128)(2,1)S(1)}, bf16[256,256]{1,0:T(8,128)(2,1)S(1)}, u32[]{:S(2)}, u32[]{:S(2)}) collective-permute-start(bf16[256,256]{1,0:T(8,128)(2,1)S(1)} %get-tuple-element.84.own_full_ref), channel_id=1, source_target_pairs={{0,1},{1,2},{2,3},{3,4},{4,5},{5,6},{6,7},{7,8},{8,9},{9,10},{10,1... | collective-permute-start | bytes 393224 | tf_op jit(solution)/shard_map/ppermute | solution.py:40
  7.7 3.4 %collective-permute-start.2 = (bf16[256,256]{1,0:T(8,128)(2,1)S(1)}, bf16[256,256]{1,0:T(8,128)(2,1)S(1)}, u32[]{:S(2)}, u32[]{:S(2)}) collective-permute-start(bf16[256,256]{1,0:T(8,128)(2,1)S(1)} %get-tuple-element.81.own_full_ref), channel_id=1, source_target_pairs={{0,1},{1,2},{2,3},{3,4},{4,5},{5,6},{6,7},{7,8},{8,9},{9,10},{10,1... | collective-permute-start | bytes 393224 | tf_op jit(solution)/shard_map/ppermute | solution.py:40
  11.1 3.4 %collective-permute-start = (bf16[256,512]{1,0:T(8,128)(2,1)S(1)}, bf16[256,512]{1,0:T(8,128)(2,1)S(1)}, u32[]{:S(2)}, u32[]{:S(2)}) collective-permute-start(bf16[256,512]{1,0:T(8,128)(2,1)S(1)} %get-tuple-element.76.own_full_ref), channel_id=1, source_target_pairs={{0,1},{1,2},{2,3},{3,4},{4,5},{5,6},{6,7},{7,8},{8,9},{9,10},{10,1... | collective-permute-start | bytes 786440 | tf_op jit(solution)/shard_map/ppermute | solution.py:40
  14.6 3.5 %collective-permute-start.5 = (bf16[2,256,256]{2,1,0:T(8,128)(2,1)S(1)}, bf16[2,256,256]{2,1,0:T(8,128)(2,1)S(1)}, u32[]{:S(2)}, u32[]{:S(2)}) collective-permute-start(bf16[2,256,256]{2,1,0:T(8,128)(2,1)S(1)} %bitcast_dynamic-update-slice_fusion.1), channel_id=1, source_target_pairs={{0,2},{1,3},{2,4},{3,5},{4,6},{5,7},{6,8},{7,9},{8,10},{9,11},{10,... | collective-permute-start | bytes 786440 | tf_op jit(solution)/shard_map/ppermute | solution.py:40
  18.1 3.5 %collective-permute-start.3 = (bf16[2,256,256]{2,1,0:T(8,128)(2,1)S(1)}, bf16[2,256,256]{2,1,0:T(8,128)(2,1)S(1)}, u32[]{:S(2)}, u32[]{:S(2)}) collective-permute-start(bf16[2,256,256]{2,1,0:T(8,128)(2,1)S(1)} %bitcast_dynamic-update-slice_fusion.2), channel_id=1, source_target_pairs={{0,2},{1,3},{2,4},{3,5},{4,6},{5,7},{6,8},{7,9},{8,10},{9,11},{10,... | collective-permute-start | bytes 786440 | tf_op jit(solution)/shard_map/ppermute | solution.py:40
  21.6 3.2 %collective-permute-start.1 = (bf16[2,256,512]{2,1,0:T(8,128)(2,1)S(1)}, bf16[2,256,512]{2,1,0:T(8,128)(2,1)S(1)}, u32[]{:S(2)}, u32[]{:S(2)}) collective-permute-start(bf16[2,256,512]{2,1,0:T(8,128)(2,1)S(1)} %bitcast_dynamic-update-slice_fusion), channel_id=1, source_target_pairs={{0,2},{1,3},{2,4},{3,5},{4,6},{5,7},{6,8},{7,9},{8,10},{9,11},{10,... | collective-permute-start | bytes 1572872 | tf_op jit(solution)/shard_map/ppermute | solution.py:40
  24.8 1.8 %collective-permute-done.5.behind_ref = bf16[2,256,256]{2,1,0:T(8,128)(2,1)S(1)} collective-permute-done((bf16[2,256,256]{2,1,0:T(8,128)(2,1)S(1)}, bf16[2,256,256]{2,1,0:T(8,128)(2,1)S(1)}, u32[]{:S(2)}, u32[]{:S(2)}) %collective-permute-start.5) | collective-permute-done | bytes 262176 | tf_op jit(solution)/shard_map/ppermute | solution.py:40
  26.5 7.6 %attention.4 = (bf16[256,4096]{1,0:T(8,128)(2,1)}, bf16[256,4096]{1,0:T(8,128)(2,1)}, bf16[2,256,256]{2,1,0:T(8,128)(2,1)S(1)}, f32[256,256]{1,0:T(8,128)S(1)}, f32[256,256]{1,0:T(8,128)S(1)}) custom-call(bf16[256,4096]{1,0:T(8,128)(2,1)} %q_ref.7, bf16[256,4096]{1,0:T(8,128)(2,1)} %g_ref.7, bf16[2,256,256]{2,1,0:T(8,128)(2,1)S(1)} %collective-permute-done.5.behind_ref, ...), custom_call_target="tpu_custom_call" | custom-call | flops 4831838208 | bytes 3538944 | tf_op jit(solution)/shard_map/attention/pallas_call | solution.py:247
  34.1 7.8 %attention.5 = (bf16[256,4096]{1,0:T(8,128)(2,1)}, bf16[256,4096]{1,0:T(8,128)(2,1)}, bf16[2,256,256]{2,1,0:T(8,128)(2,1)S(1)}, f32[256,256]{1,0:T(8,128)S(1)}, f32[256,256]{1,0:T(8,128)S(1)}) custom-call(bf16[256,4096]{1,0:T(8,128)(2,1)} %q_ref.7, bf16[256,4096]{1,0:T(8,128)(2,1)} %g_ref.7, ...), custom_call_target="tpu_custom_call", output_to_operand_aliasing={{0}: (8, {}), {1}: (9, {})} | custom-call | flops 4831838208 | bytes 3538944 | tf_op jit(solution)/shard_map/attention/pallas_call | solution.py:247
  42.0 1.9 %collective-permute-start.6 = (bf16[2,256,512]{2,1,0:T(8,128)(2,1)S(1)}, bf16[2,256,512]{2,1,0:T(8,128)(2,1)S(1)}, u32[]{:S(2)}, u32[]{:S(2)}) collective-permute-start(bf16[2,256,512]{2,1,0:T(8,128)(2,1)S(1)} %pad_maximum_fusion), channel_id=1, source_target_pairs={{2,0},{3,1},{4,2},{5,3},{6,4},{7,5},{8,6},{9,7},{10,8},{11,9},{12,... | collective-permute-start | bytes 1572872 | tf_op jit(solution)/shard_map/ppermute | solution.py:40
  43.9 7.7 %attention.6 = (bf16[256,4096]{1,0:T(8,128)(2,1)}, bf16[256,4096]{1,0:T(8,128)(2,1)}, bf16[2,256,256]{2,1,0:T(8,128)(2,1)S(1)}, f32[256,256]{1,0:T(8,128)S(1)}, f32[256,256]{1,0:T(8,128)S(1)}) custom-call(bf16[256,4096]{1,0:T(8,128)(2,1)} %q_ref.7, bf16[256,4096]{1,0:T(8,128)(2,1)} %g_ref.7, ...), custom_call_target="tpu_custom_call", output_to_operand_aliasing={{0}: (8, {}), {1}: (9, {})} | custom-call | flops 4831838208 | bytes 3538944 | tf_op jit(solution)/shard_map/attention/pallas_call | solution.py:247
  51.6 1.9 %collective-permute-start.7 = (bf16[2,256,256]{2,1,0:T(8,128)(2,1)S(1)}, bf16[2,256,256]{2,1,0:T(8,128)(2,1)S(1)}, u32[]{:S(2)}, u32[]{:S(2)}) collective-permute-start(bf16[2,256,256]{2,1,0:T(8,128)(2,1)S(1)} %get-tuple-element.96), channel_id=1, source_target_pairs={{2,0},{3,1},{4,2},{5,3},{6,4},{7,5},{8,6},{9,7},{10,8},{11,9},{12,... | collective-permute-start | bytes 786440 | tf_op jit(solution)/shard_map/ppermute | solution.py:40
  53.5 7.7 %attention.7 = (bf16[256,4096]{1,0:T(8,128)(2,1)}, bf16[256,4096]{1,0:T(8,128)(2,1)}, bf16[2,256,256]{2,1,0:T(8,128)(2,1)S(1)}, f32[256,256]{1,0:T(8,128)S(1)}, f32[256,256]{1,0:T(8,128)S(1)}) custom-call(bf16[256,4096]{1,0:T(8,128)(2,1)} %q_ref.7, bf16[256,4096]{1,0:T(8,128)(2,1)} %g_ref.7, ...), custom_call_target="tpu_custom_call", output_to_operand_aliasing={{0}: (8, {}), {1}: (9, {})} | custom-call | flops 4831838208 | bytes 3538944 | tf_op jit(solution)/shard_map/attention/pallas_call | solution.py:247
  61.2 5.4 %collective-permute-done.7 = bf16[2,256,256]{2,1,0:T(8,128)(2,1)S(1)} collective-permute-done((bf16[2,256,256]{2,1,0:T(8,128)(2,1)S(1)}, bf16[2,256,256]{2,1,0:T(8,128)(2,1)S(1)}, u32[]{:S(2)}, u32[]{:S(2)}) %collective-permute-start.7) | collective-permute-done | bytes 262176 | tf_op jit(solution)/shard_map/ppermute | solution.py:40
  66.6 0.1 slice_convert_fusion.1
  66.7 0.1 fusion.11
  66.9 1.9 %collective-permute-start.8 = (bf16[2,256,256]{2,1,0:T(8,128)(2,1)S(1)}, bf16[2,256,256]{2,1,0:T(8,128)(2,1)S(1)}, u32[]{:S(2)}, u32[]{:S(2)}) collective-permute-start(bf16[2,256,256]{2,1,0:T(8,128)(2,1)S(1)} %get-tuple-element.106), channel_id=1, source_target_pairs={{2,0},{3,1},{4,2},{5,3},{6,4},{7,5},{8,6},{9,7},{10,8},{11,9},{12,... | collective-permute-start | bytes 786440 | tf_op jit(solution)/shard_map/ppermute | solution.py:40
  68.9 1.9 %collective-permute-start.9 = (bf16[256,512]{1,0:T(8,128)(2,1)S(1)}, bf16[256,512]{1,0:T(8,128)(2,1)S(1)}, u32[]{:S(2)}, u32[]{:S(2)}) collective-permute-start(bf16[256,512]{1,0:T(8,128)(2,1)S(1)} %pad_maximum_fusion.1), channel_id=1, source_target_pairs={{1,0},{2,1},{3,2},{4,3},{5,4},{6,5},{7,6},{8,7},{9,8},{10,9},{11,1... | collective-permute-start | bytes 786440 | tf_op jit(solution)/shard_map/ppermute | solution.py:40
  70.8 0.1 fusion.4
  70.9 8.3 %collective-permute-done.8 = bf16[2,256,256]{2,1,0:T(8,128)(2,1)S(1)} collective-permute-done((bf16[2,256,256]{2,1,0:T(8,128)(2,1)S(1)}, bf16[2,256,256]{2,1,0:T(8,128)(2,1)S(1)}, u32[]{:S(2)}, u32[]{:S(2)}) %collective-permute-start.8) | collective-permute-done | bytes 262176 | tf_op jit(solution)/shard_map/ppermute | solution.py:40
  79.3 0.1 fusion.2
  79.4 1.9 %collective-permute-start.10 = (bf16[256,512]{1,0:T(8,128)(2,1)S(1)}, bf16[256,512]{1,0:T(8,128)(2,1)S(1)}, u32[]{:S(2)}, u32[]{:S(2)}) collective-permute-start(bf16[256,512]{1,0:T(8,128)(2,1)S(1)} %pad_maximum_fusion.2), channel_id=1, source_target_pairs={{1,0},{2,1},{3,2},{4,3},{5,4},{6,5},{7,6},{8,7},{9,8},{10,9},{11,1... | collective-permute-start | bytes 786440 | tf_op jit(solution)/shard_map/ppermute | solution.py:40
  81.3 2.0 %collective-permute-done.9 = bf16[256,512]{1,0:T(8,128)(2,1)S(1)} collective-permute-done((bf16[256,512]{1,0:T(8,128)(2,1)S(1)}, bf16[256,512]{1,0:T(8,128)(2,1)S(1)}, u32[]{:S(2)}, u32[]{:S(2)}) %collective-permute-start.9) | collective-permute-done | bytes 262176 | tf_op jit(solution)/shard_map/ppermute | solution.py:40
  83.3 8.4 %collective-permute-done.10 = bf16[256,512]{1,0:T(8,128)(2,1)S(1)} collective-permute-done((bf16[256,512]{1,0:T(8,128)(2,1)S(1)}, bf16[256,512]{1,0:T(8,128)(2,1)S(1)}, u32[]{:S(2)}, u32[]{:S(2)}) %collective-permute-start.10) | collective-permute-done | bytes 262176 | tf_op jit(solution)/shard_map/ppermute | solution.py:40
  91.7 0.1 fusion
  91.8 0.1 fusion.13
  92.0 0.7 pad_maximum_fusion.4
  92.7 0.7 pad_maximum_fusion.3
  (17 shorter events, 0.2 us)
Async XLA Ops:
  0.6 1.0 %copy-start = (bf16[256,512]{1,0:T(8,128)(2,1)S(1)}, bf16[256,512]{1,0:T(8,128)(2,1)}, u32[]{:S(2)}) copy-start(bf16[256,512]{1,0:T(8,128)(2,1)} %keys_ref.1) | copy-start | bytes 786436
  1.6 0.9 %copy-start.1 = (bf16[256,512]{1,0:T(8,128)(2,1)S(1)}, bf16[256,512]{1,0:T(8,128)(2,1)}, u32[]{:S(2)}) copy-start(bf16[256,512]{1,0:T(8,128)(2,1)} %values_ref.1) | copy-start | bytes 786436
  2.5 0.7 copy-start.2
  4.4 10.2 %collective-permute-start.4 = (bf16[256,256]{1,0:T(8,128)(2,1)S(1)}, bf16[256,256]{1,0:T(8,128)(2,1)S(1)}, u32[]{:S(2)}, u32[]{:S(2)}) collective-permute-start(bf16[256,256]{1,0:T(8,128)(2,1)S(1)} %get-tuple-element.84.own_full_ref), channel_id=1, source_target_pairs={{0,1},{1,2},{2,3},{3,4},{4,5},{5,6},{6,7},{7,8},{8,9},{9,10},{10,1... | collective-permute-start | bytes 393224 | tf_op jit(solution)/shard_map/ppermute | solution.py:40
  7.7 10.4 %collective-permute-start.2 = (bf16[256,256]{1,0:T(8,128)(2,1)S(1)}, bf16[256,256]{1,0:T(8,128)(2,1)S(1)}, u32[]{:S(2)}, u32[]{:S(2)}) collective-permute-start(bf16[256,256]{1,0:T(8,128)(2,1)S(1)} %get-tuple-element.81.own_full_ref), channel_id=1, source_target_pairs={{0,1},{1,2},{2,3},{3,4},{4,5},{5,6},{6,7},{7,8},{8,9},{9,10},{10,1... | collective-permute-start | bytes 393224 | tf_op jit(solution)/shard_map/ppermute | solution.py:40
  11.1 10.5 %collective-permute-start = (bf16[256,512]{1,0:T(8,128)(2,1)S(1)}, bf16[256,512]{1,0:T(8,128)(2,1)S(1)}, u32[]{:S(2)}, u32[]{:S(2)}) collective-permute-start(bf16[256,512]{1,0:T(8,128)(2,1)S(1)} %get-tuple-element.76.own_full_ref), channel_id=1, source_target_pairs={{0,1},{1,2},{2,3},{3,4},{4,5},{5,6},{6,7},{7,8},{8,9},{9,10},{10,1... | collective-permute-start | bytes 786440 | tf_op jit(solution)/shard_map/ppermute | solution.py:40
  14.6 12.0 %collective-permute-start.5 = (bf16[2,256,256]{2,1,0:T(8,128)(2,1)S(1)}, bf16[2,256,256]{2,1,0:T(8,128)(2,1)S(1)}, u32[]{:S(2)}, u32[]{:S(2)}) collective-permute-start(bf16[2,256,256]{2,1,0:T(8,128)(2,1)S(1)} %bitcast_dynamic-update-slice_fusion.1), channel_id=1, source_target_pairs={{0,2},{1,3},{2,4},{3,5},{4,6},{5,7},{6,8},{7,9},{8,10},{9,11},{10,... | collective-permute-start | bytes 786440 | tf_op jit(solution)/shard_map/ppermute | solution.py:40
  18.1 16.0 %collective-permute-start.3 = (bf16[2,256,256]{2,1,0:T(8,128)(2,1)S(1)}, bf16[2,256,256]{2,1,0:T(8,128)(2,1)S(1)}, u32[]{:S(2)}, u32[]{:S(2)}) collective-permute-start(bf16[2,256,256]{2,1,0:T(8,128)(2,1)S(1)} %bitcast_dynamic-update-slice_fusion.2), channel_id=1, source_target_pairs={{0,2},{1,3},{2,4},{3,5},{4,6},{5,7},{6,8},{7,9},{8,10},{9,11},{10,... | collective-permute-start | bytes 786440 | tf_op jit(solution)/shard_map/ppermute | solution.py:40
  21.6 22.3 %collective-permute-start.1 = (bf16[2,256,512]{2,1,0:T(8,128)(2,1)S(1)}, bf16[2,256,512]{2,1,0:T(8,128)(2,1)S(1)}, u32[]{:S(2)}, u32[]{:S(2)}) collective-permute-start(bf16[2,256,512]{2,1,0:T(8,128)(2,1)S(1)} %bitcast_dynamic-update-slice_fusion), channel_id=1, source_target_pairs={{0,2},{1,3},{2,4},{3,5},{4,6},{5,7},{6,8},{7,9},{8,10},{9,11},{10,... | collective-permute-start | bytes 1572872 | tf_op jit(solution)/shard_map/ppermute | solution.py:40
  42.0 19.3 %collective-permute-start.6 = (bf16[2,256,512]{2,1,0:T(8,128)(2,1)S(1)}, bf16[2,256,512]{2,1,0:T(8,128)(2,1)S(1)}, u32[]{:S(2)}, u32[]{:S(2)}) collective-permute-start(bf16[2,256,512]{2,1,0:T(8,128)(2,1)S(1)} %pad_maximum_fusion), channel_id=1, source_target_pairs={{2,0},{3,1},{4,2},{5,3},{6,4},{7,5},{8,6},{9,7},{10,8},{11,9},{12,... | collective-permute-start | bytes 1572872 | tf_op jit(solution)/shard_map/ppermute | solution.py:40
  51.6 15.1 %collective-permute-start.7 = (bf16[2,256,256]{2,1,0:T(8,128)(2,1)S(1)}, bf16[2,256,256]{2,1,0:T(8,128)(2,1)S(1)}, u32[]{:S(2)}, u32[]{:S(2)}) collective-permute-start(bf16[2,256,256]{2,1,0:T(8,128)(2,1)S(1)} %get-tuple-element.96), channel_id=1, source_target_pairs={{2,0},{3,1},{4,2},{5,3},{6,4},{7,5},{8,6},{9,7},{10,8},{11,9},{12,... | collective-permute-start | bytes 786440 | tf_op jit(solution)/shard_map/ppermute | solution.py:40
  66.9 12.3 %collective-permute-start.8 = (bf16[2,256,256]{2,1,0:T(8,128)(2,1)S(1)}, bf16[2,256,256]{2,1,0:T(8,128)(2,1)S(1)}, u32[]{:S(2)}, u32[]{:S(2)}) collective-permute-start(bf16[2,256,256]{2,1,0:T(8,128)(2,1)S(1)} %get-tuple-element.106), channel_id=1, source_target_pairs={{2,0},{3,1},{4,2},{5,3},{6,4},{7,5},{8,6},{9,7},{10,8},{11,9},{12,... | collective-permute-start | bytes 786440 | tf_op jit(solution)/shard_map/ppermute | solution.py:40
  68.9 14.4 %collective-permute-start.9 = (bf16[256,512]{1,0:T(8,128)(2,1)S(1)}, bf16[256,512]{1,0:T(8,128)(2,1)S(1)}, u32[]{:S(2)}, u32[]{:S(2)}) collective-permute-start(bf16[256,512]{1,0:T(8,128)(2,1)S(1)} %pad_maximum_fusion.1), channel_id=1, source_target_pairs={{1,0},{2,1},{3,2},{4,3},{5,4},{6,5},{7,6},{8,7},{9,8},{10,9},{11,1... | collective-permute-start | bytes 786440 | tf_op jit(solution)/shard_map/ppermute | solution.py:40
  79.4 12.3 %collective-permute-start.10 = (bf16[256,512]{1,0:T(8,128)(2,1)S(1)}, bf16[256,512]{1,0:T(8,128)(2,1)S(1)}, u32[]{:S(2)}, u32[]{:S(2)}) collective-permute-start(bf16[256,512]{1,0:T(8,128)(2,1)S(1)} %pad_maximum_fusion.2), channel_id=1, source_target_pairs={{1,0},{2,1},{3,2},{4,3},{5,4},{6,5},{7,6},{8,7},{9,8},{10,9},{11,1... | collective-permute-start | bytes 786440 | tf_op jit(solution)/shard_map/ppermute | solution.py:40

commit v17 on v15

--- a/solution.py
+++ b/solution.py
@@ -18,7 +18,7 @@
 UNIT = 4
 FORWARD = ((0,), (1,), (2, 3))
 OUTS = 5
-SCRATCH = 31
+SCRATCH = 37
 MASKED = -1e30
 SCALE = 1.0 / math.sqrt(HEAD_SIZE)
 EXP2_SCALE = SCALE * math.log2(math.e)
@@ -68,7 +68,8 @@
         bias_ref[:, part * 128 : (part + 1) * 128] = jnp.where(allowed, 0.0, MASKED)
 
 
-def attention_kernel(where, q_ref, g_ref, behind_ref, near_ref, own_full_ref, bias_ref, old_ref, cut_ref, *refs):
+def attention_kernel(where, q_ref, g_ref, *refs):
+    given_refs = refs[:6]
     out_ref, dq_ref, dbehind_ref, dnear_ref, down_ref = refs[-(OUTS + SCRATCH) : -SCRATCH]
     (
         key_ref, value_ref, key_t_ref, value_t_ref, key2_ref, value2_ref, key2_t_ref, value2_t_ref,
@@ -80,22 +81,27 @@
     head, *offsets = where
     key_in, value_in, key_out, value_out = (slice(at, at + HEAD_SIZE) for at in offsets)
     q_full_ref, g_full_ref, out_full_ref, dq_full_ref = q_ref, g_ref, out_ref, dq_ref
-    q_ref, g_ref, out_ref, dq_ref, own_ref, sem = copies
+    q_ref, g_ref, out_ref, dq_ref, *held_refs, sem, held_sem = copies
+    behind_ref, near_ref, own_ref, bias_ref, old_ref, cut_ref = held_refs
     rows, wide = q_ref.shape
     mine = slice(head * wide, (head + 1) * wide)
     q_copy = pltpu.make_async_copy(q_full_ref.at[:, mine], q_ref, sem.at[0])
     g_copy = pltpu.make_async_copy(g_full_ref.at[:, mine], g_ref, sem.at[1])
-    own_copy = pltpu.make_async_copy(own_full_ref, own_ref, sem.at[2 + 2 * GROUP // UNIT])
-    own_copy.start()
-    q_copy.start()
-    g_copy.start()
+    held = [
+        pltpu.make_async_copy(given, here, held_sem.at[at])
+        for at, (given, here) in enumerate(zip(given_refs, held_refs))
+    ]
+    behind_copy, near_copy, own_copy, bias_copy, old_copy, cut_copy = held
+    for copy in (own_copy, cut_copy, near_copy, behind_copy, q_copy, old_copy, bias_copy, g_copy):
+        copy.start()
     window = (SPAN - 1) * rows
     units = GROUP // UNIT
     stack = UNIT * rows
     two = slice(0, rows)
     rest = slice(rows, window)
 
-    own_copy.wait()
+    for copy in (own_copy, cut_copy, near_copy, behind_copy):
+        copy.wait()
     from_far = lax.broadcasted_iota(jnp.int32, (rows, HEAD_SIZE), 0) >= cut_ref[0, 0]
     mid, far, near, own = behind_ref.at[0], behind_ref.at[1], near_ref, own_ref
     for j, block in enumerate((mid, near)):
@@ -192,7 +198,9 @@
         return copy
 
     q_copy.wait()
+    old_copy.wait()
     scores(0, 0)
+    bias_copy.wait()
     sent = []
     for unit in range(units):
         slot = unit % 2
@@ -235,8 +243,7 @@
     fore = blocks[-1].shape[1] // pair
     where = [head, *(at * HEAD_SIZE for at in (place, fore + place, 0, 1))]
     operands = [queries, out_grad, *blocks, *masks]
-    in_specs = [query_spec] * 2 + [whole(block.shape) for block in blocks[:-1]]
-    in_specs += [pl.BlockSpec(memory_space=pl.ANY)] + [whole(mask.shape) for mask in masks]
+    in_specs = [query_spec] * 2 + [pl.BlockSpec(memory_space=pl.ANY)] * 6
     aliases = {}
     for at, array in enumerate(grads):
         if array is not None:
@@ -279,7 +286,8 @@
                 for _ in range(count)
             ]
             + [pltpu.VMEM((rows, wide), bf16)] * 4
-            + [pltpu.VMEM(blocks[-1].shape, bf16), pltpu.SemaphoreType.DMA((3 + 2 * GROUP // UNIT,))],
+            + [pltpu.VMEM(array.shape, array.dtype) for array in (*blocks, *masks)]
+            + [pltpu.SemaphoreType.DMA((2 + 2 * GROUP // UNIT,)), pltpu.SemaphoreType.DMA((6,))],
         ),
         input_output_aliases=aliases,
         compiler_params=pltpu.CompilerParams(vmem_limit_bytes=51 * 1024 * 1024),
@@ -297,8 +305,20 @@
     return (0,) * rank
 
 
-def pack_kernel(first_ref, lengths_ref, keys_ref, values_ref, *refs):
+def pack_kernel(first_ref, keys_full_ref, values_full_ref, lengths_full_ref, *refs):
+    *refs, keys_ref, values_ref, lengths_ref, sem = refs
+    copies = [
+        pltpu.make_async_copy(full, here, sem.at[at])
+        for at, (full, here) in enumerate(
+            ((lengths_full_ref, lengths_ref), (keys_full_ref, keys_ref), (values_full_ref, values_ref))
+        )
+    ]
+    for copy in copies:
+        copy.start()
+    copies[0].wait()
     write_masks(*refs[-3:], lengths_ref, first_ref, keys_ref.shape[0])
+    copies[1].wait()
+    copies[2].wait()
     for at, heads in enumerate(FORWARD):
         span = slice(heads[0] * HEAD_SIZE, (heads[-1] + 1) * HEAD_SIZE)
         width = span.stop - span.start
@@ -328,13 +348,20 @@
         pack_kernel,
         out_shape=shapes + masks,
         grid_spec=pltpu.PrefetchScalarGridSpec(
-            num_scalar_prefetch=2,
+            num_scalar_prefetch=1,
             grid=(1,),
-            in_specs=[pl.BlockSpec(keys.shape, two)] * 2,
+            in_specs=[pl.BlockSpec(memory_space=pltpu.HBM)] * 3,
             out_specs=specs + [pl.BlockSpec(mask.shape, two) for mask in masks],
+            scratch_shapes=[
+                pltpu.VMEM(keys.shape, keys.dtype),
+                pltpu.VMEM(values.shape, values.dtype),
+                pltpu.SMEM(lengths.shape, lengths.dtype),
+                pltpu.SemaphoreType.DMA((3,)),
+            ],
         ),
+        compiler_params=pltpu.CompilerParams(vmem_limit_bytes=12 * 1024 * 1024),
         name="pack",
-    )(first, lengths, keys, values)
+    )(first, keys, values, lengths)
     packed = results[: len(shapes)]
     return packed[0::2], packed[1::2], results[len(shapes) :]
 

time: 95.4 us -> 95.6 us (level)
  local copies, waits for them, and re-layouts: 5.79 us -> 2.69 us
  Pallas kernels: 33.3 us -> 34.9 us
    pallas_call x4, Pallas kernels: 29.9 us -> 33.7 us  [attention(): pl.pallas_call(functools.partial(attention_kernel, where), out_shape=[jax...]
    pallas_call x1, Pallas kernels: 3.41 us -> 1.22 us  [pack(): pl.pallas_call(pack_kernel, out_shape=shapes + masks, grid_spec=pltpu.Pre...]
    scatter x3, local copies, waits for them, and re-layouts: 2.05 us -> 0.04 us  [local(): pairs = [pair.at[1].set(near) for pair, near in zip(pairs, nears)]]
    unnamed x14 -> x6, local copies, waits for them, and re-layouts: 3.64 us -> 2.55 us
  transfers between devices with their start and end apart: 12 -> 12, of which waited for: 5 -> 5; matrix products, arithmetic and copies ran while one was open for 3% -> 1% of each run, Pallas kernels for 32% -> 36%
where the time goes in v17:
time: 95.6 us; the launch traced here: 93.7 us
  starting transfers between devices  38 us (40%)
  Pallas kernels  34.9 us (37%)
  waiting for transfers between devices  15.7 us (16%)
  local copies, waits for them, and re-layouts  2.69 us (3%)
  other arithmetic  1.45 us (2%)
    ppermute x12, starting transfers between devices, passed_along(): lax.ppermute(value, AXES, [(source, source + steps) for source in range(f...  38 us
    pallas_call x4, Pallas kernels, attention(): pl.pallas_call(functools.partial(attention_kernel, where), out_shape=[jax...  33.7 us
    ppermute x12, waiting for transfers between devices, passed_along(): lax.ppermute(value, AXES, [(source, source + steps) for source in range(f...  15.7 us
    unnamed x6, local copies, waits for them, and re-layouts  2.55 us
  transfers between devices with their start and end apart: 12, of which 5 were waited for; matrix products, arithmetic and copies ran while one was open for 1% of the time, Pallas kernels for 36%

profile of v17, /device:TPU:29, one launch (start us, length us, event | category | flops | bytes accessed | tf_op | source)
XLA Modules:
  0.0 93.7 jit_solution(18117094924919659072)
XLA Ops:
  0.6 0.9 %copy-done = bf16[256,512]{1,0:T(8,128)(2,1)S(1)} copy-done((bf16[256,512]{1,0:T(8,128)(2,1)S(1)}, bf16[256,512]{1,0:T(8,128)(2,1)}, u32[]{:S(2)}) %copy-start) | copy-done | bytes 262168
  1.6 0.9 %copy-done.1 = bf16[256,512]{1,0:T(8,128)(2,1)S(1)} copy-done((bf16[256,512]{1,0:T(8,128)(2,1)S(1)}, bf16[256,512]{1,0:T(8,128)(2,1)}, u32[]{:S(2)}) %copy-start.1) | copy-done | bytes 262168
  2.5 0.7 copy-done.2
  3.2 1.2 %pack.1 = (bf16[256,256]{1,0:T(8,128)(2,1)S(1)}, bf16[2,256,256]{2,1,0:T(8,128)(2,1)S(1)}, bf16[256,256]{1,0:T(8,128)(2,1)S(1)}, bf16[2,256,256]{2,1,0:T(8,128)(...) custom-call(s32[1]{0:T(128)} %bitcast.first_ref, ...), custom_call_target="tpu_custom_call" | custom-call | tf_op jit(solution)/shard_map/pack/pallas_call | solution.py:347
  4.4 3.3 %collective-permute-start.2 = (bf16[256,256]{1,0:T(8,128)(2,1)S(1)}, bf16[256,256]{1,0:T(8,128)(2,1)S(1)}, u32[]{:S(2)}, u32[]{:S(2)}) collective-permute-start(bf16[256,256]{1,0:T(8,128)(2,1)S(1)} %get-tuple-element.86.refs_2_), channel_id=1, source_target_pairs={{0,1},{1,2},{2,3},{3,4},{4,5},{5,6},{6,7},{7,8},{8,9},{9,10},{10,1... | collective-permute-start | bytes 393224 | tf_op jit(solution)/shard_map/ppermute | solution.py:40
  7.7 3.4 %collective-permute-start.4 = (bf16[256,256]{1,0:T(8,128)(2,1)S(1)}, bf16[256,256]{1,0:T(8,128)(2,1)S(1)}, u32[]{:S(2)}, u32[]{:S(2)}) collective-permute-start(bf16[256,256]{1,0:T(8,128)(2,1)S(1)} %get-tuple-element.85.refs_2_), channel_id=1, source_target_pairs={{0,1},{1,2},{2,3},{3,4},{4,5},{5,6},{6,7},{7,8},{8,9},{9,10},{10,1... | collective-permute-start | bytes 393224 | tf_op jit(solution)/shard_map/ppermute | solution.py:40
  11.2 3.4 %collective-permute-start = (bf16[256,512]{1,0:T(8,128)(2,1)S(1)}, bf16[256,512]{1,0:T(8,128)(2,1)S(1)}, u32[]{:S(2)}, u32[]{:S(2)}) collective-permute-start(bf16[256,512]{1,0:T(8,128)(2,1)S(1)} %get-tuple-element.104.refs_2_), channel_id=1, source_target_pairs={{0,1},{1,2},{2,3},{3,4},{4,5},{5,6},{6,7},{7,8},{8,9},{9,10},{10,1... | collective-permute-start | bytes 786440 | tf_op jit(solution)/shard_map/ppermute | solution.py:40
  14.6 3.5 %collective-permute-start.3 = (bf16[2,256,256]{2,1,0:T(8,128)(2,1)S(1)}, bf16[2,256,256]{2,1,0:T(8,128)(2,1)S(1)}, u32[]{:S(2)}, u32[]{:S(2)}) collective-permute-start(bf16[2,256,256]{2,1,0:T(8,128)(2,1)S(1)} %bitcast_dynamic-update-slice_fusion.2), channel_id=1, source_target_pairs={{0,2},{1,3},{2,4},{3,5},{4,6},{5,7},{6,8},{7,9},{8,10},{9,11},{10,... | collective-permute-start | bytes 786440 | tf_op jit(solution)/shard_map/ppermute | solution.py:40
  18.1 3.5 %collective-permute-start.6 = (bf16[2,256,256]{2,1,0:T(8,128)(2,1)S(1)}, bf16[2,256,256]{2,1,0:T(8,128)(2,1)S(1)}, u32[]{:S(2)}, u32[]{:S(2)}) collective-permute-start(bf16[2,256,256]{2,1,0:T(8,128)(2,1)S(1)} %bitcast_dynamic-update-slice_fusion.1), channel_id=1, source_target_pairs={{0,2},{1,3},{2,4},{3,5},{4,6},{5,7},{6,8},{7,9},{8,10},{9,11},{10,... | collective-permute-start | bytes 786440 | tf_op jit(solution)/shard_map/ppermute | solution.py:40
  21.7 3.2 %collective-permute-start.1 = (bf16[2,256,512]{2,1,0:T(8,128)(2,1)S(1)}, bf16[2,256,512]{2,1,0:T(8,128)(2,1)S(1)}, u32[]{:S(2)}, u32[]{:S(2)}) collective-permute-start(bf16[2,256,512]{2,1,0:T(8,128)(2,1)S(1)} %bitcast_dynamic-update-slice_fusion), channel_id=1, source_target_pairs={{0,2},{1,3},{2,4},{3,5},{4,6},{5,7},{6,8},{7,9},{8,10},{9,11},{10,... | collective-permute-start | bytes 1572872 | tf_op jit(solution)/shard_map/ppermute | solution.py:40
  24.8 1.8 %collective-permute-done.3.refs_0_ = bf16[2,256,256]{2,1,0:T(8,128)(2,1)S(1)} collective-permute-done((bf16[2,256,256]{2,1,0:T(8,128)(2,1)S(1)}, bf16[2,256,256]{2,1,0:T(8,128)(2,1)S(1)}, u32[]{:S(2)}, u32[]{:S(2)}) %collective-permute-start.3) | collective-permute-done | bytes 262176 | tf_op jit(solution)/shard_map/ppermute | solution.py:40
  26.6 8.5 %attention.4 = (bf16[256,4096]{1,0:T(8,128)(2,1)}, bf16[256,4096]{1,0:T(8,128)(2,1)}, bf16[2,256,256]{2,1,0:T(8,128)(2,1)S(1)}, f32[256,256]{1,0:T(8,128)S(1)}, f32[256,256]{1,0:T(8,128)S(1)}) custom-call(bf16[256,4096]{1,0:T(8,128)(2,1)} %q_ref.7, bf16[256,4096]{1,0:T(8,128)(2,1)} %g_ref.7, bf16[2,256,256]{2,1,0:T(8,128)(2,1)S(1)} %collective-permute-done.3.refs_0_, ...), custom_call_target="tpu_custom_call" | custom-call | flops 4831838208 | bytes 3538944 | tf_op jit(solution)/shard_map/attention/pallas_call | solution.py:254
  35.1 2.1 %collective-permute-start.5 = (bf16[2,256,256]{2,1,0:T(8,128)(2,1)S(1)}, bf16[2,256,256]{2,1,0:T(8,128)(2,1)S(1)}, u32[]{:S(2)}, u32[]{:S(2)}) collective-permute-start(bf16[2,256,256]{2,1,0:T(8,128)(2,1)S(1)} %get-tuple-element.91), channel_id=1, source_target_pairs={{2,0},{3,1},{4,2},{5,3},{6,4},{7,5},{8,6},{9,7},{10,8},{11,9},{12,... | collective-permute-start | bytes 786440 | tf_op jit(solution)/shard_map/ppermute | solution.py:40
  37.3 8.6 %attention.5 = (bf16[256,4096]{1,0:T(8,128)(2,1)}, bf16[256,4096]{1,0:T(8,128)(2,1)}, bf16[2,256,256]{2,1,0:T(8,128)(2,1)S(1)}, f32[256,256]{1,0:T(8,128)S(1)}, f32[256,256]{1,0:T(8,128)S(1)}) custom-call(bf16[256,4096]{1,0:T(8,128)(2,1)} %q_ref.7, bf16[256,4096]{1,0:T(8,128)(2,1)} %g_ref.7, ...), custom_call_target="tpu_custom_call", output_to_operand_aliasing={{0}: (8, {}), {1}: (9, {})} | custom-call | flops 4831838208 | bytes 3538944 | tf_op jit(solution)/shard_map/attention/pallas_call | solution.py:254
  45.9 2.1 %collective-permute-start.7 = (bf16[2,256,256]{2,1,0:T(8,128)(2,1)S(1)}, bf16[2,256,256]{2,1,0:T(8,128)(2,1)S(1)}, u32[]{:S(2)}, u32[]{:S(2)}) collective-permute-start(bf16[2,256,256]{2,1,0:T(8,128)(2,1)S(1)} %get-tuple-element.94), channel_id=1, source_target_pairs={{2,0},{3,1},{4,2},{5,3},{6,4},{7,5},{8,6},{9,7},{10,8},{11,9},{12,... | collective-permute-start | bytes 786440 | tf_op jit(solution)/shard_map/ppermute | solution.py:40
  48.0 1.5 %collective-permute-done.5 = bf16[2,256,256]{2,1,0:T(8,128)(2,1)S(1)} collective-permute-done((bf16[2,256,256]{2,1,0:T(8,128)(2,1)S(1)}, bf16[2,256,256]{2,1,0:T(8,128)(2,1)S(1)}, u32[]{:S(2)}, u32[]{:S(2)}) %collective-permute-start.5) | collective-permute-done | bytes 262176 | tf_op jit(solution)/shard_map/ppermute | solution.py:40
  49.5 0.1 fusion.7
  49.6 8.3 %attention.6 = (bf16[256,4096]{1,0:T(8,128)(2,1)}, bf16[256,4096]{1,0:T(8,128)(2,1)}, bf16[2,256,256]{2,1,0:T(8,128)(2,1)S(1)}, f32[256,256]{1,0:T(8,128)S(1)}, f32[256,256]{1,0:T(8,128)S(1)}) custom-call(bf16[256,4096]{1,0:T(8,128)(2,1)} %q_ref.7, bf16[256,4096]{1,0:T(8,128)(2,1)} %g_ref.7, ...), custom_call_target="tpu_custom_call", output_to_operand_aliasing={{0}: (8, {}), {1}: (9, {})} | custom-call | flops 4831838208 | bytes 3538944 | tf_op jit(solution)/shard_map/attention/pallas_call | solution.py:254
  57.9 2.2 %collective-permute-start.8 = (bf16[2,256,256]{2,1,0:T(8,128)(2,1)S(1)}, bf16[2,256,256]{2,1,0:T(8,128)(2,1)S(1)}, u32[]{:S(2)}, u32[]{:S(2)}) collective-permute-start(bf16[2,256,256]{2,1,0:T(8,128)(2,1)S(1)} %get-tuple-element.101), channel_id=1, source_target_pairs={{2,0},{3,1},{4,2},{5,3},{6,4},{7,5},{8,6},{9,7},{10,8},{11,9},{12,... | collective-permute-start | bytes 786440 | tf_op jit(solution)/shard_map/ppermute | solution.py:40
  60.2 0.1 fusion.8
  60.3 8.3 %attention.7 = (bf16[256,4096]{1,0:T(8,128)(2,1)}, bf16[256,4096]{1,0:T(8,128)(2,1)}, bf16[2,256,256]{2,1,0:T(8,128)(2,1)S(1)}, f32[256,256]{1,0:T(8,128)S(1)}, f32[256,256]{1,0:T(8,128)S(1)}) custom-call(bf16[256,4096]{1,0:T(8,128)(2,1)} %q_ref.7, bf16[256,4096]{1,0:T(8,128)(2,1)} %g_ref.7, ...), custom_call_target="tpu_custom_call", output_to_operand_aliasing={{0}: (8, {}), {1}: (9, {})} | custom-call | flops 4831838208 | bytes 3538944 | tf_op jit(solution)/shard_map/attention/pallas_call | solution.py:254
  68.6 4.6 %collective-permute-start.9 = (bf16[2,256,256]{2,1,0:T(8,128)(2,1)S(1)}, bf16[2,256,256]{2,1,0:T(8,128)(2,1)S(1)}, u32[]{:S(2)}, u32[]{:S(2)}) collective-permute-start(bf16[2,256,256]{2,1,0:T(8,128)(2,1)S(1)} %get-tuple-element.115), channel_id=1, source_target_pairs={{2,0},{3,1},{4,2},{5,3},{6,4},{7,5},{8,6},{9,7},{10,8},{11,9},{12,... | collective-permute-start | bytes 786440 | tf_op jit(solution)/shard_map/ppermute | solution.py:40
  73.2 1.9 %collective-permute-start.10 = (bf16[256,512]{1,0:T(8,128)(2,1)S(1)}, bf16[256,512]{1,0:T(8,128)(2,1)S(1)}, u32[]{:S(2)}, u32[]{:S(2)}) collective-permute-start(bf16[256,512]{1,0:T(8,128)(2,1)S(1)} %pad_maximum_fusion), channel_id=1, source_target_pairs={{1,0},{2,1},{3,2},{4,3},{5,4},{6,5},{7,6},{8,7},{9,8},{10,9},{11,1... | collective-permute-start | bytes 786440 | tf_op jit(solution)/shard_map/ppermute | solution.py:40
  75.2 3.8 %collective-permute-done.9 = bf16[2,256,256]{2,1,0:T(8,128)(2,1)S(1)} collective-permute-done((bf16[2,256,256]{2,1,0:T(8,128)(2,1)S(1)}, bf16[2,256,256]{2,1,0:T(8,128)(2,1)S(1)}, u32[]{:S(2)}, u32[]{:S(2)}) %collective-permute-start.9) | collective-permute-done | bytes 262176 | tf_op jit(solution)/shard_map/ppermute | solution.py:40
  79.0 0.1 fusion.2
  79.1 0.1 fusion.4
  79.2 4.8 %collective-permute-start.11 = (bf16[256,512]{1,0:T(8,128)(2,1)S(1)}, bf16[256,512]{1,0:T(8,128)(2,1)S(1)}, u32[]{:S(2)}, u32[]{:S(2)}) collective-permute-start(bf16[256,512]{1,0:T(8,128)(2,1)S(1)} %pad_maximum_fusion.1), channel_id=1, source_target_pairs={{1,0},{2,1},{3,2},{4,3},{5,4},{6,5},{7,6},{8,7},{9,8},{10,9},{11,1... | collective-permute-start | bytes 786440 | tf_op jit(solution)/shard_map/ppermute | solution.py:40
  83.9 3.8 %collective-permute-done.10 = bf16[256,512]{1,0:T(8,128)(2,1)S(1)} collective-permute-done((bf16[256,512]{1,0:T(8,128)(2,1)S(1)}, bf16[256,512]{1,0:T(8,128)(2,1)S(1)}, u32[]{:S(2)}, u32[]{:S(2)}) %collective-permute-start.10) | collective-permute-done | bytes 262176 | tf_op jit(solution)/shard_map/ppermute | solution.py:40
  87.7 4.9 %collective-permute-done.11 = bf16[256,512]{1,0:T(8,128)(2,1)S(1)} collective-permute-done((bf16[256,512]{1,0:T(8,128)(2,1)S(1)}, bf16[256,512]{1,0:T(8,128)(2,1)S(1)}, u32[]{:S(2)}, u32[]{:S(2)}) %collective-permute-start.11) | collective-permute-done | bytes 262176 | tf_op jit(solution)/shard_map/ppermute | solution.py:40
  92.6 0.1 fusion
  92.7 0.1 fusion.13
  92.9 0.9 pad_maximum_fusion.2
  (19 shorter events, 0.3 us)
Async XLA Ops:
  0.6 1.0 %copy-start = (bf16[256,512]{1,0:T(8,128)(2,1)S(1)}, bf16[256,512]{1,0:T(8,128)(2,1)}, u32[]{:S(2)}) copy-start(bf16[256,512]{1,0:T(8,128)(2,1)} %keys_full_ref.1) | copy-start | bytes 786436
  1.6 0.9 %copy-start.1 = (bf16[256,512]{1,0:T(8,128)(2,1)S(1)}, bf16[256,512]{1,0:T(8,128)(2,1)}, u32[]{:S(2)}) copy-start(bf16[256,512]{1,0:T(8,128)(2,1)} %values_full_ref.1) | copy-start | bytes 786436
  2.5 0.7 copy-start.2
  4.4 10.2 %collective-permute-start.2 = (bf16[256,256]{1,0:T(8,128)(2,1)S(1)}, bf16[256,256]{1,0:T(8,128)(2,1)S(1)}, u32[]{:S(2)}, u32[]{:S(2)}) collective-permute-start(bf16[256,256]{1,0:T(8,128)(2,1)S(1)} %get-tuple-element.86.refs_2_), channel_id=1, source_target_pairs={{0,1},{1,2},{2,3},{3,4},{4,5},{5,6},{6,7},{7,8},{8,9},{9,10},{10,1... | collective-permute-start | bytes 393224 | tf_op jit(solution)/shard_map/ppermute | solution.py:40
  7.7 10.4 %collective-permute-start.4 = (bf16[256,256]{1,0:T(8,128)(2,1)S(1)}, bf16[256,256]{1,0:T(8,128)(2,1)S(1)}, u32[]{:S(2)}, u32[]{:S(2)}) collective-permute-start(bf16[256,256]{1,0:T(8,128)(2,1)S(1)} %get-tuple-element.85.refs_2_), channel_id=1, source_target_pairs={{0,1},{1,2},{2,3},{3,4},{4,5},{5,6},{6,7},{7,8},{8,9},{9,10},{10,1... | collective-permute-start | bytes 393224 | tf_op jit(solution)/shard_map/ppermute | solution.py:40
  11.2 10.5 %collective-permute-start = (bf16[256,512]{1,0:T(8,128)(2,1)S(1)}, bf16[256,512]{1,0:T(8,128)(2,1)S(1)}, u32[]{:S(2)}, u32[]{:S(2)}) collective-permute-start(bf16[256,512]{1,0:T(8,128)(2,1)S(1)} %get-tuple-element.104.refs_2_), channel_id=1, source_target_pairs={{0,1},{1,2},{2,3},{3,4},{4,5},{5,6},{6,7},{7,8},{8,9},{9,10},{10,1... | collective-permute-start | bytes 786440 | tf_op jit(solution)/shard_map/ppermute | solution.py:40
  14.6 12.0 %collective-permute-start.3 = (bf16[2,256,256]{2,1,0:T(8,128)(2,1)S(1)}, bf16[2,256,256]{2,1,0:T(8,128)(2,1)S(1)}, u32[]{:S(2)}, u32[]{:S(2)}) collective-permute-start(bf16[2,256,256]{2,1,0:T(8,128)(2,1)S(1)} %bitcast_dynamic-update-slice_fusion.2), channel_id=1, source_target_pairs={{0,2},{1,3},{2,4},{3,5},{4,6},{5,7},{6,8},{7,9},{8,10},{9,11},{10,... | collective-permute-start | bytes 786440 | tf_op jit(solution)/shard_map/ppermute | solution.py:40
  18.1 19.1 %collective-permute-start.6 = (bf16[2,256,256]{2,1,0:T(8,128)(2,1)S(1)}, bf16[2,256,256]{2,1,0:T(8,128)(2,1)S(1)}, u32[]{:S(2)}, u32[]{:S(2)}) collective-permute-start(bf16[2,256,256]{2,1,0:T(8,128)(2,1)S(1)} %bitcast_dynamic-update-slice_fusion.1), channel_id=1, source_target_pairs={{0,2},{1,3},{2,4},{3,5},{4,6},{5,7},{6,8},{7,9},{8,10},{9,11},{10,... | collective-permute-start | bytes 786440 | tf_op jit(solution)/shard_map/ppermute | solution.py:40
  21.7 28.0 %collective-permute-start.1 = (bf16[2,256,512]{2,1,0:T(8,128)(2,1)S(1)}, bf16[2,256,512]{2,1,0:T(8,128)(2,1)S(1)}, u32[]{:S(2)}, u32[]{:S(2)}) collective-permute-start(bf16[2,256,512]{2,1,0:T(8,128)(2,1)S(1)} %bitcast_dynamic-update-slice_fusion), channel_id=1, source_target_pairs={{0,2},{1,3},{2,4},{3,5},{4,6},{5,7},{6,8},{7,9},{8,10},{9,11},{10,... | collective-permute-start | bytes 1572872 | tf_op jit(solution)/shard_map/ppermute | solution.py:40
  35.1 14.4 %collective-permute-start.5 = (bf16[2,256,256]{2,1,0:T(8,128)(2,1)S(1)}, bf16[2,256,256]{2,1,0:T(8,128)(2,1)S(1)}, u32[]{:S(2)}, u32[]{:S(2)}) collective-permute-start(bf16[2,256,256]{2,1,0:T(8,128)(2,1)S(1)} %get-tuple-element.91), channel_id=1, source_target_pairs={{2,0},{3,1},{4,2},{5,3},{6,4},{7,5},{8,6},{9,7},{10,8},{11,9},{12,... | collective-permute-start | bytes 786440 | tf_op jit(solution)/shard_map/ppermute | solution.py:40
  45.9 14.3 %collective-permute-start.7 = (bf16[2,256,256]{2,1,0:T(8,128)(2,1)S(1)}, bf16[2,256,256]{2,1,0:T(8,128)(2,1)S(1)}, u32[]{:S(2)}, u32[]{:S(2)}) collective-permute-start(bf16[2,256,256]{2,1,0:T(8,128)(2,1)S(1)} %get-tuple-element.94), channel_id=1, source_target_pairs={{2,0},{3,1},{4,2},{5,3},{6,4},{7,5},{8,6},{9,7},{10,8},{11,9},{12,... | collective-permute-start | bytes 786440 | tf_op jit(solution)/shard_map/ppermute | solution.py:40
  57.9 17.2 %collective-permute-start.8 = (bf16[2,256,256]{2,1,0:T(8,128)(2,1)S(1)}, bf16[2,256,256]{2,1,0:T(8,128)(2,1)S(1)}, u32[]{:S(2)}, u32[]{:S(2)}) collective-permute-start(bf16[2,256,256]{2,1,0:T(8,128)(2,1)S(1)} %get-tuple-element.101), channel_id=1, source_target_pairs={{2,0},{3,1},{4,2},{5,3},{6,4},{7,5},{8,6},{9,7},{10,8},{11,9},{12,... | collective-permute-start | bytes 786440 | tf_op jit(solution)/shard_map/ppermute | solution.py:40
  68.6 10.4 %collective-permute-start.9 = (bf16[2,256,256]{2,1,0:T(8,128)(2,1)S(1)}, bf16[2,256,256]{2,1,0:T(8,128)(2,1)S(1)}, u32[]{:S(2)}, u32[]{:S(2)}) collective-permute-start(bf16[2,256,256]{2,1,0:T(8,128)(2,1)S(1)} %get-tuple-element.115), channel_id=1, source_target_pairs={{2,0},{3,1},{4,2},{5,3},{6,4},{7,5},{8,6},{9,7},{10,8},{11,9},{12,... | collective-permute-start | bytes 786440 | tf_op jit(solution)/shard_map/ppermute | solution.py:40
  73.2 14.5 %collective-permute-start.10 = (bf16[256,512]{1,0:T(8,128)(2,1)S(1)}, bf16[256,512]{1,0:T(8,128)(2,1)S(1)}, u32[]{:S(2)}, u32[]{:S(2)}) collective-permute-start(bf16[256,512]{1,0:T(8,128)(2,1)S(1)} %pad_maximum_fusion), channel_id=1, source_target_pairs={{1,0},{2,1},{3,2},{4,3},{5,4},{6,5},{7,6},{8,7},{9,8},{10,9},{11,1... | collective-permute-start | bytes 786440 | tf_op jit(solution)/shard_map/ppermute | solution.py:40
  79.2 13.4 %collective-permute-start.11 = (bf16[256,512]{1,0:T(8,128)(2,1)S(1)}, bf16[256,512]{1,0:T(8,128)(2,1)S(1)}, u32[]{:S(2)}, u32[]{:S(2)}) collective-permute-start(bf16[256,512]{1,0:T(8,128)(2,1)S(1)} %pad_maximum_fusion.1), channel_id=1, source_target_pairs={{1,0},{2,1},{3,2},{4,3},{5,4},{6,5},{7,6},{8,7},{9,8},{10,9},{11,1... | collective-permute-start | bytes 786440 | tf_op jit(solution)/shard_map/ppermute | solution.py:40

commit v18 on v15

--- a/solution.py
+++ b/solution.py
@@ -18,7 +18,7 @@
 UNIT = 4
 FORWARD = ((0,), (1,), (2, 3))
 OUTS = 5
-SCRATCH = 31
+SCRATCH = 30
 MASKED = -1e30
 SCALE = 1.0 / math.sqrt(HEAD_SIZE)
 EXP2_SCALE = SCALE * math.log2(math.e)
@@ -68,7 +68,7 @@
         bias_ref[:, part * 128 : (part + 1) * 128] = jnp.where(allowed, 0.0, MASKED)
 
 
-def attention_kernel(where, q_ref, g_ref, behind_ref, near_ref, own_full_ref, bias_ref, old_ref, cut_ref, *refs):
+def attention_kernel(where, q_ref, g_ref, behind_ref, near_ref, own_ref, bias_ref, old_ref, cut_ref, *refs):
     out_ref, dq_ref, dbehind_ref, dnear_ref, down_ref = refs[-(OUTS + SCRATCH) : -SCRATCH]
     (
         key_ref, value_ref, key_t_ref, value_t_ref, key2_ref, value2_ref, key2_t_ref, value2_t_ref,
@@ -80,13 +80,11 @@
     head, *offsets = where
     key_in, value_in, key_out, value_out = (slice(at, at + HEAD_SIZE) for at in offsets)
     q_full_ref, g_full_ref, out_full_ref, dq_full_ref = q_ref, g_ref, out_ref, dq_ref
-    q_ref, g_ref, out_ref, dq_ref, own_ref, sem = copies
+    q_ref, g_ref, out_ref, dq_ref, sem = copies
     rows, wide = q_ref.shape
     mine = slice(head * wide, (head + 1) * wide)
     q_copy = pltpu.make_async_copy(q_full_ref.at[:, mine], q_ref, sem.at[0])
     g_copy = pltpu.make_async_copy(g_full_ref.at[:, mine], g_ref, sem.at[1])
-    own_copy = pltpu.make_async_copy(own_full_ref, own_ref, sem.at[2 + 2 * GROUP // UNIT])
-    own_copy.start()
     q_copy.start()
     g_copy.start()
     window = (SPAN - 1) * rows
@@ -95,7 +93,6 @@
     two = slice(0, rows)
     rest = slice(rows, window)
 
-    own_copy.wait()
     from_far = lax.broadcasted_iota(jnp.int32, (rows, HEAD_SIZE), 0) >= cut_ref[0, 0]
     mid, far, near, own = behind_ref.at[0], behind_ref.at[1], near_ref, own_ref
     for j, block in enumerate((mid, near)):
@@ -235,8 +232,7 @@
     fore = blocks[-1].shape[1] // pair
     where = [head, *(at * HEAD_SIZE for at in (place, fore + place, 0, 1))]
     operands = [queries, out_grad, *blocks, *masks]
-    in_specs = [query_spec] * 2 + [whole(block.shape) for block in blocks[:-1]]
-    in_specs += [pl.BlockSpec(memory_space=pl.ANY)] + [whole(mask.shape) for mask in masks]
+    in_specs = [query_spec] * 2 + [whole(array.shape) for array in (*blocks, *masks)]
     aliases = {}
     for at, array in enumerate(grads):
         if array is not None:
@@ -279,10 +275,10 @@
                 for _ in range(count)
             ]
             + [pltpu.VMEM((rows, wide), bf16)] * 4
-            + [pltpu.VMEM(blocks[-1].shape, bf16), pltpu.SemaphoreType.DMA((3 + 2 * GROUP // UNIT,))],
+            + [pltpu.SemaphoreType.DMA((2 + 2 * GROUP // UNIT,))],
         ),
         input_output_aliases=aliases,
-        compiler_params=pltpu.CompilerParams(vmem_limit_bytes=51 * 1024 * 1024),
+        compiler_params=pltpu.CompilerParams(vmem_limit_bytes=48 * 1024 * 1024),
         cost_estimate=pl.CostEstimate(
             flops=12 * rows * GROUP * window * HEAD_SIZE * 2,
             bytes_accessed=4 * rows * wide * 2 + 22 * rows * pair,
@@ -333,6 +329,7 @@
             in_specs=[pl.BlockSpec(keys.shape, two)] * 2,
             out_specs=specs + [pl.BlockSpec(mask.shape, two) for mask in masks],
         ),
+        compiler_params=pltpu.CompilerParams(vmem_limit_bytes=12 * 1024 * 1024),
         name="pack",
     )(first, lengths, keys, values)
     packed = results[: len(shapes)]

time: 95.4 us -> 93.2 us (0.977); the launches traced: 93.9 us -> 92.7 us
  waiting for transfers between devices: 15 us -> 24.6 us
  Pallas kernels: 33.3 us -> 27.8 us
  starting transfers between devices: 37.4 us -> 33.7 us
  local copies, waits for them, and re-layouts: 5.79 us -> 4.29 us
    ppermute x12, waiting for transfers between devices: 15 us -> 24.6 us  [passed_along(): lax.ppermute(value, AXES, [(source, source + steps) for source in range(f...]
    ppermute x12, starting transfers between devices: 37.4 us -> 33.7 us  [passed_along(): lax.ppermute(value, AXES, [(source, source + steps) for source in range(f...]
    pallas_call x4, Pallas kernels: 29.9 us -> 26.6 us  [attention(): pl.pallas_call(functools.partial(attention_kernel, where), out_shape=[jax...]
    pallas_call x1, Pallas kernels: 3.41 us -> 1.17 us  [pack(): pl.pallas_call(pack_kernel, out_shape=shapes + masks, grid_spec=pltpu.Pre...]
    scatter x3, local copies, waits for them, and re-layouts: 2.05 us -> 0.04 us  [local(): pairs = [pair.at[1].set(near) for pair, near in zip(pairs, nears)]]
    unnamed x14 -> x10, local copies, waits for them, and re-layouts: 3.64 us -> 4.14 us
  transfers between devices with their start and end apart: 12 -> 12, of which waited for: 5 -> 5; matrix products, arithmetic and copies ran while one was open for 3% -> 1% of each run, Pallas kernels for 32% -> 29%
where the time goes in v18:
time: 93.2 us; the launch traced here: 92.7 us
  starting transfers between devices  33.7 us (36%)
  Pallas kernels  27.8 us (30%)
  waiting for transfers between devices  24.6 us (26%)
  local copies, waits for them, and re-layouts  4.29 us (5%)
  other arithmetic  1.46 us (2%)
  between operations  0.96 us (1%)
    ppermute x12, starting transfers between devices, passed_along(): lax.ppermute(value, AXES, [(source, source + steps) for source in range(f...  33.7 us
    pallas_call x4, Pallas kernels, attention(): pl.pallas_call(functools.partial(attention_kernel, where), out_shape=[jax...  26.6 us
    ppermute x12, waiting for transfers between devices, passed_along(): lax.ppermute(value, AXES, [(source, source + steps) for source in range(f...  24.6 us
    unnamed x10, local copies, waits for them, and re-layouts  4.14 us
  transfers between devices with their start and end apart: 12, of which 5 were waited for; matrix products, arithmetic and copies ran while one was open for 1% of the time, Pallas kernels for 29%

profile of v18, /device:TPU:29, one launch (start us, length us, event | category | flops | bytes accessed | tf_op | source)
XLA Modules:
  0.0 92.7 jit_solution(1495841715127252955)
XLA Ops:
  0.6 0.9 %copy-done = bf16[256,512]{1,0:T(8,128)(2,1)S(1)} copy-done((bf16[256,512]{1,0:T(8,128)(2,1)S(1)}, bf16[256,512]{1,0:T(8,128)(2,1)}, u32[]{:S(2)}) %copy-start) | copy-done | bytes 262168
  1.6 0.9 %copy-done.1 = bf16[256,512]{1,0:T(8,128)(2,1)S(1)} copy-done((bf16[256,512]{1,0:T(8,128)(2,1)S(1)}, bf16[256,512]{1,0:T(8,128)(2,1)}, u32[]{:S(2)}) %copy-start.1) | copy-done | bytes 262168
  2.5 0.7 copy-done.2
  3.2 1.2 %pack.1 = (bf16[256,256]{1,0:T(8,128)(2,1)S(1)}, bf16[2,256,256]{2,1,0:T(8,128)(2,1)S(1)}, bf16[256,256]{1,0:T(8,128)(2,1)S(1)}, bf16[2,256,256]{2,1,0:T(8,128)(...) custom-call(s32[1]{0:T(128)} %bitcast.first_ref, ...), custom_call_target="tpu_custom_call" | custom-call | tf_op jit(solution)/shard_map/pack/pallas_call | solution.py:323
  4.4 3.3 %collective-permute-start.2 = (bf16[256,256]{1,0:T(8,128)(2,1)S(1)}, bf16[256,256]{1,0:T(8,128)(2,1)S(1)}, u32[]{:S(2)}, u32[]{:S(2)}) collective-permute-start(bf16[256,256]{1,0:T(8,128)(2,1)S(1)} %get-tuple-element.86.own_ref), channel_id=1, source_target_pairs={{0,1},{1,2},{2,3},{3,4},{4,5},{5,6},{6,7},{7,8},{8,9},{9,10},{10,1... | collective-permute-start | bytes 393224 | tf_op jit(solution)/shard_map/ppermute | solution.py:40
  7.7 3.4 %collective-permute-start.4 = (bf16[256,256]{1,0:T(8,128)(2,1)S(1)}, bf16[256,256]{1,0:T(8,128)(2,1)S(1)}, u32[]{:S(2)}, u32[]{:S(2)}) collective-permute-start(bf16[256,256]{1,0:T(8,128)(2,1)S(1)} %get-tuple-element.85.own_ref), channel_id=1, source_target_pairs={{0,1},{1,2},{2,3},{3,4},{4,5},{5,6},{6,7},{7,8},{8,9},{9,10},{10,1... | collective-permute-start | bytes 393224 | tf_op jit(solution)/shard_map/ppermute | solution.py:40
  11.1 3.4 %collective-permute-start = (bf16[256,512]{1,0:T(8,128)(2,1)S(1)}, bf16[256,512]{1,0:T(8,128)(2,1)S(1)}, u32[]{:S(2)}, u32[]{:S(2)}) collective-permute-start(bf16[256,512]{1,0:T(8,128)(2,1)S(1)} %get-tuple-element.104.own_ref), channel_id=1, source_target_pairs={{0,1},{1,2},{2,3},{3,4},{4,5},{5,6},{6,7},{7,8},{8,9},{9,10},{10,1... | collective-permute-start | bytes 786440 | tf_op jit(solution)/shard_map/ppermute | solution.py:40
  14.6 3.5 %collective-permute-start.3 = (bf16[2,256,256]{2,1,0:T(8,128)(2,1)S(1)}, bf16[2,256,256]{2,1,0:T(8,128)(2,1)S(1)}, u32[]{:S(2)}, u32[]{:S(2)}) collective-permute-start(bf16[2,256,256]{2,1,0:T(8,128)(2,1)S(1)} %bitcast_dynamic-update-slice_fusion.2), channel_id=1, source_target_pairs={{0,2},{1,3},{2,4},{3,5},{4,6},{5,7},{6,8},{7,9},{8,10},{9,11},{10,... | collective-permute-start | bytes 786440 | tf_op jit(solution)/shard_map/ppermute | solution.py:40
  18.1 3.5 %collective-permute-start.6 = (bf16[2,256,256]{2,1,0:T(8,128)(2,1)S(1)}, bf16[2,256,256]{2,1,0:T(8,128)(2,1)S(1)}, u32[]{:S(2)}, u32[]{:S(2)}) collective-permute-start(bf16[2,256,256]{2,1,0:T(8,128)(2,1)S(1)} %bitcast_dynamic-update-slice_fusion.1), channel_id=1, source_target_pairs={{0,2},{1,3},{2,4},{3,5},{4,6},{5,7},{6,8},{7,9},{8,10},{9,11},{10,... | collective-permute-start | bytes 786440 | tf_op jit(solution)/shard_map/ppermute | solution.py:40
  21.6 3.2 %collective-permute-start.1 = (bf16[2,256,512]{2,1,0:T(8,128)(2,1)S(1)}, bf16[2,256,512]{2,1,0:T(8,128)(2,1)S(1)}, u32[]{:S(2)}, u32[]{:S(2)}) collective-permute-start(bf16[2,256,512]{2,1,0:T(8,128)(2,1)S(1)} %bitcast_dynamic-update-slice_fusion), channel_id=1, source_target_pairs={{0,2},{1,3},{2,4},{3,5},{4,6},{5,7},{6,8},{7,9},{8,10},{9,11},{10,... | collective-permute-start | bytes 1572872 | tf_op jit(solution)/shard_map/ppermute | solution.py:40
  24.8 1.8 %collective-permute-done.3.behind_ref = bf16[2,256,256]{2,1,0:T(8,128)(2,1)S(1)} collective-permute-done((bf16[2,256,256]{2,1,0:T(8,128)(2,1)S(1)}, bf16[2,256,256]{2,1,0:T(8,128)(2,1)S(1)}, u32[]{:S(2)}, u32[]{:S(2)}) %collective-permute-start.3) | collective-permute-done | bytes 262176 | tf_op jit(solution)/shard_map/ppermute | solution.py:40
  26.5 1.6 %copy-done.3 = bf16[256,4096]{1,0:T(8,128)(2,1)S(1)} copy-done((bf16[256,4096]{1,0:T(8,128)(2,1)S(1)}, bf16[256,4096]{1,0:T(8,128)(2,1)}, u32[]{:S(2)}) %copy-start.3) | copy-done | bytes 2097176
  28.1 6.6 %attention.4 = (bf16[256,4096]{1,0:T(8,128)(2,1)}, bf16[256,4096]{1,0:T(8,128)(2,1)}, bf16[2,256,256]{2,1,0:T(8,128)(2,1)S(1)}, f32[256,256]{1,0:T(8,128)S(1)}, f32[256,256]{1,0:T(8,128)S(1)}) custom-call(bf16[256,4096]{1,0:T(8,128)(2,1)S(1)} %copy-done.3, bf16[256,4096]{1,0:T(8,128)(2,1)} %g_ref.7, ...), custom_call_target="tpu_custom_call" | custom-call | flops 4831838208 | bytes 3538944 | tf_op jit(solution)/shard_map/attention/pallas_call | solution.py:243
  34.8 2.1 %collective-permute-start.5 = (bf16[2,256,256]{2,1,0:T(8,128)(2,1)S(1)}, bf16[2,256,256]{2,1,0:T(8,128)(2,1)S(1)}, u32[]{:S(2)}, u32[]{:S(2)}) collective-permute-start(bf16[2,256,256]{2,1,0:T(8,128)(2,1)S(1)} %get-tuple-element.91), channel_id=1, source_target_pairs={{2,0},{3,1},{4,2},{5,3},{6,4},{7,5},{8,6},{9,7},{10,8},{11,9},{12,... | collective-permute-start | bytes 786440 | tf_op jit(solution)/shard_map/ppermute | solution.py:40
  36.9 6.7 %attention.5 = (bf16[256,4096]{1,0:T(8,128)(2,1)}, bf16[256,4096]{1,0:T(8,128)(2,1)}, bf16[2,256,256]{2,1,0:T(8,128)(2,1)S(1)}, f32[256,256]{1,0:T(8,128)S(1)}, f32[256,256]{1,0:T(8,128)S(1)}) custom-call(bf16[256,4096]{1,0:T(8,128)(2,1)S(1)} %copy-done.3, bf16[256,4096]{1,0:T(8,128)(2,1)} %g_ref.7, ...), custom_call_target="tpu_custom_call", output_to_operand_aliasing={{0}: (8, {}), {1}: (9, {})} | custom-call | flops 4831838208 | bytes 3538944 | tf_op jit(solution)/shard_map/attention/pallas_call | solution.py:243
  43.6 2.3 %collective-permute-start.7 = (bf16[2,256,256]{2,1,0:T(8,128)(2,1)S(1)}, bf16[2,256,256]{2,1,0:T(8,128)(2,1)S(1)}, u32[]{:S(2)}, u32[]{:S(2)}) collective-permute-start(bf16[2,256,256]{2,1,0:T(8,128)(2,1)S(1)} %get-tuple-element.94), channel_id=1, source_target_pairs={{2,0},{3,1},{4,2},{5,3},{6,4},{7,5},{8,6},{9,7},{10,8},{11,9},{12,... | collective-permute-start | bytes 786440 | tf_op jit(solution)/shard_map/ppermute | solution.py:40
  45.9 3.6 %collective-permute-done.5 = bf16[2,256,256]{2,1,0:T(8,128)(2,1)S(1)} collective-permute-done((bf16[2,256,256]{2,1,0:T(8,128)(2,1)S(1)}, bf16[2,256,256]{2,1,0:T(8,128)(2,1)S(1)}, u32[]{:S(2)}, u32[]{:S(2)}) %collective-permute-start.5) | collective-permute-done | bytes 262176 | tf_op jit(solution)/shard_map/ppermute | solution.py:40
  49.5 0.1 fusion.7
  49.6 6.6 %attention.6 = (bf16[256,4096]{1,0:T(8,128)(2,1)}, bf16[256,4096]{1,0:T(8,128)(2,1)}, bf16[2,256,256]{2,1,0:T(8,128)(2,1)S(1)}, f32[256,256]{1,0:T(8,128)S(1)}, f32[256,256]{1,0:T(8,128)S(1)}) custom-call(bf16[256,4096]{1,0:T(8,128)(2,1)S(1)} %copy-done.4, bf16[256,4096]{1,0:T(8,128)(2,1)} %g_ref.7, ...), custom_call_target="tpu_custom_call", output_to_operand_aliasing={{0}: (8, {}), {1}: (9, {})} | custom-call | flops 4831838208 | bytes 3538944 | tf_op jit(solution)/shard_map/attention/pallas_call | solution.py:243
  56.2 2.2 %collective-permute-start.8 = (bf16[2,256,256]{2,1,0:T(8,128)(2,1)S(1)}, bf16[2,256,256]{2,1,0:T(8,128)(2,1)S(1)}, u32[]{:S(2)}, u32[]{:S(2)}) collective-permute-start(bf16[2,256,256]{2,1,0:T(8,128)(2,1)S(1)} %get-tuple-element.101), channel_id=1, source_target_pairs={{2,0},{3,1},{4,2},{5,3},{6,4},{7,5},{8,6},{9,7},{10,8},{11,9},{12,... | collective-permute-start | bytes 786440 | tf_op jit(solution)/shard_map/ppermute | solution.py:40
  58.6 6.7 %attention.7 = (bf16[256,4096]{1,0:T(8,128)(2,1)}, bf16[256,4096]{1,0:T(8,128)(2,1)}, bf16[2,256,256]{2,1,0:T(8,128)(2,1)S(1)}, f32[256,256]{1,0:T(8,128)S(1)}, f32[256,256]{1,0:T(8,128)S(1)}) custom-call(bf16[256,4096]{1,0:T(8,128)(2,1)S(1)} %copy-done.4, bf16[256,4096]{1,0:T(8,128)(2,1)} %g_ref.7, ...), custom_call_target="tpu_custom_call", output_to_operand_aliasing={{0}: (8, {}), {1}: (9, {})} | custom-call | flops 4831838208 | bytes 3538944 | tf_op jit(solution)/shard_map/attention/pallas_call | solution.py:243
  65.2 3.0 %collective-permute-start.9 = (bf16[2,256,256]{2,1,0:T(8,128)(2,1)S(1)}, bf16[2,256,256]{2,1,0:T(8,128)(2,1)S(1)}, u32[]{:S(2)}, u32[]{:S(2)}) collective-permute-start(bf16[2,256,256]{2,1,0:T(8,128)(2,1)S(1)} %get-tuple-element.115), channel_id=1, source_target_pairs={{2,0},{3,1},{4,2},{5,3},{6,4},{7,5},{8,6},{9,7},{10,8},{11,9},{12,... | collective-permute-start | bytes 786440 | tf_op jit(solution)/shard_map/ppermute | solution.py:40
  68.2 1.9 %collective-permute-start.10 = (bf16[256,512]{1,0:T(8,128)(2,1)S(1)}, bf16[256,512]{1,0:T(8,128)(2,1)S(1)}, u32[]{:S(2)}, u32[]{:S(2)}) collective-permute-start(bf16[256,512]{1,0:T(8,128)(2,1)S(1)} %pad_maximum_fusion), channel_id=1, source_target_pairs={{1,0},{2,1},{3,2},{4,3},{5,4},{6,5},{7,6},{8,7},{9,8},{10,9},{11,1... | collective-permute-start | bytes 786440 | tf_op jit(solution)/shard_map/ppermute | solution.py:40
  70.2 7.2 %collective-permute-done.9 = bf16[2,256,256]{2,1,0:T(8,128)(2,1)S(1)} collective-permute-done((bf16[2,256,256]{2,1,0:T(8,128)(2,1)S(1)}, bf16[2,256,256]{2,1,0:T(8,128)(2,1)S(1)}, u32[]{:S(2)}, u32[]{:S(2)}) %collective-permute-start.9) | collective-permute-done | bytes 262176 | tf_op jit(solution)/shard_map/ppermute | solution.py:40
  77.5 0.1 fusion.2
  77.5 0.1 fusion.4
  77.6 1.9 %collective-permute-start.11 = (bf16[256,512]{1,0:T(8,128)(2,1)S(1)}, bf16[256,512]{1,0:T(8,128)(2,1)S(1)}, u32[]{:S(2)}, u32[]{:S(2)}) collective-permute-start(bf16[256,512]{1,0:T(8,128)(2,1)S(1)} %pad_maximum_fusion.1), channel_id=1, source_target_pairs={{1,0},{2,1},{3,2},{4,3},{5,4},{6,5},{7,6},{8,7},{9,8},{10,9},{11,1... | collective-permute-start | bytes 786440 | tf_op jit(solution)/shard_map/ppermute | solution.py:40
  79.6 3.1 %collective-permute-done.10 = bf16[256,512]{1,0:T(8,128)(2,1)S(1)} collective-permute-done((bf16[256,512]{1,0:T(8,128)(2,1)S(1)}, bf16[256,512]{1,0:T(8,128)(2,1)S(1)}, u32[]{:S(2)}, u32[]{:S(2)}) %collective-permute-start.10) | collective-permute-done | bytes 262176 | tf_op jit(solution)/shard_map/ppermute | solution.py:40
  82.7 8.9 %collective-permute-done.11 = bf16[256,512]{1,0:T(8,128)(2,1)S(1)} collective-permute-done((bf16[256,512]{1,0:T(8,128)(2,1)S(1)}, bf16[256,512]{1,0:T(8,128)(2,1)S(1)}, u32[]{:S(2)}, u32[]{:S(2)}) %collective-permute-start.11) | collective-permute-done | bytes 262176 | tf_op jit(solution)/shard_map/ppermute | solution.py:40
  91.6 0.1 fusion
  91.8 0.1 fusion.13
  91.9 0.9 pad_maximum_fusion.2
  (23 shorter events, 0.3 us)
Async XLA Ops:
  0.6 1.0 %copy-start = (bf16[256,512]{1,0:T(8,128)(2,1)S(1)}, bf16[256,512]{1,0:T(8,128)(2,1)}, u32[]{:S(2)}) copy-start(bf16[256,512]{1,0:T(8,128)(2,1)} %keys_ref.1) | copy-start | bytes 786436
  1.6 0.9 %copy-start.1 = (bf16[256,512]{1,0:T(8,128)(2,1)S(1)}, bf16[256,512]{1,0:T(8,128)(2,1)}, u32[]{:S(2)}) copy-start(bf16[256,512]{1,0:T(8,128)(2,1)} %values_ref.1) | copy-start | bytes 786436
  2.5 0.7 copy-start.2
  4.4 10.2 %collective-permute-start.2 = (bf16[256,256]{1,0:T(8,128)(2,1)S(1)}, bf16[256,256]{1,0:T(8,128)(2,1)S(1)}, u32[]{:S(2)}, u32[]{:S(2)}) collective-permute-start(bf16[256,256]{1,0:T(8,128)(2,1)S(1)} %get-tuple-element.86.own_ref), channel_id=1, source_target_pairs={{0,1},{1,2},{2,3},{3,4},{4,5},{5,6},{6,7},{7,8},{8,9},{9,10},{10,1... | collective-permute-start | bytes 393224 | tf_op jit(solution)/shard_map/ppermute | solution.py:40
  7.7 10.4 %collective-permute-start.4 = (bf16[256,256]{1,0:T(8,128)(2,1)S(1)}, bf16[256,256]{1,0:T(8,128)(2,1)S(1)}, u32[]{:S(2)}, u32[]{:S(2)}) collective-permute-start(bf16[256,256]{1,0:T(8,128)(2,1)S(1)} %get-tuple-element.85.own_ref), channel_id=1, source_target_pairs={{0,1},{1,2},{2,3},{3,4},{4,5},{5,6},{6,7},{7,8},{8,9},{9,10},{10,1... | collective-permute-start | bytes 393224 | tf_op jit(solution)/shard_map/ppermute | solution.py:40
  11.1 10.5 %collective-permute-start = (bf16[256,512]{1,0:T(8,128)(2,1)S(1)}, bf16[256,512]{1,0:T(8,128)(2,1)S(1)}, u32[]{:S(2)}, u32[]{:S(2)}) collective-permute-start(bf16[256,512]{1,0:T(8,128)(2,1)S(1)} %get-tuple-element.104.own_ref), channel_id=1, source_target_pairs={{0,1},{1,2},{2,3},{3,4},{4,5},{5,6},{6,7},{7,8},{8,9},{9,10},{10,1... | collective-permute-start | bytes 786440 | tf_op jit(solution)/shard_map/ppermute | solution.py:40
  14.6 12.0 %collective-permute-start.3 = (bf16[2,256,256]{2,1,0:T(8,128)(2,1)S(1)}, bf16[2,256,256]{2,1,0:T(8,128)(2,1)S(1)}, u32[]{:S(2)}, u32[]{:S(2)}) collective-permute-start(bf16[2,256,256]{2,1,0:T(8,128)(2,1)S(1)} %bitcast_dynamic-update-slice_fusion.2), channel_id=1, source_target_pairs={{0,2},{1,3},{2,4},{3,5},{4,6},{5,7},{6,8},{7,9},{8,10},{9,11},{10,... | collective-permute-start | bytes 786440 | tf_op jit(solution)/shard_map/ppermute | solution.py:40
  18.1 18.8 %collective-permute-start.6 = (bf16[2,256,256]{2,1,0:T(8,128)(2,1)S(1)}, bf16[2,256,256]{2,1,0:T(8,128)(2,1)S(1)}, u32[]{:S(2)}, u32[]{:S(2)}) collective-permute-start(bf16[2,256,256]{2,1,0:T(8,128)(2,1)S(1)} %bitcast_dynamic-update-slice_fusion.1), channel_id=1, source_target_pairs={{0,2},{1,3},{2,4},{3,5},{4,6},{5,7},{6,8},{7,9},{8,10},{9,11},{10,... | collective-permute-start | bytes 786440 | tf_op jit(solution)/shard_map/ppermute | solution.py:40
  21.6 28.0 %collective-permute-start.1 = (bf16[2,256,512]{2,1,0:T(8,128)(2,1)S(1)}, bf16[2,256,512]{2,1,0:T(8,128)(2,1)S(1)}, u32[]{:S(2)}, u32[]{:S(2)}) collective-permute-start(bf16[2,256,512]{2,1,0:T(8,128)(2,1)S(1)} %bitcast_dynamic-update-slice_fusion), channel_id=1, source_target_pairs={{0,2},{1,3},{2,4},{3,5},{4,6},{5,7},{6,8},{7,9},{8,10},{9,11},{10,... | collective-permute-start | bytes 1572872 | tf_op jit(solution)/shard_map/ppermute | solution.py:40
  26.5 1.6 %copy-start.3 = (bf16[256,4096]{1,0:T(8,128)(2,1)S(1)}, bf16[256,4096]{1,0:T(8,128)(2,1)}, u32[]{:S(2)}) copy-start(bf16[256,4096]{1,0:T(8,128)(2,1)} %q_ref.7) | copy-start | bytes 6291460
  34.8 14.7 %collective-permute-start.5 = (bf16[2,256,256]{2,1,0:T(8,128)(2,1)S(1)}, bf16[2,256,256]{2,1,0:T(8,128)(2,1)S(1)}, u32[]{:S(2)}, u32[]{:S(2)}) collective-permute-start(bf16[2,256,256]{2,1,0:T(8,128)(2,1)S(1)} %get-tuple-element.91), channel_id=1, source_target_pairs={{2,0},{3,1},{4,2},{5,3},{6,4},{7,5},{8,6},{9,7},{10,8},{11,9},{12,... | collective-permute-start | bytes 786440 | tf_op jit(solution)/shard_map/ppermute | solution.py:40
  43.6 6.0 %copy-start.4 = (bf16[256,4096]{1,0:T(8,128)(2,1)S(1)}, bf16[256,4096]{1,0:T(8,128)(2,1)}, u32[]{:S(2)}) copy-start(bf16[256,4096]{1,0:T(8,128)(2,1)} %q_ref.7) | copy-start | bytes 6291460
  43.6 14.9 %collective-permute-start.7 = (bf16[2,256,256]{2,1,0:T(8,128)(2,1)S(1)}, bf16[2,256,256]{2,1,0:T(8,128)(2,1)S(1)}, u32[]{:S(2)}, u32[]{:S(2)}) collective-permute-start(bf16[2,256,256]{2,1,0:T(8,128)(2,1)S(1)} %get-tuple-element.94), channel_id=1, source_target_pairs={{2,0},{3,1},{4,2},{5,3},{6,4},{7,5},{8,6},{9,7},{10,8},{11,9},{12,... | collective-permute-start | bytes 786440 | tf_op jit(solution)/shard_map/ppermute | solution.py:40
  56.2 13.9 %collective-permute-start.8 = (bf16[2,256,256]{2,1,0:T(8,128)(2,1)S(1)}, bf16[2,256,256]{2,1,0:T(8,128)(2,1)S(1)}, u32[]{:S(2)}, u32[]{:S(2)}) collective-permute-start(bf16[2,256,256]{2,1,0:T(8,128)(2,1)S(1)} %get-tuple-element.101), channel_id=1, source_target_pairs={{2,0},{3,1},{4,2},{5,3},{6,4},{7,5},{8,6},{9,7},{10,8},{11,9},{12,... | collective-permute-start | bytes 786440 | tf_op jit(solution)/shard_map/ppermute | solution.py:40
  65.2 12.2 %collective-permute-start.9 = (bf16[2,256,256]{2,1,0:T(8,128)(2,1)S(1)}, bf16[2,256,256]{2,1,0:T(8,128)(2,1)S(1)}, u32[]{:S(2)}, u32[]{:S(2)}) collective-permute-start(bf16[2,256,256]{2,1,0:T(8,128)(2,1)S(1)} %get-tuple-element.115), channel_id=1, source_target_pairs={{2,0},{3,1},{4,2},{5,3},{6,4},{7,5},{8,6},{9,7},{10,8},{11,9},{12,... | collective-permute-start | bytes 786440 | tf_op jit(solution)/shard_map/ppermute | solution.py:40
  68.2 14.4 %collective-permute-start.10 = (bf16[256,512]{1,0:T(8,128)(2,1)S(1)}, bf16[256,512]{1,0:T(8,128)(2,1)S(1)}, u32[]{:S(2)}, u32[]{:S(2)}) collective-permute-start(bf16[256,512]{1,0:T(8,128)(2,1)S(1)} %pad_maximum_fusion), channel_id=1, source_target_pairs={{1,0},{2,1},{3,2},{4,3},{5,4},{6,5},{7,6},{8,7},{9,8},{10,9},{11,1... | collective-permute-start | bytes 786440 | tf_op jit(solution)/shard_map/ppermute | solution.py:40
  77.6 14.0 %collective-permute-start.11 = (bf16[256,512]{1,0:T(8,128)(2,1)S(1)}, bf16[256,512]{1,0:T(8,128)(2,1)S(1)}, u32[]{:S(2)}, u32[]{:S(2)}) collective-permute-start(bf16[256,512]{1,0:T(8,128)(2,1)S(1)} %pad_maximum_fusion.1), channel_id=1, source_target_pairs={{1,0},{2,1},{3,2},{4,3},{5,4},{6,5},{7,6},{8,7},{9,8},{10,9},{11,1... | collective-permute-start | bytes 786440 | tf_op jit(solution)/shard_map/ppermute | solution.py:40

commit v19 on v18

--- a/solution.py
+++ b/solution.py
@@ -369,13 +369,12 @@
     gots = [passed_along(parts[0][0], -2)]
     attend(1)
     gots.append(passed_along(parts[1][0], -2))
-    gots[0], _ = lax.optimization_barrier((gots[0], parts[1][0]))
+    attend(2)
+    gots.append(passed_along(parts[2][0], -2))
+    gots[0], gots[1], _ = lax.optimization_barrier((gots[0], gots[1], parts[2][0]))
     nears, owns = zip(second_hop(*parts[0][1:], gots[0]))
-    (nears,) = attend(2, nears)
-    gots.append(passed_along(parts[2][0], -2))
-    gots[1], _ = lax.optimization_barrier((gots[1], parts[2][0]))
     more = second_hop(*parts[1][1:], gots[1])
-    (nears, *more) = attend(3, (nears, *more))
+    (nears, *more) = attend(3, (*nears, *more))
     gots[2], near = lax.optimization_barrier((gots[2], parts[3][1]))
     gots.append(passed_along(parts[3][0], -2))
     parts[3][1] = near

time: 93.2 us -> 89.6 us (0.961); the launches traced: 92.7 us -> 88.1 us
  waiting for transfers between devices: 24.6 us -> 14.9 us
  starting transfers between devices: 33.7 us -> 38.8 us
    ppermute x12, waiting for transfers between devices: 24.6 us -> 14.9 us  [passed_along(): lax.ppermute(value, AXES, [(source, source + steps) for source in range(f...]
    ppermute x12, starting transfers between devices: 33.7 us -> 38.8 us  [passed_along(): lax.ppermute(value, AXES, [(source, source + steps) for source in range(f...]
  transfers between devices with their start and end apart: 12 -> 12, of which waited for: 5 -> 6; matrix products, arithmetic and copies ran while one was open for 1% -> 1% of each run, Pallas kernels for 29% -> 30%
where the time goes in v19:
time: 89.6 us; the launch traced here: 88.1 us
  starting transfers between devices  38.8 us (43%)
  Pallas kernels  27.8 us (31%)
  waiting for transfers between devices  14.9 us (17%)
  local copies, waits for them, and re-layouts  4.29 us (5%)
  other arithmetic  1.45 us (2%)
  between operations  0.94 us (1%)
    ppermute x12, starting transfers between devices, passed_along(): lax.ppermute(value, AXES, [(source, source + steps) for source in range(f...  38.8 us
    pallas_call x4, Pallas kernels, attention(): pl.pallas_call(functools.partial(attention_kernel, where), out_shape=[jax...  26.6 us
    ppermute x12, waiting for transfers between devices, passed_along(): lax.ppermute(value, AXES, [(source, source + steps) for source in range(f...  14.9 us
    unnamed x10, local copies, waits for them, and re-layouts  4.14 us
  transfers between devices with their start and end apart: 12, of which 6 were waited for; matrix products, arithmetic and copies ran while one was open for 1% of the time, Pallas kernels for 30%

profile of v19, /device:TPU:29, one launch (start us, length us, event | category | flops | bytes accessed | tf_op | source)
XLA Modules:
  0.0 88.1 jit_solution(697827420438385631)
XLA Ops:
  0.6 0.9 %copy-done = bf16[256,512]{1,0:T(8,128)(2,1)S(1)} copy-done((bf16[256,512]{1,0:T(8,128)(2,1)S(1)}, bf16[256,512]{1,0:T(8,128)(2,1)}, u32[]{:S(2)}) %copy-start) | copy-done | bytes 262168
  1.6 0.9 %copy-done.1 = bf16[256,512]{1,0:T(8,128)(2,1)S(1)} copy-done((bf16[256,512]{1,0:T(8,128)(2,1)S(1)}, bf16[256,512]{1,0:T(8,128)(2,1)}, u32[]{:S(2)}) %copy-start.1) | copy-done | bytes 262168
  2.5 0.7 copy-done.2
  3.2 1.2 %pack.1 = (bf16[256,256]{1,0:T(8,128)(2,1)S(1)}, bf16[2,256,256]{2,1,0:T(8,128)(2,1)S(1)}, bf16[256,256]{1,0:T(8,128)(2,1)S(1)}, bf16[2,256,256]{2,1,0:T(8,128)(...) custom-call(s32[1]{0:T(128)} %bitcast.first_ref, ...), custom_call_target="tpu_custom_call" | custom-call | tf_op jit(solution)/shard_map/pack/pallas_call | solution.py:323
  4.4 3.3 %collective-permute-start.2 = (bf16[256,256]{1,0:T(8,128)(2,1)S(1)}, bf16[256,256]{1,0:T(8,128)(2,1)S(1)}, u32[]{:S(2)}, u32[]{:S(2)}) collective-permute-start(bf16[256,256]{1,0:T(8,128)(2,1)S(1)} %get-tuple-element.84.own_ref), channel_id=1, source_target_pairs={{0,1},{1,2},{2,3},{3,4},{4,5},{5,6},{6,7},{7,8},{8,9},{9,10},{10,1... | collective-permute-start | bytes 393224 | tf_op jit(solution)/shard_map/ppermute | solution.py:40
  7.7 3.4 %collective-permute-start.4 = (bf16[256,256]{1,0:T(8,128)(2,1)S(1)}, bf16[256,256]{1,0:T(8,128)(2,1)S(1)}, u32[]{:S(2)}, u32[]{:S(2)}) collective-permute-start(bf16[256,256]{1,0:T(8,128)(2,1)S(1)} %get-tuple-element.83.own_ref), channel_id=1, source_target_pairs={{0,1},{1,2},{2,3},{3,4},{4,5},{5,6},{6,7},{7,8},{8,9},{9,10},{10,1... | collective-permute-start | bytes 393224 | tf_op jit(solution)/shard_map/ppermute | solution.py:40
  11.1 3.4 %collective-permute-start = (bf16[256,512]{1,0:T(8,128)(2,1)S(1)}, bf16[256,512]{1,0:T(8,128)(2,1)S(1)}, u32[]{:S(2)}, u32[]{:S(2)}) collective-permute-start(bf16[256,512]{1,0:T(8,128)(2,1)S(1)} %get-tuple-element.100.own_ref), channel_id=1, source_target_pairs={{0,1},{1,2},{2,3},{3,4},{4,5},{5,6},{6,7},{7,8},{8,9},{9,10},{10,1... | collective-permute-start | bytes 786440 | tf_op jit(solution)/shard_map/ppermute | solution.py:40
  14.6 3.5 %collective-permute-start.3 = (bf16[2,256,256]{2,1,0:T(8,128)(2,1)S(1)}, bf16[2,256,256]{2,1,0:T(8,128)(2,1)S(1)}, u32[]{:S(2)}, u32[]{:S(2)}) collective-permute-start(bf16[2,256,256]{2,1,0:T(8,128)(2,1)S(1)} %bitcast_dynamic-update-slice_fusion.2), channel_id=1, source_target_pairs={{0,2},{1,3},{2,4},{3,5},{4,6},{5,7},{6,8},{7,9},{8,10},{9,11},{10,... | collective-permute-start | bytes 786440 | tf_op jit(solution)/shard_map/ppermute | solution.py:40
  18.1 3.5 %collective-permute-start.6 = (bf16[2,256,256]{2,1,0:T(8,128)(2,1)S(1)}, bf16[2,256,256]{2,1,0:T(8,128)(2,1)S(1)}, u32[]{:S(2)}, u32[]{:S(2)}) collective-permute-start(bf16[2,256,256]{2,1,0:T(8,128)(2,1)S(1)} %bitcast_dynamic-update-slice_fusion.1), channel_id=1, source_target_pairs={{0,2},{1,3},{2,4},{3,5},{4,6},{5,7},{6,8},{7,9},{8,10},{9,11},{10,... | collective-permute-start | bytes 786440 | tf_op jit(solution)/shard_map/ppermute | solution.py:40
  21.6 3.2 %collective-permute-start.1 = (bf16[2,256,512]{2,1,0:T(8,128)(2,1)S(1)}, bf16[2,256,512]{2,1,0:T(8,128)(2,1)S(1)}, u32[]{:S(2)}, u32[]{:S(2)}) collective-permute-start(bf16[2,256,512]{2,1,0:T(8,128)(2,1)S(1)} %bitcast_dynamic-update-slice_fusion), channel_id=1, source_target_pairs={{0,2},{1,3},{2,4},{3,5},{4,6},{5,7},{6,8},{7,9},{8,10},{9,11},{10,... | collective-permute-start | bytes 1572872 | tf_op jit(solution)/shard_map/ppermute | solution.py:40
  24.8 1.8 %collective-permute-done.3.behind_ref = bf16[2,256,256]{2,1,0:T(8,128)(2,1)S(1)} collective-permute-done((bf16[2,256,256]{2,1,0:T(8,128)(2,1)S(1)}, bf16[2,256,256]{2,1,0:T(8,128)(2,1)S(1)}, u32[]{:S(2)}, u32[]{:S(2)}) %collective-permute-start.3) | collective-permute-done | bytes 262176 | tf_op jit(solution)/shard_map/ppermute | solution.py:40
  26.5 1.6 %copy-done.3 = bf16[256,4096]{1,0:T(8,128)(2,1)S(1)} copy-done((bf16[256,4096]{1,0:T(8,128)(2,1)S(1)}, bf16[256,4096]{1,0:T(8,128)(2,1)}, u32[]{:S(2)}) %copy-start.3) | copy-done | bytes 2097176
  28.1 6.6 %attention.4 = (bf16[256,4096]{1,0:T(8,128)(2,1)}, bf16[256,4096]{1,0:T(8,128)(2,1)}, bf16[2,256,256]{2,1,0:T(8,128)(2,1)S(1)}, f32[256,256]{1,0:T(8,128)S(1)}, f32[256,256]{1,0:T(8,128)S(1)}) custom-call(bf16[256,4096]{1,0:T(8,128)(2,1)S(1)} %copy-done.3, bf16[256,4096]{1,0:T(8,128)(2,1)} %g_ref.7, ...), custom_call_target="tpu_custom_call" | custom-call | flops 4831838208 | bytes 3538944 | tf_op jit(solution)/shard_map/attention/pallas_call | solution.py:243
  34.8 2.1 %collective-permute-start.5 = (bf16[2,256,256]{2,1,0:T(8,128)(2,1)S(1)}, bf16[2,256,256]{2,1,0:T(8,128)(2,1)S(1)}, u32[]{:S(2)}, u32[]{:S(2)}) collective-permute-start(bf16[2,256,256]{2,1,0:T(8,128)(2,1)S(1)} %get-tuple-element.89), channel_id=1, source_target_pairs={{2,0},{3,1},{4,2},{5,3},{6,4},{7,5},{8,6},{9,7},{10,8},{11,9},{12,... | collective-permute-start | bytes 786440 | tf_op jit(solution)/shard_map/ppermute | solution.py:40
  36.9 6.7 %attention.5 = (bf16[256,4096]{1,0:T(8,128)(2,1)}, bf16[256,4096]{1,0:T(8,128)(2,1)}, bf16[2,256,256]{2,1,0:T(8,128)(2,1)S(1)}, f32[256,256]{1,0:T(8,128)S(1)}, f32[256,256]{1,0:T(8,128)S(1)}) custom-call(bf16[256,4096]{1,0:T(8,128)(2,1)S(1)} %copy-done.3, bf16[256,4096]{1,0:T(8,128)(2,1)} %g_ref.7, ...), custom_call_target="tpu_custom_call", output_to_operand_aliasing={{0}: (8, {}), {1}: (9, {})} | custom-call | flops 4831838208 | bytes 3538944 | tf_op jit(solution)/shard_map/attention/pallas_call | solution.py:243
  43.6 2.1 %collective-permute-start.7 = (bf16[2,256,256]{2,1,0:T(8,128)(2,1)S(1)}, bf16[2,256,256]{2,1,0:T(8,128)(2,1)S(1)}, u32[]{:S(2)}, u32[]{:S(2)}) collective-permute-start(bf16[2,256,256]{2,1,0:T(8,128)(2,1)S(1)} %get-tuple-element.92), channel_id=1, source_target_pairs={{2,0},{3,1},{4,2},{5,3},{6,4},{7,5},{8,6},{9,7},{10,8},{11,9},{12,... | collective-permute-start | bytes 786440 | tf_op jit(solution)/shard_map/ppermute | solution.py:40
  45.7 0.5 collective-permute-done.1.behind_ref
  46.2 6.6 %attention.6 = (bf16[256,4096]{1,0:T(8,128)(2,1)}, bf16[256,4096]{1,0:T(8,128)(2,1)}, bf16[2,256,256]{2,1,0:T(8,128)(2,1)S(1)}, f32[256,256]{1,0:T(8,128)S(1)}, f32[256,256]{1,0:T(8,128)S(1)}) custom-call(bf16[256,4096]{1,0:T(8,128)(2,1)S(1)} %copy-done.4, bf16[256,4096]{1,0:T(8,128)(2,1)} %g_ref.7, ...), custom_call_target="tpu_custom_call", output_to_operand_aliasing={{0}: (8, {}), {1}: (9, {})} | custom-call | flops 4831838208 | bytes 3538944 | tf_op jit(solution)/shard_map/attention/pallas_call | solution.py:243
  52.9 2.7 %collective-permute-start.8 = (bf16[2,256,256]{2,1,0:T(8,128)(2,1)S(1)}, bf16[2,256,256]{2,1,0:T(8,128)(2,1)S(1)}, u32[]{:S(2)}, u32[]{:S(2)}) collective-permute-start(bf16[2,256,256]{2,1,0:T(8,128)(2,1)S(1)} %get-tuple-element.95), channel_id=1, source_target_pairs={{2,0},{3,1},{4,2},{5,3},{6,4},{7,5},{8,6},{9,7},{10,8},{11,9},{12,... | collective-permute-start | bytes 786440 | tf_op jit(solution)/shard_map/ppermute | solution.py:40
  55.5 0.4 collective-permute-done.7
  56.0 0.1 fusion.7
  56.2 6.6 %attention.7 = (bf16[256,4096]{1,0:T(8,128)(2,1)}, bf16[256,4096]{1,0:T(8,128)(2,1)}, bf16[2,256,256]{2,1,0:T(8,128)(2,1)S(1)}, f32[256,256]{1,0:T(8,128)S(1)}, f32[256,256]{1,0:T(8,128)S(1)}) custom-call(bf16[256,4096]{1,0:T(8,128)(2,1)S(1)} %copy-done.4, bf16[256,4096]{1,0:T(8,128)(2,1)} %g_ref.7, ...), custom_call_target="tpu_custom_call", output_to_operand_aliasing={{0}: (8, {}), {1}: (9, {})} | custom-call | flops 4831838208 | bytes 3538944 | tf_op jit(solution)/shard_map/attention/pallas_call | solution.py:243
  62.8 4.8 %collective-permute-start.9 = (bf16[2,256,256]{2,1,0:T(8,128)(2,1)S(1)}, bf16[2,256,256]{2,1,0:T(8,128)(2,1)S(1)}, u32[]{:S(2)}, u32[]{:S(2)}) collective-permute-start(bf16[2,256,256]{2,1,0:T(8,128)(2,1)S(1)} %get-tuple-element.111), channel_id=1, source_target_pairs={{2,0},{3,1},{4,2},{5,3},{6,4},{7,5},{8,6},{9,7},{10,8},{11,9},{12,... | collective-permute-start | bytes 786440 | tf_op jit(solution)/shard_map/ppermute | solution.py:40
  67.6 1.9 %collective-permute-start.10 = (bf16[256,512]{1,0:T(8,128)(2,1)S(1)}, bf16[256,512]{1,0:T(8,128)(2,1)S(1)}, u32[]{:S(2)}, u32[]{:S(2)}) collective-permute-start(bf16[256,512]{1,0:T(8,128)(2,1)S(1)} %pad_maximum_fusion), channel_id=1, source_target_pairs={{1,0},{2,1},{3,2},{4,3},{5,4},{6,5},{7,6},{8,7},{9,8},{10,9},{11,1... | collective-permute-start | bytes 786440 | tf_op jit(solution)/shard_map/ppermute | solution.py:40
  69.6 0.1 fusion.4
  69.7 3.5 %collective-permute-done.9 = bf16[2,256,256]{2,1,0:T(8,128)(2,1)S(1)} collective-permute-done((bf16[2,256,256]{2,1,0:T(8,128)(2,1)S(1)}, bf16[2,256,256]{2,1,0:T(8,128)(2,1)S(1)}, u32[]{:S(2)}, u32[]{:S(2)}) %collective-permute-start.9) | collective-permute-done | bytes 262176 | tf_op jit(solution)/shard_map/ppermute | solution.py:40
  73.3 4.9 %collective-permute-start.11 = (bf16[256,512]{1,0:T(8,128)(2,1)S(1)}, bf16[256,512]{1,0:T(8,128)(2,1)S(1)}, u32[]{:S(2)}, u32[]{:S(2)}) collective-permute-start(bf16[256,512]{1,0:T(8,128)(2,1)S(1)} %pad_maximum_fusion.1), channel_id=1, source_target_pairs={{1,0},{2,1},{3,2},{4,3},{5,4},{6,5},{7,6},{8,7},{9,8},{10,9},{11,1... | collective-permute-start | bytes 786440 | tf_op jit(solution)/shard_map/ppermute | solution.py:40
  78.2 4.0 %collective-permute-done.10 = bf16[256,512]{1,0:T(8,128)(2,1)S(1)} collective-permute-done((bf16[256,512]{1,0:T(8,128)(2,1)S(1)}, bf16[256,512]{1,0:T(8,128)(2,1)S(1)}, u32[]{:S(2)}, u32[]{:S(2)}) %collective-permute-start.10) | collective-permute-done | bytes 262176 | tf_op jit(solution)/shard_map/ppermute | solution.py:40
  82.2 4.8 %collective-permute-done.11 = bf16[256,512]{1,0:T(8,128)(2,1)S(1)} collective-permute-done((bf16[256,512]{1,0:T(8,128)(2,1)S(1)}, bf16[256,512]{1,0:T(8,128)(2,1)S(1)}, u32[]{:S(2)}, u32[]{:S(2)}) %collective-permute-start.11) | collective-permute-done | bytes 262176 | tf_op jit(solution)/shard_map/ppermute | solution.py:40
  87.0 0.1 fusion
  87.2 0.1 fusion.13
  87.3 0.9 pad_maximum_fusion.2
  (23 shorter events, 0.4 us)
Async XLA Ops:
  0.6 1.0 %copy-start = (bf16[256,512]{1,0:T(8,128)(2,1)S(1)}, bf16[256,512]{1,0:T(8,128)(2,1)}, u32[]{:S(2)}) copy-start(bf16[256,512]{1,0:T(8,128)(2,1)} %keys_ref.1) | copy-start | bytes 786436
  1.6 0.9 %copy-start.1 = (bf16[256,512]{1,0:T(8,128)(2,1)S(1)}, bf16[256,512]{1,0:T(8,128)(2,1)}, u32[]{:S(2)}) copy-start(bf16[256,512]{1,0:T(8,128)(2,1)} %values_ref.1) | copy-start | bytes 786436
  2.5 0.7 copy-start.2
  4.4 10.2 %collective-permute-start.2 = (bf16[256,256]{1,0:T(8,128)(2,1)S(1)}, bf16[256,256]{1,0:T(8,128)(2,1)S(1)}, u32[]{:S(2)}, u32[]{:S(2)}) collective-permute-start(bf16[256,256]{1,0:T(8,128)(2,1)S(1)} %get-tuple-element.84.own_ref), channel_id=1, source_target_pairs={{0,1},{1,2},{2,3},{3,4},{4,5},{5,6},{6,7},{7,8},{8,9},{9,10},{10,1... | collective-permute-start | bytes 393224 | tf_op jit(solution)/shard_map/ppermute | solution.py:40
  7.7 10.4 %collective-permute-start.4 = (bf16[256,256]{1,0:T(8,128)(2,1)S(1)}, bf16[256,256]{1,0:T(8,128)(2,1)S(1)}, u32[]{:S(2)}, u32[]{:S(2)}) collective-permute-start(bf16[256,256]{1,0:T(8,128)(2,1)S(1)} %get-tuple-element.83.own_ref), channel_id=1, source_target_pairs={{0,1},{1,2},{2,3},{3,4},{4,5},{5,6},{6,7},{7,8},{8,9},{9,10},{10,1... | collective-permute-start | bytes 393224 | tf_op jit(solution)/shard_map/ppermute | solution.py:40
  11.1 10.5 %collective-permute-start = (bf16[256,512]{1,0:T(8,128)(2,1)S(1)}, bf16[256,512]{1,0:T(8,128)(2,1)S(1)}, u32[]{:S(2)}, u32[]{:S(2)}) collective-permute-start(bf16[256,512]{1,0:T(8,128)(2,1)S(1)} %get-tuple-element.100.own_ref), channel_id=1, source_target_pairs={{0,1},{1,2},{2,3},{3,4},{4,5},{5,6},{6,7},{7,8},{8,9},{9,10},{10,1... | collective-permute-start | bytes 786440 | tf_op jit(solution)/shard_map/ppermute | solution.py:40
  14.6 12.0 %collective-permute-start.3 = (bf16[2,256,256]{2,1,0:T(8,128)(2,1)S(1)}, bf16[2,256,256]{2,1,0:T(8,128)(2,1)S(1)}, u32[]{:S(2)}, u32[]{:S(2)}) collective-permute-start(bf16[2,256,256]{2,1,0:T(8,128)(2,1)S(1)} %bitcast_dynamic-update-slice_fusion.2), channel_id=1, source_target_pairs={{0,2},{1,3},{2,4},{3,5},{4,6},{5,7},{6,8},{7,9},{8,10},{9,11},{10,... | collective-permute-start | bytes 786440 | tf_op jit(solution)/shard_map/ppermute | solution.py:40
  18.1 18.8 %collective-permute-start.6 = (bf16[2,256,256]{2,1,0:T(8,128)(2,1)S(1)}, bf16[2,256,256]{2,1,0:T(8,128)(2,1)S(1)}, u32[]{:S(2)}, u32[]{:S(2)}) collective-permute-start(bf16[2,256,256]{2,1,0:T(8,128)(2,1)S(1)} %bitcast_dynamic-update-slice_fusion.1), channel_id=1, source_target_pairs={{0,2},{1,3},{2,4},{3,5},{4,6},{5,7},{6,8},{7,9},{8,10},{9,11},{10,... | collective-permute-start | bytes 786440 | tf_op jit(solution)/shard_map/ppermute | solution.py:40
  21.6 24.6 %collective-permute-start.1 = (bf16[2,256,512]{2,1,0:T(8,128)(2,1)S(1)}, bf16[2,256,512]{2,1,0:T(8,128)(2,1)S(1)}, u32[]{:S(2)}, u32[]{:S(2)}) collective-permute-start(bf16[2,256,512]{2,1,0:T(8,128)(2,1)S(1)} %bitcast_dynamic-update-slice_fusion), channel_id=1, source_target_pairs={{0,2},{1,3},{2,4},{3,5},{4,6},{5,7},{6,8},{7,9},{8,10},{9,11},{10,... | collective-permute-start | bytes 1572872 | tf_op jit(solution)/shard_map/ppermute | solution.py:40
  26.5 1.6 %copy-start.3 = (bf16[256,4096]{1,0:T(8,128)(2,1)S(1)}, bf16[256,4096]{1,0:T(8,128)(2,1)}, u32[]{:S(2)}) copy-start(bf16[256,4096]{1,0:T(8,128)(2,1)} %q_ref.7) | copy-start | bytes 6291460
  34.8 20.7 %collective-permute-start.5 = (bf16[2,256,256]{2,1,0:T(8,128)(2,1)S(1)}, bf16[2,256,256]{2,1,0:T(8,128)(2,1)S(1)}, u32[]{:S(2)}, u32[]{:S(2)}) collective-permute-start(bf16[2,256,256]{2,1,0:T(8,128)(2,1)S(1)} %get-tuple-element.89), channel_id=1, source_target_pairs={{2,0},{3,1},{4,2},{5,3},{6,4},{7,5},{8,6},{9,7},{10,8},{11,9},{12,... | collective-permute-start | bytes 786440 | tf_op jit(solution)/shard_map/ppermute | solution.py:40
  36.9 9.3 %copy-start.4 = (bf16[256,4096]{1,0:T(8,128)(2,1)S(1)}, bf16[256,4096]{1,0:T(8,128)(2,1)}, u32[]{:S(2)}) copy-start(bf16[256,4096]{1,0:T(8,128)(2,1)} %q_ref.7) | copy-start | bytes 6291460
  43.6 12.3 %collective-permute-start.7 = (bf16[2,256,256]{2,1,0:T(8,128)(2,1)S(1)}, bf16[2,256,256]{2,1,0:T(8,128)(2,1)S(1)}, u32[]{:S(2)}, u32[]{:S(2)}) collective-permute-start(bf16[2,256,256]{2,1,0:T(8,128)(2,1)S(1)} %get-tuple-element.92), channel_id=1, source_target_pairs={{2,0},{3,1},{4,2},{5,3},{6,4},{7,5},{8,6},{9,7},{10,8},{11,9},{12,... | collective-permute-start | bytes 786440 | tf_op jit(solution)/shard_map/ppermute | solution.py:40
  52.9 16.7 %collective-permute-start.8 = (bf16[2,256,256]{2,1,0:T(8,128)(2,1)S(1)}, bf16[2,256,256]{2,1,0:T(8,128)(2,1)S(1)}, u32[]{:S(2)}, u32[]{:S(2)}) collective-permute-start(bf16[2,256,256]{2,1,0:T(8,128)(2,1)S(1)} %get-tuple-element.95), channel_id=1, source_target_pairs={{2,0},{3,1},{4,2},{5,3},{6,4},{7,5},{8,6},{9,7},{10,8},{11,9},{12,... | collective-permute-start | bytes 786440 | tf_op jit(solution)/shard_map/ppermute | solution.py:40
  62.8 10.4 %collective-permute-start.9 = (bf16[2,256,256]{2,1,0:T(8,128)(2,1)S(1)}, bf16[2,256,256]{2,1,0:T(8,128)(2,1)S(1)}, u32[]{:S(2)}, u32[]{:S(2)}) collective-permute-start(bf16[2,256,256]{2,1,0:T(8,128)(2,1)S(1)} %get-tuple-element.111), channel_id=1, source_target_pairs={{2,0},{3,1},{4,2},{5,3},{6,4},{7,5},{8,6},{9,7},{10,8},{11,9},{12,... | collective-permute-start | bytes 786440 | tf_op jit(solution)/shard_map/ppermute | solution.py:40
  67.6 14.6 %collective-permute-start.10 = (bf16[256,512]{1,0:T(8,128)(2,1)S(1)}, bf16[256,512]{1,0:T(8,128)(2,1)S(1)}, u32[]{:S(2)}, u32[]{:S(2)}) collective-permute-start(bf16[256,512]{1,0:T(8,128)(2,1)S(1)} %pad_maximum_fusion), channel_id=1, source_target_pairs={{1,0},{2,1},{3,2},{4,3},{5,4},{6,5},{7,6},{8,7},{9,8},{10,9},{11,1... | collective-permute-start | bytes 786440 | tf_op jit(solution)/shard_map/ppermute | solution.py:40
  73.3 13.7 %collective-permute-start.11 = (bf16[256,512]{1,0:T(8,128)(2,1)S(1)}, bf16[256,512]{1,0:T(8,128)(2,1)S(1)}, u32[]{:S(2)}, u32[]{:S(2)}) collective-permute-start(bf16[256,512]{1,0:T(8,128)(2,1)S(1)} %pad_maximum_fusion.1), channel_id=1, source_target_pairs={{1,0},{2,1},{3,2},{4,3},{5,4},{6,5},{7,6},{8,7},{9,8},{10,9},{11,1... | collective-permute-start | bytes 786440 | tf_op jit(solution)/shard_map/ppermute | solution.py:40

commit v20 on v19

--- a/solution.py
+++ b/solution.py
@@ -278,7 +278,7 @@
             + [pltpu.SemaphoreType.DMA((2 + 2 * GROUP // UNIT,))],
         ),
         input_output_aliases=aliases,
-        compiler_params=pltpu.CompilerParams(vmem_limit_bytes=48 * 1024 * 1024),
+        compiler_params=pltpu.CompilerParams(vmem_limit_bytes=51 * 1024 * 1024),
         cost_estimate=pl.CostEstimate(
             flops=12 * rows * GROUP * window * HEAD_SIZE * 2,
             bytes_accessed=4 * rows * wide * 2 + 22 * rows * pair,

time: 89.6 us -> 91.3 us (1.019)
  Pallas kernels: 27.8 us -> 31 us
  local copies, waits for them, and re-layouts: 4.29 us -> 2.69 us
    pallas_call x4, Pallas kernels: 26.6 us -> 29.9 us  [attention(): pl.pallas_call(functools.partial(attention_kernel, where), out_shape=[jax...]
    unnamed x10 -> x6, local copies, waits for them, and re-layouts: 4.14 us -> 2.55 us
  transfers between devices with their start and end apart: 12 -> 12, of which waited for: 6 -> 5; matrix products, arithmetic and copies ran while one was open for 1% -> 1% of each run, Pallas kernels for 30% -> 33%
where the time goes in v20:
time: 91.3 us; the launch traced here: 89.8 us
  starting transfers between devices  39.5 us (43%)
  Pallas kernels  31 us (34%)
  waiting for transfers between devices  14.2 us (16%)
  local copies, waits for them, and re-layouts  2.69 us (3%)
  other arithmetic  1.44 us (2%)
  between operations  0.95 us (1%)
    ppermute x12, starting transfers between devices, passed_along(): lax.ppermute(value, AXES, [(source, source + steps) for source in range(f...  39.5 us
    pallas_call x4, Pallas kernels, attention(): pl.pallas_call(functools.partial(attention_kernel, where), out_shape=[jax...  29.9 us
    ppermute x12, waiting for transfers between devices, passed_along(): lax.ppermute(value, AXES, [(source, source + steps) for source in range(f...  14.2 us
    unnamed x6, local copies, waits for them, and re-layouts  2.55 us
  transfers between devices with their start and end apart: 12, of which 5 were waited for; matrix products, arithmetic and copies ran while one was open for 1% of the time, Pallas kernels for 33%

profile of v20, /device:TPU:29, one launch (start us, length us, event | category | flops | bytes accessed | tf_op | source)
XLA Modules:
  0.0 89.8 jit_solution(10352618211009672265)
XLA Ops:
  0.6 0.9 %copy-done = bf16[256,512]{1,0:T(8,128)(2,1)S(1)} copy-done((bf16[256,512]{1,0:T(8,128)(2,1)S(1)}, bf16[256,512]{1,0:T(8,128)(2,1)}, u32[]{:S(2)}) %copy-start) | copy-done | bytes 262168
  1.6 0.9 %copy-done.1 = bf16[256,512]{1,0:T(8,128)(2,1)S(1)} copy-done((bf16[256,512]{1,0:T(8,128)(2,1)S(1)}, bf16[256,512]{1,0:T(8,128)(2,1)}, u32[]{:S(2)}) %copy-start.1) | copy-done | bytes 262168
  2.5 0.7 copy-done.2
  3.2 1.2 %pack.1 = (bf16[256,256]{1,0:T(8,128)(2,1)S(1)}, bf16[2,256,256]{2,1,0:T(8,128)(2,1)S(1)}, bf16[256,256]{1,0:T(8,128)(2,1)S(1)}, bf16[2,256,256]{2,1,0:T(8,128)(...) custom-call(s32[1]{0:T(128)} %bitcast.first_ref, ...), custom_call_target="tpu_custom_call" | custom-call | tf_op jit(solution)/shard_map/pack/pallas_call | solution.py:323
  4.4 3.3 %collective-permute-start.2 = (bf16[256,256]{1,0:T(8,128)(2,1)S(1)}, bf16[256,256]{1,0:T(8,128)(2,1)S(1)}, u32[]{:S(2)}, u32[]{:S(2)}) collective-permute-start(bf16[256,256]{1,0:T(8,128)(2,1)S(1)} %get-tuple-element.84.own_ref), channel_id=1, source_target_pairs={{0,1},{1,2},{2,3},{3,4},{4,5},{5,6},{6,7},{7,8},{8,9},{9,10},{10,1... | collective-permute-start | bytes 393224 | tf_op jit(solution)/shard_map/ppermute | solution.py:40
  7.7 3.4 %collective-permute-start.4 = (bf16[256,256]{1,0:T(8,128)(2,1)S(1)}, bf16[256,256]{1,0:T(8,128)(2,1)S(1)}, u32[]{:S(2)}, u32[]{:S(2)}) collective-permute-start(bf16[256,256]{1,0:T(8,128)(2,1)S(1)} %get-tuple-element.83.own_ref), channel_id=1, source_target_pairs={{0,1},{1,2},{2,3},{3,4},{4,5},{5,6},{6,7},{7,8},{8,9},{9,10},{10,1... | collective-permute-start | bytes 393224 | tf_op jit(solution)/shard_map/ppermute | solution.py:40
  11.1 3.4 %collective-permute-start = (bf16[256,512]{1,0:T(8,128)(2,1)S(1)}, bf16[256,512]{1,0:T(8,128)(2,1)S(1)}, u32[]{:S(2)}, u32[]{:S(2)}) collective-permute-start(bf16[256,512]{1,0:T(8,128)(2,1)S(1)} %get-tuple-element.100.own_ref), channel_id=1, source_target_pairs={{0,1},{1,2},{2,3},{3,4},{4,5},{5,6},{6,7},{7,8},{8,9},{9,10},{10,1... | collective-permute-start | bytes 786440 | tf_op jit(solution)/shard_map/ppermute | solution.py:40
  14.6 3.5 %collective-permute-start.3 = (bf16[2,256,256]{2,1,0:T(8,128)(2,1)S(1)}, bf16[2,256,256]{2,1,0:T(8,128)(2,1)S(1)}, u32[]{:S(2)}, u32[]{:S(2)}) collective-permute-start(bf16[2,256,256]{2,1,0:T(8,128)(2,1)S(1)} %bitcast_dynamic-update-slice_fusion.2), channel_id=1, source_target_pairs={{0,2},{1,3},{2,4},{3,5},{4,6},{5,7},{6,8},{7,9},{8,10},{9,11},{10,... | collective-permute-start | bytes 786440 | tf_op jit(solution)/shard_map/ppermute | solution.py:40
  18.1 3.5 %collective-permute-start.6 = (bf16[2,256,256]{2,1,0:T(8,128)(2,1)S(1)}, bf16[2,256,256]{2,1,0:T(8,128)(2,1)S(1)}, u32[]{:S(2)}, u32[]{:S(2)}) collective-permute-start(bf16[2,256,256]{2,1,0:T(8,128)(2,1)S(1)} %bitcast_dynamic-update-slice_fusion.1), channel_id=1, source_target_pairs={{0,2},{1,3},{2,4},{3,5},{4,6},{5,7},{6,8},{7,9},{8,10},{9,11},{10,... | collective-permute-start | bytes 786440 | tf_op jit(solution)/shard_map/ppermute | solution.py:40
  21.6 3.2 %collective-permute-start.1 = (bf16[2,256,512]{2,1,0:T(8,128)(2,1)S(1)}, bf16[2,256,512]{2,1,0:T(8,128)(2,1)S(1)}, u32[]{:S(2)}, u32[]{:S(2)}) collective-permute-start(bf16[2,256,512]{2,1,0:T(8,128)(2,1)S(1)} %bitcast_dynamic-update-slice_fusion), channel_id=1, source_target_pairs={{0,2},{1,3},{2,4},{3,5},{4,6},{5,7},{6,8},{7,9},{8,10},{9,11},{10,... | collective-permute-start | bytes 1572872 | tf_op jit(solution)/shard_map/ppermute | solution.py:40
  24.8 1.8 %collective-permute-done.3.behind_ref = bf16[2,256,256]{2,1,0:T(8,128)(2,1)S(1)} collective-permute-done((bf16[2,256,256]{2,1,0:T(8,128)(2,1)S(1)}, bf16[2,256,256]{2,1,0:T(8,128)(2,1)S(1)}, u32[]{:S(2)}, u32[]{:S(2)}) %collective-permute-start.3) | collective-permute-done | bytes 262176 | tf_op jit(solution)/shard_map/ppermute | solution.py:40
  26.5 7.4 %attention.4 = (bf16[256,4096]{1,0:T(8,128)(2,1)}, bf16[256,4096]{1,0:T(8,128)(2,1)}, bf16[2,256,256]{2,1,0:T(8,128)(2,1)S(1)}, f32[256,256]{1,0:T(8,128)S(1)}, f32[256,256]{1,0:T(8,128)S(1)}) custom-call(bf16[256,4096]{1,0:T(8,128)(2,1)} %q_ref.7, bf16[256,4096]{1,0:T(8,128)(2,1)} %g_ref.7, bf16[2,256,256]{2,1,0:T(8,128)(2,1)S(1)} %collective-permute-done.3.behind_ref, ...), custom_call_target="tpu_custom_call" | custom-call | flops 4831838208 | bytes 3538944 | tf_op jit(solution)/shard_map/attention/pallas_call | solution.py:243
  34.0 2.1 %collective-permute-start.5 = (bf16[2,256,256]{2,1,0:T(8,128)(2,1)S(1)}, bf16[2,256,256]{2,1,0:T(8,128)(2,1)S(1)}, u32[]{:S(2)}, u32[]{:S(2)}) collective-permute-start(bf16[2,256,256]{2,1,0:T(8,128)(2,1)S(1)} %get-tuple-element.89), channel_id=1, source_target_pairs={{2,0},{3,1},{4,2},{5,3},{6,4},{7,5},{8,6},{9,7},{10,8},{11,9},{12,... | collective-permute-start | bytes 786440 | tf_op jit(solution)/shard_map/ppermute | solution.py:40
  36.1 7.5 %attention.5 = (bf16[256,4096]{1,0:T(8,128)(2,1)}, bf16[256,4096]{1,0:T(8,128)(2,1)}, bf16[2,256,256]{2,1,0:T(8,128)(2,1)S(1)}, f32[256,256]{1,0:T(8,128)S(1)}, f32[256,256]{1,0:T(8,128)S(1)}) custom-call(bf16[256,4096]{1,0:T(8,128)(2,1)} %q_ref.7, bf16[256,4096]{1,0:T(8,128)(2,1)} %g_ref.7, ...), custom_call_target="tpu_custom_call", output_to_operand_aliasing={{0}: (8, {}), {1}: (9, {})} | custom-call | flops 4831838208 | bytes 3538944 | tf_op jit(solution)/shard_map/attention/pallas_call | solution.py:243
  43.6 2.1 %collective-permute-start.7 = (bf16[2,256,256]{2,1,0:T(8,128)(2,1)S(1)}, bf16[2,256,256]{2,1,0:T(8,128)(2,1)S(1)}, u32[]{:S(2)}, u32[]{:S(2)}) collective-permute-start(bf16[2,256,256]{2,1,0:T(8,128)(2,1)S(1)} %get-tuple-element.92), channel_id=1, source_target_pairs={{2,0},{3,1},{4,2},{5,3},{6,4},{7,5},{8,6},{9,7},{10,8},{11,9},{12,... | collective-permute-start | bytes 786440 | tf_op jit(solution)/shard_map/ppermute | solution.py:40
  45.7 0.5 collective-permute-done.1.behind_ref
  46.2 7.5 %attention.6 = (bf16[256,4096]{1,0:T(8,128)(2,1)}, bf16[256,4096]{1,0:T(8,128)(2,1)}, bf16[2,256,256]{2,1,0:T(8,128)(2,1)S(1)}, f32[256,256]{1,0:T(8,128)S(1)}, f32[256,256]{1,0:T(8,128)S(1)}) custom-call(bf16[256,4096]{1,0:T(8,128)(2,1)} %q_ref.7, bf16[256,4096]{1,0:T(8,128)(2,1)} %g_ref.7, ...), custom_call_target="tpu_custom_call", output_to_operand_aliasing={{0}: (8, {}), {1}: (9, {})} | custom-call | flops 4831838208 | bytes 3538944 | tf_op jit(solution)/shard_map/attention/pallas_call | solution.py:243
  53.7 2.7 %collective-permute-start.8 = (bf16[2,256,256]{2,1,0:T(8,128)(2,1)S(1)}, bf16[2,256,256]{2,1,0:T(8,128)(2,1)S(1)}, u32[]{:S(2)}, u32[]{:S(2)}) collective-permute-start(bf16[2,256,256]{2,1,0:T(8,128)(2,1)S(1)} %get-tuple-element.95), channel_id=1, source_target_pairs={{2,0},{3,1},{4,2},{5,3},{6,4},{7,5},{8,6},{9,7},{10,8},{11,9},{12,... | collective-permute-start | bytes 786440 | tf_op jit(solution)/shard_map/ppermute | solution.py:40
  56.5 0.1 fusion.7
  56.5 0.1 fusion.8
  56.6 7.5 %attention.7 = (bf16[256,4096]{1,0:T(8,128)(2,1)}, bf16[256,4096]{1,0:T(8,128)(2,1)}, bf16[2,256,256]{2,1,0:T(8,128)(2,1)S(1)}, f32[256,256]{1,0:T(8,128)S(1)}, f32[256,256]{1,0:T(8,128)S(1)}) custom-call(bf16[256,4096]{1,0:T(8,128)(2,1)} %q_ref.7, bf16[256,4096]{1,0:T(8,128)(2,1)} %g_ref.7, ...), custom_call_target="tpu_custom_call", output_to_operand_aliasing={{0}: (8, {}), {1}: (9, {})} | custom-call | flops 4831838208 | bytes 3538944 | tf_op jit(solution)/shard_map/attention/pallas_call | solution.py:243
  64.1 5.2 %collective-permute-start.9 = (bf16[2,256,256]{2,1,0:T(8,128)(2,1)S(1)}, bf16[2,256,256]{2,1,0:T(8,128)(2,1)S(1)}, u32[]{:S(2)}, u32[]{:S(2)}) collective-permute-start(bf16[2,256,256]{2,1,0:T(8,128)(2,1)S(1)} %get-tuple-element.111), channel_id=1, source_target_pairs={{2,0},{3,1},{4,2},{5,3},{6,4},{7,5},{8,6},{9,7},{10,8},{11,9},{12,... | collective-permute-start | bytes 786440 | tf_op jit(solution)/shard_map/ppermute | solution.py:40
  69.3 1.9 %collective-permute-start.10 = (bf16[256,512]{1,0:T(8,128)(2,1)S(1)}, bf16[256,512]{1,0:T(8,128)(2,1)S(1)}, u32[]{:S(2)}, u32[]{:S(2)}) collective-permute-start(bf16[256,512]{1,0:T(8,128)(2,1)S(1)} %pad_maximum_fusion), channel_id=1, source_target_pairs={{1,0},{2,1},{3,2},{4,3},{5,4},{6,5},{7,6},{8,7},{9,8},{10,9},{11,1... | collective-permute-start | bytes 786440 | tf_op jit(solution)/shard_map/ppermute | solution.py:40
  71.3 0.1 fusion.4
  71.4 3.1 %collective-permute-done.9 = bf16[2,256,256]{2,1,0:T(8,128)(2,1)S(1)} collective-permute-done((bf16[2,256,256]{2,1,0:T(8,128)(2,1)S(1)}, bf16[2,256,256]{2,1,0:T(8,128)(2,1)S(1)}, u32[]{:S(2)}, u32[]{:S(2)}) %collective-permute-start.9) | collective-permute-done | bytes 262176 | tf_op jit(solution)/shard_map/ppermute | solution.py:40
  74.5 0.1 fusion.2
  74.6 5.2 %collective-permute-start.11 = (bf16[256,512]{1,0:T(8,128)(2,1)S(1)}, bf16[256,512]{1,0:T(8,128)(2,1)S(1)}, u32[]{:S(2)}, u32[]{:S(2)}) collective-permute-start(bf16[256,512]{1,0:T(8,128)(2,1)S(1)} %pad_maximum_fusion.1), channel_id=1, source_target_pairs={{1,0},{2,1},{3,2},{4,3},{5,4},{6,5},{7,6},{8,7},{9,8},{10,9},{11,1... | collective-permute-start | bytes 786440 | tf_op jit(solution)/shard_map/ppermute | solution.py:40
  79.9 4.0 %collective-permute-done.10 = bf16[256,512]{1,0:T(8,128)(2,1)S(1)} collective-permute-done((bf16[256,512]{1,0:T(8,128)(2,1)S(1)}, bf16[256,512]{1,0:T(8,128)(2,1)S(1)}, u32[]{:S(2)}, u32[]{:S(2)}) %collective-permute-start.10) | collective-permute-done | bytes 262176 | tf_op jit(solution)/shard_map/ppermute | solution.py:40
  83.8 4.8 %collective-permute-done.11 = bf16[256,512]{1,0:T(8,128)(2,1)S(1)} collective-permute-done((bf16[256,512]{1,0:T(8,128)(2,1)S(1)}, bf16[256,512]{1,0:T(8,128)(2,1)S(1)}, u32[]{:S(2)}, u32[]{:S(2)}) %collective-permute-start.11) | collective-permute-done | bytes 262176 | tf_op jit(solution)/shard_map/ppermute | solution.py:40
  88.7 0.1 fusion
  88.8 0.1 fusion.13
  88.9 0.9 pad_maximum_fusion.2
  (19 shorter events, 0.3 us)
Async XLA Ops:
  0.6 1.0 %copy-start = (bf16[256,512]{1,0:T(8,128)(2,1)S(1)}, bf16[256,512]{1,0:T(8,128)(2,1)}, u32[]{:S(2)}) copy-start(bf16[256,512]{1,0:T(8,128)(2,1)} %keys_ref.1) | copy-start | bytes 786436
  1.6 0.9 %copy-start.1 = (bf16[256,512]{1,0:T(8,128)(2,1)S(1)}, bf16[256,512]{1,0:T(8,128)(2,1)}, u32[]{:S(2)}) copy-start(bf16[256,512]{1,0:T(8,128)(2,1)} %values_ref.1) | copy-start | bytes 786436
  2.5 0.7 copy-start.2
  4.4 10.2 %collective-permute-start.2 = (bf16[256,256]{1,0:T(8,128)(2,1)S(1)}, bf16[256,256]{1,0:T(8,128)(2,1)S(1)}, u32[]{:S(2)}, u32[]{:S(2)}) collective-permute-start(bf16[256,256]{1,0:T(8,128)(2,1)S(1)} %get-tuple-element.84.own_ref), channel_id=1, source_target_pairs={{0,1},{1,2},{2,3},{3,4},{4,5},{5,6},{6,7},{7,8},{8,9},{9,10},{10,1... | collective-permute-start | bytes 393224 | tf_op jit(solution)/shard_map/ppermute | solution.py:40
  7.7 10.4 %collective-permute-start.4 = (bf16[256,256]{1,0:T(8,128)(2,1)S(1)}, bf16[256,256]{1,0:T(8,128)(2,1)S(1)}, u32[]{:S(2)}, u32[]{:S(2)}) collective-permute-start(bf16[256,256]{1,0:T(8,128)(2,1)S(1)} %get-tuple-element.83.own_ref), channel_id=1, source_target_pairs={{0,1},{1,2},{2,3},{3,4},{4,5},{5,6},{6,7},{7,8},{8,9},{9,10},{10,1... | collective-permute-start | bytes 393224 | tf_op jit(solution)/shard_map/ppermute | solution.py:40
  11.1 10.5 %collective-permute-start = (bf16[256,512]{1,0:T(8,128)(2,1)S(1)}, bf16[256,512]{1,0:T(8,128)(2,1)S(1)}, u32[]{:S(2)}, u32[]{:S(2)}) collective-permute-start(bf16[256,512]{1,0:T(8,128)(2,1)S(1)} %get-tuple-element.100.own_ref), channel_id=1, source_target_pairs={{0,1},{1,2},{2,3},{3,4},{4,5},{5,6},{6,7},{7,8},{8,9},{9,10},{10,1... | collective-permute-start | bytes 786440 | tf_op jit(solution)/shard_map/ppermute | solution.py:40
  14.6 12.0 %collective-permute-start.3 = (bf16[2,256,256]{2,1,0:T(8,128)(2,1)S(1)}, bf16[2,256,256]{2,1,0:T(8,128)(2,1)S(1)}, u32[]{:S(2)}, u32[]{:S(2)}) collective-permute-start(bf16[2,256,256]{2,1,0:T(8,128)(2,1)S(1)} %bitcast_dynamic-update-slice_fusion.2), channel_id=1, source_target_pairs={{0,2},{1,3},{2,4},{3,5},{4,6},{5,7},{6,8},{7,9},{8,10},{9,11},{10,... | collective-permute-start | bytes 786440 | tf_op jit(solution)/shard_map/ppermute | solution.py:40
  18.1 18.0 %collective-permute-start.6 = (bf16[2,256,256]{2,1,0:T(8,128)(2,1)S(1)}, bf16[2,256,256]{2,1,0:T(8,128)(2,1)S(1)}, u32[]{:S(2)}, u32[]{:S(2)}) collective-permute-start(bf16[2,256,256]{2,1,0:T(8,128)(2,1)S(1)} %bitcast_dynamic-update-slice_fusion.1), channel_id=1, source_target_pairs={{0,2},{1,3},{2,4},{3,5},{4,6},{5,7},{6,8},{7,9},{8,10},{9,11},{10,... | collective-permute-start | bytes 786440 | tf_op jit(solution)/shard_map/ppermute | solution.py:40
  21.6 24.6 %collective-permute-start.1 = (bf16[2,256,512]{2,1,0:T(8,128)(2,1)S(1)}, bf16[2,256,512]{2,1,0:T(8,128)(2,1)S(1)}, u32[]{:S(2)}, u32[]{:S(2)}) collective-permute-start(bf16[2,256,512]{2,1,0:T(8,128)(2,1)S(1)} %bitcast_dynamic-update-slice_fusion), channel_id=1, source_target_pairs={{0,2},{1,3},{2,4},{3,5},{4,6},{5,7},{6,8},{7,9},{8,10},{9,11},{10,... | collective-permute-start | bytes 1572872 | tf_op jit(solution)/shard_map/ppermute | solution.py:40
  34.0 22.4 %collective-permute-start.5 = (bf16[2,256,256]{2,1,0:T(8,128)(2,1)S(1)}, bf16[2,256,256]{2,1,0:T(8,128)(2,1)S(1)}, u32[]{:S(2)}, u32[]{:S(2)}) collective-permute-start(bf16[2,256,256]{2,1,0:T(8,128)(2,1)S(1)} %get-tuple-element.89), channel_id=1, source_target_pairs={{2,0},{3,1},{4,2},{5,3},{6,4},{7,5},{8,6},{9,7},{10,8},{11,9},{12,... | collective-permute-start | bytes 786440 | tf_op jit(solution)/shard_map/ppermute | solution.py:40
  43.6 12.8 %collective-permute-start.7 = (bf16[2,256,256]{2,1,0:T(8,128)(2,1)S(1)}, bf16[2,256,256]{2,1,0:T(8,128)(2,1)S(1)}, u32[]{:S(2)}, u32[]{:S(2)}) collective-permute-start(bf16[2,256,256]{2,1,0:T(8,128)(2,1)S(1)} %get-tuple-element.92), channel_id=1, source_target_pairs={{2,0},{3,1},{4,2},{5,3},{6,4},{7,5},{8,6},{9,7},{10,8},{11,9},{12,... | collective-permute-start | bytes 786440 | tf_op jit(solution)/shard_map/ppermute | solution.py:40
  53.7 17.5 %collective-permute-start.8 = (bf16[2,256,256]{2,1,0:T(8,128)(2,1)S(1)}, bf16[2,256,256]{2,1,0:T(8,128)(2,1)S(1)}, u32[]{:S(2)}, u32[]{:S(2)}) collective-permute-start(bf16[2,256,256]{2,1,0:T(8,128)(2,1)S(1)} %get-tuple-element.95), channel_id=1, source_target_pairs={{2,0},{3,1},{4,2},{5,3},{6,4},{7,5},{8,6},{9,7},{10,8},{11,9},{12,... | collective-permute-start | bytes 786440 | tf_op jit(solution)/shard_map/ppermute | solution.py:40
  64.1 10.4 %collective-permute-start.9 = (bf16[2,256,256]{2,1,0:T(8,128)(2,1)S(1)}, bf16[2,256,256]{2,1,0:T(8,128)(2,1)S(1)}, u32[]{:S(2)}, u32[]{:S(2)}) collective-permute-start(bf16[2,256,256]{2,1,0:T(8,128)(2,1)S(1)} %get-tuple-element.111), channel_id=1, source_target_pairs={{2,0},{3,1},{4,2},{5,3},{6,4},{7,5},{8,6},{9,7},{10,8},{11,9},{12,... | collective-permute-start | bytes 786440 | tf_op jit(solution)/shard_map/ppermute | solution.py:40
  69.3 14.6 %collective-permute-start.10 = (bf16[256,512]{1,0:T(8,128)(2,1)S(1)}, bf16[256,512]{1,0:T(8,128)(2,1)S(1)}, u32[]{:S(2)}, u32[]{:S(2)}) collective-permute-start(bf16[256,512]{1,0:T(8,128)(2,1)S(1)} %pad_maximum_fusion), channel_id=1, source_target_pairs={{1,0},{2,1},{3,2},{4,3},{5,4},{6,5},{7,6},{8,7},{9,8},{10,9},{11,1... | collective-permute-start | bytes 786440 | tf_op jit(solution)/shard_map/ppermute | solution.py:40
  74.6 14.0 %collective-permute-start.11 = (bf16[256,512]{1,0:T(8,128)(2,1)S(1)}, bf16[256,512]{1,0:T(8,128)(2,1)S(1)}, u32[]{:S(2)}, u32[]{:S(2)}) collective-permute-start(bf16[256,512]{1,0:T(8,128)(2,1)S(1)} %pad_maximum_fusion.1), channel_id=1, source_target_pairs={{1,0},{2,1},{3,2},{4,3},{5,4},{6,5},{7,6},{8,7},{9,8},{10,9},{11,1... | collective-permute-start | bytes 786440 | tf_op jit(solution)/shard_map/ppermute | solution.py:40
